TPU v7x, 32 devices: a whole 2x2x4 slice. The times are simulated.
32 devices in a mesh: dp: 2 (over x), lon: 8 (over z, core), mp: 2 (over y).
Axes of the slice: x: 2, y: 2, z: 4, core: 2. Of those that a mesh axis runs over, the one named last changes fastest.
Arguments:
- dataset: float32 [12, 48, 128, 32], P(None, None, None, 'lon'), may hold values from -22 to 22
- indices: int32 [4], P('dp'), may hold values from 0 to 11, as said below
- run_count: float32 [48], replicated, may hold values from 4096 to 16384
- run_mean: float32 [48], replicated, may hold values from -2 to 2
- run_var: float32 [48], replicated, may hold values from 0.3 to 6
- w_embed: bfloat16 [192, 1024], replicated, may hold values from -0.4375 to 0.4375
- pos_embed: bfloat16 [1024, 1024], P('lon'), may hold values from -3 to 3
- gains: float32 [2, 1024], replicated, may hold values from 0.1 to 1.9
- w_qkv: bfloat16 [3, 1024, 1024], P(None, None, 'mp'), may hold values from -0.1875 to 0.1875
- w_out: bfloat16 [1024, 1024], P('mp'), may hold values from -1 to 1
- w_up: bfloat16 [1024, 4096], P(None, 'mp'), may hold values from -0.1875 to 0.1875
- w_down: bfloat16 [4096, 1024], P('mp'), may hold values from -0.09375 to 0.09375
- w_head: bfloat16 [1024, 192], replicated, may hold values from -0.1875 to 0.1875
- cotangent: float32 [4, 1024, 192], P('dp', 'lon'), may hold values from -6 to 6
Outputs:
- pred: float32 [4, 1024, 192], P('dp', 'lon')
- new_count: float32 [48], replicated
- new_mean: float32 [48], replicated
- new_var: float32 [48], replicated
- grad_fields: float32 [4, 48, 128, 32], P('dp', None, None, 'lon')
- grad_embed: float32 [192, 1024], P(None, ('dp', 'lon'))
- grad_pos: float32 [1024, 1024], P('lon', 'dp')
- grad_gains: float32 [2, 1024], P(None, ('dp', 'lon'))
- grad_qkv: float32 [3, 1024, 1024], P(None, ('dp', 'lon'), 'mp')
- grad_out: float32 [1024, 1024], P('mp', ('dp', 'lon'))
- grad_up: float32 [1024, 4096], P(('dp', 'lon'), 'mp')
- grad_down: float32 [4096, 1024], P('mp', ('dp', 'lon'))
- grad_head: float32 [1024, 192], P(('dp', 'lon'))
Inputs may be any that keep to these rules, and one draw needn't show every extreme that they name: The 4 indices name different items.
All inputs are finite; a program needn't handle non-finite values.
Results may differ from a plain program's by a relative error of at most 0.024.
Values may be sent and summed in bfloat16 or wider, within the bound.
No kernel may reach another device: no remote copies, remote signals or barrier semaphores. Data moves between devices by JAX's collectives and lax.ppermute only.
A program may use at most 256 MiB of HBM per device.

v0:
```python
import functools
import math

import jax
import jax.numpy as jnp
from jax import lax
from jax.experimental import pallas as pl
from jax.experimental.pallas import tpu as pltpu
from jax.sharding import PartitionSpec as P

HDIM = 64
PATCH = 2
LANES = 128
NORM_EPS = 1e-06
STAT_EPS = 1e-06
BF = jnp.bfloat16
F32 = jnp.float32
MIB = 2**20


def swap(block, axis, distance):
    route = [(i, i ^ distance) for i in range(lax.axis_size(axis))]
    return lax.ppermute(block, axis, route)


def from_behind(block, axis, distance):
    size = lax.axis_size(axis)
    route = [((i - distance) % size, i) for i in range(size)]
    return lax.ppermute(block, axis, route)


def pick(x, index, axis):
    return lax.dynamic_index_in_dim(x, index, axis, keepdims=False)


def halve(total, dims):
    for axis, bit in dims:
        side = (lax.axis_index(axis) // bit) % 2
        got = swap(pick(total, 1 - side, 0), axis, bit)
        total = (pick(total, side, 0).astype(F32) + got.astype(F32)).astype(BF)
    return total


def scatter(total):
    dp, lon = lax.axis_size("dp"), lax.axis_size("lon")
    dims = []
    for axis, size in (("dp", dp), ("lon", lon)):
        bit = size // 2
        while bit:
            dims.append((axis, bit))
            bit //= 2
    rows, columns = total.shape
    total = total.astype(BF).reshape((2,) * len(dims) + (rows // (dp * lon), columns))
    order = sorted(range(len(dims)), key=lambda i: (dims[i][1] > 1 or dims[i][0] == "dp", i))
    total = total.transpose([*order, len(dims), len(dims) + 1])
    return halve(total, [dims[i] for i in order]).astype(F32)


def nt(a, b):
    return lax.dot_general(a, b, (((1,), (1,)), ((), ())), preferred_element_type=F32)


def nn(a, b):
    return lax.dot_general(a, b, (((1,), (0,)), ((), ())), preferred_element_type=F32)


def item_mask(rows, lanes, item):
    lane = lax.broadcasted_iota(jnp.int32, (rows, lanes), 1)
    return (lane >= item * HDIM) & (lane < (item + 1) * HDIM)


def interleave(first, second):
    low = item_mask(first.shape[0], LANES, 0)
    return (
        jnp.where(low, first, pltpu.roll(second, HDIM, 1)),
        jnp.where(low, pltpu.roll(first, HDIM, 1), second),
    )


def norm_parts(hidden):
    centred = hidden - jnp.mean(hidden, axis=-1, keepdims=True)
    variance = jnp.mean(centred * centred, axis=-1, keepdims=True)
    inverse = lax.rsqrt(variance + NORM_EPS)
    return centred * inverse, inverse


def norm_back(unit, inverse, scaling, grad):
    scaled = grad * scaling
    back = inverse * (
        scaled
        - jnp.mean(scaled, axis=-1, keepdims=True)
        - unit * jnp.mean(scaled * unit, axis=-1, keepdims=True)
    )
    return back, jnp.sum(grad * unit, axis=0, keepdims=True)


def emit_turned(x, ids_ref, outs, hold):
    turned = x.T.astype(BF)
    if len(outs) == 1:
        outs[0][...] = turned
        return
    keep, send = outs
    parts, rows, tokens = keep.shape
    hold[...] = turned.reshape(parts, 2, rows, tokens)
    core = ids_ref[0]
    keep[...] = hold[:, pl.ds(core, 1)].reshape(parts, rows, tokens)
    send[...] = hold[:, pl.ds(1 - core, 1)].reshape(parts, rows, tokens)


def call(body, name, outs, *args, grid=(), in_specs=None, out_specs=None, scratch=(), limit=24, flops=0):
    vmem = pl.BlockSpec(memory_space=pltpu.VMEM)
    smem = pl.BlockSpec(memory_space=pltpu.SMEM)
    if in_specs is None:
        in_specs = [smem if a.dtype == jnp.int32 else vmem for a in args]
    if out_specs is None:
        out_specs = [vmem] * len(outs)
    nbytes = sum(math.prod(a.shape) * a.dtype.itemsize for a in [*args, *outs])
    return pl.pallas_call(
        body,
        grid=grid,
        out_shape=list(outs),
        in_specs=in_specs,
        out_specs=out_specs,
        scratch_shapes=list(scratch),
        compiler_params=pltpu.CompilerParams(vmem_limit_bytes=limit * MIB),
        cost_estimate=pl.CostEstimate(flops=int(flops), bytes_accessed=nbytes, transcendentals=0),
        name=name,
    )(*args)


def shape(dims, kind=BF):
    return jax.ShapeDtypeStruct(dims, kind)


def start_kernel(local_count, ids_ref, mom_ref, run_ref, fields_ref, edge_ref, we_ref, pos_ref, gains_ref, wq_ref,
                 stats_ref, hidden_ref, patches_ref, qkv_ref, *rest):
    turned, (column_ref, hold) = rest[:-2], rest[-2:]
    members = mom_ref.shape[0]
    items, rows, height = fields_ref.shape
    variables = edge_ref.shape[1]
    cols = rows // variables
    half = height // PATCH
    moments = mom_ref[...]
    batch_count = local_count * members
    batch_mean = jnp.sum(moments, axis=0, keepdims=True) * (1.0 / members)
    off = moments - batch_mean
    spread = jnp.sum(pltpu.roll(moments, HDIM, 1) + local_count * off * off, axis=0, keepdims=True)
    run_count, run_mean, run_var = (run_ref[k : k + 1, :] for k in range(3))
    new_count = run_count + batch_count
    shift = batch_mean - run_mean
    new_mean = run_mean + shift * (batch_count / new_count)
    new_var = (
        run_var * run_count + spread + shift * shift * (run_count * batch_count / new_count)
    ) / new_count
    stats_ref[0:1, :] = new_count
    stats_ref[1:2, :] = new_mean
    stats_ref[2:3, :] = new_var
    column_ref[...] = jnp.zeros_like(column_ref)
    column_ref[0:1, :] = new_mean
    column_ref[1:2, :] = lax.rsqrt(new_var + STAT_EPS)
    column = column_ref[...].T
    centre, inverse = column[0:variables, 0:1], column[0:variables, 1:2]

    def scaled(block):
        return ((block - centre) * inverse).astype(BF)

    row = lax.broadcasted_iota(jnp.int32, (2 * height, LANES), 0)
    lane = lax.broadcasted_iota(jnp.int32, (2 * height, LANES), 1)
    sort = [
        jnp.where(
            (row // height == lane // half) & (row % height == PATCH * (lane % half) + a), 1.0, 0.0
        ).astype(BF)
        for a in range(PATCH)
    ]
    features = PATCH * PATCH * variables
    out = lax.broadcasted_iota(jnp.int32, (features, features), 0)
    src = lax.broadcasted_iota(jnp.int32, (features, features), 1)
    natural = jnp.where(
        (out // 4 == src % variables) & (out % 4 == src // variables), 1.0, 0.0
    ).astype(BF)
    hidden = []
    for item in range(items):
        west = scaled(edge_ref[item].astype(F32))
        own = [
            scaled(fields_ref[item, pl.ds(c, variables, stride=cols), :]) for c in range(cols - 1)
        ]
        first = jnp.concatenate([west, own[0]], axis=0)
        second = jnp.concatenate([own[1], own[2]], axis=0)
        both = jnp.concatenate([first, second], axis=1)
        patches = jnp.concatenate([nn(both, sort[a]) for a in range(PATCH)], axis=0)
        patches_ref[:, item * LANES : (item + 1) * LANES] = nn(natural, patches.astype(BF)).astype(BF)
        hidden.append(nn(patches.T.astype(BF), we_ref[...]) + pos_ref[...].astype(F32))
    hidden = jnp.concatenate(hidden, axis=0)
    hidden_ref[...] = hidden
    unit, _ = norm_parts(hidden)
    normed = unit * gains_ref[0:1, :]
    low = normed.astype(BF)
    emit_turned(normed, ids_ref, turned, hold)
    for c in range(3):
        product = nn(low, wq_ref[c])
        for t in range(product.shape[1] // LANES):
            tile = product[:, t * LANES : (t + 1) * LANES]
            a, b = interleave(tile[:LANES], tile[LANES:])
            qkv_ref[2 * t, c] = a.astype(BF)
            qkv_ref[2 * t + 1, c] = b.astype(BF)


def cotangent_kernel(ids_ref, ct_ref, wh_ref, wd_ref, two_ref, act_ref, low_ref, *rest):
    turned, hold = rest[:-1], rest[-1]
    grads = []
    low_ref[...] = jnp.zeros_like(low_ref)
    for item in range(ct_ref.shape[0]):
        ct = ct_ref[item].T.astype(BF)
        low_ref[item * LANES : (item + 1) * LANES, 0 : ct.shape[1]] = ct
        grads.append(nn(ct, wh_ref[...]))
    d_two = jnp.concatenate(grads, axis=0)
    two_ref[...] = d_two
    emit_turned(d_two, ids_ref, turned, hold)
    act_ref[...] = nt(d_two.astype(BF), wd_ref[...])


def attend_kernel(items, scale, q_ref, kv_ref, o_ref, ot_ref, pt_ref, vt_ref):
    keys = kv_ref.shape[0] * kv_ref.shape[2]

    @pl.when(pl.program_id(0) == 0)
    def _():
        vt_ref[...] = kv_ref[:, 2].reshape(keys, LANES).astype(F32).T.astype(BF)

    rows = q_ref.shape[0] * q_ref.shape[2]
    queries = q_ref[:, 0].reshape(rows, LANES) * BF(scale)
    key_rows = kv_ref[:, 1].reshape(keys, LANES)
    for item in range(items):
        chosen = jnp.where(item_mask(rows, LANES, item), queries, BF(0))
        scores = nt(key_rows, chosen)
        top = jnp.max(scores, axis=0, keepdims=True)
        raised = jnp.exp(scores - top)
        total = jnp.sum(raised, axis=0, keepdims=True)
        weights = (raised * (1.0 / total)).astype(BF)
        pt_ref[item] = weights
        span = slice(item * HDIM, (item + 1) * HDIM)
        ot_ref[span, :] = nn(vt_ref[span, :], weights)
    o_ref[...] = ot_ref[...].T.astype(BF).reshape(o_ref.shape)


def attend(q, kv, items, scale):
    peers, _, tokens, lanes = q.shape
    rows, keys = peers * tokens, kv.shape[0] * tokens
    step = max(1, min(peers, 256 * 1024 // keys // tokens))
    block = step * tokens
    return call(
        functools.partial(attend_kernel, items, scale),
        "attend",
        [shape((peers, tokens, lanes)), shape((lanes, rows), F32), shape((items, keys, rows))],
        q,
        kv,
        grid=(peers // step,),
        in_specs=[
            pl.BlockSpec((step, 3, tokens, lanes), lambda j: (j, 0, 0, 0)),
            pl.BlockSpec(kv.shape, lambda j: (0, 0, 0, 0)),
        ],
        out_specs=[
            pl.BlockSpec((step, tokens, lanes), lambda j: (j, 0, 0)),
            pl.BlockSpec((lanes, block), lambda j: (0, j)),
            pl.BlockSpec((items, keys, block), lambda j: (0, 0, j)),
        ],
        scratch=[pltpu.VMEM((lanes, keys), BF)],
        limit=24 if keys <= 2048 else 56,
        flops=8 * rows * keys * lanes,
    )


def attend_back_kernel(items, scale, q_ref, kv_ref, d_ref, ot_ref, pt_ref, dq_ref, *rest):
    dkv_ref, (kt_ref, dqt_ref, dk_sum, dv_sum) = rest[:-4], rest[-4:]
    step = pl.program_id(0)
    keys = kv_ref.shape[0] * kv_ref.shape[2]

    @pl.when(step == 0)
    def _():
        kt_ref[...] = (kv_ref[:, 1].reshape(keys, LANES).astype(F32) * scale).T.astype(BF)
        dk_sum[...] = jnp.zeros_like(dk_sum)
        dv_sum[...] = jnp.zeros_like(dv_sum)

    peers, _, tokens, _ = q_ref.shape
    rows = peers * tokens
    queries = q_ref[:, 0].reshape(rows, LANES) * BF(scale)
    grads = d_ref[...].reshape(rows, LANES)
    value_rows = kv_ref[:, 2].reshape(keys, LANES)
    product = grads.astype(F32).T * ot_ref[...]
    for item in range(items):
        span = slice(item * HDIM, (item + 1) * HDIM)
        mask = item_mask(rows, LANES, item)
        grad = jnp.where(mask, grads, BF(0))
        query = jnp.where(mask, queries, BF(0))
        delta = jnp.sum(product[span, :], axis=0, keepdims=True)
        weights = pt_ref[item]
        back = (weights.astype(F32) * (nt(value_rows, grad) - delta)).astype(BF)
        dv_sum[...] += nn(weights, grad)
        dk_sum[...] += nn(back, query)
        dqt_ref[span, :] = nn(kt_ref[span, :], back)
    d_query = dqt_ref[...].T.astype(BF).reshape(peers, tokens, LANES)
    if dkv_ref:
        dq_ref[...] = d_query
    else:
        dq_ref[pl.ds(step * peers, peers), 0] = d_query

    @pl.when(step == pl.num_programs(0) - 1)
    def _():
        for c, total in ((1, dk_sum), (2, dv_sum)):
            total = total[...].reshape(kv_ref.shape[0], tokens, LANES)
            if dkv_ref:
                dkv_ref[0][:, c - 1] = total
            else:
                dq_ref[:, c] = total.astype(BF)


def attend_back(q, kv, d, ot, pt, items, scale):
    peers, _, tokens, lanes = q.shape
    rows, keys = peers * tokens, kv.shape[0] * tokens
    step = max(1, min(peers, 256 * 1024 // keys // tokens))
    block = step * tokens
    if q.shape == kv.shape:
        outs = [shape(q.shape)]
        out_specs = [pl.BlockSpec(q.shape, lambda j: (0, 0, 0, 0))]
    else:
        outs = [shape((peers, tokens, lanes)), shape((kv.shape[0], 2, tokens, lanes), F32)]
        out_specs = [
            pl.BlockSpec((step, tokens, lanes), lambda j: (j, 0, 0)),
            pl.BlockSpec(outs[1].shape, lambda j: (0, 0, 0, 0)),
        ]
    return call(
        functools.partial(attend_back_kernel, items, scale),
        "attend_back",
        outs,
        q,
        kv,
        d,
        ot,
        pt,
        grid=(peers // step,),
        in_specs=[
            pl.BlockSpec((step, 3, tokens, lanes), lambda j: (j, 0, 0, 0)),
            pl.BlockSpec(kv.shape, lambda j: (0, 0, 0, 0)),
            pl.BlockSpec((step, tokens, lanes), lambda j: (j, 0, 0)),
            pl.BlockSpec((lanes, block), lambda j: (0, j)),
            pl.BlockSpec((items, keys, block), lambda j: (0, 0, j)),
        ],
        out_specs=out_specs,
        scratch=[
            pltpu.VMEM((lanes, keys), BF),
            pltpu.VMEM((lanes, block), F32),
            pltpu.VMEM((keys, lanes), F32),
            pltpu.VMEM((keys, lanes), F32),
        ],
        limit=24 if keys <= 2048 else 60,
        flops=16 * rows * keys * lanes,
    )


def unpack(blocks_ref, index, out_ref, base):
    heads = blocks_ref.shape[0]
    for t in range(heads // 2):
        pair = [
            (blocks_ref[2 * t + s] if index is None else blocks_ref[2 * t + s, index]).astype(F32)
            for s in range(2)
        ]
        for item, tile in enumerate(interleave(*pair)):
            out_ref[item * LANES : (item + 1) * LANES, base + t * LANES : base + (t + 1) * LANES] = (
                tile.astype(BF)
            )


def pack(product, out_ref):
    for t in range(product.shape[1] // LANES):
        tile = product[:, t * LANES : (t + 1) * LANES]
        for s, block in enumerate(interleave(tile[:LANES], tile[LANES:])):
            out_ref[2 * t + s] = block.astype(BF)


def project_kernel(o_ref, wo_ref, mixed_ref, branch_ref):
    unpack(o_ref, None, mixed_ref, 0)
    branch_ref[...] = nn(mixed_ref[...], wo_ref[...]).astype(BF)


def forward_kernel(ids_ref, zero_ref, own_ref, got_ref, gains_ref, wu_ref, dact_ref,
                   one_ref, norm_ref, pre_ref, act_ref, *rest):
    turned, (normed_ref, total_ref, hold) = rest[:-3], rest[-3:]
    step = pl.program_id(0)

    @pl.when(step == 0)
    def _():
        hidden = zero_ref[...] + (own_ref[...].astype(F32) + got_ref[...].astype(F32))
        one_ref[...] = hidden
        unit, _ = norm_parts(hidden)
        normed = unit * gains_ref[1:2, :]
        normed_ref[...] = normed.astype(BF)
        emit_turned(normed, ids_ref, turned, hold)
        total_ref[...] = jnp.zeros_like(total_ref)

    pre = nn(normed_ref[...], wu_ref[...])
    chance = 0.5 * (1.0 + lax.erf(pre * (1.0 / math.sqrt(2.0))))
    slope = chance + pre * jnp.exp(-0.5 * pre * pre) * (1.0 / math.sqrt(2.0 * math.pi))
    act_ref[...] = (pre * chance).astype(BF)
    d_pre = (dact_ref[...] * slope).astype(BF)
    pre_ref[...] = d_pre
    total_ref[...] += nt(d_pre, wu_ref[...])

    @pl.when(step == pl.num_programs(0) - 1)
    def _():
        norm_ref[...] = total_ref[...].astype(BF)


def second_kernel(ids_ref, one_ref, two_ref, own_ref, got_ref, gains_ref, wo_ref,
                  d_ref, gain_ref, mixed_ref, *rest):
    turned, hold = rest[:-1], rest[-1]
    unit, inverse = norm_parts(one_ref[...])
    grad = own_ref[...].astype(F32) + got_ref[...].astype(F32)
    back, gain = norm_back(unit, inverse, gains_ref[1:2, :], grad)
    gain_ref[...] = gain
    d_one = two_ref[...] + back
    d_ref[...] = d_one
    pack(nt(d_one.astype(BF), wo_ref[...]), mixed_ref)
    emit_turned(d_one, ids_ref, turned, hold)


def head_kernel(ids_ref, one_ref, own_ref, got_ref, wh_ref, pred_ref, *rest):
    turned, hold = rest[:-1], rest[-1]
    hidden = one_ref[...] + (own_ref[...].astype(F32) + got_ref[...].astype(F32))
    low = hidden.astype(BF)
    for item in range(pred_ref.shape[0]):
        pred_ref[item] = nt(wh_ref[...], low[item * LANES : (item + 1) * LANES])
    emit_turned(hidden, ids_ref, turned, hold)


def third_kernel(back_ref, wq_ref, dqkv_ref, norm_ref):
    width = wq_ref.shape[2]
    total = None
    for c in range(3):
        unpack(back_ref, c, dqkv_ref, c * width)
        part = nt(dqkv_ref[:, c * width : (c + 1) * width], wq_ref[c])
        total = part if total is None else total + part
    norm_ref[...] = total.astype(BF)


def last_kernel(cols, zero_ref, done_ref, own_ref, got_ref, gains_ref, gain_two_ref, patches_ref, we_ref,
                pos_ref, embed_ref, fields_ref, edge_ref, rows_ref):
    unit, inverse = norm_parts(zero_ref[...])
    grad = own_ref[...].astype(F32) + got_ref[...].astype(F32)
    back, gain = norm_back(unit, inverse, gains_ref[0:1, :], grad)
    d_zero = done_ref[...] + back
    low = d_zero.astype(BF)
    items, variables, height = edge_ref.shape
    pos = d_zero[0:LANES]
    for item in range(1, items):
        pos = pos + d_zero[item * LANES : (item + 1) * LANES]
    for k in range(pos_ref.shape[0]):
        width = pos_ref.shape[2]
        pos_ref[k] = pos[:, k * width : (k + 1) * width].astype(BF)
    features = patches_ref.shape[0]
    rows_ref[...] = jnp.zeros_like(rows_ref)
    rows_ref[0:features, :] = nn(patches_ref[...], low)
    rows_ref[features : features + 1, :] = gain
    rows_ref[features + 1 : features + 2, :] = gain_two_ref[...]
    embed_ref[...] = rows_ref[...].T.astype(BF).reshape(embed_ref.shape)
    half = height // PATCH
    row = lax.broadcasted_iota(jnp.int32, (LANES, height), 0)
    lane = lax.broadcasted_iota(jnp.int32, (LANES, height), 1)
    fields_ref[...] = jnp.zeros_like(fields_ref)
    for item in range(items):
        d_patches = nt(we_ref[...], low[item * LANES : (item + 1) * LANES])
        high = d_patches.astype(BF)
        rest = (d_patches - high.astype(F32)).astype(BF)
        for j in range(2):
            total = None
            for a in range(PATCH):
                place = jnp.where(
                    (row // half == j) & (lane == PATCH * (row % half) + a), 1.0, 0.0
                ).astype(BF)
                span = slice(a * 2 * variables, (a + 1) * 2 * variables)
                part = nn(high[span], place) + nn(rest[span], place)
                total = part if total is None else total + part
            for b in range(PATCH):
                block = total[b * variables : (b + 1) * variables]
                column = 2 * j + b - 1
                if column < 0:
                    edge_ref[item] = block.astype(BF)
                else:
                    fields_ref[item, pl.ds(column, variables, stride=cols), :] = block


def grads_kernel(ids_ref, *refs):
    groups, outs, holds = (refs[0:4], refs[4:8]), (refs[8:10], refs[10:12]), refs[12:14]
    for (own, got, b_own, b_got), (send, keep), hold, axis in zip(groups, outs, holds, (1, 2)):
        parts, rows, tokens = own.shape
        product = nn(own[...].reshape(parts * rows, tokens), b_own[...])
        product = product + nn(got[...].reshape(parts * rows, tokens), b_got[...])
        hold[...] = product.astype(BF).reshape(hold.shape)
        side = ids_ref[axis]
        for out, at in ((send, 1 - side), (keep, side)):
            for k in range(parts // 2):
                place = at * (parts // 2) + k if axis == 1 else 2 * k + at
                out[k] = hold[place]


def grads(ids, first, second):
    outs, holds = [], []
    for own, _, b_own, _ in (first, second):
        parts, rows, _ = own.shape
        outs += [shape((parts // 2, rows, b_own.shape[1]))] * 2
        holds.append(pltpu.VMEM((parts, rows, b_own.shape[1]), BF))
    flops = sum(4 * a[0].size * a[2].shape[1] for a in (first, second))
    return call(grads_kernel, "grads", outs, ids, *first, *second, scratch=holds, limit=32, flops=flops)


def fold_kernel(ids_ref, keep_a, got_a, keep_b, got_b, send_a, left_a, send_b, left_b, hold_a, hold_b):
    hold_a[...] = (keep_a[...].astype(F32) + got_a[...].astype(F32)).astype(BF)
    hold_b[...] = (keep_b[...].astype(F32) + got_b[...].astype(F32)).astype(BF)
    near, dp = ids_ref[2], ids_ref[1]
    for out_a, out_b, flip in ((send_a, send_b, True), (left_a, left_b, False)):
        for k in range(2):
            out_a[k] = hold_a[2 * k + (1 - near if flip else near)]
            out_b[k] = hold_b[2 * (1 - dp if flip else dp) + k]


def merge_kernel(ids_ref, keep_a, got_a, keep_b, got_b, send, left, hold):
    width = keep_a.shape[2]
    hold[:, :, 0:width] = (keep_a[...].astype(F32) + got_a[...].astype(F32)).astype(BF)
    hold[:, :, width:] = (keep_b[...].astype(F32) + got_b[...].astype(F32)).astype(BF)
    far = ids_ref[3]
    send[...] = hold[1 - far]
    left[...] = hold[far]


def spread_sum(ids, first, second):
    send_a, keep_a, send_b, keep_b = grads(ids, first, second)
    got_a, got_b = swap(send_a, "dp", 1), swap(send_b, "lon", 2)
    halves = [shape((2, *x.shape[1:])) for x in (keep_a, keep_a, keep_b, keep_b)]
    holds = [pltpu.VMEM(x.shape, BF) for x in (keep_a, keep_b)]
    send_a, keep_a, send_b, keep_b = call(
        fold_kernel, "fold", halves, ids, keep_a, got_a, keep_b, got_b, scratch=holds
    )
    got_a, got_b = swap(send_a, "lon", 2), swap(send_b, "dp", 1)
    rows, width = keep_a.shape[1], keep_a.shape[2] + keep_b.shape[2]
    send, keep = call(
        merge_kernel, "merge", [shape((rows, width))] * 2, ids, keep_a, got_a, keep_b, got_b,
        scratch=[pltpu.VMEM((2, rows, width), BF)],
    )
    return keep.astype(F32) + swap(send, "lon", 4).astype(F32)


def local(
    dataset,
    indices,
    run_count,
    run_mean,
    run_var,
    w_embed,
    pos_embed,
    gains,
    w_qkv,
    w_out,
    w_up,
    w_down,
    w_head,
    cotangent,
):
    items = indices.shape[0]
    variables, height, columns = dataset.shape[1:]
    dp, lon = lax.axis_size("dp"), lax.axis_size("lon")
    everyone = dp * lon
    width = w_embed.shape[1]
    local_width = w_qkv.shape[2]
    heads = local_width // HDIM
    item_tokens = cotangent.shape[1]
    tokens = items * item_tokens
    features = w_embed.shape[0]
    hidden_units = w_up.shape[1]
    scale = 1.0 / math.sqrt(HDIM)
    group, far = heads, lon // heads
    groups = [[group * g + i for i in range(group)] for g in range(far)]
    across = [[i + group * g for g in range(far)] for i in range(group)]
    assert items * HDIM == LANES and item_tokens == LANES and height == LANES and columns == 4
    lon_at, dp_at = lax.axis_index("lon"), lax.axis_index("dp")
    ids = jnp.stack([lon_at % 2, dp_at, lon_at // 2 % 2, lon_at // 4 % 2]).astype(jnp.int32)
    paired = dp == 2 and lon == 8
    parts, rows = width // (2 * (width // everyone)), width // everyone
    turned_shape = (
        [shape((parts, rows, tokens))] * 2 if paired else [shape((width, tokens))]
    )
    turned_hold = pltpu.VMEM((parts, 2, rows, tokens) if paired else (8, LANES), BF)

    fields = jnp.concatenate(
        [lax.dynamic_slice_in_dim(dataset, indices[i], 1, 0) for i in range(items)]
    )
    fields = fields.transpose(0, 1, 3, 2)
    edge = from_behind(fields[:, :, columns - 1].astype(BF), "lon", 1)
    local_count = float(items * height * columns)
    local_mean = jnp.mean(fields, axis=(0, 2, 3))
    local_spread = jnp.sum(jnp.square(fields - local_mean[None, :, None, None]), axis=(0, 2, 3))
    gap = jnp.zeros((HDIM - variables,), F32)
    moments = jnp.concatenate([local_mean, gap, local_spread, gap])
    moments = lax.all_to_all(
        jnp.broadcast_to(moments, (everyone, 1, LANES)), ("dp", "lon"), 0, 0
    ).reshape(everyone, LANES)
    run = jnp.pad(jnp.stack([run_count, run_mean, run_var]), ((0, 5), (0, LANES - variables)))
    we_sorted = (
        w_embed.reshape(variables, PATCH, PATCH, width).transpose(1, 2, 0, 3).reshape(features, width)
    )
    wh_turned = w_head.T

    out = call(
        functools.partial(start_kernel, local_count),
        "start",
        [
            shape((8, LANES), F32),
            shape((tokens, width), F32),
            shape((features, tokens)),
            shape((heads, 3, item_tokens, LANES)),
            *turned_shape,
        ],
        ids, moments, run, fields.reshape(items, variables * columns, height), edge,
        we_sorted, pos_embed, gains, w_qkv,
        scratch=[pltpu.VMEM((LANES, LANES), F32), turned_hold],
        flops=2 * tokens * width * (features + 3 * local_width),
    )
    stats, hidden_zero, patches, packed = out[:4]
    normed_one = out[4:]
    sent = lax.all_to_all(packed, "lon", 0, 0, axis_index_groups=groups if far > 1 else None)
    kv = sent
    if far > 1:
        kv = lax.all_gather(sent, "lon", axis=0, tiled=True, axis_index_groups=across)

    out = call(
        cotangent_kernel,
        "cotangent",
        [
            shape((tokens, width), F32),
            shape((tokens, hidden_units), F32),
            shape((tokens, 2 * LANES)),
            *turned_shape,
        ],
        ids, cotangent.transpose(0, 2, 1), wh_turned, w_down,
        scratch=[turned_hold],
        flops=2 * tokens * width * (features + hidden_units),
    )
    d_two, d_act, grad_pred = out[:3]
    d_two_turned = out[3:]

    attended, attended_t, weights_t = attend(sent, kv, items, scale)
    attended = lax.all_to_all(attended, "lon", 0, 0, axis_index_groups=groups if far > 1 else None)
    mixed, branch = call(
        project_kernel,
        "project",
        [shape((tokens, local_width)), shape((tokens, width))],
        attended, w_out,
        flops=2 * tokens * width * local_width,
    )
    branch_got = swap(branch, "mp", 1)
    block = min(512, hidden_units)
    column = lambda j: (0, j)
    whole = lambda j: (0, 0)
    full = pl.BlockSpec((tokens, width), whole)
    turned_specs = (
        [pl.BlockSpec((parts, rows, tokens), lambda j: (0, 0, 0))] * 2
        if paired
        else [pl.BlockSpec((width, tokens), whole)]
    )
    out = call(
        forward_kernel,
        "forward",
        [
            shape((tokens, width), F32),
            shape((tokens, width)),
            shape((tokens, hidden_units)),
            shape((tokens, hidden_units)),
            *turned_shape,
        ],
        ids, hidden_zero, branch, branch_got, gains, w_up, d_act,
        grid=(hidden_units // block,),
        in_specs=[
            pl.BlockSpec(memory_space=pltpu.SMEM),
            full,
            full,
            full,
            pl.BlockSpec(gains.shape, whole),
            pl.BlockSpec((width, block), column),
            pl.BlockSpec((tokens, block), column),
        ],
        out_specs=[
            full,
            full,
            pl.BlockSpec((tokens, block), column),
            pl.BlockSpec((tokens, block), column),
            *turned_specs,
        ],
        scratch=[pltpu.VMEM((tokens, width), BF), pltpu.VMEM((tokens, width), F32), turned_hold],
        flops=4 * tokens * width * hidden_units,
    )
    hidden_one, d_norm, d_pre, activated = out[:4]
    normed_two = out[4:]
    d_norm_got = swap(d_norm, "mp", 1)

    if paired:
        up_down = spread_sum(
            ids,
            (normed_two[0], swap(normed_two[1], "lon", 1), d_pre, swap(d_pre, "lon", 1)),
            (d_two_turned[0], swap(d_two_turned[1], "lon", 1), activated, swap(activated, "lon", 1)),
        )
        grad_up, grad_down = up_down[:, :hidden_units], up_down[:, hidden_units:]
    else:
        grad_up, grad_down = scatter(nn(normed_two[0], d_pre)), scatter(nn(d_two_turned[0], activated))

    forward = nn(activated, w_down).astype(BF)
    forward_got = swap(forward, "mp", 1)

    out = call(
        second_kernel,
        "second",
        [
            shape((tokens, width), F32),
            shape((1, width), F32),
            shape((heads, item_tokens, LANES)),
            *turned_shape,
        ],
        ids, hidden_one, d_two, d_norm, d_norm_got, gains, w_out,
        scratch=[turned_hold],
        flops=2 * tokens * width * local_width,
    )
    d_one, gain_two, d_mixed = out[:3]
    d_one_turned = out[3:]
    d_heads = lax.all_to_all(d_mixed, "lon", 0, 0, axis_index_groups=groups if far > 1 else None)
    out = call(
        head_kernel,
        "head",
        [shape((items, features, item_tokens), F32), *turned_shape],
        ids, hidden_one, forward, forward_got, wh_turned,
        scratch=[turned_hold],
        flops=2 * tokens * width * features,
    )
    pred, hidden_turned = out[0].transpose(0, 2, 1), out[1:]

    back = attend_back(sent, kv, d_heads, attended_t, weights_t, items, scale)
    if far > 1:
        d_query, d_kv = back
        d_kv = lax.psum_scatter(
            d_kv, "lon", scatter_dimension=0, tiled=True, axis_index_groups=across
        ).astype(BF)
        back = [jnp.concatenate([d_query[:, None], d_kv], axis=1)]
    back = lax.all_to_all(back[0], "lon", 0, 0, axis_index_groups=groups if far > 1 else None)
    d_qkv, d_norm = call(
        third_kernel,
        "third",
        [shape((tokens, 3 * local_width)), shape((tokens, width))],
        back, w_qkv,
        flops=6 * tokens * width * local_width,
    )
    d_norm_got = swap(d_norm, "mp", 1)
    if paired:
        out_head = spread_sum(
            ids,
            (d_one_turned[0], swap(d_one_turned[1], "lon", 1), mixed, swap(mixed, "lon", 1)),
            (hidden_turned[0], swap(hidden_turned[1], "lon", 1), grad_pred, swap(grad_pred, "lon", 1)),
        )
        grad_out, grad_head = out_head[:, :local_width], out_head[:, local_width:]
        side = swap(normed_one[1], "lon", 1)
        d_qkv_got = swap(d_qkv, "lon", 1)
        cut = 3 * local_width // 2
        grad_qkv = spread_sum(
            ids,
            (normed_one[0], side, d_qkv[:, :cut], d_qkv_got[:, :cut]),
            (normed_one[0], side, d_qkv[:, cut:], d_qkv_got[:, cut:]),
        )
    else:
        grad_out, grad_head = scatter(nn(d_one_turned[0], mixed)), scatter(nn(hidden_turned[0], grad_pred))
        grad_qkv = scatter(nn(normed_one[0], d_qkv))

    pos, embed, d_fields, d_edge = call(
        functools.partial(last_kernel, columns),
        "last",
        [
            shape((dp, item_tokens, width // dp)),
            shape((everyone, rows, 2 * LANES)),
            shape((items, variables * columns, height), F32),
            shape((items, variables, height)),
        ],
        hidden_zero, d_one, d_norm, d_norm_got, gains, gain_two, patches, we_sorted,
        scratch=[pltpu.VMEM((2 * LANES, width), F32)],
        flops=4 * tokens * width * features,
    )
    east = from_behind(d_edge, "lon", -1).astype(F32)
    grad_pos = pick(pos, dp_at, 0).astype(F32)
    for k in range(1, dp):
        grad_pos = grad_pos + swap(pick(pos, dp_at ^ k, 0), "dp", k).astype(F32)
    embed = lax.all_to_all(embed, ("dp", "lon"), 0, 0)
    embed = jnp.sum(embed.astype(F32), axis=0)
    d_fields = d_fields.reshape(items, variables, columns, height)
    grad_fields = jnp.concatenate([d_fields[:, :, : columns - 1], east[:, :, None]], axis=2)
    return (
        pred,
        stats[0, :variables],
        stats[1, :variables],
        stats[2, :variables],
        grad_fields.transpose(0, 1, 3, 2),
        embed[:, :features].T,
        grad_pos,
        embed[:, features : features + 2].T,
        grad_qkv.reshape(rows, 3, local_width).transpose(1, 0, 2),
        grad_out.T,
        grad_up,
        grad_down.T,
        grad_head[:, :features],
    )


def solution(mesh):
    in_specs = (
        P(None, None, None, "lon"),
        P("dp"),
        P(),
        P(),
        P(),
        P(),
        P("lon", None),
        P(),
        P(None, None, "mp"),
        P("mp", None),
        P(None, "mp"),
        P("mp", None),
        P(),
        P("dp", "lon", None),
    )
    out_specs = (
        P("dp", "lon", None),
        P(),
        P(),
        P(),
        P("dp", None, None, "lon"),
        P(None, ("dp", "lon")),
        P("lon", "dp"),
        P(None, ("dp", "lon")),
        P(None, ("dp", "lon"), "mp"),
        P("mp", ("dp", "lon")),
        P(("dp", "lon"), "mp"),
        P("mp", ("dp", "lon")),
        P(("dp", "lon"), None),
    )
    return jax.shard_map(local, mesh=mesh, in_specs=in_specs, out_specs=out_specs, check_vma=False)
```

profile of v0, /device:TPU:0, one launch (start us, length us, event | category | flops | bytes accessed | tf_op | source)
XLA Modules:
  0.0 296.5 jit_solution(1740902783599195062)
XLA Ops:
  0.7 1.4 fusion.5
  8.3 7.4 %all-to-all-start = ((f32[16,1,128]{2,1,0:T(1,128)}), f32[16,1,128]{2,1,0:T(1,128)S(1)}, u32[]{:S(2)}, u32[]{:S(2)}) async-start(f32[16,1,128]{2,1,0:T(1,128)} %broadcast_in_dim.10), calls=%async_computation | async-start | bytes 16384 | tf_op jit(solution)/shard_map/all_to_all | solution.py:601
  18.2 1.9 reshape.55
  24.5 3.1 %start.1 = (f32[8,128]{1,0:T(8,128)S(1)}, f32[256,1024]{1,0:T(8,128)S(1)}, bf16[192,256]{1,0:T(8,128)(2,1)S(1)}, bf16[8,3,128,128]{3,2,1,0:T(8,128)(2,1)S(1)}, b...) custom-call(s32[4]{0:T(128)S(1)} %pad_add_fusion.ids_ref, f32[16,128]{1,0:T(8,128)S(1)} %bitcast.60, ...), custom_call_target="tpu_custom_call" | custom-call | flops 905969664 | bytes 6504464 | tf_op jit(solution)/shard_map/start/pallas_call | solution.py:118
  29.1 25.2 %all_to_all.30.q_ref.kv_ref = bf16[8,3,128,128]{3,2,1,0:T(8,128)(2,1)S(1)} all-to-all(bf16[8,3,128,128]{3,2,1,0:T(8,128)(2,1)S(1)} %get-tuple-element.80), channel_id=1, replica_groups=mesh['dp'=2,'lon'=8,'mp'=2] {'lon'}, dimensions={0} | all-to-all | bytes 1572864 | tf_op jit(solution)/shard_map/all_to_all | solution.py:627
  54.3 8.1 %attend.1 = (bf16[8,128,128]{2,1,0:T(8,128)(2,1)S(1)}, f32[128,1024]{1,0:T(8,128)S(1)}, bf16[2,1024,1024]{2,1,0:T(8,128)(2,1)S(1)}) custom-call(bf16[8,3,128,128]{3,2,1,0:T(8,128)(2,1)S(1)} %all_to_all.30.q_ref.kv_ref, bf16[8,3,128,128]{3,2,1,0:T(8,128)(2,1)S(1)} %all_to_all.30.q_ref.kv_ref), custom_call_target="tpu_custom_call" | custom-call | flops 1073741824 | bytes 6553600 | tf_op jit(solution)/shard_map/attend/pallas_call | solution.py:118
  63.3 2.0 copy-done.53
  66.1 12.4 %all_to_all.31.o_ref = bf16[8,128,128]{2,1,0:T(8,128)(2,1)S(1)} all-to-all(bf16[8,128,128]{2,1,0:T(8,128)(2,1)S(1)} %get-tuple-element.81), channel_id=1, replica_groups=mesh['dp'=2,'lon'=8,'mp'=2] {'lon'}, dimensions={0} | all-to-all | bytes 524288 | tf_op jit(solution)/shard_map/all_to_all | solution.py:649
  79.7 1.5 collective-permute-start.1
  81.3 2.0 cotangent.1
  83.4 9.7 %collective-permute-done.1.got_ref = bf16[256,1024]{1,0:T(8,128)(2,1)S(1)} collective-permute-done((bf16[256,1024]{1,0:T(8,128)(2,1)S(1)}, bf16[256,1024]{1,0:T(8,128)(2,1)S(1)}, u32[]{:S(2)}, u32[]{:S(2)}) %collective-permute-start.1) | collective-permute-done | bytes 524320 | tf_op jit(solution)/shard_map/ppermute | solution.py:23
  93.1 6.4 %forward.1 = (f32[256,1024]{1,0:T(8,128)S(1)}, bf16[256,1024]{1,0:T(8,128)(2,1)S(1)}, bf16[256,2048]{1,0:T(8,128)(2,1)}, bf16[256,2048]{1,0:T(8,128)(2,1)}, bf16...) custom-call(s32[4]{0:T(128)S(1)} %pad_add_fusion.ids_ref, f32[256,1024]{1,0:T(8,128)S(1)} %get-tuple-element.79.zero_ref, ...), custom_call_target="tpu_custom_call" | custom-call | flops 2147483648 | bytes 12591120 | tf_op jit(solution)/shard_map/forward/pallas_call | solution.py:118
  99.5 1.6 collective-permute-start.3
  101.6 10.3 %collective-permute-done.3.got_ref = bf16[256,1024]{1,0:T(8,128)(2,1)S(1)} collective-permute-done((bf16[256,1024]{1,0:T(8,128)(2,1)S(1)}, bf16[256,1024]{1,0:T(8,128)(2,1)S(1)}, u32[]{:S(2)}, u32[]{:S(2)}) %collective-permute-start.3) | collective-permute-done | bytes 524320 | tf_op jit(solution)/shard_map/ppermute | solution.py:23
  111.9 1.8 second.1
  116.9 4.2 %all-to-all-start.3 = ((bf16[8,128,128]{2,1,0:T(8,128)(2,1)}), bf16[8,128,128]{2,1,0:T(8,128)(2,1)}, u32[]{:S(2)}, u32[]{:S(2)}) async-start(bf16[8,128,128]{2,1,0:T(8,128)(2,1)} %copy-done.25), calls=%async_computation.3 | async-start | bytes 524288 | tf_op jit(solution)/shard_map/all_to_all | solution.py:730
  121.3 4.6 %convolution_convert_fusion.own_ref = bf16[256,1024]{1,0:T(8,128)(2,1)} fusion(bf16[256,2048]{1,0:T(8,128)(2,1)} %get-tuple-element.85.refs_6_, bf16[2048,1024]{1,0:T(8,128)(2,1)} %wd_ref.1), kind=kOutput, calls=%fused_computation | convolution fusion | flops 1074003968 | bytes 5767168 | tf_op jit(solution)/shard_map/dot_general | solution.py:64
  125.9 1.5 collective-permute-start.2
  127.5 3.2 %all-to-all-done.3.d_ref = bf16[8,128,128]{2,1,0:T(8,128)(2,1)} async-done(((bf16[8,128,128]{2,1,0:T(8,128)(2,1)}), bf16[8,128,128]{2,1,0:T(8,128)(2,1)}, u32[]{:S(2)}, u32[]{:S(2)}) %all-to-all-start.3) | async-done | bytes 262176 | tf_op jit(solution)/shard_map/all_to_all | solution.py:730
  131.8 2.2 copy-done.54
  135.1 6.3 %attend_back.1 = bf16[8,3,128,128]{3,2,1,0:T(8,128)(2,1)S(1)} custom-call(bf16[8,3,128,128]{3,2,1,0:T(8,128)(2,1)S(1)} %copy-done.19, bf16[8,3,128,128]{3,2,1,0:T(8,128)(2,1)S(1)} %copy-done.19, bf16[8,128,128]{2,1,0:T(8,128)(2,1)} %all-to-all-done.3.d_ref, f32[128,1024]{1,0:T(8,128)S(1)} %copy-done.56, bf16[2,1024,1024]{2,1,0:T(8,128)(2,1)S(1)} %copy-done.54), custom_call_target="tpu_custom_call" | custom-call | flops 2147483648 | bytes 7340032 | tf_op jit(solution)/shard_map/attend_back/pallas_call | solution.py:118
  142.2 4.2 %all-to-all-start.4 = ((bf16[8,3,128,128]{3,2,1,0:T(8,128)(2,1)}), bf16[8,3,128,128]{3,2,1,0:T(8,128)(2,1)}, u32[]{:S(2)}, u32[]{:S(2)}) async-start(bf16[8,3,128,128]{3,2,1,0:T(8,128)(2,1)} %copy-done.17), calls=%async_computation.4 | async-start | bytes 1572864 | tf_op jit(solution)/shard_map/all_to_all | solution.py:748
  148.9 6.0 %grads.5 = (bf16[4,64,2048]{2,1,0:T(8,128)(2,1)}, bf16[4,64,2048]{2,1,0:T(8,128)(2,1)S(1)}, bf16[4,64,2048]{2,1,0:T(8,128)(2,1)}, bf16[4,64,2048]{2,1,0:T(8,128)(2,1)S(1)}) custom-call(s32[4]{0:T(128)S(1)} %pad_add_fusion.ids_ref, bf16[8,64,256]{2,1,0:T(8,128)(2,1)S(1)} %copy-done.51, bf16[8,64,256]{2,1,0:T(8,128)(2,1)} %collective-permute-done.23.refs_1_, ...), custom_call_target="tpu_custom_call" | custom-call | flops 2147483648 | bytes 9437200 | tf_op jit(solution)/shard_map/grads/pallas_call | solution.py:118
  154.9 1.5 collective-permute-start.27
  156.4 1.7 collective-permute-start.28
  158.6 2.3 head.1
  161.1 1.4 collective-permute-done.16.refs_5_
  164.7 24.4 %collective-permute-done.19.got_b = bf16[4,64,256]{2,1,0:T(8,128)(2,1)S(1)} collective-permute-done((bf16[4,64,256]{2,1,0:T(8,128)(2,1)S(1)}, bf16[4,64,256]{2,1,0:T(8,128)(2,1)S(1)}, u32[]{:S(2)}, u32[]{:S(2)}) %collective-permute-start.19) | collective-permute-done | bytes 131104 | tf_op jit(solution)/shard_map/ppermute | solution.py:23
  192.9 3.4 %collective-permute-done.21.got_b = bf16[2,64,256]{2,1,0:T(8,128)(2,1)} collective-permute-done((bf16[2,64,256]{2,1,0:T(8,128)(2,1)}, bf16[2,64,256]{2,1,0:T(8,128)(2,1)}, u32[]{:S(2)}, u32[]{:S(2)}) %collective-permute-start.21) | collective-permute-done | bytes 65568 | tf_op jit(solution)/shard_map/ppermute | solution.py:23
  199.1 1.6 merge.4
  201.4 1.6 collective-permute-start.22
  206.8 3.5 %fold.5 = (bf16[2,64,2048]{2,1,0:T(8,128)(2,1)}, bf16[2,64,2048]{2,1,0:T(8,128)(2,1)S(1)}, bf16[2,64,2048]{2,1,0:T(8,128)(2,1)}, bf16[2,64,2048]{2,1,0:T(8,128)(2,1)S(1)}) custom-call(s32[4]{0:T(128)S(1)} %pad_add_fusion.ids_ref, bf16[4,64,2048]{2,1,0:T(8,128)(2,1)S(1)} %copy-done.11, bf16[4,64,2048]{2,1,0:T(8,128)(2,1)} %collective-permute-done.27.got_a, ...), custom_call_target="tpu_custom_call" | custom-call | bytes 6291472 | tf_op jit(solution)/shard_map/fold/pallas_call | solution.py:118
  213.6 2.9 third.1
  216.4 1.5 collective-permute-start.4
  221.4 5.1 %collective-permute-done.29.got_a = bf16[2,64,2048]{2,1,0:T(8,128)(2,1)} collective-permute-done((bf16[2,64,2048]{2,1,0:T(8,128)(2,1)}, bf16[2,64,2048]{2,1,0:T(8,128)(2,1)}, u32[]{:S(2)}, u32[]{:S(2)}) %collective-permute-start.29) | collective-permute-done | bytes 524320 | tf_op jit(solution)/shard_map/ppermute | solution.py:23
  226.9 2.6 merge.5
  229.5 1.6 collective-permute-start.31
  231.1 2.6 last.1
  234.6 3.8 %all-to-all-start.5 = ((bf16[16,64,256]{2,1,0:T(8,128)(2,1)}), bf16[16,64,256]{2,1,0:T(8,128)(2,1)S(1)}, u32[]{:S(2)}, u32[]{:S(2)}) async-start(bf16[16,64,256]{2,1,0:T(8,128)(2,1)} %get-tuple-element.99), calls=%async_computation.5 | async-start | bytes 1048576 | tf_op jit(solution)/shard_map/all_to_all | solution.py:793
  238.4 1.7 collective-permute-start.6
  240.1 4.1 %collective-permute-done.5 = bf16[2,48,128]{2,1,0:T(8,128)(2,1)S(1)} collective-permute-done((bf16[2,48,128]{2,1,0:T(8,128)(2,1)S(1)}, bf16[2,48,128]{2,1,0:T(8,128)(2,1)S(1)}, u32[]{:S(2)}, u32[]{:S(2)}) %collective-permute-start.5) | collective-permute-done | bytes 24608 | tf_op jit(solution)/shard_map/ppermute | solution.py:29
  245.0 1.9 collective-permute-done.6
  249.7 2.1 grads.3
  253.1 8.7 %collective-permute-done.31 = bf16[64,4096]{1,0:T(8,128)(2,1)} collective-permute-done((bf16[64,4096]{1,0:T(8,128)(2,1)}, bf16[64,4096]{1,0:T(8,128)(2,1)}, u32[]{:S(2)}, u32[]{:S(2)}) %collective-permute-start.31) | collective-permute-done | bytes 524320 | tf_op jit(solution)/shard_map/ppermute | solution.py:23
  263.3 4.4 %collective-permute-done.10.got_b = bf16[4,64,768]{2,1,0:T(8,128)(2,1)S(1)} collective-permute-done((bf16[4,64,768]{2,1,0:T(8,128)(2,1)S(1)}, bf16[4,64,768]{2,1,0:T(8,128)(2,1)S(1)}, u32[]{:S(2)}, u32[]{:S(2)}) %collective-permute-start.10) | collective-permute-done | bytes 393248 | tf_op jit(solution)/shard_map/ppermute | solution.py:23
  270.8 5.1 %collective-permute-done.11.got_a = bf16[2,64,768]{2,1,0:T(8,128)(2,1)S(1)} collective-permute-done((bf16[2,64,768]{2,1,0:T(8,128)(2,1)S(1)}, bf16[2,64,768]{2,1,0:T(8,128)(2,1)S(1)}, u32[]{:S(2)}, u32[]{:S(2)}) %collective-permute-start.11) | collective-permute-done | bytes 196640 | tf_op jit(solution)/shard_map/ppermute | solution.py:23
  276.6 9.0 %collective-permute-start.13 = (bf16[64,1536]{1,0:T(8,128)(2,1)S(1)}, bf16[64,1536]{1,0:T(8,128)(2,1)S(1)}, u32[]{:S(2)}, u32[]{:S(2)}) collective-permute-start(bf16[64,1536]{1,0:T(8,128)(2,1)S(1)} %get-tuple-element.113), channel_id=1, source_target_pairs={{0,8},{2,10},{4,12},{6,14},{8,0},{10,2},{12,4},{14,6},{1,9},{3,11}... | collective-permute-start | bytes 589832 | tf_op jit(solution)/shard_map/ppermute | solution.py:23
  287.1 8.2 %collective-permute-done.13 = bf16[64,1536]{1,0:T(8,128)(2,1)S(1)} collective-permute-done((bf16[64,1536]{1,0:T(8,128)(2,1)S(1)}, bf16[64,1536]{1,0:T(8,128)(2,1)S(1)}, u32[]{:S(2)}, u32[]{:S(2)}) %collective-permute-start.13) | collective-permute-done | bytes 196640 | tf_op jit(solution)/shard_map/ppermute | solution.py:23
  (195 shorter events, 57.9 us)
Async XLA Ops:
  0.6 21.3 %copy-start = (bf16[3,1024,512]{2,1,0:T(8,128)(2,1)S(1)}, bf16[3,1024,512]{2,1,0:T(8,128)(2,1)}, u32[]{:S(2)}) copy-start(bf16[3,1024,512]{2,1,0:T(8,128)(2,1)} %wq_ref.3) | copy-start | bytes 9437188
  8.3 13.7 %all-to-all-start = ((f32[16,1,128]{2,1,0:T(1,128)}), f32[16,1,128]{2,1,0:T(1,128)S(1)}, u32[]{:S(2)}, u32[]{:S(2)}) async-start(f32[16,1,128]{2,1,0:T(1,128)} %broadcast_in_dim.10), calls=%async_computation | async-start | bytes 16384 | tf_op jit(solution)/shard_map/all_to_all | solution.py:601
  16.3 5.7 %collective-permute-start = (bf16[2,48,128]{2,1,0:T(8,128)(2,1)}, bf16[2,48,128]{2,1,0:T(8,128)(2,1)}, u32[]{:S(2)}, u32[]{:S(2)}) collective-permute-start(bf16[2,48,128]{2,1,0:T(8,128)(2,1)} %fusion), channel_id=1, source_target_pairs={{14,0},{0,2},{2,4},{4,6},{6,8},{8,10},{10,12},{12,14},{15,1},{1,3}... | collective-permute-start | bytes 73736 | tf_op jit(solution)/shard_map/ppermute | solution.py:29
  24.5 54.0 %copy-start.1 = (bf16[512,1024]{1,0:T(8,128)(2,1)S(1)}, bf16[512,1024]{1,0:T(8,128)(2,1)}, u32[]{:S(2)}) copy-start(bf16[512,1024]{1,0:T(8,128)(2,1)} %wo_ref.3) | copy-start | bytes 3145732
  29.0 25.3 %copy-start.38 = (bf16[192,256]{1,0:T(8,128)(2,1)}, bf16[192,256]{1,0:T(8,128)(2,1)S(1)}, u32[]{:S(2)}) copy-start(bf16[192,256]{1,0:T(8,128)(2,1)S(1)} %get-tuple-element.96.patches_ref) | copy-start | bytes 294916
  29.0 25.3 %copy-start.42 = (f32[8,128]{1,0:T(8,128)}, f32[8,128]{1,0:T(8,128)S(1)}, u32[]{:S(2)}) copy-start(f32[8,128]{1,0:T(8,128)S(1)} %get-tuple-element.87) | copy-start | bytes 12292
  29.0 64.0 %copy-start.6 = (f32[256,1024]{1,0:T(8,128)}, f32[256,1024]{1,0:T(8,128)S(1)}, u32[]{:S(2)}) copy-start(f32[256,1024]{1,0:T(8,128)S(1)} %get-tuple-element.79.zero_ref) | copy-start | bytes 3145732
  29.0 52.2 %copy-start.5 = (bf16[2048,1024]{1,0:T(8,128)(2,1)S(1)}, bf16[2048,1024]{1,0:T(8,128)(2,1)}, u32[]{:S(2)}) copy-start(bf16[2048,1024]{1,0:T(8,128)(2,1)} %wd_ref.1) | copy-start | bytes 12582916
  29.0 52.2 %copy-start.8 = (bf16[1024,192]{0,1:T(8,128)(2,1)S(1)}, bf16[1024,192]{0,1:T(8,128)(2,1)}, u32[]{:S(2)}) copy-start(bf16[1024,192]{0,1:T(8,128)(2,1)} %param.26) | copy-start | bytes 1179652
  29.0 52.2 %copy-start.30 = (f32[2,128,192]{1,2,0:T(8,128)S(1)}, f32[2,128,192]{1,2,0:T(8,128)}, u32[]{:S(2)}) copy-start(f32[2,128,192]{1,2,0:T(8,128)} %param.27) | copy-start | bytes 589828
  66.1 26.9 %copy-start.2 = (bf16[1024,2048]{1,0:T(8,128)(2,1)S(1)}, bf16[1024,2048]{1,0:T(8,128)(2,1)}, u32[]{:S(2)}) copy-start(bf16[1024,2048]{1,0:T(8,128)(2,1)} %wu_ref.1) | copy-start | bytes 12582916
  66.1 26.9 %copy-start.32 = (f32[2,1024]{1,0:T(2,128)S(1)}, f32[2,1024]{1,0:T(2,128)}, u32[]{:S(2)}) copy-start(f32[2,1024]{1,0:T(2,128)} %gains_ref.7) | copy-start | bytes 24580
  79.7 13.3 %collective-permute-start.1 = (bf16[256,1024]{1,0:T(8,128)(2,1)S(1)}, bf16[256,1024]{1,0:T(8,128)(2,1)S(1)}, u32[]{:S(2)}, u32[]{:S(2)}) collective-permute-start(bf16[256,1024]{1,0:T(8,128)(2,1)S(1)} %get-tuple-element.82.own_ref), channel_id=1, source_target_pairs={{0,1},{1,0},{2,3},{3,2},{4,5},{5,4},{6,7},{7,6},{8,9},{9,8},{10,11... | collective-permute-start | bytes 1572872 | tf_op jit(solution)/shard_map/ppermute | solution.py:23
  99.5 12.4 %collective-permute-start.3 = (bf16[256,1024]{1,0:T(8,128)(2,1)S(1)}, bf16[256,1024]{1,0:T(8,128)(2,1)S(1)}, u32[]{:S(2)}, u32[]{:S(2)}) collective-permute-start(bf16[256,1024]{1,0:T(8,128)(2,1)S(1)} %get-tuple-element.89.own_ref), channel_id=1, source_target_pairs={{0,1},{1,0},{2,3},{3,2},{4,5},{5,4},{6,7},{7,6},{8,9},{9,8},{10,11... | collective-permute-start | bytes 1572872 | tf_op jit(solution)/shard_map/ppermute | solution.py:23
  101.1 45.8 %collective-permute-start.24 = (bf16[256,2048]{1,0:T(8,128)(2,1)}, bf16[256,2048]{1,0:T(8,128)(2,1)}, u32[]{:S(2)}, u32[]{:S(2)}) collective-permute-start(bf16[256,2048]{1,0:T(8,128)(2,1)} %get-tuple-element.132.refs_2_), channel_id=1, source_target_pairs={{0,2},{2,0},{4,6},{6,4},{8,10},{10,8},{12,14},{14,12},{1,3},{3,1},... | collective-permute-start | bytes 3145736 | tf_op jit(solution)/shard_map/ppermute | solution.py:23
  101.1 45.8 %collective-permute-start.26 = (bf16[256,2048]{1,0:T(8,128)(2,1)}, bf16[256,2048]{1,0:T(8,128)(2,1)}, u32[]{:S(2)}, u32[]{:S(2)}) collective-permute-start(bf16[256,2048]{1,0:T(8,128)(2,1)} %get-tuple-element.85.refs_6_), channel_id=1, source_target_pairs={{0,2},{2,0},{4,6},{6,4},{8,10},{10,8},{12,14},{14,12},{1,3},{3,1},... | collective-permute-start | bytes 3145736 | tf_op jit(solution)/shard_map/ppermute | solution.py:23
  116.9 13.8 %all-to-all-start.3 = ((bf16[8,128,128]{2,1,0:T(8,128)(2,1)}), bf16[8,128,128]{2,1,0:T(8,128)(2,1)}, u32[]{:S(2)}, u32[]{:S(2)}) async-start(bf16[8,128,128]{2,1,0:T(8,128)(2,1)} %copy-done.25), calls=%async_computation.3 | async-start | bytes 524288 | tf_op jit(solution)/shard_map/all_to_all | solution.py:730
  121.1 25.3 %collective-permute-start.25 = (bf16[8,64,256]{2,1,0:T(8,128)(2,1)}, bf16[8,64,256]{2,1,0:T(8,128)(2,1)}, u32[]{:S(2)}, u32[]{:S(2)}) collective-permute-start(bf16[8,64,256]{2,1,0:T(8,128)(2,1)} %copy-done.52), channel_id=1, source_target_pairs={{0,2},{2,0},{4,6},{6,4},{8,10},{10,8},{12,14},{14,12},{1,3},{3,1},... | collective-permute-start | bytes 786440 | tf_op jit(solution)/shard_map/ppermute | solution.py:23
  125.9 32.2 %collective-permute-start.2 = (bf16[256,1024]{1,0:T(8,128)(2,1)}, bf16[256,1024]{1,0:T(8,128)(2,1)}, u32[]{:S(2)}, u32[]{:S(2)}) collective-permute-start(bf16[256,1024]{1,0:T(8,128)(2,1)} %convolution_convert_fusion.own_ref), channel_id=1, source_target_pairs={{0,1},{1,0},{2,3},{3,2},{4,5},{5,4},{6,7},{7,6},{8,9},{9,8},{10,11... | collective-permute-start | bytes 1572872 | tf_op jit(solution)/shard_map/ppermute | solution.py:23
  127.4 19.5 %collective-permute-start.23 = (bf16[8,64,256]{2,1,0:T(8,128)(2,1)}, bf16[8,64,256]{2,1,0:T(8,128)(2,1)}, u32[]{:S(2)}, u32[]{:S(2)}) collective-permute-start(bf16[8,64,256]{2,1,0:T(8,128)(2,1)} %get-tuple-element.131), channel_id=1, source_target_pairs={{0,2},{2,0},{4,6},{6,4},{8,10},{10,8},{12,14},{14,12},{1,3},{3,1},... | collective-permute-start | bytes 786440 | tf_op jit(solution)/shard_map/ppermute | solution.py:23
  142.2 71.3 %all-to-all-start.4 = ((bf16[8,3,128,128]{3,2,1,0:T(8,128)(2,1)}), bf16[8,3,128,128]{3,2,1,0:T(8,128)(2,1)}, u32[]{:S(2)}, u32[]{:S(2)}) async-start(bf16[8,3,128,128]{3,2,1,0:T(8,128)(2,1)} %copy-done.17), calls=%async_computation.4 | async-start | bytes 1572864 | tf_op jit(solution)/shard_map/all_to_all | solution.py:748
  146.5 14.5 %collective-permute-start.17 = (bf16[256,256]{1,0:T(8,128)(2,1)}, bf16[256,256]{1,0:T(8,128)(2,1)S(1)}, u32[]{:S(2)}, u32[]{:S(2)}) collective-permute-start(bf16[256,256]{1,0:T(8,128)(2,1)} %copy-done.35), channel_id=1, source_target_pairs={{0,2},{2,0},{4,6},{6,4},{8,10},{10,8},{12,14},{14,12},{1,3},{3,1},... | collective-permute-start | bytes 393224 | tf_op jit(solution)/shard_map/ppermute | solution.py:23
  154.9 49.4 %collective-permute-start.27 = (bf16[4,64,2048]{2,1,0:T(8,128)(2,1)}, bf16[4,64,2048]{2,1,0:T(8,128)(2,1)}, u32[]{:S(2)}, u32[]{:S(2)}) collective-permute-start(bf16[4,64,2048]{2,1,0:T(8,128)(2,1)} %get-tuple-element.136), channel_id=1, source_target_pairs={{0,16},{16,0},{1,17},{17,1},{2,18},{18,2},{3,19},{19,3},{4,20},{20... | collective-permute-start | bytes 3145736 | tf_op jit(solution)/shard_map/ppermute | solution.py:23
  156.4 47.9 %collective-permute-start.28 = (bf16[4,64,2048]{2,1,0:T(8,128)(2,1)}, bf16[4,64,2048]{2,1,0:T(8,128)(2,1)}, u32[]{:S(2)}, u32[]{:S(2)}) collective-permute-start(bf16[4,64,2048]{2,1,0:T(8,128)(2,1)} %get-tuple-element.138), channel_id=1, source_target_pairs={{0,4},{2,6},{4,0},{6,2},{8,12},{10,14},{12,8},{14,10},{1,5},{3,7},... | collective-permute-start | bytes 3145736 | tf_op jit(solution)/shard_map/ppermute | solution.py:23
  158.1 3.0 %collective-permute-start.15 = (bf16[256,512]{1,0:T(8,128)(2,1)S(1)}, bf16[256,512]{1,0:T(8,128)(2,1)S(1)}, u32[]{:S(2)}, u32[]{:S(2)}) collective-permute-start(bf16[256,512]{1,0:T(8,128)(2,1)S(1)} %copy-done.27), channel_id=1, source_target_pairs={{0,2},{2,0},{4,6},{6,4},{8,10},{10,8},{12,14},{14,12},{1,3},{3,1},... | collective-permute-start | bytes 786440 | tf_op jit(solution)/shard_map/ppermute | solution.py:23
  158.1 3.0 %collective-permute-start.14 = (bf16[8,64,256]{2,1,0:T(8,128)(2,1)S(1)}, bf16[8,64,256]{2,1,0:T(8,128)(2,1)S(1)}, u32[]{:S(2)}, u32[]{:S(2)}) collective-permute-start(bf16[8,64,256]{2,1,0:T(8,128)(2,1)S(1)} %copy-done.47), channel_id=1, source_target_pairs={{0,2},{2,0},{4,6},{6,4},{8,10},{10,8},{12,14},{14,12},{1,3},{3,1},... | collective-permute-start | bytes 786440 | tf_op jit(solution)/shard_map/ppermute | solution.py:23
  160.9 1.6 collective-permute-start.16
  163.7 25.3 %collective-permute-start.18 = (bf16[4,64,512]{2,1,0:T(8,128)(2,1)S(1)}, bf16[4,64,512]{2,1,0:T(8,128)(2,1)S(1)}, u32[]{:S(2)}, u32[]{:S(2)}) collective-permute-start(bf16[4,64,512]{2,1,0:T(8,128)(2,1)S(1)} %get-tuple-element.121), channel_id=1, source_target_pairs={{0,16},{16,0},{1,17},{17,1},{2,18},{18,2},{3,19},{19,3},{4,20},{20... | collective-permute-start | bytes 786440 | tf_op jit(solution)/shard_map/ppermute | solution.py:23
  164.3 24.7 %collective-permute-start.19 = (bf16[4,64,256]{2,1,0:T(8,128)(2,1)S(1)}, bf16[4,64,256]{2,1,0:T(8,128)(2,1)S(1)}, u32[]{:S(2)}, u32[]{:S(2)}) collective-permute-start(bf16[4,64,256]{2,1,0:T(8,128)(2,1)S(1)} %get-tuple-element.123), channel_id=1, source_target_pairs={{0,4},{2,6},{4,0},{6,2},{8,12},{10,14},{12,8},{14,10},{1,5},{3,7},... | collective-permute-start | bytes 393224 | tf_op jit(solution)/shard_map/ppermute | solution.py:23
  191.7 5.7 %collective-permute-start.20 = (bf16[2,64,512]{2,1,0:T(8,128)(2,1)}, bf16[2,64,512]{2,1,0:T(8,128)(2,1)}, u32[]{:S(2)}, u32[]{:S(2)}) collective-permute-start(bf16[2,64,512]{2,1,0:T(8,128)(2,1)} %get-tuple-element.125), channel_id=1, source_target_pairs={{0,4},{2,6},{4,0},{6,2},{8,12},{10,14},{12,8},{14,10},{1,5},{3,7},... | collective-permute-start | bytes 393224 | tf_op jit(solution)/shard_map/ppermute | solution.py:23
  191.7 4.6 %collective-permute-start.21 = (bf16[2,64,256]{2,1,0:T(8,128)(2,1)}, bf16[2,64,256]{2,1,0:T(8,128)(2,1)}, u32[]{:S(2)}, u32[]{:S(2)}) collective-permute-start(bf16[2,64,256]{2,1,0:T(8,128)(2,1)} %get-tuple-element.127), channel_id=1, source_target_pairs={{0,16},{16,0},{1,17},{17,1},{2,18},{18,2},{3,19},{19,3},{4,20},{20... | collective-permute-start | bytes 196616 | tf_op jit(solution)/shard_map/ppermute | solution.py:23
  201.4 16.6 %collective-permute-start.22 = (bf16[64,768]{1,0:T(8,128)(2,1)}, bf16[64,768]{1,0:T(8,128)(2,1)}, u32[]{:S(2)}, u32[]{:S(2)}) collective-permute-start(bf16[64,768]{1,0:T(8,128)(2,1)} %get-tuple-element.129), channel_id=1, source_target_pairs={{0,8},{2,10},{4,12},{6,14},{8,0},{10,2},{12,4},{14,6},{1,9},{3,11}... | collective-permute-start | bytes 294920 | tf_op jit(solution)/shard_map/ppermute | solution.py:23
  204.3 44.4 %collective-permute-start.7 = (bf16[8,64,256]{2,1,0:T(8,128)(2,1)}, bf16[8,64,256]{2,1,0:T(8,128)(2,1)}, u32[]{:S(2)}, u32[]{:S(2)}) collective-permute-start(bf16[8,64,256]{2,1,0:T(8,128)(2,1)} %copy-done.45), channel_id=1, source_target_pairs={{0,2},{2,0},{4,6},{6,4},{8,10},{10,8},{12,14},{14,12},{1,3},{3,1},... | collective-permute-start | bytes 786440 | tf_op jit(solution)/shard_map/ppermute | solution.py:23
  211.9 14.6 %collective-permute-start.29 = (bf16[2,64,2048]{2,1,0:T(8,128)(2,1)}, bf16[2,64,2048]{2,1,0:T(8,128)(2,1)}, u32[]{:S(2)}, u32[]{:S(2)}) collective-permute-start(bf16[2,64,2048]{2,1,0:T(8,128)(2,1)} %get-tuple-element.140), channel_id=1, source_target_pairs={{0,4},{2,6},{4,0},{6,2},{8,12},{10,14},{12,8},{14,10},{1,5},{3,7},... | collective-permute-start | bytes 1572872 | tf_op jit(solution)/shard_map/ppermute | solution.py:23
  212.6 14.4 %collective-permute-start.30 = (bf16[2,64,2048]{2,1,0:T(8,128)(2,1)}, bf16[2,64,2048]{2,1,0:T(8,128)(2,1)}, u32[]{:S(2)}, u32[]{:S(2)}) collective-permute-start(bf16[2,64,2048]{2,1,0:T(8,128)(2,1)} %get-tuple-element.142), channel_id=1, source_target_pairs={{0,16},{16,0},{1,17},{17,1},{2,18},{18,2},{3,19},{19,3},{4,20},{20... | collective-permute-start | bytes 1572872 | tf_op jit(solution)/shard_map/ppermute | solution.py:23
  213.5 17.5 %copy-start.7 = (f32[256,1024]{1,0:T(8,128)S(1)}, f32[256,1024]{1,0:T(8,128)}, u32[]{:S(2)}) copy-start(f32[256,1024]{1,0:T(8,128)} %copy-done.6) | copy-start | bytes 3145732
  213.5 17.5 %copy-start.15 = (f32[256,1024]{1,0:T(8,128)S(1)}, f32[256,1024]{1,0:T(8,128)}, u32[]{:S(2)}) copy-start(f32[256,1024]{1,0:T(8,128)} %copy-done.14) | copy-start | bytes 3145732
  216.4 14.6 %collective-permute-start.4 = (bf16[256,1024]{1,0:T(8,128)(2,1)S(1)}, bf16[256,1024]{1,0:T(8,128)(2,1)S(1)}, u32[]{:S(2)}, u32[]{:S(2)}) collective-permute-start(bf16[256,1024]{1,0:T(8,128)(2,1)S(1)} %get-tuple-element.94.own_ref), channel_id=1, source_target_pairs={{0,1},{1,0},{2,3},{3,2},{4,5},{5,4},{6,7},{7,6},{8,9},{9,8},{10,11... | collective-permute-start | bytes 1572872 | tf_op jit(solution)/shard_map/ppermute | solution.py:23
  220.2 27.3 %collective-permute-start.8 = (bf16[256,1536]{1,0:T(8,128)(2,1)}, bf16[256,1536]{1,0:T(8,128)(2,1)}, u32[]{:S(2)}, u32[]{:S(2)}) collective-permute-start(bf16[256,1536]{1,0:T(8,128)(2,1)} %get-tuple-element.103), channel_id=1, source_target_pairs={{0,2},{2,0},{4,6},{6,4},{8,10},{10,8},{12,14},{14,12},{1,3},{3,1},... | collective-permute-start | bytes 2359304 | tf_op jit(solution)/shard_map/ppermute | solution.py:23
  229.5 32.3 %collective-permute-start.31 = (bf16[64,4096]{1,0:T(8,128)(2,1)}, bf16[64,4096]{1,0:T(8,128)(2,1)}, u32[]{:S(2)}, u32[]{:S(2)}) collective-permute-start(bf16[64,4096]{1,0:T(8,128)(2,1)} %get-tuple-element.144), channel_id=1, source_target_pairs={{0,8},{2,10},{4,12},{6,14},{8,0},{10,2},{12,4},{14,6},{1,9},{3,11}... | collective-permute-start | bytes 1572872 | tf_op jit(solution)/shard_map/ppermute | solution.py:23
  233.7 10.5 %collective-permute-start.5 = (bf16[2,48,128]{2,1,0:T(8,128)(2,1)S(1)}, bf16[2,48,128]{2,1,0:T(8,128)(2,1)S(1)}, u32[]{:S(2)}, u32[]{:S(2)}) collective-permute-start(bf16[2,48,128]{2,1,0:T(8,128)(2,1)S(1)} %get-tuple-element.98), channel_id=1, source_target_pairs={{2,0},{4,2},{6,4},{8,6},{10,8},{12,10},{14,12},{0,14},{3,1},{5,3},... | collective-permute-start | bytes 73736 | tf_op jit(solution)/shard_map/ppermute | solution.py:29
  234.6 51.1 %all-to-all-start.5 = ((bf16[16,64,256]{2,1,0:T(8,128)(2,1)}), bf16[16,64,256]{2,1,0:T(8,128)(2,1)S(1)}, u32[]{:S(2)}, u32[]{:S(2)}) async-start(bf16[16,64,256]{2,1,0:T(8,128)(2,1)} %get-tuple-element.99), calls=%async_computation.5 | async-start | bytes 1048576 | tf_op jit(solution)/shard_map/all_to_all | solution.py:793
  238.4 8.4 %collective-permute-start.6 = (bf16[128,512]{1,0:T(8,128)(2,1)S(1)}, bf16[128,512]{1,0:T(8,128)(2,1)S(1)}, u32[]{:S(2)}, u32[]{:S(2)}) collective-permute-start(bf16[128,512]{1,0:T(8,128)(2,1)S(1)} %dynamic-slice_bitcast_fusion), channel_id=1, source_target_pairs={{0,16},{16,0},{1,17},{17,1},{2,18},{18,2},{3,19},{19,3},{4,20},{20... | collective-permute-start | bytes 393224 | tf_op jit(solution)/shard_map/ppermute | solution.py:23
  251.8 11.5 %collective-permute-start.9 = (bf16[4,64,768]{2,1,0:T(8,128)(2,1)S(1)}, bf16[4,64,768]{2,1,0:T(8,128)(2,1)S(1)}, u32[]{:S(2)}, u32[]{:S(2)}) collective-permute-start(bf16[4,64,768]{2,1,0:T(8,128)(2,1)S(1)} %get-tuple-element.105), channel_id=1, source_target_pairs={{0,16},{16,0},{1,17},{17,1},{2,18},{18,2},{3,19},{19,3},{4,20},{20... | collective-permute-start | bytes 1179656 | tf_op jit(solution)/shard_map/ppermute | solution.py:23
  252.2 15.6 %collective-permute-start.10 = (bf16[4,64,768]{2,1,0:T(8,128)(2,1)S(1)}, bf16[4,64,768]{2,1,0:T(8,128)(2,1)S(1)}, u32[]{:S(2)}, u32[]{:S(2)}) collective-permute-start(bf16[4,64,768]{2,1,0:T(8,128)(2,1)S(1)} %get-tuple-element.107), channel_id=1, source_target_pairs={{0,4},{2,6},{4,0},{6,2},{8,12},{10,14},{12,8},{14,10},{1,5},{3,7},... | collective-permute-start | bytes 1179656 | tf_op jit(solution)/shard_map/ppermute | solution.py:23
  268.7 7.2 %collective-permute-start.11 = (bf16[2,64,768]{2,1,0:T(8,128)(2,1)S(1)}, bf16[2,64,768]{2,1,0:T(8,128)(2,1)S(1)}, u32[]{:S(2)}, u32[]{:S(2)}) collective-permute-start(bf16[2,64,768]{2,1,0:T(8,128)(2,1)S(1)} %get-tuple-element.109), channel_id=1, source_target_pairs={{0,4},{2,6},{4,0},{6,2},{8,12},{10,14},{12,8},{14,10},{1,5},{3,7},... | collective-permute-start | bytes 589832 | tf_op jit(solution)/shard_map/ppermute | solution.py:23
  268.8 7.1 %collective-permute-start.12 = (bf16[2,64,768]{2,1,0:T(8,128)(2,1)S(1)}, bf16[2,64,768]{2,1,0:T(8,128)(2,1)S(1)}, u32[]{:S(2)}, u32[]{:S(2)}) collective-permute-start(bf16[2,64,768]{2,1,0:T(8,128)(2,1)S(1)} %get-tuple-element.111), channel_id=1, source_target_pairs={{0,16},{16,0},{1,17},{17,1},{2,18},{18,2},{3,19},{19,3},{4,20},{20... | collective-permute-start | bytes 589832 | tf_op jit(solution)/shard_map/ppermute | solution.py:23
  276.6 18.6 %collective-permute-start.13 = (bf16[64,1536]{1,0:T(8,128)(2,1)S(1)}, bf16[64,1536]{1,0:T(8,128)(2,1)S(1)}, u32[]{:S(2)}, u32[]{:S(2)}) collective-permute-start(bf16[64,1536]{1,0:T(8,128)(2,1)S(1)} %get-tuple-element.113), channel_id=1, source_target_pairs={{0,8},{2,10},{4,12},{6,14},{8,0},{10,2},{12,4},{14,6},{1,9},{3,11}... | collective-permute-start | bytes 589832 | tf_op jit(solution)/shard_map/ppermute | solution.py:23
  (45 other events, 235.7 us)
where the time goes:
time: 298 us; the launch traced here: 296 us
  waiting for transfers between devices  92.4 us (31%)
  Pallas kernels  56 us (19%)
  starting transfers between devices  52.2 us (18%)
  local copies, waits for them, and re-layouts  42.4 us (14%)
  blocking collectives  37.6 us (13%)
  other arithmetic  6.19 us (2%)
  between operations  5.08 us (2%)
  matrix products  4.56 us (2%)
    ppermute x30, waiting for transfers between devices, swap(): return lax.ppermute(block, axis, route)  84.4 us
    pallas_call x19, Pallas kernels, call(): pl.pallas_call(body, grid=grid, out_shape=list(outs), in_specs=in_specs,...  56 us
    ppermute x30, starting transfers between devices, swap(): return lax.ppermute(block, axis, route)  31.3 us
    unnamed x118, local copies, waits for them, and re-layouts  29 us
    all_to_all x1, blocking collectives, local(): lax.all_to_all(packed, 'lon', 0, 0, axis_index_groups=groups if far > 1 e...  25.2 us
    all_to_all x1, blocking collectives, local(): lax.all_to_all(attended, 'lon', 0, 0, axis_index_groups=groups if far > 1...  12.4 us
    all_to_all x1, starting transfers between devices, local(): lax.all_to_all(jnp.broadcast_to(moments, (everyone, 1, LANES)), ('dp', 'l...  7.36 us
  transfers between devices with their start and end apart: 36, of which 17 were waited for; matrix products, arithmetic and copies ran while one was open for 7% of the time, Pallas kernels for 13%

commit v1 on v0

v1 whole, which is shorter than its diff:
```python
import functools
import math

import jax
import jax.numpy as jnp
from jax import lax
from jax.experimental import pallas as pl
from jax.experimental.pallas import tpu as pltpu
from jax.sharding import PartitionSpec as P

HDIM = 64
PATCH = 2
LANES = 128
NORM_EPS = 1e-06
STAT_EPS = 1e-06
BF = jnp.bfloat16
F32 = jnp.float32
MIB = 2**20


def swap(block, axis, distance):
    route = [(i, i ^ distance) for i in range(lax.axis_size(axis))]
    return lax.ppermute(block, axis, route)


def from_behind(block, axis, distance):
    size = lax.axis_size(axis)
    route = [((i - distance) % size, i) for i in range(size)]
    return lax.ppermute(block, axis, route)


def pick(x, index, axis):
    return lax.dynamic_index_in_dim(x, index, axis, keepdims=False)


def halve(total, dims):
    for axis, bit in dims:
        side = (lax.axis_index(axis) // bit) % 2
        got = swap(pick(total, 1 - side, 0), axis, bit)
        total = (pick(total, side, 0).astype(F32) + got.astype(F32)).astype(BF)
    return total


def scatter(total):
    dp, lon = lax.axis_size("dp"), lax.axis_size("lon")
    dims = []
    for axis, size in (("dp", dp), ("lon", lon)):
        bit = size // 2
        while bit:
            dims.append((axis, bit))
            bit //= 2
    rows, columns = total.shape
    total = total.astype(BF).reshape((2,) * len(dims) + (rows // (dp * lon), columns))
    order = sorted(range(len(dims)), key=lambda i: (dims[i][1] > 1 or dims[i][0] == "dp", i))
    total = total.transpose([*order, len(dims), len(dims) + 1])
    return halve(total, [dims[i] for i in order]).astype(F32)


def nt(a, b):
    return lax.dot_general(a, b, (((1,), (1,)), ((), ())), preferred_element_type=F32)


def nn(a, b):
    return lax.dot_general(a, b, (((1,), (0,)), ((), ())), preferred_element_type=F32)


def item_mask(rows, lanes, item):
    lane = lax.broadcasted_iota(jnp.int32, (rows, lanes), 1)
    return (lane >= item * HDIM) & (lane < (item + 1) * HDIM)


def interleave(first, second):
    low = item_mask(first.shape[0], LANES, 0)
    return (
        jnp.where(low, first, pltpu.roll(second, HDIM, 1)),
        jnp.where(low, pltpu.roll(first, HDIM, 1), second),
    )


def norm_parts(hidden):
    centred = hidden - jnp.mean(hidden, axis=-1, keepdims=True)
    variance = jnp.mean(centred * centred, axis=-1, keepdims=True)
    inverse = lax.rsqrt(variance + NORM_EPS)
    return centred * inverse, inverse


def norm_back(unit, inverse, scaling, grad):
    scaled = grad * scaling
    back = inverse * (
        scaled
        - jnp.mean(scaled, axis=-1, keepdims=True)
        - unit * jnp.mean(scaled * unit, axis=-1, keepdims=True)
    )
    return back, jnp.sum(grad * unit, axis=0, keepdims=True)


def emit_turned(x, ids_ref, outs, hold):
    turned = x.T.astype(BF)
    if len(outs) == 1:
        outs[0][...] = turned
        return
    keep, send = outs
    parts, rows, tokens = keep.shape
    hold[...] = turned.reshape(parts, 2, rows, tokens)
    core = ids_ref[0]
    keep[...] = hold[:, pl.ds(core, 1)].reshape(parts, rows, tokens)
    send[...] = hold[:, pl.ds(1 - core, 1)].reshape(parts, rows, tokens)


class Warm:
    def __init__(self, value):
        self.value = value


def call(body, name, outs, *args, after=(), grid=(), in_specs=None, out_specs=None, scratch=(), limit=24, flops=0):
    vmem = pl.BlockSpec(memory_space=pltpu.VMEM)
    smem = pl.BlockSpec(memory_space=pltpu.SMEM)
    shapes = [o.value if isinstance(o, Warm) else o for o in outs]
    plain = [a.value if isinstance(a, Warm) else a for a in args]
    if in_specs is None:
        in_specs = [smem if a.dtype == jnp.int32 else vmem for a in plain]
    if out_specs is None:
        out_specs = [vmem] * len(outs)
    token = pl.BlockSpec((8, LANES), lambda *at: (0, 0)) if grid else vmem
    nbytes = sum(math.prod(a.shape) * a.dtype.itemsize for a in [*plain, *shapes])
    here, skip, there = len(args), len(after), len(outs)

    def with_token(*refs):
        refs = list(refs)
        refs[here + skip + there][...] = jnp.zeros((8, LANES), F32)
        body(*refs[:here], *refs[here + skip : here + skip + there], *refs[here + skip + there + 1 :])

    def cold(x):
        if isinstance(x, Warm):
            return x.value
        return x if x.dtype == jnp.int32 else pltpu.with_memory_space_constraint(x, pltpu.HBM)

    return pl.pallas_call(
        with_token,
        grid=grid,
        out_shape=[
            *[o.value if isinstance(o, Warm) else pltpu.HBM(o.shape, o.dtype) for o in outs],
            pltpu.HBM((8, LANES), F32),
        ],
        in_specs=[*in_specs, *[pl.BlockSpec(memory_space=pl.ANY)] * skip],
        out_specs=[*out_specs, token],
        scratch_shapes=list(scratch),
        compiler_params=pltpu.CompilerParams(vmem_limit_bytes=limit * MIB),
        cost_estimate=pl.CostEstimate(flops=int(flops), bytes_accessed=nbytes, transcendentals=0),
        name=name,
    )(*[cold(a) for a in args], *[cold(a) for a in after])


def shape(dims, kind=BF):
    return jax.ShapeDtypeStruct(dims, kind)


def warm(dims, kind=BF):
    return Warm(shape(dims, kind))


def feature_order(variables, back):
    features = PATCH * PATCH * variables
    natural = lax.broadcasted_iota(jnp.int32, (features, features), 1 if back else 0)
    sorted_ = lax.broadcasted_iota(jnp.int32, (features, features), 0 if back else 1)
    hit = (natural // 4 == sorted_ % variables) & (natural % 4 == sorted_ // variables)
    return jnp.where(hit, 1.0, 0.0).astype(BF)


def send_pairs(ids_ref, hold, messages):
    if len(messages) == 1:
        messages[0][...] = hold[...]
        return
    for k, message in enumerate(messages):
        message[...] = hold[pl.ds(2 * ids_ref[4 + k], 2)]


def moments_kernel(index_ref, data_ref, fields_ref, edge_ref, moments_ref, turn_ref, sems):
    items, variables, height = edge_ref.shape
    cols = fields_ref.shape[1] // variables
    copies = [
        pltpu.make_async_copy(data_ref.at[index_ref[i]], fields_ref.at[i], sems.at[i])
        for i in range(items)
    ]
    for copy in copies:
        copy.start()
    turn_ref[...] = jnp.zeros_like(turn_ref)
    for copy in copies:
        copy.wait()
    blocks = [
        fields_ref[i, pl.ds(c, variables, stride=cols), :] for i in range(items) for c in range(cols)
    ]
    for i in range(items):
        edge_ref[i] = blocks[i * cols + cols - 1].astype(BF)
    count = float(items * cols * height)
    mean = jnp.sum(sum(blocks), axis=1, keepdims=True) * (1.0 / count)
    spread = jnp.sum(sum(jnp.square(b - mean) for b in blocks), axis=1, keepdims=True)
    turn_ref[0:variables, 0:1] = mean
    turn_ref[HDIM : HDIM + variables, 0:1] = spread
    turned = turn_ref[...].T
    moments_ref[...] = jnp.broadcast_to(turned[0:1, :][None], moments_ref.shape)


def start_kernel(local_count, ids_ref, mom_ref, count_ref, mean_ref, var_ref, fields_ref, edge_ref, we_ref,
                 pos_ref, gains_ref, wq_ref, new_count_ref, new_mean_ref, new_var_ref, hidden_ref, patches_ref,
                 *rest):
    (*outs, column_ref, run_ref, hold, weights, sem, qkv_ref) = rest
    if len(outs) > 2:
        messages, turned = outs[:-2], outs[-2:]
    else:
        messages, turned = outs[:1], outs[1:]
    copy = pltpu.make_async_copy(wq_ref, weights, sem)
    copy.start()
    members = mom_ref.shape[0]
    items, rows, height = fields_ref.shape
    variables = edge_ref.shape[1]
    cols = rows // variables
    half = height // PATCH
    moments = mom_ref[:, 0, :]
    run_ref[...] = jnp.zeros_like(run_ref)
    for k, ref in enumerate((count_ref, mean_ref, var_ref)):
        run_ref[k : k + 1, 0:variables] = ref[...]
    batch_count = local_count * members
    batch_mean = jnp.sum(moments, axis=0, keepdims=True) * (1.0 / members)
    off = moments - batch_mean
    spread = jnp.sum(pltpu.roll(moments, HDIM, 1) + local_count * off * off, axis=0, keepdims=True)
    run_count, run_mean, run_var = (run_ref[k : k + 1, :] for k in range(3))
    new_count = run_count + batch_count
    shift = batch_mean - run_mean
    new_mean = run_mean + shift * (batch_count / new_count)
    new_var = (
        run_var * run_count + spread + shift * shift * (run_count * batch_count / new_count)
    ) / new_count
    new_count_ref[...] = new_count[:, 0:variables]
    new_mean_ref[...] = new_mean[:, 0:variables]
    new_var_ref[...] = new_var[:, 0:variables]
    column_ref[...] = jnp.zeros_like(column_ref)
    column_ref[0:1, :] = new_mean
    column_ref[1:2, :] = lax.rsqrt(new_var + STAT_EPS)
    column = column_ref[...].T
    centre, inverse = column[0:variables, 0:1], column[0:variables, 1:2]

    def scaled(block):
        return ((block - centre) * inverse).astype(BF)

    row = lax.broadcasted_iota(jnp.int32, (2 * height, LANES), 0)
    lane = lax.broadcasted_iota(jnp.int32, (2 * height, LANES), 1)
    sort = [
        jnp.where(
            (row // height == lane // half) & (row % height == PATCH * (lane % half) + a), 1.0, 0.0
        ).astype(BF)
        for a in range(PATCH)
    ]
    natural = feature_order(variables, False)
    hidden = []
    for item in range(items):
        west = scaled(edge_ref[item].astype(F32))
        own = [
            scaled(fields_ref[item, pl.ds(c, variables, stride=cols), :]) for c in range(cols - 1)
        ]
        first = jnp.concatenate([west, own[0]], axis=0)
        second = jnp.concatenate([own[1], own[2]], axis=0)
        both = jnp.concatenate([first, second], axis=1)
        patches = jnp.concatenate([nn(both, sort[a]) for a in range(PATCH)], axis=0)
        patches = nn(natural, patches.astype(BF))
        patches_ref[:, item * LANES : (item + 1) * LANES] = patches.astype(BF)
        hidden.append(nn(patches.T.astype(BF), we_ref[...]) + pos_ref[...].astype(F32))
    hidden = jnp.concatenate(hidden, axis=0)
    hidden_ref[...] = hidden
    unit, _ = norm_parts(hidden)
    normed = unit * gains_ref[0:1, :]
    low = normed.astype(BF)
    emit_turned(normed, ids_ref, turned, hold)
    copy.wait()
    for c in range(3):
        product = nn(low, weights[c])
        for t in range(product.shape[1] // LANES):
            tile = product[:, t * LANES : (t + 1) * LANES]
            a, b = interleave(tile[:LANES], tile[LANES:])
            qkv_ref[2 * t, c] = a.astype(BF)
            qkv_ref[2 * t + 1, c] = b.astype(BF)
    send_pairs(ids_ref, qkv_ref, messages)


def cotangent_kernel(ids_ref, ct_ref, wh_ref, wd_ref, two_ref, act_ref, ct_turned_ref, *rest):
    if rest:
        mine_ref, hold = rest
        hold[...] = wh_ref[...].astype(F32).T.astype(BF).reshape(hold.shape)
        mine_ref[...] = hold[ids_ref[8]]
    grads = []
    for item in range(ct_ref.shape[0]):
        ct = ct_ref[item].T.astype(BF)
        ct_turned_ref[:, item * LANES : (item + 1) * LANES] = ct_ref[item].astype(BF)
        grads.append(nn(ct, wh_ref[...]))
    d_two = jnp.concatenate(grads, axis=0)
    two_ref[...] = d_two
    act_ref[...] = nt(d_two.astype(BF), wd_ref[...])


def attend_kernel(items, scale, q_ref, kv_ref, o_ref, ot_ref, pt_ref, vt_ref):
    keys = kv_ref.shape[0] * kv_ref.shape[2]

    @pl.when(pl.program_id(0) == 0)
    def _():
        vt_ref[...] = kv_ref[:, 2].reshape(keys, LANES).astype(F32).T.astype(BF)

    rows = q_ref.shape[0] * q_ref.shape[2]
    queries = q_ref[:, 0].reshape(rows, LANES) * BF(scale)
    key_rows = kv_ref[:, 1].reshape(keys, LANES)
    for item in range(items):
        chosen = jnp.where(item_mask(rows, LANES, item), queries, BF(0))
        scores = nt(key_rows, chosen)
        top = jnp.max(scores, axis=0, keepdims=True)
        raised = jnp.exp(scores - top)
        total = jnp.sum(raised, axis=0, keepdims=True)
        weights = (raised * (1.0 / total)).astype(BF)
        pt_ref[item] = weights
        span = slice(item * HDIM, (item + 1) * HDIM)
        ot_ref[span, :] = nn(vt_ref[span, :], weights)
    o_ref[...] = ot_ref[...].T.astype(BF).reshape(o_ref.shape)


def attend(q, kv, items, scale, after):
    peers, _, tokens, lanes = q.shape
    rows, keys = peers * tokens, kv.shape[0] * tokens
    step = max(1, min(peers, 256 * 1024 // keys // tokens))
    block = step * tokens
    return call(
        functools.partial(attend_kernel, items, scale),
        "attend",
        [
            shape((peers, tokens, lanes)),
            shape((lanes, rows), F32),
            shape((items, keys, rows)),
        ],
        Warm(q),
        Warm(kv),
        after=after,
        grid=(peers // step,),
        in_specs=[
            pl.BlockSpec((step, 3, tokens, lanes), lambda j: (j, 0, 0, 0)),
            pl.BlockSpec(kv.shape, lambda j: (0, 0, 0, 0)),
        ],
        out_specs=[
            pl.BlockSpec((step, tokens, lanes), lambda j: (j, 0, 0)),
            pl.BlockSpec((lanes, block), lambda j: (0, j)),
            pl.BlockSpec((items, keys, block), lambda j: (0, 0, j)),
        ],
        scratch=[pltpu.VMEM((lanes, keys), BF)],
        limit=24 if keys <= 2048 else 56,
        flops=8 * rows * keys * lanes,
    )


def pair_attend_kernel(items, scale, *refs):
    sources, (*outs, ot_ref, pt_ref, query_rows, key_rows, vt_ref) = refs[:8], refs[8:]
    tokens = sources[0].shape[2]
    step = pl.program_id(1)

    @pl.when(step == 0)
    def _():
        for k, source in enumerate(sources):
            span = slice(k * tokens, (k + 1) * tokens)
            if k < len(outs):
                query_rows[span, :] = source[0, 0] * BF(scale)
            key_rows[span, :] = source[0, 1]
            vt_ref[:, span] = source[0, 2].astype(F32).T.astype(BF)

    block = ot_ref.shape[2]
    queries = query_rows[pl.ds(pl.multiple_of(step * block, block), block), :]
    for item in range(items):
        chosen = jnp.where(item_mask(block, LANES, item), queries, BF(0))
        scores = nt(key_rows[...], chosen)
        top = jnp.max(scores, axis=0, keepdims=True)
        raised = jnp.exp(scores - top)
        total = jnp.sum(raised, axis=0, keepdims=True)
        weights = (raised * (1.0 / total)).astype(BF)
        pt_ref[0, item] = weights
        span = slice(item * HDIM, (item + 1) * HDIM)
        ot_ref[0, span, :] = nn(vt_ref[span, :], weights)
    attended = ot_ref[0].T.astype(BF)
    per = block // tokens
    for j in range(len(outs) // per):

        @pl.when(step == j)
        def _():
            for k in range(per):
                outs[j * per + k][0] = attended[k * tokens : (k + 1) * tokens]


def pair_attend(own, other, items, scale, after):
    _, _, tokens, lanes = own[0].shape
    rows, keys = len(own) * tokens, 2 * len(own) * tokens
    block = rows // 2
    message = pl.BlockSpec((1, tokens, lanes), lambda h, j: (h, 0, 0))
    *outs, ot, pt, token = call(
        functools.partial(pair_attend_kernel, items, scale),
        "attend",
        [
            *[shape((2, tokens, lanes))] * len(own),
            shape((2, lanes, rows), F32),
            shape((2, items, keys, rows)),
        ],
        own[0],
        *[Warm(x) for x in [*own[1:], *other]],
        after=after,
        grid=(2, 2),
        in_specs=[pl.BlockSpec((1, 3, tokens, lanes), lambda h, j: (h, 0, 0, 0))] * (2 * len(own)),
        out_specs=[
            *[message] * len(own),
            pl.BlockSpec((1, lanes, block), lambda h, j: (h, 0, j)),
            pl.BlockSpec((1, items, keys, block), lambda h, j: (h, 0, 0, j)),
        ],
        scratch=[
            pltpu.VMEM((rows, lanes), BF),
            pltpu.VMEM((keys, lanes), BF),
            pltpu.VMEM((lanes, keys), BF),
        ],
        flops=16 * rows * keys * lanes,
    )
    return outs, ot, pt, token


def pair_attend_back_kernel(items, scale, ids_ref, *refs):
    sources, grads_ref, refs = refs[:8], refs[8], refs[9:]
    ot_ref, pt_ref, *outs, cross_ref, query_rows, key_rows, value_rows, kt_ref, grad_rows, dqt_ref, dk_sum, dv_sum = refs
    tokens = sources[0].shape[2]
    step = pl.program_id(1)

    @pl.when(step == 0)
    def _():
        for k, source in enumerate(sources):
            span = slice(k * tokens, (k + 1) * tokens)
            if k < len(outs):
                query_rows[span, :] = source[0, 0] * BF(scale)
                grad_rows[span, :] = grads_ref[ids_ref[4 + k], 0]
            key_rows[span, :] = source[0, 1]
            kt_ref[:, span] = (source[0, 1].astype(F32) * scale).T.astype(BF)
            value_rows[span, :] = source[0, 2]
        dk_sum[...] = jnp.zeros_like(dk_sum)
        dv_sum[...] = jnp.zeros_like(dv_sum)

    block = ot_ref.shape[2]
    at = pl.ds(pl.multiple_of(step * block, block), block)
    queries, grad_block = query_rows[at, :], grad_rows[at, :]
    product = grad_block.astype(F32).T * ot_ref[0]
    for item in range(items):
        span = slice(item * HDIM, (item + 1) * HDIM)
        mask = item_mask(block, LANES, item)
        grad = jnp.where(mask, grad_block, BF(0))
        query = jnp.where(mask, queries, BF(0))
        delta = jnp.sum(product[span, :], axis=0, keepdims=True)
        weights = pt_ref[0, item]
        back = (weights.astype(F32) * (nt(value_rows[...], grad) - delta)).astype(BF)
        dv_sum[...] += nn(weights, grad)
        dk_sum[...] += nn(back, query)
        dqt_ref[span, :] = nn(kt_ref[span, :], back)
    d_query = dqt_ref[...].T.astype(BF)
    per = block // tokens
    for j in range(len(outs) // per):

        @pl.when(step == j)
        def _():
            for k in range(per):
                outs[j * per + k][0, 0] = d_query[k * tokens : (k + 1) * tokens]

    @pl.when(step == pl.num_programs(1) - 1)
    def _():
        for k in range(2 * len(outs)):
            span = slice(k * tokens, (k + 1) * tokens)
            for c, total in ((0, dk_sum), (1, dv_sum)):
                if k < len(outs):
                    outs[k][0, 1 + c] = total[span, :].astype(BF)
                else:
                    cross_ref[k - len(outs), 0, c] = total[span, :].astype(BF)


def pair_attend_back(ids, own, other, d, ot, pt, items, scale, after):
    _, _, tokens, lanes = own[0].shape
    count = len(own)
    rows, keys = count * tokens, 2 * count * tokens
    block = rows // 2
    head = pl.BlockSpec((1, 3, tokens, lanes), lambda h, j: (h, 0, 0, 0))
    *outs, cross, token = call(
        functools.partial(pair_attend_back_kernel, items, scale),
        "attend_back",
        [*[shape((2, 3, tokens, lanes))] * count, shape((count, 2, 2, tokens, lanes))],
        ids, *own, *other, d, ot, pt,
        after=after,
        grid=(2, 2),
        in_specs=[
            pl.BlockSpec(memory_space=pltpu.SMEM),
            *[head] * (2 * count),
            pl.BlockSpec((count, 1, tokens, lanes), lambda h, j: (0, h, 0, 0)),
            pl.BlockSpec((1, lanes, block), lambda h, j: (h, 0, j)),
            pl.BlockSpec((1, items, keys, block), lambda h, j: (h, 0, 0, j)),
        ],
        out_specs=[
            *[head] * count,
            pl.BlockSpec((count, 1, 2, tokens, lanes), lambda h, j: (0, h, 0, 0, 0)),
        ],
        scratch=[
            pltpu.VMEM((rows, lanes), BF),
            pltpu.VMEM((keys, lanes), BF),
            pltpu.VMEM((keys, lanes), BF),
            pltpu.VMEM((lanes, keys), BF),
            pltpu.VMEM((rows, lanes), BF),
            pltpu.VMEM((lanes, block), F32),
            pltpu.VMEM((keys, lanes), F32),
            pltpu.VMEM((keys, lanes), F32),
        ],
        flops=32 * rows * keys * lanes,
    )
    return outs, cross, token


def combine_kernel(*refs):
    count = (len(refs) - 1) // 2
    own, cross_ref, outs = refs[:count], refs[count], refs[count + 1 :]
    for k in range(count):
        outs[k][:, 0] = own[k][:, 0]
        for c in range(2):
            outs[k][:, 1 + c] = plus(own[k].at[:, 1 + c], cross_ref.at[k, :, c])


def attend_back_kernel(items, scale, q_ref, kv_ref, d_ref, ot_ref, pt_ref, dq_ref, *rest):
    dkv_ref, (kt_ref, dqt_ref, dk_sum, dv_sum) = rest[:-4], rest[-4:]
    step = pl.program_id(0)
    keys = kv_ref.shape[0] * kv_ref.shape[2]

    @pl.when(step == 0)
    def _():
        kt_ref[...] = (kv_ref[:, 1].reshape(keys, LANES).astype(F32) * scale).T.astype(BF)
        dk_sum[...] = jnp.zeros_like(dk_sum)
        dv_sum[...] = jnp.zeros_like(dv_sum)

    peers, _, tokens, _ = q_ref.shape
    rows = peers * tokens
    queries = q_ref[:, 0].reshape(rows, LANES) * BF(scale)
    grads = d_ref[...].reshape(rows, LANES)
    value_rows = kv_ref[:, 2].reshape(keys, LANES)
    product = grads.astype(F32).T * ot_ref[...]
    for item in range(items):
        span = slice(item * HDIM, (item + 1) * HDIM)
        mask = item_mask(rows, LANES, item)
        grad = jnp.where(mask, grads, BF(0))
        query = jnp.where(mask, queries, BF(0))
        delta = jnp.sum(product[span, :], axis=0, keepdims=True)
        weights = pt_ref[item]
        back = (weights.astype(F32) * (nt(value_rows, grad) - delta)).astype(BF)
        dv_sum[...] += nn(weights, grad)
        dk_sum[...] += nn(back, query)
        dqt_ref[span, :] = nn(kt_ref[span, :], back)
    d_query = dqt_ref[...].T.astype(BF).reshape(peers, tokens, LANES)
    if dkv_ref:
        dq_ref[...] = d_query
    else:
        dq_ref[pl.ds(step * peers, peers), 0] = d_query

    @pl.when(step == pl.num_programs(0) - 1)
    def _():
        for c, total in ((1, dk_sum), (2, dv_sum)):
            total = total[...].reshape(kv_ref.shape[0], tokens, LANES)
            if dkv_ref:
                dkv_ref[0][:, c - 1] = total
            else:
                dq_ref[:, c] = total.astype(BF)


def attend_back(q, kv, d, ot, pt, items, scale, after):
    peers, _, tokens, lanes = q.shape
    rows, keys = peers * tokens, kv.shape[0] * tokens
    step = max(1, min(peers, 256 * 1024 // keys // tokens))
    block = step * tokens
    if q.shape == kv.shape:
        outs = [shape(q.shape)]
        out_specs = [pl.BlockSpec(q.shape, lambda j: (0, 0, 0, 0))]
    else:
        outs = [shape((peers, tokens, lanes)), shape((kv.shape[0], 2, tokens, lanes), F32)]
        out_specs = [
            pl.BlockSpec((step, tokens, lanes), lambda j: (j, 0, 0)),
            pl.BlockSpec(outs[1].shape, lambda j: (0, 0, 0, 0)),
        ]
    *back, token = call(
        functools.partial(attend_back_kernel, items, scale),
        "attend_back",
        outs,
        Warm(q),
        Warm(kv),
        d,
        ot,
        pt,
        after=after,
        grid=(peers // step,),
        in_specs=[
            pl.BlockSpec((step, 3, tokens, lanes), lambda j: (j, 0, 0, 0)),
            pl.BlockSpec(kv.shape, lambda j: (0, 0, 0, 0)),
            pl.BlockSpec((step, tokens, lanes), lambda j: (j, 0, 0)),
            pl.BlockSpec((lanes, block), lambda j: (0, j)),
            pl.BlockSpec((items, keys, block), lambda j: (0, 0, j)),
        ],
        out_specs=out_specs,
        scratch=[
            pltpu.VMEM((lanes, keys), BF),
            pltpu.VMEM((lanes, block), F32),
            pltpu.VMEM((keys, lanes), F32),
            pltpu.VMEM((keys, lanes), F32),
        ],
        limit=24 if keys <= 2048 else 60,
        flops=16 * rows * keys * lanes,
    )
    return back, token


def unpack(ids_ref, sources, index, out_ref, base):
    several = len(sources) > 1
    count = len(sources) if several else sources[0].shape[0] // 2
    for t in range(count):
        source, head = (sources[t], 0) if several else (sources[0], 2 * t)
        pair = [
            (source[head + s] if index is None else source[head + s, index]).astype(F32) for s in range(2)
        ]
        at = base + (pl.multiple_of(ids_ref[4 + t] * LANES, LANES) if several else t * LANES)
        for item, tile in enumerate(interleave(*pair)):
            out_ref[item * LANES : (item + 1) * LANES, pl.ds(at, LANES)] = tile.astype(BF)


def pack(product, out_ref):
    for t in range(product.shape[1] // LANES):
        tile = product[:, t * LANES : (t + 1) * LANES]
        for s, block in enumerate(interleave(tile[:LANES], tile[LANES:])):
            out_ref[2 * t + s] = block.astype(BF)


def project_kernel(ids_ref, *refs):
    *sources, wo_ref, mixed_ref, branch_ref = refs
    unpack(ids_ref, sources, None, mixed_ref, 0)
    branch_ref[...] = nn(mixed_ref[...], wo_ref[...]).astype(BF)


def forward_kernel(ids_ref, zero_ref, own_ref, got_ref, gains_ref, wu_ref, dact_ref,
                   one_ref, copy_ref, norm_ref, pre_ref, act_ref, other_ref, *rest):
    turned, (normed_ref, total_ref, hold) = rest[:-3], rest[-3:]
    step = pl.program_id(0)

    @pl.when(step == 0)
    def _():
        hidden = zero_ref[...] + (own_ref[...].astype(F32) + got_ref[...].astype(F32))
        one_ref[...] = hidden
        copy_ref[...] = hidden
        unit, _ = norm_parts(hidden)
        normed = unit * gains_ref[1:2, :]
        normed_ref[...] = normed.astype(BF)
        emit_turned(normed, ids_ref, turned, hold)
        total_ref[...] = jnp.zeros_like(total_ref)

    pre = nn(normed_ref[...], wu_ref[...])
    chance = 0.5 * (1.0 + lax.erf(pre * (1.0 / math.sqrt(2.0))))
    slope = chance + pre * jnp.exp(-0.5 * pre * pre) * (1.0 / math.sqrt(2.0 * math.pi))
    activated = (pre * chance).astype(BF)
    act_ref[0] = activated
    block = activated.shape[1]
    per_half = other_ref.shape[1] // block

    @pl.when(step // per_half == 1 - ids_ref[0])
    def _():
        at = pl.multiple_of(step % per_half * block, LANES)
        other_ref[:, pl.ds(at, block)] = activated

    d_pre = (dact_ref[...] * slope).astype(BF)
    pre_ref[...] = d_pre
    total_ref[...] += nt(d_pre, wu_ref[...])

    @pl.when(step == pl.num_programs(0) - 1)
    def _():
        norm_ref[...] = total_ref[...].astype(BF)


def second_kernel(ids_ref, one_ref, two_ref, own_ref, got_ref, gains_ref, wo_ref, d_ref, gain_ref, *rest):
    heads_ref, *turned, hold = rest
    unit, inverse = norm_parts(one_ref[...])
    grad = own_ref[...].astype(F32) + got_ref[...].astype(F32)
    back, gain = norm_back(unit, inverse, gains_ref[1:2, :], grad)
    gain_ref[...] = gain
    d_one = two_ref[...] + back
    d_ref[...] = d_one
    pack(nt(d_one.astype(BF), wo_ref[...]), heads_ref)
    emit_turned(d_one, ids_ref, turned, hold)


def head_kernel(ids_ref, one_ref, own_ref, got_ref, wh_ref, pred_ref, *rest):
    turned, hold = rest[:-1], rest[-1]
    hidden = one_ref[...] + (own_ref[...].astype(F32) + got_ref[...].astype(F32))
    low = hidden.astype(BF)
    for item in range(pred_ref.shape[0]):
        pred_ref[item] = nt(wh_ref[...], low[item * LANES : (item + 1) * LANES])
    emit_turned(hidden, ids_ref, turned, hold)


def third_kernel(count, ids_ref, *refs):
    sources, (wq_ref, dqkv_ref, norm_ref) = refs[:count], refs[count:]
    width = wq_ref.shape[2]
    total = None
    for c in range(3):
        unpack(ids_ref, sources, c, dqkv_ref, c * width)
        part = nt(dqkv_ref[:, c * width : (c + 1) * width], wq_ref[c])
        total = part if total is None else total + part
    norm_ref[...] = total.astype(BF)


def last_kernel(cols, ids_ref, zero_ref, done_ref, own_ref, got_ref, gains_ref, gain_two_ref, patches_ref, we_ref,
                pos_send, pos_keep, fields_ref, edge_ref, *rest):
    embed, (rows_ref, pos_ref, hold) = rest[:-3], rest[-3:]
    unit, inverse = norm_parts(zero_ref[...])
    grad = own_ref[...].astype(F32) + got_ref[...].astype(F32)
    back, gain = norm_back(unit, inverse, gains_ref[0:1, :], grad)
    d_zero = done_ref[...] + back
    low = d_zero.astype(BF)
    items, variables, height = edge_ref.shape
    pos = d_zero[0:LANES]
    for item in range(1, items):
        pos = pos + d_zero[item * LANES : (item + 1) * LANES]
    width = pos_ref.shape[2]
    for k in range(2):
        pos_ref[k] = pos[:, k * width : (k + 1) * width].astype(BF)
    pos_send[...] = pos_ref[1 - ids_ref[1]]
    pos_keep[...] = pos_ref[ids_ref[1]]
    features = patches_ref.shape[0]
    rows_ref[...] = jnp.zeros_like(rows_ref)
    rows_ref[0:features, :] = nn(patches_ref[...], low)
    rows_ref[features : features + 1, :] = gain
    rows_ref[features + 1 : features + 2, :] = gain_two_ref[...]
    emit_turned(rows_ref[...], ids_ref, embed, hold)
    half = height // PATCH
    row = lax.broadcasted_iota(jnp.int32, (LANES, height), 0)
    lane = lax.broadcasted_iota(jnp.int32, (LANES, height), 1)
    fields_ref[...] = jnp.zeros_like(fields_ref)
    order = feature_order(variables, True)
    for item in range(items):
        d_patches = nt(we_ref[...], low[item * LANES : (item + 1) * LANES])
        high = d_patches.astype(BF)
        rest = (d_patches - high.astype(F32)).astype(BF)
        high, rest = nn(order, high).astype(BF), nn(order, rest).astype(BF)
        for j in range(2):
            total = None
            for a in range(PATCH):
                place = jnp.where(
                    (row // half == j) & (lane == PATCH * (row % half) + a), 1.0, 0.0
                ).astype(BF)
                span = slice(a * 2 * variables, (a + 1) * 2 * variables)
                part = nn(high[span], place) + nn(rest[span], place)
                total = part if total is None else total + part
            for b in range(PATCH):
                block = total[b * variables : (b + 1) * variables]
                column = 2 * j + b - 1
                if column < 0:
                    edge_ref[item] = block.astype(BF)
                else:
                    fields_ref[item, pl.ds(column, variables, stride=cols), :] = block


def down_kernel(act_ref, wd_ref, out_ref):
    width = act_ref.shape[2]
    total = nn(act_ref[0], wd_ref[0:width, :]) + nn(act_ref[1], wd_ref[width:, :])
    out_ref[...] = total.astype(BF)


def pin(xs, after):
    def body(*refs):
        pass

    anywhere = pl.BlockSpec(memory_space=pl.ANY)
    several = isinstance(xs, (list, tuple))
    xs = list(xs) if several else [xs]
    out = pl.pallas_call(
        body,
        out_shape=[pltpu.HBM(x.shape, x.dtype) for x in xs],
        in_specs=[anywhere] * (len(xs) + len(after)),
        out_specs=[anywhere] * len(xs),
        input_output_aliases={k: k for k in range(len(xs))},
        name="pin",
    )(*[pltpu.with_memory_space_constraint(x, pltpu.HBM) for x in xs], *after)
    return out if several else out[0]


def product_of(own, got, b_own, b_got):
    parts, rows, tokens = own.shape
    total = nn(own[...].reshape(parts * rows, tokens), b_own)
    return total + nn(got[...].reshape(parts * rows, tokens), b_got)


def split_dp(ids_ref, hold, send, keep, columns):
    half = hold.shape[0] // 2
    for out, at in ((send, 1 - ids_ref[1]), (keep, ids_ref[1])):
        for k in range(half):
            out[k, :, 0:columns] = hold[at * half + k]


def split_near(ids_ref, hold, send, keep, columns):
    for out, at in ((send, 1 - ids_ref[2]), (keep, ids_ref[2])):
        for k in range(hold.shape[0] // 2):
            out[k, :, 0:columns] = hold[2 * k + at]


def plus(a, b):
    return (a[...].astype(F32) + b[...].astype(F32)).astype(BF)


def grads_ff_kernel(ids_ref, at_own, at_got, pre_own, pre_got, ct_own, ct_got, act_own, act_got,
                    send_a, keep_a, send_b, keep_b, hold, inner):
    parts, rows, total = hold.shape
    columns = total - keep_b.shape[2]
    product = product_of(at_own, at_got, pre_own[...], pre_got[...])
    hold[...] = product.astype(BF).reshape(hold.shape)
    split_dp(ids_ref, hold.at[:, :, 0:columns], send_a, keep_a, columns)
    split_near(ids_ref, hold.at[:, :, columns:], send_b, keep_b, total - columns)
    product = (nn(ct_own[...], act_own[ids_ref[0]]) + nn(ct_got[...], act_got[...])).astype(BF)
    tiles, groups = inner.shape[1], inner.shape[3] // LANES
    for k in range(2):
        for q in range(tiles):
            for g in range(groups):
                inner[k, q, :, g * LANES : (g + 1) * LANES] = product[
                    g * rows : (g + 1) * rows, (k * tiles + q) * LANES : (k * tiles + q + 1) * LANES
                ]
    for q in range(tiles):
        send_a[q, :, columns:] = inner[1 - ids_ref[1], q]
        keep_a[q, :, columns:] = inner[ids_ref[1], q]


def fold_ff_kernel(ids_ref, keep_a, got_a, keep_b, got_b, send_a, left_a, send_b, left_b, hold, hold_b):
    columns = hold.shape[2]
    extra = keep_a.shape[2] - columns
    hold[...] = plus(keep_a.at[:, :, 0:columns], got_a.at[:, :, 0:columns])
    split_near(ids_ref, hold, send_a, left_a, columns)
    for q in range(keep_a.shape[0]):
        total = plus(keep_a.at[q, :, columns:], got_a.at[q, :, columns:])
        at = columns + q % 2 * extra
        for out in (send_a, left_a):
            out[q // 2, :, at : at + extra] = total
    hold_b[...] = plus(keep_b, got_b)
    split_dp(ids_ref, hold_b, send_b, left_b, hold_b.shape[2])


def merge_ff_kernel(ids_ref, keep_a, got_a, keep_b, got_b, send, left, hold):
    columns = hold.shape[2] - keep_b.shape[2]
    extra = keep_a.shape[2] - columns
    hold[:, :, 0:columns] = plus(keep_a.at[:, :, 0:columns], got_a.at[:, :, 0:columns])
    hold[:, :, columns:] = plus(keep_b, got_b)
    far = ids_ref[3]
    width = hold.shape[2]
    send[:, 0:width] = hold[1 - far]
    left[:, 0:width] = hold[far]
    for k in range(2):
        total = plus(keep_a.at[k, :, columns:], got_a.at[k, :, columns:])
        at = width + k * extra
        for out in (send, left):
            out[:, at : at + extra] = total


def grads_oh_kernel(ids_ref, one_own, one_got, mixed_own, mixed_got, two_own, two_got, ct_own, ct_got,
                    send, keep, hold):
    width, features = mixed_own.shape[1], ct_own.shape[0]
    shape3 = hold.shape[:2]
    product = product_of(one_own, one_got, mixed_own[...], mixed_got[...])
    hold[:, :, 0:width] = product.astype(BF).reshape(*shape3, width)
    hold[:, :, width:] = jnp.zeros((*shape3, hold.shape[2] - width), BF)
    product = product_of(
        two_own, two_got, ct_own[...].astype(F32).T.astype(BF), ct_got[...].astype(F32).T.astype(BF)
    )
    hold[:, :, width : width + features] = product.astype(BF).reshape(*shape3, features)
    split_dp(ids_ref, hold, send, keep, hold.shape[2])


def grads_q_kernel(ids_ref, at_own, at_got, b_own, b_got, send_a, keep_a, send_b, keep_b, hold):
    cut, total = keep_a.shape[2], hold.shape[2]
    hold[...] = product_of(at_own, at_got, b_own[...], b_got[...]).astype(BF).reshape(hold.shape)
    split_dp(ids_ref, hold.at[:, :, 0:cut], send_a, keep_a, cut)
    split_near(ids_ref, hold.at[:, :, cut:], send_b, keep_b, total - cut)


def fold_q_kernel(ids_ref, keep_a, got_a, keep_b, got_b, up_keep, up_got, oh_keep, oh_got, embed_own, embed_got,
                  send_a, left_a, send_b, left_b, send_o, left_o, hold_a, hold_b, hold_o, hold_e):
    hold_a[...] = plus(keep_a, got_a)
    split_near(ids_ref, hold_a, send_a, left_a, hold_a.shape[2])
    hold_b[...] = plus(keep_b, got_b)
    columns = hold_b.shape[2]
    split_dp(ids_ref, hold_b, send_b, left_b, columns)
    hold_o[...] = plus(oh_keep, oh_got)
    split_near(ids_ref, hold_o, send_o, left_o, hold_o.shape[2])
    hold_e[...] = plus(embed_own, embed_got)
    width = hold_e.shape[2]
    for out, at in ((send_b, 1 - ids_ref[1]), (left_b, ids_ref[1])):
        for k in range(4):
            start = columns + k % 2 * width
            out[k // 2, :, start : start + width] = hold_e[4 * at + k]
    start = columns + 2 * width
    half = send_b.shape[2] - start
    for k in range(2):
        at = up_keep.shape[1] - (2 - k) * half
        total = plus(up_keep.at[:, at : at + half], up_got.at[:, at : at + half])
        for out in (send_b, left_b):
            out[k, :, start:] = total


def merge_q_kernel(ids_ref, keep_a, got_a, keep_b, got_b, oh_keep, oh_got, send, left, pair_ref, *rest):
    *embeds, hold, hold_e = rest
    width = embeds[0].shape[1]
    half = pair_ref.shape[2] // 2
    first = keep_a.shape[2]
    columns = keep_b.shape[2] - half - 2 * width
    hold[:, :, 0:first] = plus(keep_a, got_a)
    hold[:, :, first : first + columns] = plus(keep_b.at[:, :, 0:columns], got_b.at[:, :, 0:columns])
    hold[:, :, first + columns :] = plus(oh_keep, oh_got)
    far, near = ids_ref[3], ids_ref[2]
    send[...] = hold[1 - far]
    left[...] = hold[far]
    for k in range(2):
        span = slice(k * half, (k + 1) * half)
        pair_ref[0, :, span] = keep_b[k, :, columns + 2 * width :]
        pair_ref[1, :, span] = got_b[k, :, columns + 2 * width :]
    for k in range(4):
        span = slice(columns + k % 2 * width, columns + (k % 2 + 1) * width)
        hold_e[k] = plus(keep_b.at[k // 2, :, span], got_b.at[k // 2, :, span])
    for out, at in zip(
        embeds, (2 * far + near, 2 * far + 1 - near, 2 * (1 - far) + near, 2 * (1 - far) + 1 - near)
    ):
        out[...] = hold_e[at]


def expand(ids_ref, rows_ref, pair_own, pair_got, out_ref, block):
    rows = rows_ref.shape[0]
    groups = block.shape[0] // rows
    tiles = block.shape[1] // LANES
    for a, b in ((0, 0), (0, 1), (1, 0), (1, 1)):
        source = pair_got if a else pair_own
        for q in range(tiles):
            for g in range(groups):
                at = (q * groups + g) * LANES
                block[g * rows : (g + 1) * rows, q * LANES : (q + 1) * LANES] = source[b, :, at : at + LANES]
        core, dp = (1 - ids_ref[0] if a else ids_ref[0]), (1 - ids_ref[1] if b else ids_ref[1])
        at = pl.multiple_of((core * 2 + dp) * block.shape[1], LANES)
        out_ref[:, pl.ds(at, block.shape[1])] = nn(rows_ref[...], block[...])


def insert_east(cols, fields_ref, east_ref, out_ref):
    variables = east_ref.shape[1]
    out_ref[...] = fields_ref[...]
    for item in range(east_ref.shape[0]):
        out_ref[item, pl.ds(cols - 1, variables, stride=cols), :] = east_ref[item].astype(F32)


def close_kernel(cols, ids_ref, fields_ref, east_ref, pos_ref, pos_got_ref, *refs):
    outs = refs
    if len(refs) > 2:
        (up_ref, up_got_ref, rows_ref, pair_own, pair_got), outs, block = refs[:5], refs[5:-1], refs[-1]
        width = outs[2].shape[1]
        outs[2][...] = up_ref[:, 0:width].astype(F32) + up_got_ref[:, 0:width].astype(F32)
        expand(ids_ref, rows_ref, pair_own, pair_got, outs[3], block)
    insert_east(cols, fields_ref, east_ref, outs[0])
    outs[1][...] = pos_ref[...].astype(F32) + pos_got_ref[...].astype(F32)


def end_kernel(count, *refs):
    parts, refs = refs[:count], refs[count:]
    if len(refs) > 2:
        (keep_ref, got_ref), refs = refs[:2], refs[2:]
        out_ref, head_ref, grad_ref = refs[2:]
        both = keep_ref[...].astype(F32) + got_ref[...].astype(F32)
        width = grad_ref.shape[2]
        for c in range(3):
            grad_ref[c] = both[:, c * width : (c + 1) * width]
        out_ref[...] = both[:, 3 * width : 4 * width]
        head_ref[...] = both[:, 4 * width : 4 * width + head_ref.shape[1]]
    parts = [parts[0].at[k] for k in range(parts[0].shape[0])] if count == 1 else parts
    total = parts[0][...].astype(F32)
    for part in parts[1:]:
        total = total + part[...].astype(F32)
    features = refs[0].shape[1]
    refs[0][...] = total[:, 0:features]
    refs[1][...] = total[:, LANES:].T[features - LANES : features - LANES + 2, :]


def local(
    dataset,
    indices,
    run_count,
    run_mean,
    run_var,
    w_embed,
    pos_embed,
    gains,
    w_qkv,
    w_out,
    w_up,
    w_down,
    w_head,
    cotangent,
):
    items = indices.shape[0]
    variables, height, columns = dataset.shape[1:]
    dp, lon = lax.axis_size("dp"), lax.axis_size("lon")
    everyone = dp * lon
    width = w_embed.shape[1]
    local_width = w_qkv.shape[2]
    heads = local_width // HDIM
    item_tokens = cotangent.shape[1]
    tokens = items * item_tokens
    features = w_embed.shape[0]
    hidden_units = w_up.shape[1]
    scale = 1.0 / math.sqrt(HDIM)
    group, far = heads, lon // heads
    groups = [[group * g + i for i in range(group)] for g in range(far)]
    across = [[i + group * g for g in range(far)] for i in range(group)]
    assert items * HDIM == LANES and item_tokens == LANES and height == LANES and columns == 4
    lon_at, dp_at = lax.axis_index("lon"), lax.axis_index("dp")
    ids = [lon_at % 2, dp_at, lon_at // 2 % 2, lon_at // 4 % 2, *[lon_at // 2 ^ k for k in range(4)], dp_at * lon + lon_at]
    ids = jnp.stack(ids).astype(jnp.int32)
    paired = dp == 2 and lon == 8
    parts, rows = width // (2 * (width // everyone)), width // everyone
    turned_shape = (
        [shape((parts, rows, tokens))] * 2 if paired else [shape((width, tokens))]
    )
    turned_hold = pltpu.VMEM((parts, 2, rows, tokens) if paired else (8, LANES), BF)

    alone = dict(axis_index_groups=groups) if far > 1 else {}

    vmem, smem = pl.BlockSpec(memory_space=pltpu.VMEM), pl.BlockSpec(memory_space=pltpu.SMEM)
    assert dp == 2

    data = dataset.transpose(0, 1, 3, 2).reshape(dataset.shape[0], variables * columns, height)
    fields, edge, moments, _ = call(
        moments_kernel,
        "moments",
        [
            warm((items, variables * columns, height), F32),
            warm((items, variables, height)),
            warm((everyone, 8, LANES), F32),
        ],
        indices, data,
        in_specs=[pl.BlockSpec(memory_space=pltpu.SMEM), pl.BlockSpec(memory_space=pl.ANY)],
        scratch=[pltpu.VMEM((LANES, LANES), F32), pltpu.SemaphoreType.DMA((items,))],
    )
    edge = from_behind(edge, "lon", 1)
    moments = lax.all_to_all(moments, ("dp", "lon"), 0, 0)
    wh_turned = w_head.T

    out = call(
        functools.partial(start_kernel, float(items * height * columns)),
        "start",
        [
            *[shape((1, variables), F32)] * 3,
            shape((tokens, width), F32),
            shape((features, tokens)),
            *([shape((2, 3, item_tokens, LANES))] * 4 if paired else [shape((heads, 3, item_tokens, LANES))]),
            *turned_shape,
        ],
        ids, Warm(moments), *[r.reshape(1, variables) for r in (run_count, run_mean, run_var)],
        Warm(fields), Warm(edge), w_embed, pos_embed, gains, w_qkv,
        in_specs=[smem, *[vmem] * 9, pl.BlockSpec(memory_space=pl.ANY)],
        scratch=[
            pltpu.VMEM((LANES, LANES), F32),
            pltpu.VMEM((8, LANES), F32),
            turned_hold,
            pltpu.VMEM(w_qkv.shape, BF),
            pltpu.SemaphoreType.DMA,
            pltpu.VMEM((heads, 3, item_tokens, LANES), BF),
        ],
        flops=2 * tokens * width * (features + 3 * local_width),
    )
    count = 4 if paired else 1
    stats, (hidden_zero, patches), packed = out[:3], out[3:5], out[5 : 5 + count]
    normed_one, token = out[5 + count : -1], out[-1]

    def along(messages):
        return [messages[0], *[swap(messages[k], "lon", 2 * k) for k in range(1, count)]]

    if paired:
        own = along(packed)
    else:
        sent = lax.all_to_all(packed[0], "lon", 0, 0, **alone)
        kv = sent
        if far > 1:
            kv = lax.all_gather(sent, "lon", axis=0, tiled=True, axis_index_groups=across)

    d_two, d_act, ct_turned, *mine, token = call(
        cotangent_kernel,
        "cotangent",
        [
            shape((tokens, width), F32),
            shape((tokens, hidden_units), F32),
            shape((features, tokens)),
            *[shape((rows, features))] * paired,
        ],
        ids, cotangent.transpose(0, 2, 1), wh_turned, w_down,
        after=[token],
        scratch=[pltpu.VMEM((everyone, rows, features), BF)] * paired,
        flops=2 * tokens * width * (features + hidden_units),
    )

    if paired:
        ct_got = swap(ct_turned, "lon", 1)
        own[0] = pin(own[0], [token])
        other = [swap(x, "lon", 1) for x in own]
    if paired:
        attended, attended_t, weights_t, token = pair_attend(own, other, items, scale, [token])
        attended = along(attended)
    else:
        attended, attended_t, weights_t, token = attend(sent, kv, items, scale, [token])
        attended = [lax.all_to_all(attended, "lon", 0, 0, **alone)]
    mixed, branch, token = call(
        project_kernel,
        "project",
        [shape((tokens, local_width)), warm((tokens, width))],
        ids, attended[0], *[Warm(x) for x in attended[1:]], Warm(w_out),
        after=[token],
        flops=2 * tokens * width * local_width,
    )
    branch_got = swap(branch, "mp", 1)
    block = min(512, hidden_units // 2)
    per_half = hidden_units // 2 // block
    column = lambda j: (0, j)
    whole = lambda j: (0, 0)
    full = pl.BlockSpec((tokens, width), whole)
    turned_specs = (
        [pl.BlockSpec((parts, rows, tokens), lambda j: (0, 0, 0))] * 2
        if paired
        else [pl.BlockSpec((width, tokens), whole)]
    )
    out = call(
        forward_kernel,
        "forward",
        [
            warm((tokens, width), F32),
            shape((tokens, width), F32),
            warm((tokens, width)),
            shape((tokens, hidden_units)),
            shape((2, tokens, hidden_units // 2)),
            shape((tokens, hidden_units // 2)),
            *turned_shape,
        ],
        ids, Warm(hidden_zero), Warm(branch), Warm(branch_got), gains, Warm(w_up), Warm(d_act),
        after=[token],
        grid=(hidden_units // block,),
        in_specs=[
            pl.BlockSpec(memory_space=pltpu.SMEM),
            full,
            full,
            full,
            pl.BlockSpec(gains.shape, whole),
            pl.BlockSpec((width, block), column),
            pl.BlockSpec((tokens, block), column),
        ],
        out_specs=[
            full,
            full,
            full,
            pl.BlockSpec((tokens, block), column),
            pl.BlockSpec((1, tokens, block), lambda j: (j // per_half, 0, j % per_half)),
            pl.BlockSpec((tokens, hidden_units // 2), whole),
            *turned_specs,
        ],
        scratch=[pltpu.VMEM((tokens, width), BF), pltpu.VMEM((tokens, width), F32), turned_hold],
        flops=4 * tokens * width * hidden_units,
    )
    hidden_one, hidden_copy, d_norm, d_pre, activated, act_send = out[:6]
    normed_two, token = out[6:-1], out[-1]
    d_norm_got = swap(d_norm, "mp", 1)
    half = hidden_units // 2
    if paired:
        inner_columns = features // rows * LANES
        first = half - LANES
        out_a = shape((parts // 2, rows, first + inner_columns))
        out_b = shape((parts // 2, rows, hidden_units - first))
        send_a, keep_a, send_b, keep_b, token = call(
            grads_ff_kernel,
            "grads_ff",
            [out_a, out_a, out_b, out_b],
            ids, normed_two[0], Warm(swap(normed_two[1], "lon", 1)), d_pre, Warm(swap(d_pre, "lon", 1)),
            ct_turned, Warm(ct_got), activated, Warm(swap(act_send, "lon", 1)),
            after=[token],
            scratch=[
                pltpu.VMEM((parts, rows, hidden_units), BF),
                pltpu.VMEM((2, parts // 2, rows, inner_columns), BF),
            ],
            limit=32,
            flops=2 * tokens * (width + features) * hidden_units,
        )
        got_a, got_b = swap(send_a, "dp", 1), swap(send_b, "lon", 2)
    forward, token = call(
        down_kernel,
        "down",
        [shape((tokens, width))],
        activated, w_down,
        after=[token],
        flops=2 * tokens * width * hidden_units,
    )

    out = call(
        second_kernel,
        "second",
        [
            shape((tokens, width), F32),
            shape((1, width), F32),
            shape((heads, item_tokens, LANES)),
            *turned_shape,
        ],
        ids, Warm(hidden_one), Warm(d_two), Warm(d_norm), Warm(d_norm_got), gains, Warm(w_out),
        after=[token],
        scratch=[turned_hold],
        flops=2 * tokens * width * local_width,
    )
    d_one, gain_two, d_mixed = out[0], out[1], out[2:3]
    d_one_turned, token = out[3:-1], out[-1]
    if paired:
        chips = [[2 * k + c for k in range(lon // 2)] for c in range(2)]
        d_heads = lax.all_to_all(
            d_mixed[0].reshape(lon // 2, 2, item_tokens, LANES), "lon", 0, 0, axis_index_groups=chips
        )
    else:
        d_heads = lax.all_to_all(d_mixed[0], "lon", 0, 0, **alone)
    forward_got = swap(forward, "mp", 1)
    if paired:
        out_a = shape((2, rows, first + 2 * inner_columns))
        out_b = shape((2, rows, hidden_units - first))
        send_a, keep_a, send_b, keep_b, token = call(
            fold_ff_kernel,
            "fold_ff",
            [out_a, out_a, out_b, out_b],
            ids, keep_a, Warm(got_a), keep_b, Warm(got_b),
            after=[token],
            scratch=[
                pltpu.VMEM((parts // 2, rows, first), BF),
                pltpu.VMEM((parts // 2, rows, hidden_units - first), BF),
            ],
        )
        send_a, send_b = pin([send_a, send_b], [d_heads])
        got_a, got_b = swap(send_a, "lon", 2), swap(send_b, "dp", 1)

    if paired:
        back, cross, token = pair_attend_back(
            ids, own, other, d_heads, attended_t, weights_t, items, scale, [token]
        )
        *back, token = call(
            combine_kernel,
            "combine",
            [shape(x.shape) for x in back],
            *back, Warm(swap(pin(cross, [got_a, got_b, forward_got]), "lon", 1)),
            after=[token],
        )
        back = along(back)
    else:
        back, token = attend_back(sent, kv, d_heads, attended_t, weights_t, items, scale, [token])
        if far > 1:
            d_query, d_kv = back
            d_kv = lax.psum_scatter(
                d_kv, "lon", scatter_dimension=0, tiled=True, axis_index_groups=across
            ).astype(BF)
            back = [jnp.concatenate([d_query[:, None], d_kv], axis=1)]
        back = [lax.all_to_all(back[0], "lon", 0, 0, **alone)]
    out = call(
        head_kernel,
        "head",
        [shape((items, features, item_tokens), F32), *turned_shape],
        ids, hidden_copy, forward, Warm(forward_got), wh_turned,
        after=[token],
        scratch=[turned_hold],
        flops=2 * tokens * width * features,
    )
    pred, hidden_turned, token = out[0].transpose(0, 2, 1), list(out[1:-1]), out[-1]
    if paired:
        up_send, up_keep, token = call(
            merge_ff_kernel,
            "merge_ff",
            [shape((rows, hidden_units + 4 * inner_columns))] * 2,
            ids, keep_a, Warm(got_a), keep_b, Warm(got_b),
            after=[token],
            scratch=[pltpu.VMEM((2, rows, hidden_units), BF)],
        )
    d_qkv, d_norm, token = call(
        functools.partial(third_kernel, count),
        "third",
        [shape((tokens, 3 * local_width)), warm((tokens, width))],
        ids, back[0], *[Warm(x) for x in back[1:]], Warm(w_qkv),
        after=[token],
        flops=6 * tokens * width * local_width,
    )
    d_norm_got = swap(d_norm, "mp", 1)
    if paired:
        up_send, hidden_turned[1] = pin([up_send, hidden_turned[1]], [token])
        up_got = swap(up_send, "lon", 4)
        wide = local_width + 2 * LANES
        cut = 3 * local_width // 2 + LANES
        first, second = (shape((parts // 2, rows, c)) for c in (cut, 3 * local_width - cut))
        send_a, keep_a, send_b, keep_b, token = call(
            grads_q_kernel,
            "grads_q",
            [first, first, second, second],
            ids, normed_one[0], Warm(swap(normed_one[1], "lon", 1)), d_qkv, Warm(swap(d_qkv, "lon", 1)),
            after=[token],
            scratch=[pltpu.VMEM((parts, rows, 3 * local_width), BF)],
            flops=6 * tokens * width * local_width,
        )
        oh_send, oh_keep, token = call(
            grads_oh_kernel,
            "grads_oh",
            [shape((parts // 2, rows, wide))] * 2,
            ids, d_one_turned[0], Warm(swap(d_one_turned[1], "lon", 1)), mixed, Warm(swap(mixed, "lon", 1)),
            hidden_turned[0], Warm(swap(hidden_turned[1], "lon", 1)), ct_turned, Warm(ct_got),
            after=[token],
            scratch=[pltpu.VMEM((parts, rows, wide), BF)],
            flops=2 * tokens * width * wide,
        )
        oh_got = swap(oh_send, "dp", 1)
        got_a, got_b = swap(send_a, "dp", 1), swap(send_b, "lon", 2)

    out = call(
        functools.partial(last_kernel, columns),
        "last",
        [
            *[shape((item_tokens, width // 2))] * 2,
            shape((items, variables * columns, height), F32),
            shape((items, variables, height)),
            *([shape((parts, rows, 2 * LANES))] * 2 if paired else [shape((width, 2 * LANES))]),
        ],
        ids, Warm(hidden_zero), Warm(d_one), Warm(d_norm), Warm(d_norm_got), gains, gain_two, patches, w_embed,
        after=[token],
        scratch=[
            pltpu.VMEM((2 * LANES, width), F32),
            pltpu.VMEM((2, item_tokens, width // 2), BF),
            pltpu.VMEM((parts, 2, rows, 2 * LANES) if paired else (8, LANES), BF),
        ],
        flops=4 * tokens * width * features,
    )
    pos_send, pos, d_fields, d_edge = out[:4]
    embed, token = out[4:-1], out[-1]
    if not paired:
        east, pos_got = from_behind(d_edge, "lon", -1), swap(pos_send, "dp", 1)
    more, more_outs, more_scratch, rest, rest_outs = [], [], [], [], []
    if paired:
        embed_width = embed[0].shape[2]
        step_a, side = shape((2, rows, cut)), shape((2, rows, wide))
        step_b = shape((2, rows, 3 * local_width - cut + 2 * embed_width + 2 * inner_columns))
        send_a, keep_a, send_b, keep_b, oh_send, oh_keep, token = call(
            fold_q_kernel,
            "fold_q",
            [step_a, step_a, step_b, step_b, side, side],
            ids, keep_a, Warm(got_a), keep_b, Warm(got_b), up_keep, Warm(up_got), oh_keep, Warm(oh_got),
            embed[0], Warm(swap(embed[1], "lon", 1)),
            after=[token],
            scratch=[
                pltpu.VMEM(keep_a.shape, BF),
                pltpu.VMEM(keep_b.shape, BF),
                pltpu.VMEM(oh_keep.shape, BF),
                pltpu.VMEM(embed[0].shape, BF),
            ],
        )
        got_a, got_b, oh_got = swap(send_a, "lon", 2), swap(send_b, "dp", 1), swap(oh_send, "lon", 2)
        d_edge, pos_send = pin([d_edge, pos_send], [token])
        east, pos_got = from_behind(d_edge, "lon", -1), swap(pos_send, "dp", 1)
        final, block = shape((rows, 3 * local_width + wide)), shape((rows, embed_width))
        send, keep, pair, *embed, token = call(
            merge_q_kernel,
            "merge_q",
            [final, final, shape((2, rows, 4 * inner_columns)), *[block] * 4],
            ids, keep_a, Warm(got_a), keep_b, Warm(got_b), oh_keep, Warm(oh_got),
            after=[token, east, pos_got],
            scratch=[pltpu.VMEM((2, *final.shape), BF), pltpu.VMEM((4, *block.shape), BF)],
        )
        embed = [embed[0], *[Warm(swap(e, "lon", 2 * (k + 1))) for k, e in enumerate(embed[1:])]]
        more = [up_keep, Warm(up_got), mine[0], pair, Warm(swap(pair, "lon", 1))]
        more_outs = [shape((rows, hidden_units), F32)] * 2
        more_scratch = [pltpu.VMEM((features, hidden_units // 4), BF)]
        rest = [keep, Warm(swap(send, "lon", 4))]
        rest_outs = [
            shape((rows, local_width), F32),
            shape((rows, features), F32),
            shape((3, rows, local_width), F32),
        ]
    else:
        embed = [lax.all_to_all(embed[0].reshape(everyone, rows, 2 * LANES), ("dp", "lon"), 0, 0)]
    *closed, token = call(
        functools.partial(close_kernel, columns),
        "close",
        [shape(d_fields.shape, F32), shape(pos.shape, F32), *more_outs],
        ids, d_fields, Warm(east), pos, Warm(pos_got), *more,
        after=[token],
        scratch=more_scratch,
    )
    *ended, token = call(
        functools.partial(end_kernel, len(embed)),
        "end",
        [shape((rows, features), F32), shape((2, rows), F32), *rest_outs],
        *embed, *rest,
        after=[token],
    )
    if paired:
        grad_up, grad_down, (grad_out, grad_head, grad_qkv) = closed[2], closed[3], ended[2:]
    else:
        flat = activated.transpose(1, 0, 2).reshape(tokens, hidden_units)
        grad_up = scatter(nn(normed_two[0], d_pre))
        grad_down = scatter(nn(d_two.T.astype(BF), flat))
        grad_out = scatter(nn(d_one_turned[0], mixed))
        grad_head = scatter(nt(hidden_turned[0], ct_turned))
        grad_qkv = scatter(nn(normed_one[0], d_qkv)).reshape(rows, 3, local_width).transpose(1, 0, 2)
    return (
        pred,
        *[x.reshape(variables) for x in stats],
        closed[0].reshape(items, variables, columns, height).transpose(0, 1, 3, 2),
        ended[0].T,
        closed[1],
        ended[1],
        grad_qkv,
        grad_out.T,
        grad_up,
        grad_down.T,
        grad_head,
    )


def solution(mesh):
    in_specs = (
        P(None, None, None, "lon"),
        P("dp"),
        P(),
        P(),
        P(),
        P(),
        P("lon", None),
        P(),
        P(None, None, "mp"),
        P("mp", None),
        P(None, "mp"),
        P("mp", None),
        P(),
        P("dp", "lon", None),
    )
    out_specs = (
        P("dp", "lon", None),
        P(),
        P(),
        P(),
        P("dp", None, None, "lon"),
        P(None, ("dp", "lon")),
        P("lon", "dp"),
        P(None, ("dp", "lon")),
        P(None, ("dp", "lon"), "mp"),
        P("mp", ("dp", "lon")),
        P(("dp", "lon"), "mp"),
        P("mp", ("dp", "lon")),
        P(("dp", "lon"), None),
    )
    return jax.shard_map(local, mesh=mesh, in_specs=in_specs, out_specs=out_specs, check_vma=False)
```

time: 298 us -> 234 us (0.79)
  blocking collectives: 37.6 us -> 0 us
  local copies, waits for them, and re-layouts: 42.4 us -> 8.33 us
  Pallas kernels: 56 us -> 87.5 us
  waiting for transfers between devices: 92.4 us -> 80 us
  other arithmetic: 6.19 us -> 0 us
  matrix products: 4.56 us -> 0 us
  between operations: 5.08 us -> 0.94 us
  starting transfers between devices: 52.2 us -> 56 us
    all_to_all x2 -> x0, blocking collectives: 37.6 us -> none  [the longest x1 25.2 us: local(): lax.all_to_all(packed, 'lon', 0, 0, axis_index_groups=groups if far > 1 e...]
    pallas_call x19 -> x27, Pallas kernels: 56 us -> 87.5 us  [the longest x22 87.5 us: call(): pl.pallas_call(with_token, grid=grid, out_shape=[*[o.value if isinstance(...]
    unnamed x118 -> x52, local copies, waits for them, and re-layouts: 29 us -> 8.24 us
    ppermute x30 -> x45, waiting for transfers between devices: 84.4 us -> 67.7 us  [swap(): return lax.ppermute(block, axis, route)]
    ppermute x30 -> x45, starting transfers between devices: 31.3 us -> 42.2 us  [swap(): return lax.ppermute(block, axis, route)]
    all_to_all x4 -> x2, starting transfers between devices: 19.6 us -> 11 us  [the longest x1 7.37 us: local(): moments = lax.all_to_all(moments, ('dp', 'lon'), 0, 0)]
    ppermute x2, waiting for transfers between devices: 4.1 us -> 9.33 us  [from_behind(): return lax.ppermute(block, axis, route)]
    dot_general x1 -> x0, matrix products: 4.56 us -> none  [nn(): lax.dot_general(a, b, (((1,), (0,)), ((), ())), preferred_element_type=F32)]
  transfers between devices with their start and end apart: 36 -> 49, of which waited for: 17 -> 24; matrix products, arithmetic and copies ran while one was open for 7% -> 0% of each run, Pallas kernels for 13% -> 20%
where the time goes in v1:
time: 234 us; the launch traced here: 233 us
  Pallas kernels  87.5 us (37%)
  waiting for transfers between devices  80 us (34%)
  starting transfers between devices  56 us (24%)
  local copies, waits for them, and re-layouts  8.33 us (4%)
    pallas_call x22, Pallas kernels, call(): pl.pallas_call(with_token, grid=grid, out_shape=[*[o.value if isinstance(...  87.5 us
    ppermute x45, waiting for transfers between devices, swap(): return lax.ppermute(block, axis, route)  67.7 us
    ppermute x45, starting transfers between devices, swap(): return lax.ppermute(block, axis, route)  42.2 us
    ppermute x2, waiting for transfers between devices, from_behind(): return lax.ppermute(block, axis, route)  9.33 us
    unnamed x52, local copies, waits for them, and re-layouts  8.24 us
    all_to_all x1, starting transfers between devices, local(): moments = lax.all_to_all(moments, ('dp', 'lon'), 0, 0)  7.37 us
  transfers between devices with their start and end apart: 49, of which 24 were waited for; matrix products, arithmetic and copies ran while one was open for 0% of the time, Pallas kernels for 20%

profile of v1, /device:TPU:0, one launch (start us, length us, event | category | flops | bytes accessed | tf_op | source)
XLA Modules:
  0.0 232.7 jit_solution(16453895674643599856)
XLA Ops:
  1.3 2.4 %moments.1 = (f32[2,192,128]{2,1,0:T(8,128)S(1)}, bf16[2,48,128]{2,1,0:T(8,128)(2,1)S(1)}, f32[16,8,128]{2,1,0:T(8,128)}, f32[8,128]{1,0:T(8,128)}) custom-call(s32[2]{0:T(128)S(1)} %copy-done.14, f32[12,192,128]{2,1,0:T(8,128)} %bitcast.30), custom_call_target="tpu_custom_call" | custom-call | bytes 1466376 | tf_op jit(solution)/shard_map/moments/pallas_call | solution.py:138
  3.7 7.4 %all-to-all-start = ((f32[16,8,128]{2,1,0:T(8,128)}), f32[16,8,128]{2,1,0:T(8,128)S(1)}, u32[]{:S(2)}, u32[]{:S(2)}) async-start(f32[16,8,128]{2,1,0:T(8,128)} %get-tuple-element.137), calls=%async_computation | async-start | bytes 131072 | tf_op jit(solution)/shard_map/all_to_all | solution.py:1044
  11.6 5.5 %collective-permute-done.refs_6_ = bf16[2,48,128]{2,1,0:T(8,128)(2,1)S(1)} collective-permute-done((bf16[2,48,128]{2,1,0:T(8,128)(2,1)S(1)}, bf16[2,48,128]{2,1,0:T(8,128)(2,1)S(1)}, u32[]{:S(2)}, u32[]{:S(2)}) %collective-permute-start) | collective-permute-done | bytes 24608 | tf_op jit(solution)/shard_map/ppermute | solution.py:29
  18.2 5.7 %start.1 = (f32[1,48]{1,0:T(1,128)}, f32[1,48]{1,0:T(1,128)}, f32[1,48]{1,0:T(1,128)}, f32[256,1024]{1,0:T(8,128)}, bf16[192,256]{1,0:T(8,128)(2,1)}, /*index=5*...) custom-call(s32[9]{0:T(128)S(1)} %stack.39.refs_0_, ...), custom_call_target="tpu_custom_call" | custom-call | flops 905969664 | bytes 6554788 | tf_op jit(solution)/shard_map/start/pallas_call | solution.py:138
  24.9 3.4 %collective-permute-start.3 = (bf16[2,3,128,128]{3,2,1,0:T(8,128)(2,1)}, bf16[2,3,128,128]{3,2,1,0:T(8,128)(2,1)S(1)}, u32[]{:S(2)}, u32[]{:S(2)}) collective-permute-start(bf16[2,3,128,128]{3,2,1,0:T(8,128)(2,1)} %get-tuple-element.146), channel_id=1, source_target_pairs={{0,12},{2,14},{4,8},{6,10},{8,4},{10,6},{12,0},{14,2},{1,13},{3,15... | collective-permute-start | bytes 589832 | tf_op jit(solution)/shard_map/ppermute | solution.py:23
  28.3 5.4 %cotangent.1 = (f32[256,1024]{1,0:T(8,128)}, f32[256,2048]{1,0:T(8,128)}, bf16[192,256]{1,0:T(8,128)(2,1)}, bf16[64,192]{1,0:T(8,128)(2,1)}, f32[8,128]{1,0:T(8,128)}) custom-call(s32[9]{0:T(128)S(1)} %stack.39.refs_0_, f32[2,192,128]{2,1,0:T(8,128)} %bitcast.32, bf16[192,1024]{1,0:T(8,128)(2,1)} %bitcast.28, bf16[2048,1024]{1,0:T(8,128)(2,1)} %refs_1_.1, ...), custom_call_target="tpu_custom_call" | custom-call | flops 1174405120 | bytes 8052772 | tf_op jit(solution)/shard_map/cotangent/pallas_call | solution.py:138
  34.3 7.1 %collective-permute-done.2.refs_2_.refs_3_ = bf16[2,3,128,128]{3,2,1,0:T(8,128)(2,1)S(1)} collective-permute-done((bf16[2,3,128,128]{3,2,1,0:T(8,128)(2,1)}, bf16[2,3,128,128]{3,2,1,0:T(8,128)(2,1)S(1)}, u32[]{:S(2)}, u32[]{:S(2)}) %collective-permute-start.2) | collective-permute-done | bytes 196640 | tf_op jit(solution)/shard_map/ppermute | solution.py:23
  43.1 10.0 %attend.1 = (bf16[2,128,128]{2,1,0:T(8,128)(2,1)}, bf16[2,128,128]{2,1,0:T(8,128)(2,1)}, bf16[2,128,128]{2,1,0:T(8,128)(2,1)}, bf16[2,128,128]{2,1,0:T(8,128)(2,...) custom-call(bf16[2,3,128,128]{3,2,1,0:T(8,128)(2,1)} %pin.5.refs_0_.refs_1_, ...), custom_call_target="tpu_custom_call" | custom-call | flops 1073741824 | bytes 6553600 | tf_op jit(solution)/shard_map/attend/pallas_call | solution.py:138
  54.5 2.6 %collective-permute-start.8 = (bf16[2,128,128]{2,1,0:T(8,128)(2,1)}, bf16[2,128,128]{2,1,0:T(8,128)(2,1)S(1)}, u32[]{:S(2)}, u32[]{:S(2)}) collective-permute-start(bf16[2,128,128]{2,1,0:T(8,128)(2,1)} %get-tuple-element.148), channel_id=1, source_target_pairs={{0,4},{2,6},{4,0},{6,2},{8,12},{10,14},{12,8},{14,10},{1,5},{3,7},... | collective-permute-start | bytes 196616 | tf_op jit(solution)/shard_map/ppermute | solution.py:23
  60.9 2.7 %collective-permute-done.9.refs_3_ = bf16[2,128,128]{2,1,0:T(8,128)(2,1)S(1)} collective-permute-done((bf16[2,128,128]{2,1,0:T(8,128)(2,1)}, bf16[2,128,128]{2,1,0:T(8,128)(2,1)S(1)}, u32[]{:S(2)}, u32[]{:S(2)}) %collective-permute-start.9) | collective-permute-done | bytes 65568 | tf_op jit(solution)/shard_map/ppermute | solution.py:23
  63.6 1.8 project.1
  67.0 12.1 %collective-permute-done.11.refs_3_ = bf16[256,1024]{1,0:T(8,128)(2,1)S(1)} collective-permute-done((bf16[256,1024]{1,0:T(8,128)(2,1)S(1)}, bf16[256,1024]{1,0:T(8,128)(2,1)S(1)}, u32[]{:S(2)}, u32[]{:S(2)}) %collective-permute-start.11) | collective-permute-done | bytes 524320 | tf_op jit(solution)/shard_map/ppermute | solution.py:23
  80.7 7.8 %forward.1 = (f32[256,1024]{1,0:T(8,128)S(1)}, f32[256,1024]{1,0:T(8,128)}, bf16[256,1024]{1,0:T(8,128)(2,1)S(1)}, bf16[256,2048]{1,0:T(8,128)(2,1)}, bf16[2,256...) custom-call(s32[9]{0:T(128)S(1)} %stack.39.refs_0_, ...), custom_call_target="tpu_custom_call" | custom-call | flops 2147483648 | bytes 14164004 | tf_op jit(solution)/shard_map/forward/pallas_call | solution.py:138
  92.8 4.6 %grads_ff.1 = (bf16[4,64,1280]{2,1,0:T(8,128)(2,1)}, bf16[4,64,1280]{2,1,0:T(8,128)(2,1)}, bf16[4,64,1152]{2,1,0:T(8,128)(2,1)}, bf16[4,64,1152]{2,1,0:T(8,128)(2,1)}, f32[8,128]{1,0:T(8,128)}) custom-call(s32[9]{0:T(128)S(1)} %stack.39.refs_0_, bf16[8,64,256]{2,1,0:T(8,128)(2,1)} %get-tuple-element.157.refs_1_, ...), custom_call_target="tpu_custom_call" | custom-call | flops 1275068416 | bytes 6881316 | tf_op jit(solution)/shard_map/grads_ff/pallas_call | solution.py:138
  97.8 4.6 %down.1 = (bf16[256,1024]{1,0:T(8,128)(2,1)}, f32[8,128]{1,0:T(8,128)}) custom-call(bf16[2,256,1024]{2,1,0:T(8,128)(2,1)} %get-tuple-element.156.refs_7_.refs_0_, bf16[2048,1024]{1,0:T(8,128)(2,1)} %refs_1_.1, f32[8,128]{1,0:T(8,128)} %get-tuple-element.163.refs_2_), custom_call_target="tpu_custom_call" | custom-call | flops 1073741824 | bytes 5767168 | tf_op jit(solution)/shard_map/down/pallas_call | solution.py:138
  103.6 2.9 %second.1 = (f32[256,1024]{1,0:T(8,128)}, f32[1,1024]{1,0:T(1,128)}, bf16[8,128,128]{2,1,0:T(8,128)(2,1)}, bf16[8,64,256]{2,1,0:T(8,128)(2,1)}, bf16[8,64,256]{2,1,0:T(8,128)(2,1)}, /*index=5*/f32[8,128]{1,0:T(8,128)}) custom-call(s32[9]{0:T(128)S(1)} %stack.39.refs_0_, f32[256,1024]{1,0:T(8,128)S(1)} %get-tuple-element.165.refs_1_, ...), custom_call_target="tpu_custom_call" | custom-call | flops 268435456 | bytes 6041636 | tf_op jit(solution)/shard_map/second/pallas_call | solution.py:138
  106.5 3.6 %all-to-all-start.1 = ((bf16[4,2,128,128]{3,2,1,0:T(8,128)(2,1)}), bf16[4,2,128,128]{3,2,1,0:T(8,128)(2,1)S(1)}, u32[]{:S(2)}, u32[]{:S(2)}) async-start(bf16[4,2,128,128]{3,2,1,0:T(8,128)(2,1)} %bitcast.31), calls=%async_computation.1 | async-start | bytes 524288 | tf_op jit(solution)/shard_map/all_to_all | solution.py:1216
  110.1 1.6 collective-permute-start.16
  111.7 2.1 collective-permute-done.19.refs_4_
  114.4 2.6 %fold_ff.1 = (bf16[2,64,1664]{2,1,0:T(8,128)(2,1)}, bf16[2,64,1664]{2,1,0:T(8,128)(2,1)}, bf16[2,64,1152]{2,1,0:T(8,128)(2,1)}, bf16[2,64,1152]{2,1,0:T(8,128)(2,1)}, f32[8,128]{1,0:T(8,128)}) custom-call(s32[9]{0:T(128)S(1)} %stack.39.refs_0_, bf16[4,64,1280]{2,1,0:T(8,128)(2,1)} %get-tuple-element.172.refs_1_, ...), custom_call_target="tpu_custom_call" | custom-call | bytes 3932196 | tf_op jit(solution)/shard_map/fold_ff/pallas_call | solution.py:138
  117.1 1.8 all-to-all-done.1.refs_9_.refs_2_
  120.9 8.5 %attend_back.1 = (bf16[2,3,128,128]{3,2,1,0:T(8,128)(2,1)}, bf16[2,3,128,128]{3,2,1,0:T(8,128)(2,1)}, bf16[2,3,128,128]{3,2,1,0:T(8,128)(2,1)}, bf16[2,3,128,128...) custom-call(s32[9]{0:T(128)S(1)} %stack.39.refs_0_, ...), custom_call_target="tpu_custom_call" | custom-call | flops 2147483648 | bytes 7864356 | tf_op jit(solution)/shard_map/attend_back/pallas_call | solution.py:138
  130.1 2.1 collective-permute-done.22.refs_4_
  132.3 2.1 combine.1
  134.4 2.0 collective-permute-start.23
  136.5 2.3 collective-permute-start.25
  138.8 2.8 %head.1 = (f32[2,192,128]{2,1,0:T(8,128)}, bf16[8,64,256]{2,1,0:T(8,128)(2,1)}, bf16[8,64,256]{2,1,0:T(8,128)(2,1)}, f32[8,128]{1,0:T(8,128)}) custom-call(s32[9]{0:T(128)S(1)} %stack.39.refs_0_, f32[256,1024]{1,0:T(8,128)} %get-tuple-element.155.refs_1_, bf16[256,1024]{1,0:T(8,128)(2,1)} %get-tuple-element.164.refs_2_, ...), custom_call_target="tpu_custom_call" | custom-call | flops 100663296 | bytes 3211300 | tf_op jit(solution)/shard_map/head/pallas_call | solution.py:138
  142.6 2.4 %merge_ff.1 = (bf16[64,3584]{1,0:T(8,128)(2,1)}, bf16[64,3584]{1,0:T(8,128)(2,1)}, f32[8,128]{1,0:T(8,128)}) custom-call(s32[9]{0:T(128)S(1)} %stack.39.refs_0_, bf16[2,64,1664]{2,1,0:T(8,128)(2,1)} %get-tuple-element.198.refs_1_, bf16[2,64,1664]{2,1,0:T(8,128)(2,1)} %collective-permute-done.20.refs_1_.refs_2_, ...), custom_call_target="tpu_custom_call" | custom-call | bytes 2359332 | tf_op jit(solution)/shard_map/merge_ff/pallas_call | solution.py:138
  145.1 8.7 %collective-permute-done.24.refs_3_ = bf16[2,3,128,128]{3,2,1,0:T(8,128)(2,1)S(1)} collective-permute-done((bf16[2,3,128,128]{3,2,1,0:T(8,128)(2,1)}, bf16[2,3,128,128]{3,2,1,0:T(8,128)(2,1)S(1)}, u32[]{:S(2)}, u32[]{:S(2)}) %collective-permute-start.24) | collective-permute-done | bytes 196640 | tf_op jit(solution)/shard_map/ppermute | solution.py:23
  153.7 3.1 %third.1 = (bf16[256,1536]{1,0:T(8,128)(2,1)}, bf16[256,1024]{1,0:T(8,128)(2,1)}, f32[8,128]{1,0:T(8,128)}) custom-call(s32[9]{0:T(128)S(1)} %stack.39.refs_0_, bf16[2,3,128,128]{3,2,1,0:T(8,128)(2,1)} %get-tuple-element.194.refs_1_, bf16[2,3,128,128]{3,2,1,0:T(8,128)(2,1)S(1)} %collective-permute-done.23.refs_2_, ...), custom_call_target="tpu_custom_call" | custom-call | flops 805306368 | bytes 5242916 | tf_op jit(solution)/shard_map/third/pallas_call | solution.py:138
  160.5 3.3 %collective-permute-start.34 = (bf16[64,3584]{1,0:T(8,128)(2,1)}, bf16[64,3584]{1,0:T(8,128)(2,1)S(1)}, u32[]{:S(2)}, u32[]{:S(2)}) collective-permute-start(bf16[64,3584]{1,0:T(8,128)(2,1)} %get-tuple-element.226), channel_id=1, source_target_pairs={{0,8},{2,10},{4,12},{6,14},{8,0},{10,2},{12,4},{14,6},{1,9},{3,11}... | collective-permute-start | bytes 1376264 | tf_op jit(solution)/shard_map/ppermute | solution.py:23
  164.8 3.6 %grads_q.1 = (bf16[4,64,896]{2,1,0:T(8,128)(2,1)}, bf16[4,64,896]{2,1,0:T(8,128)(2,1)}, bf16[4,64,640]{2,1,0:T(8,128)(2,1)}, bf16[4,64,640]{2,1,0:T(8,128)(2,1)}, f32[8,128]{1,0:T(8,128)}) custom-call(s32[9]{0:T(128)S(1)} %stack.39.refs_0_, bf16[8,64,256]{2,1,0:T(8,128)(2,1)} %get-tuple-element.213.refs_1_, bf16[8,64,256]{2,1,0:T(8,128)(2,1)S(1)} %copy-done.16, ...), custom_call_target="tpu_custom_call" | custom-call | flops 805306368 | bytes 3670052 | tf_op jit(solution)/shard_map/grads_q/pallas_call | solution.py:138
  169.5 2.7 %grads_oh.1 = (bf16[4,64,768]{2,1,0:T(8,128)(2,1)}, bf16[4,64,768]{2,1,0:T(8,128)(2,1)}, f32[8,128]{1,0:T(8,128)}) custom-call(s32[9]{0:T(128)S(1)} %stack.39.refs_0_, bf16[8,64,256]{2,1,0:T(8,128)(2,1)} %get-tuple-element.205.refs_1_, bf16[8,64,256]{2,1,0:T(8,128)(2,1)} %collective-permute-done.27.refs_2_, bf16[256,512]{1,0:T(8,128)(2,1)} %get-tuple-element.207.refs_3_, ...), custom_call_target="tpu_custom_call" | custom-call | flops 402653184 | bytes 2555940 | tf_op jit(solution)/shard_map/grads_oh/pallas_call | solution.py:138
  173.6 4.1 %last.1 = (bf16[128,512]{1,0:T(8,128)(2,1)}, bf16[128,512]{1,0:T(8,128)(2,1)}, f32[2,192,128]{2,1,0:T(8,128)}, bf16[2,48,128]{2,1,0:T(8,128)(2,1)}, bf16[8,64,25...) custom-call(s32[9]{0:T(128)S(1)} %stack.39.refs_0_, f32[256,1024]{1,0:T(8,128)S(1)} %copy-done.4, ...), custom_call_target="tpu_custom_call" | custom-call | flops 201326592 | bytes 4657188 | tf_op jit(solution)/shard_map/last/pallas_call | solution.py:138
  177.6 7.4 %collective-permute-done.34.refs_6_ = bf16[64,3584]{1,0:T(8,128)(2,1)S(1)} collective-permute-done((bf16[64,3584]{1,0:T(8,128)(2,1)}, bf16[64,3584]{1,0:T(8,128)(2,1)S(1)}, u32[]{:S(2)}, u32[]{:S(2)}) %collective-permute-start.34) | collective-permute-done | bytes 458784 | tf_op jit(solution)/shard_map/ppermute | solution.py:23
  185.0 4.7 %collective-permute-done.33.refs_4_ = bf16[4,64,640]{2,1,0:T(8,128)(2,1)S(1)} collective-permute-done((bf16[4,64,640]{2,1,0:T(8,128)(2,1)}, bf16[4,64,640]{2,1,0:T(8,128)(2,1)S(1)}, u32[]{:S(2)}, u32[]{:S(2)}) %collective-permute-start.33) | collective-permute-done | bytes 327712 | tf_op jit(solution)/shard_map/ppermute | solution.py:23
  189.8 3.1 %fold_q.1 = (bf16[2,64,896]{2,1,0:T(8,128)(2,1)}, bf16[2,64,896]{2,1,0:T(8,128)(2,1)}, bf16[2,64,1920]{2,1,0:T(8,128)(2,1)}, bf16[2,64,1920]{2,1,0:T(8,128)(2,1)...) custom-call(s32[9]{0:T(128)S(1)} %stack.39.refs_0_, ...), custom_call_target="tpu_custom_call" | custom-call | bytes 5636132 | tf_op jit(solution)/shard_map/fold_q/pallas_call | solution.py:138
  194.4 2.0 collective-permute-start.41
  197.0 2.4 %collective-permute-start.37 = (bf16[2,48,128]{2,1,0:T(8,128)(2,1)}, bf16[2,48,128]{2,1,0:T(8,128)(2,1)S(1)}, u32[]{:S(2)}, u32[]{:S(2)}) collective-permute-start(bf16[2,48,128]{2,1,0:T(8,128)(2,1)} %get-tuple-element.233), channel_id=1, source_target_pairs={{2,0},{4,2},{6,4},{8,6},{10,8},{12,10},{14,12},{0,14},{3,1},{5,3},... | collective-permute-start | bytes 73736 | tf_op jit(solution)/shard_map/ppermute | solution.py:29
  199.3 3.8 %collective-permute-done.37.refs_8_.refs_2_ = bf16[2,48,128]{2,1,0:T(8,128)(2,1)S(1)} collective-permute-done((bf16[2,48,128]{2,1,0:T(8,128)(2,1)}, bf16[2,48,128]{2,1,0:T(8,128)(2,1)S(1)}, u32[]{:S(2)}, u32[]{:S(2)}) %collective-permute-start.37) | collective-permute-done | bytes 24608 | tf_op jit(solution)/shard_map/ppermute | solution.py:29
  203.1 4.9 %collective-permute-done.38.refs_9_.refs_4_ = bf16[128,512]{1,0:T(8,128)(2,1)S(1)} collective-permute-done((bf16[128,512]{1,0:T(8,128)(2,1)}, bf16[128,512]{1,0:T(8,128)(2,1)S(1)}, u32[]{:S(2)}, u32[]{:S(2)}) %collective-permute-start.38) | collective-permute-done | bytes 131104 | tf_op jit(solution)/shard_map/ppermute | solution.py:23
  208.7 2.4 %merge_q.1 = (bf16[64,2304]{1,0:T(8,128)(2,1)}, bf16[64,2304]{1,0:T(8,128)(2,1)}, bf16[2,64,1536]{2,1,0:T(8,128)(2,1)}, bf16[64,256]{1,0:T(8,128)(2,1)}, bf16[64...) custom-call(s32[9]{0:T(128)S(1)} %stack.39.refs_0_, ...), custom_call_target="tpu_custom_call" | custom-call | bytes 2949156 | tf_op jit(solution)/shard_map/merge_q/pallas_call | solution.py:138
  211.2 3.1 %collective-permute-start.46 = (bf16[64,2304]{1,0:T(8,128)(2,1)}, bf16[64,2304]{1,0:T(8,128)(2,1)S(1)}, u32[]{:S(2)}, u32[]{:S(2)}) collective-permute-start(bf16[64,2304]{1,0:T(8,128)(2,1)} %get-tuple-element.251), channel_id=1, source_target_pairs={{0,8},{2,10},{4,12},{6,14},{8,0},{10,2},{12,4},{14,6},{1,9},{3,11}... | collective-permute-start | bytes 884744 | tf_op jit(solution)/shard_map/ppermute | solution.py:23
  214.4 2.4 %collective-permute-start.43 = (bf16[64,256]{1,0:T(8,128)(2,1)}, bf16[64,256]{1,0:T(8,128)(2,1)S(1)}, u32[]{:S(2)}, u32[]{:S(2)}) collective-permute-start(bf16[64,256]{1,0:T(8,128)(2,1)} %get-tuple-element.247), channel_id=1, source_target_pairs={{0,4},{2,6},{4,0},{6,2},{8,12},{10,14},{12,8},{14,10},{1,5},{3,7},... | collective-permute-start | bytes 98312 | tf_op jit(solution)/shard_map/ppermute | solution.py:23
  216.8 2.3 collective-permute-start.45
  220.7 2.8 %close.1 = (f32[2,192,128]{2,1,0:T(8,128)}, f32[128,512]{1,0:T(8,128)}, f32[64,2048]{1,0:T(8,128)}, f32[64,2048]{1,0:T(8,128)}, f32[8,128]{1,0:T(8,128)}) custom-call(s32[9]{0:T(128)S(1)} %stack.39.refs_0_, f32[2,192,128]{2,1,0:T(8,128)} %get-tuple-element.218.refs_1_, bf16[2,48,128]{2,1,0:T(8,128)(2,1)S(1)} %copy-done.13, ...), custom_call_target="tpu_custom_call" | custom-call | bytes 3719204 | tf_op jit(solution)/shard_map/close/pallas_call | solution.py:138
  223.5 7.3 %collective-permute-done.44.refs_2_ = bf16[64,256]{1,0:T(8,128)(2,1)S(1)} collective-permute-done((bf16[64,256]{1,0:T(8,128)(2,1)}, bf16[64,256]{1,0:T(8,128)(2,1)S(1)}, u32[]{:S(2)}, u32[]{:S(2)}) %collective-permute-start.44) | collective-permute-done | bytes 32800 | tf_op jit(solution)/shard_map/ppermute | solution.py:23
  230.9 1.9 end.1
  (130 shorter events, 35.5 us)
Async XLA Ops:
  3.7 14.5 %all-to-all-start = ((f32[16,8,128]{2,1,0:T(8,128)}), f32[16,8,128]{2,1,0:T(8,128)S(1)}, u32[]{:S(2)}, u32[]{:S(2)}) async-start(f32[16,8,128]{2,1,0:T(8,128)} %get-tuple-element.137), calls=%async_computation | async-start | bytes 131072 | tf_op jit(solution)/shard_map/all_to_all | solution.py:1044
  11.1 6.0 %collective-permute-start = (bf16[2,48,128]{2,1,0:T(8,128)(2,1)S(1)}, bf16[2,48,128]{2,1,0:T(8,128)(2,1)S(1)}, u32[]{:S(2)}, u32[]{:S(2)}) collective-permute-start(bf16[2,48,128]{2,1,0:T(8,128)(2,1)S(1)} %get-tuple-element.139), channel_id=1, source_target_pairs={{14,0},{0,2},{2,4},{4,6},{6,8},{8,10},{10,12},{12,14},{15,1},{1,3}... | collective-permute-start | bytes 73736 | tf_op jit(solution)/shard_map/ppermute | solution.py:29
  23.9 9.9 %collective-permute-start.1 = (bf16[2,3,128,128]{3,2,1,0:T(8,128)(2,1)}, bf16[2,3,128,128]{3,2,1,0:T(8,128)(2,1)S(1)}, u32[]{:S(2)}, u32[]{:S(2)}) collective-permute-start(bf16[2,3,128,128]{3,2,1,0:T(8,128)(2,1)} %get-tuple-element.144), channel_id=1, source_target_pairs={{0,4},{2,6},{4,0},{6,2},{8,12},{10,14},{12,8},{14,10},{1,5},{3,7},... | collective-permute-start | bytes 589832 | tf_op jit(solution)/shard_map/ppermute | solution.py:23
  24.0 17.4 %collective-permute-start.2 = (bf16[2,3,128,128]{3,2,1,0:T(8,128)(2,1)}, bf16[2,3,128,128]{3,2,1,0:T(8,128)(2,1)S(1)}, u32[]{:S(2)}, u32[]{:S(2)}) collective-permute-start(bf16[2,3,128,128]{3,2,1,0:T(8,128)(2,1)} %get-tuple-element.145), channel_id=1, source_target_pairs={{0,8},{2,10},{4,12},{6,14},{8,0},{10,2},{12,4},{14,6},{1,9},{3,11}... | collective-permute-start | bytes 589832 | tf_op jit(solution)/shard_map/ppermute | solution.py:23
  24.9 16.5 %collective-permute-start.3 = (bf16[2,3,128,128]{3,2,1,0:T(8,128)(2,1)}, bf16[2,3,128,128]{3,2,1,0:T(8,128)(2,1)S(1)}, u32[]{:S(2)}, u32[]{:S(2)}) collective-permute-start(bf16[2,3,128,128]{3,2,1,0:T(8,128)(2,1)} %get-tuple-element.146), channel_id=1, source_target_pairs={{0,12},{2,14},{4,8},{6,10},{8,4},{10,6},{12,0},{14,2},{1,13},{3,15... | collective-permute-start | bytes 589832 | tf_op jit(solution)/shard_map/ppermute | solution.py:23
  33.7 8.1 %collective-permute-start.4 = (bf16[2,3,128,128]{3,2,1,0:T(8,128)(2,1)}, bf16[2,3,128,128]{3,2,1,0:T(8,128)(2,1)S(1)}, u32[]{:S(2)}, u32[]{:S(2)}) collective-permute-start(bf16[2,3,128,128]{3,2,1,0:T(8,128)(2,1)} %pin.5.refs_0_.refs_1_), channel_id=1, source_target_pairs={{0,2},{2,0},{4,6},{6,4},{8,10},{10,8},{12,14},{14,12},{1,3},{3,1},... | collective-permute-start | bytes 589832 | tf_op jit(solution)/shard_map/ppermute | solution.py:23
  33.8 8.1 %collective-permute-start.5 = (bf16[2,3,128,128]{3,2,1,0:T(8,128)(2,1)S(1)}, bf16[2,3,128,128]{3,2,1,0:T(8,128)(2,1)S(1)}, u32[]{:S(2)}, u32[]{:S(2)}) collective-permute-start(bf16[2,3,128,128]{3,2,1,0:T(8,128)(2,1)S(1)} %collective-permute-done.1.refs_1_.refs_2_), channel_id=1, source_target_pairs={{0,2},{2,0},{4,6},{6,4},{8,10},{10,8},{12,14},{14,12},{1,3},{3,1},... | collective-permute-start | bytes 589832 | tf_op jit(solution)/shard_map/ppermute | solution.py:23
  41.4 1.7 collective-permute-start.7
  53.1 6.4 %collective-permute-start.10 = (bf16[2,128,128]{2,1,0:T(8,128)(2,1)}, bf16[2,128,128]{2,1,0:T(8,128)(2,1)S(1)}, u32[]{:S(2)}, u32[]{:S(2)}) collective-permute-start(bf16[2,128,128]{2,1,0:T(8,128)(2,1)} %get-tuple-element.150), channel_id=1, source_target_pairs={{0,12},{2,14},{4,8},{6,10},{8,4},{10,6},{12,0},{14,2},{1,13},{3,15... | collective-permute-start | bytes 196616 | tf_op jit(solution)/shard_map/ppermute | solution.py:23
  54.5 6.4 %collective-permute-start.8 = (bf16[2,128,128]{2,1,0:T(8,128)(2,1)}, bf16[2,128,128]{2,1,0:T(8,128)(2,1)S(1)}, u32[]{:S(2)}, u32[]{:S(2)}) collective-permute-start(bf16[2,128,128]{2,1,0:T(8,128)(2,1)} %get-tuple-element.148), channel_id=1, source_target_pairs={{0,4},{2,6},{4,0},{6,2},{8,12},{10,14},{12,8},{14,10},{1,5},{3,7},... | collective-permute-start | bytes 196616 | tf_op jit(solution)/shard_map/ppermute | solution.py:23
  57.1 6.5 %collective-permute-start.9 = (bf16[2,128,128]{2,1,0:T(8,128)(2,1)}, bf16[2,128,128]{2,1,0:T(8,128)(2,1)S(1)}, u32[]{:S(2)}, u32[]{:S(2)}) collective-permute-start(bf16[2,128,128]{2,1,0:T(8,128)(2,1)} %get-tuple-element.149), channel_id=1, source_target_pairs={{0,8},{2,10},{4,12},{6,14},{8,0},{10,2},{12,4},{14,6},{1,9},{3,11}... | collective-permute-start | bytes 196616 | tf_op jit(solution)/shard_map/ppermute | solution.py:23
  65.5 13.7 %collective-permute-start.11 = (bf16[256,1024]{1,0:T(8,128)(2,1)S(1)}, bf16[256,1024]{1,0:T(8,128)(2,1)S(1)}, u32[]{:S(2)}, u32[]{:S(2)}) collective-permute-start(bf16[256,1024]{1,0:T(8,128)(2,1)S(1)} %get-tuple-element.152.refs_2_), channel_id=1, source_target_pairs={{0,1},{1,0},{2,3},{3,2},{4,5},{5,4},{6,7},{7,6},{8,9},{9,8},{10,11... | collective-permute-start | bytes 1572872 | tf_op jit(solution)/shard_map/ppermute | solution.py:23
  88.6 4.2 %collective-permute-start.13 = (bf16[256,2048]{1,0:T(8,128)(2,1)}, bf16[256,2048]{1,0:T(8,128)(2,1)S(1)}, u32[]{:S(2)}, u32[]{:S(2)}) collective-permute-start(bf16[256,2048]{1,0:T(8,128)(2,1)} %get-tuple-element.159.refs_3_), channel_id=1, source_target_pairs={{0,2},{2,0},{4,6},{6,4},{8,10},{10,8},{12,14},{14,12},{1,3},{3,1},... | collective-permute-start | bytes 3145736 | tf_op jit(solution)/shard_map/ppermute | solution.py:23
  88.7 4.1 %collective-permute-start.15 = (bf16[256,1024]{1,0:T(8,128)(2,1)}, bf16[256,1024]{1,0:T(8,128)(2,1)S(1)}, u32[]{:S(2)}, u32[]{:S(2)}) collective-permute-start(bf16[256,1024]{1,0:T(8,128)(2,1)} %get-tuple-element.161), channel_id=1, source_target_pairs={{0,2},{2,0},{4,6},{6,4},{8,10},{10,8},{12,14},{14,12},{1,3},{3,1},... | collective-permute-start | bytes 1572872 | tf_op jit(solution)/shard_map/ppermute | solution.py:23
  89.2 3.6 %collective-permute-start.12 = (bf16[8,64,256]{2,1,0:T(8,128)(2,1)}, bf16[8,64,256]{2,1,0:T(8,128)(2,1)S(1)}, u32[]{:S(2)}, u32[]{:S(2)}) collective-permute-start(bf16[8,64,256]{2,1,0:T(8,128)(2,1)} %get-tuple-element.158), channel_id=1, source_target_pairs={{0,2},{2,0},{4,6},{6,4},{8,10},{10,8},{12,14},{14,12},{1,3},{3,1},... | collective-permute-start | bytes 786440 | tf_op jit(solution)/shard_map/ppermute | solution.py:23
  89.3 14.3 %collective-permute-start.17 = (bf16[256,1024]{1,0:T(8,128)(2,1)S(1)}, bf16[256,1024]{1,0:T(8,128)(2,1)S(1)}, u32[]{:S(2)}, u32[]{:S(2)}) collective-permute-start(bf16[256,1024]{1,0:T(8,128)(2,1)S(1)} %get-tuple-element.167.refs_3_), channel_id=1, source_target_pairs={{0,1},{1,0},{2,3},{3,2},{4,5},{5,4},{6,7},{7,6},{8,9},{9,8},{10,11... | collective-permute-start | bytes 1572872 | tf_op jit(solution)/shard_map/ppermute | solution.py:23
  90.8 1.6 collective-permute-start.14
  97.4 17.0 %collective-permute-start.18 = (bf16[4,64,1280]{2,1,0:T(8,128)(2,1)}, bf16[4,64,1280]{2,1,0:T(8,128)(2,1)S(1)}, u32[]{:S(2)}, u32[]{:S(2)}) collective-permute-start(bf16[4,64,1280]{2,1,0:T(8,128)(2,1)} %get-tuple-element.173), channel_id=1, source_target_pairs={{0,16},{16,0},{1,17},{17,1},{2,18},{18,2},{3,19},{19,3},{4,20},{20... | collective-permute-start | bytes 1966088 | tf_op jit(solution)/shard_map/ppermute | solution.py:23
  97.8 16.0 %collective-permute-start.19 = (bf16[4,64,1152]{2,1,0:T(8,128)(2,1)}, bf16[4,64,1152]{2,1,0:T(8,128)(2,1)S(1)}, u32[]{:S(2)}, u32[]{:S(2)}) collective-permute-start(bf16[4,64,1152]{2,1,0:T(8,128)(2,1)} %get-tuple-element.175), channel_id=1, source_target_pairs={{0,4},{2,6},{4,0},{6,2},{8,12},{10,14},{12,8},{14,10},{1,5},{3,7},... | collective-permute-start | bytes 1769480 | tf_op jit(solution)/shard_map/ppermute | solution.py:23
  106.5 12.4 %all-to-all-start.1 = ((bf16[4,2,128,128]{3,2,1,0:T(8,128)(2,1)}), bf16[4,2,128,128]{3,2,1,0:T(8,128)(2,1)S(1)}, u32[]{:S(2)}, u32[]{:S(2)}) async-start(bf16[4,2,128,128]{3,2,1,0:T(8,128)(2,1)} %bitcast.31), calls=%async_computation.1 | async-start | bytes 524288 | tf_op jit(solution)/shard_map/all_to_all | solution.py:1216
  110.1 19.3 %collective-permute-start.16 = (bf16[256,1024]{1,0:T(8,128)(2,1)}, bf16[256,1024]{1,0:T(8,128)(2,1)}, u32[]{:S(2)}, u32[]{:S(2)}) collective-permute-start(bf16[256,1024]{1,0:T(8,128)(2,1)} %get-tuple-element.164.refs_2_), channel_id=1, source_target_pairs={{0,1},{1,0},{2,3},{3,2},{4,5},{5,4},{6,7},{7,6},{8,9},{9,8},{10,11... | collective-permute-start | bytes 1572872 | tf_op jit(solution)/shard_map/ppermute | solution.py:23
  119.6 10.2 %collective-permute-start.20 = (bf16[2,64,1664]{2,1,0:T(8,128)(2,1)}, bf16[2,64,1664]{2,1,0:T(8,128)(2,1)}, u32[]{:S(2)}, u32[]{:S(2)}) collective-permute-start(bf16[2,64,1664]{2,1,0:T(8,128)(2,1)} %get-tuple-element.185), channel_id=1, source_target_pairs={{0,4},{2,6},{4,0},{6,2},{8,12},{10,14},{12,8},{14,10},{1,5},{3,7},... | collective-permute-start | bytes 1277960 | tf_op jit(solution)/shard_map/ppermute | solution.py:23
  119.8 9.7 %collective-permute-start.21 = (bf16[2,64,1152]{2,1,0:T(8,128)(2,1)}, bf16[2,64,1152]{2,1,0:T(8,128)(2,1)S(1)}, u32[]{:S(2)}, u32[]{:S(2)}) collective-permute-start(bf16[2,64,1152]{2,1,0:T(8,128)(2,1)} %get-tuple-element.186), channel_id=1, source_target_pairs={{0,16},{16,0},{1,17},{17,1},{2,18},{18,2},{3,19},{19,3},{4,20},{20... | collective-permute-start | bytes 884744 | tf_op jit(solution)/shard_map/ppermute | solution.py:23
  130.1 2.1 collective-permute-start.22
  134.4 10.6 %collective-permute-start.23 = (bf16[2,3,128,128]{3,2,1,0:T(8,128)(2,1)}, bf16[2,3,128,128]{3,2,1,0:T(8,128)(2,1)S(1)}, u32[]{:S(2)}, u32[]{:S(2)}) collective-permute-start(bf16[2,3,128,128]{3,2,1,0:T(8,128)(2,1)} %get-tuple-element.195), channel_id=1, source_target_pairs={{0,4},{2,6},{4,0},{6,2},{8,12},{10,14},{12,8},{14,10},{1,5},{3,7},... | collective-permute-start | bytes 589832 | tf_op jit(solution)/shard_map/ppermute | solution.py:23
  136.4 17.3 %collective-permute-start.24 = (bf16[2,3,128,128]{3,2,1,0:T(8,128)(2,1)}, bf16[2,3,128,128]{3,2,1,0:T(8,128)(2,1)S(1)}, u32[]{:S(2)}, u32[]{:S(2)}) collective-permute-start(bf16[2,3,128,128]{3,2,1,0:T(8,128)(2,1)} %get-tuple-element.196), channel_id=1, source_target_pairs={{0,8},{2,10},{4,12},{6,14},{8,0},{10,2},{12,4},{14,6},{1,9},{3,11}... | collective-permute-start | bytes 589832 | tf_op jit(solution)/shard_map/ppermute | solution.py:23
  136.5 17.2 %collective-permute-start.25 = (bf16[2,3,128,128]{3,2,1,0:T(8,128)(2,1)}, bf16[2,3,128,128]{3,2,1,0:T(8,128)(2,1)S(1)}, u32[]{:S(2)}, u32[]{:S(2)}) collective-permute-start(bf16[2,3,128,128]{3,2,1,0:T(8,128)(2,1)} %get-tuple-element.197), channel_id=1, source_target_pairs={{0,12},{2,14},{4,8},{6,10},{8,4},{10,6},{12,0},{14,2},{1,13},{3,15... | collective-permute-start | bytes 589832 | tf_op jit(solution)/shard_map/ppermute | solution.py:23
  156.8 3.7 %collective-permute-start.31 = (bf16[256,1536]{1,0:T(8,128)(2,1)}, bf16[256,1536]{1,0:T(8,128)(2,1)}, u32[]{:S(2)}, u32[]{:S(2)}) collective-permute-start(bf16[256,1536]{1,0:T(8,128)(2,1)} %get-tuple-element.215.refs_3_), channel_id=1, source_target_pairs={{0,2},{2,0},{4,6},{6,4},{8,10},{10,8},{12,14},{14,12},{1,3},{3,1},... | collective-permute-start | bytes 2359304 | tf_op jit(solution)/shard_map/ppermute | solution.py:23
  156.8 2.8 %collective-permute-start.30 = (bf16[8,64,256]{2,1,0:T(8,128)(2,1)}, bf16[8,64,256]{2,1,0:T(8,128)(2,1)S(1)}, u32[]{:S(2)}, u32[]{:S(2)}) collective-permute-start(bf16[8,64,256]{2,1,0:T(8,128)(2,1)} %get-tuple-element.214), channel_id=1, source_target_pairs={{0,2},{2,0},{4,6},{6,4},{8,10},{10,8},{12,14},{14,12},{1,3},{3,1},... | collective-permute-start | bytes 786440 | tf_op jit(solution)/shard_map/ppermute | solution.py:23
  157.3 16.2 %collective-permute-start.26 = (bf16[256,1024]{1,0:T(8,128)(2,1)}, bf16[256,1024]{1,0:T(8,128)(2,1)S(1)}, u32[]{:S(2)}, u32[]{:S(2)}) collective-permute-start(bf16[256,1024]{1,0:T(8,128)(2,1)} %get-tuple-element.202.refs_3_), channel_id=1, source_target_pairs={{0,1},{1,0},{2,3},{3,2},{4,5},{5,4},{6,7},{7,6},{8,9},{9,8},{10,11... | collective-permute-start | bytes 1572872 | tf_op jit(solution)/shard_map/ppermute | solution.py:23
  158.9 9.5 %collective-permute-start.28 = (bf16[256,512]{1,0:T(8,128)(2,1)}, bf16[256,512]{1,0:T(8,128)(2,1)S(1)}, u32[]{:S(2)}, u32[]{:S(2)}) collective-permute-start(bf16[256,512]{1,0:T(8,128)(2,1)} %get-tuple-element.207.refs_3_), channel_id=1, source_target_pairs={{0,2},{2,0},{4,6},{6,4},{8,10},{10,8},{12,14},{14,12},{1,3},{3,1},... | collective-permute-start | bytes 786440 | tf_op jit(solution)/shard_map/ppermute | solution.py:23
  158.9 10.6 %collective-permute-start.27 = (bf16[8,64,256]{2,1,0:T(8,128)(2,1)}, bf16[8,64,256]{2,1,0:T(8,128)(2,1)}, u32[]{:S(2)}, u32[]{:S(2)}) collective-permute-start(bf16[8,64,256]{2,1,0:T(8,128)(2,1)} %get-tuple-element.206), channel_id=1, source_target_pairs={{0,2},{2,0},{4,6},{6,4},{8,10},{10,8},{12,14},{14,12},{1,3},{3,1},... | collective-permute-start | bytes 786440 | tf_op jit(solution)/shard_map/ppermute | solution.py:23
  160.4 9.2 %collective-permute-start.29 = (bf16[8,64,256]{2,1,0:T(8,128)(2,1)}, bf16[8,64,256]{2,1,0:T(8,128)(2,1)S(1)}, u32[]{:S(2)}, u32[]{:S(2)}) collective-permute-start(bf16[8,64,256]{2,1,0:T(8,128)(2,1)} %get-tuple-element.212), channel_id=1, source_target_pairs={{0,2},{2,0},{4,6},{6,4},{8,10},{10,8},{12,14},{14,12},{1,3},{3,1},... | collective-permute-start | bytes 786440 | tf_op jit(solution)/shard_map/ppermute | solution.py:23
  160.5 24.5 %collective-permute-start.34 = (bf16[64,3584]{1,0:T(8,128)(2,1)}, bf16[64,3584]{1,0:T(8,128)(2,1)S(1)}, u32[]{:S(2)}, u32[]{:S(2)}) collective-permute-start(bf16[64,3584]{1,0:T(8,128)(2,1)} %get-tuple-element.226), channel_id=1, source_target_pairs={{0,8},{2,10},{4,12},{6,14},{8,0},{10,2},{12,4},{14,6},{1,9},{3,11}... | collective-permute-start | bytes 1376264 | tf_op jit(solution)/shard_map/ppermute | solution.py:23
  168.4 21.4 %collective-permute-start.32 = (bf16[4,64,896]{2,1,0:T(8,128)(2,1)}, bf16[4,64,896]{2,1,0:T(8,128)(2,1)S(1)}, u32[]{:S(2)}, u32[]{:S(2)}) collective-permute-start(bf16[4,64,896]{2,1,0:T(8,128)(2,1)} %get-tuple-element.222), channel_id=1, source_target_pairs={{0,16},{16,0},{1,17},{17,1},{2,18},{18,2},{3,19},{19,3},{4,20},{20... | collective-permute-start | bytes 1376264 | tf_op jit(solution)/shard_map/ppermute | solution.py:23
  172.2 17.5 %collective-permute-start.35 = (bf16[4,64,768]{2,1,0:T(8,128)(2,1)}, bf16[4,64,768]{2,1,0:T(8,128)(2,1)S(1)}, u32[]{:S(2)}, u32[]{:S(2)}) collective-permute-start(bf16[4,64,768]{2,1,0:T(8,128)(2,1)} %get-tuple-element.228), channel_id=1, source_target_pairs={{0,16},{16,0},{1,17},{17,1},{2,18},{18,2},{3,19},{19,3},{4,20},{20... | collective-permute-start | bytes 1179656 | tf_op jit(solution)/shard_map/ppermute | solution.py:23
  173.1 16.6 %collective-permute-start.33 = (bf16[4,64,640]{2,1,0:T(8,128)(2,1)}, bf16[4,64,640]{2,1,0:T(8,128)(2,1)S(1)}, u32[]{:S(2)}, u32[]{:S(2)}) collective-permute-start(bf16[4,64,640]{2,1,0:T(8,128)(2,1)} %get-tuple-element.224), channel_id=1, source_target_pairs={{0,4},{2,6},{4,0},{6,2},{8,12},{10,14},{12,8},{14,10},{1,5},{3,7},... | collective-permute-start | bytes 983048 | tf_op jit(solution)/shard_map/ppermute | solution.py:23
  177.6 7.4 %collective-permute-start.36 = (bf16[8,64,256]{2,1,0:T(8,128)(2,1)}, bf16[8,64,256]{2,1,0:T(8,128)(2,1)S(1)}, u32[]{:S(2)}, u32[]{:S(2)}) collective-permute-start(bf16[8,64,256]{2,1,0:T(8,128)(2,1)} %get-tuple-element.230), channel_id=1, source_target_pairs={{0,2},{2,0},{4,6},{6,4},{8,10},{10,8},{12,14},{14,12},{1,3},{3,1},... | collective-permute-start | bytes 786440 | tf_op jit(solution)/shard_map/ppermute | solution.py:23
  192.9 15.2 %collective-permute-start.40 = (bf16[2,64,1920]{2,1,0:T(8,128)(2,1)}, bf16[2,64,1920]{2,1,0:T(8,128)(2,1)S(1)}, u32[]{:S(2)}, u32[]{:S(2)}) collective-permute-start(bf16[2,64,1920]{2,1,0:T(8,128)(2,1)} %get-tuple-element.240), channel_id=1, source_target_pairs={{0,16},{16,0},{1,17},{17,1},{2,18},{18,2},{3,19},{19,3},{4,20},{20... | collective-permute-start | bytes 1474568 | tf_op jit(solution)/shard_map/ppermute | solution.py:23
  194.4 13.7 %collective-permute-start.39 = (bf16[2,64,896]{2,1,0:T(8,128)(2,1)}, bf16[2,64,896]{2,1,0:T(8,128)(2,1)S(1)}, u32[]{:S(2)}, u32[]{:S(2)}) collective-permute-start(bf16[2,64,896]{2,1,0:T(8,128)(2,1)} %get-tuple-element.238), channel_id=1, source_target_pairs={{0,4},{2,6},{4,0},{6,2},{8,12},{10,14},{12,8},{14,10},{1,5},{3,7},... | collective-permute-start | bytes 688136 | tf_op jit(solution)/shard_map/ppermute | solution.py:23
  194.4 13.7 %collective-permute-start.41 = (bf16[2,64,768]{2,1,0:T(8,128)(2,1)}, bf16[2,64,768]{2,1,0:T(8,128)(2,1)S(1)}, u32[]{:S(2)}, u32[]{:S(2)}) collective-permute-start(bf16[2,64,768]{2,1,0:T(8,128)(2,1)} %get-tuple-element.242), channel_id=1, source_target_pairs={{0,4},{2,6},{4,0},{6,2},{8,12},{10,14},{12,8},{14,10},{1,5},{3,7},... | collective-permute-start | bytes 589832 | tf_op jit(solution)/shard_map/ppermute | solution.py:23
  196.4 11.7 %collective-permute-start.38 = (bf16[128,512]{1,0:T(8,128)(2,1)}, bf16[128,512]{1,0:T(8,128)(2,1)S(1)}, u32[]{:S(2)}, u32[]{:S(2)}) collective-permute-start(bf16[128,512]{1,0:T(8,128)(2,1)} %get-tuple-element.235), channel_id=1, source_target_pairs={{0,16},{16,0},{1,17},{17,1},{2,18},{18,2},{3,19},{19,3},{4,20},{20... | collective-permute-start | bytes 393224 | tf_op jit(solution)/shard_map/ppermute | solution.py:23
  197.0 6.2 %collective-permute-start.37 = (bf16[2,48,128]{2,1,0:T(8,128)(2,1)}, bf16[2,48,128]{2,1,0:T(8,128)(2,1)S(1)}, u32[]{:S(2)}, u32[]{:S(2)}) collective-permute-start(bf16[2,48,128]{2,1,0:T(8,128)(2,1)} %get-tuple-element.233), channel_id=1, source_target_pairs={{2,0},{4,2},{6,4},{8,6},{10,8},{12,10},{14,12},{0,14},{3,1},{5,3},... | collective-permute-start | bytes 73736 | tf_op jit(solution)/shard_map/ppermute | solution.py:29
  211.2 7.9 %collective-permute-start.42 = (bf16[2,64,1536]{2,1,0:T(8,128)(2,1)}, bf16[2,64,1536]{2,1,0:T(8,128)(2,1)S(1)}, u32[]{:S(2)}, u32[]{:S(2)}) collective-permute-start(bf16[2,64,1536]{2,1,0:T(8,128)(2,1)} %get-tuple-element.243.refs_8_), channel_id=1, source_target_pairs={{0,2},{2,0},{4,6},{6,4},{8,10},{10,8},{12,14},{14,12},{1,3},{3,1},... | collective-permute-start | bytes 1179656 | tf_op jit(solution)/shard_map/ppermute | solution.py:23
  211.2 19.6 %collective-permute-start.46 = (bf16[64,2304]{1,0:T(8,128)(2,1)}, bf16[64,2304]{1,0:T(8,128)(2,1)S(1)}, u32[]{:S(2)}, u32[]{:S(2)}) collective-permute-start(bf16[64,2304]{1,0:T(8,128)(2,1)} %get-tuple-element.251), channel_id=1, source_target_pairs={{0,8},{2,10},{4,12},{6,14},{8,0},{10,2},{12,4},{14,6},{1,9},{3,11}... | collective-permute-start | bytes 884744 | tf_op jit(solution)/shard_map/ppermute | solution.py:23
  214.4 9.2 %collective-permute-start.43 = (bf16[64,256]{1,0:T(8,128)(2,1)}, bf16[64,256]{1,0:T(8,128)(2,1)S(1)}, u32[]{:S(2)}, u32[]{:S(2)}) collective-permute-start(bf16[64,256]{1,0:T(8,128)(2,1)} %get-tuple-element.247), channel_id=1, source_target_pairs={{0,4},{2,6},{4,0},{6,2},{8,12},{10,14},{12,8},{14,10},{1,5},{3,7},... | collective-permute-start | bytes 98312 | tf_op jit(solution)/shard_map/ppermute | solution.py:23
  216.7 14.1 %collective-permute-start.44 = (bf16[64,256]{1,0:T(8,128)(2,1)}, bf16[64,256]{1,0:T(8,128)(2,1)S(1)}, u32[]{:S(2)}, u32[]{:S(2)}) collective-permute-start(bf16[64,256]{1,0:T(8,128)(2,1)} %get-tuple-element.248), channel_id=1, source_target_pairs={{0,8},{2,10},{4,12},{6,14},{8,0},{10,2},{12,4},{14,6},{1,9},{3,11}... | collective-permute-start | bytes 98312 | tf_op jit(solution)/shard_map/ppermute | solution.py:23
  216.8 14.0 %collective-permute-start.45 = (bf16[64,256]{1,0:T(8,128)(2,1)}, bf16[64,256]{1,0:T(8,128)(2,1)S(1)}, u32[]{:S(2)}, u32[]{:S(2)}) collective-permute-start(bf16[64,256]{1,0:T(8,128)(2,1)} %get-tuple-element.249), channel_id=1, source_target_pairs={{0,12},{2,14},{4,8},{6,10},{8,4},{10,6},{12,0},{14,2},{1,13},{3,15... | collective-permute-start | bytes 98312 | tf_op jit(solution)/shard_map/ppermute | solution.py:23
  (27 other events, 492.1 us)

commit v2 on v1

--- a/solution.py
+++ b/solution.py
@@ -282,11 +282,13 @@
     send_pairs(ids_ref, qkv_ref, messages)
 
 
-def cotangent_kernel(ids_ref, ct_ref, wh_ref, wd_ref, two_ref, act_ref, ct_turned_ref, *rest):
-    if rest:
-        mine_ref, hold = rest
+def cotangent_kernel(ids_ref, ct_ref, wh_ref, wd_ref, *refs):
+    if len(refs) > 3:
+        two_ref, act_ref, ct_turned_ref, mine_ref, hold = refs
         hold[...] = wh_ref[...].astype(F32).T.astype(BF).reshape(hold.shape)
         mine_ref[...] = hold[ids_ref[8]]
+    else:
+        two_ref, act_ref, ct_turned_ref = refs
     grads = []
     for item in range(ct_ref.shape[0]):
         ct = ct_ref[item].T.astype(BF)
@@ -294,7 +296,7 @@
         grads.append(nn(ct, wh_ref[...]))
     d_two = jnp.concatenate(grads, axis=0)
     two_ref[...] = d_two
-    act_ref[...] = nt(d_two.astype(BF), wd_ref[...])
+    act_ref[...] = nt(d_two.astype(BF), wd_ref[...]).astype(BF)
 
 
 def attend_kernel(items, scale, q_ref, kv_ref, o_ref, ot_ref, pt_ref, vt_ref):
@@ -353,24 +355,19 @@
 
 
 def pair_attend_kernel(items, scale, *refs):
-    sources, (*outs, ot_ref, pt_ref, query_rows, key_rows, vt_ref) = refs[:8], refs[8:]
+    sources, (*outs, ot_ref, pt_ref, query_ref, key_ref, value_ref, vt_ref) = refs[:8], refs[8:]
     tokens = sources[0].shape[2]
-    step = pl.program_id(1)
-
-    @pl.when(step == 0)
-    def _():
-        for k, source in enumerate(sources):
-            span = slice(k * tokens, (k + 1) * tokens)
-            if k < len(outs):
-                query_rows[span, :] = source[0, 0] * BF(scale)
-            key_rows[span, :] = source[0, 1]
-            vt_ref[:, span] = source[0, 2].astype(F32).T.astype(BF)
-
-    block = ot_ref.shape[2]
-    queries = query_rows[pl.ds(pl.multiple_of(step * block, block), block), :]
+    for k, source in enumerate(sources):
+        span = slice(k * tokens, (k + 1) * tokens)
+        if k < len(outs):
+            query_ref[0, span, :] = source[0, 0] * BF(scale)
+        key_ref[0, span, :] = source[0, 1]
+        value_ref[0, span, :] = source[0, 2]
+        vt_ref[:, span] = source[0, 2].astype(F32).T.astype(BF)
+    queries = query_ref[0]
     for item in range(items):
-        chosen = jnp.where(item_mask(block, LANES, item), queries, BF(0))
-        scores = nt(key_rows[...], chosen)
+        chosen = jnp.where(item_mask(queries.shape[0], LANES, item), queries, BF(0))
+        scores = nt(key_ref[0], chosen)
         top = jnp.max(scores, axis=0, keepdims=True)
         raised = jnp.exp(scores - top)
         total = jnp.sum(raised, axis=0, keepdims=True)
@@ -379,136 +376,113 @@
         span = slice(item * HDIM, (item + 1) * HDIM)
         ot_ref[0, span, :] = nn(vt_ref[span, :], weights)
     attended = ot_ref[0].T.astype(BF)
-    per = block // tokens
-    for j in range(len(outs) // per):
-
-        @pl.when(step == j)
-        def _():
-            for k in range(per):
-                outs[j * per + k][0] = attended[k * tokens : (k + 1) * tokens]
+    for k, out in enumerate(outs):
+        out[0] = attended[k * tokens : (k + 1) * tokens]
 
 
 def pair_attend(own, other, items, scale, after):
     _, _, tokens, lanes = own[0].shape
     rows, keys = len(own) * tokens, 2 * len(own) * tokens
-    block = rows // 2
-    message = pl.BlockSpec((1, tokens, lanes), lambda h, j: (h, 0, 0))
-    *outs, ot, pt, token = call(
+    wide = lambda *dims: pl.BlockSpec((1, *dims), lambda h: (h, *[0] * len(dims)))
+    *outs, ot, pt, q, k, v, token = call(
         functools.partial(pair_attend_kernel, items, scale),
         "attend",
         [
             *[shape((2, tokens, lanes))] * len(own),
             shape((2, lanes, rows), F32),
             shape((2, items, keys, rows)),
+            shape((2, rows, lanes)),
+            shape((2, keys, lanes)),
+            shape((2, keys, lanes)),
         ],
         own[0],
         *[Warm(x) for x in [*own[1:], *other]],
         after=after,
-        grid=(2, 2),
-        in_specs=[pl.BlockSpec((1, 3, tokens, lanes), lambda h, j: (h, 0, 0, 0))] * (2 * len(own)),
+        grid=(2,),
+        in_specs=[wide(3, tokens, lanes)] * (2 * len(own)),
         out_specs=[
-            *[message] * len(own),
-            pl.BlockSpec((1, lanes, block), lambda h, j: (h, 0, j)),
-            pl.BlockSpec((1, items, keys, block), lambda h, j: (h, 0, 0, j)),
-        ],
-        scratch=[
-            pltpu.VMEM((rows, lanes), BF),
-            pltpu.VMEM((keys, lanes), BF),
-            pltpu.VMEM((lanes, keys), BF),
-        ],
+            *[wide(tokens, lanes)] * len(own),
+            wide(lanes, rows),
+            wide(items, keys, rows),
+            wide(rows, lanes),
+            wide(keys, lanes),
+            wide(keys, lanes),
+        ],
+        scratch=[pltpu.VMEM((lanes, keys), BF)],
+        limit=32,
         flops=16 * rows * keys * lanes,
     )
-    return outs, ot, pt, token
-
-
-def pair_attend_back_kernel(items, scale, ids_ref, *refs):
-    sources, grads_ref, refs = refs[:8], refs[8], refs[9:]
-    ot_ref, pt_ref, *outs, cross_ref, query_rows, key_rows, value_rows, kt_ref, grad_rows, dqt_ref, dk_sum, dv_sum = refs
-    tokens = sources[0].shape[2]
-    step = pl.program_id(1)
-
-    @pl.when(step == 0)
-    def _():
-        for k, source in enumerate(sources):
-            span = slice(k * tokens, (k + 1) * tokens)
-            if k < len(outs):
-                query_rows[span, :] = source[0, 0] * BF(scale)
-                grad_rows[span, :] = grads_ref[ids_ref[4 + k], 0]
-            key_rows[span, :] = source[0, 1]
-            kt_ref[:, span] = (source[0, 1].astype(F32) * scale).T.astype(BF)
-            value_rows[span, :] = source[0, 2]
-        dk_sum[...] = jnp.zeros_like(dk_sum)
-        dv_sum[...] = jnp.zeros_like(dv_sum)
-
-    block = ot_ref.shape[2]
-    at = pl.ds(pl.multiple_of(step * block, block), block)
-    queries, grad_block = query_rows[at, :], grad_rows[at, :]
-    product = grad_block.astype(F32).T * ot_ref[0]
+    return outs, (q, k, v, ot, pt), token
+
+
+def pair_attend_back_kernel(items, scale, ids_ref, query_ref, key_ref, value_ref, ot_ref, pt_ref, grads_ref, *refs):
+    *outs, cross_ref, kt_ref, grad_rows, dqt_ref, dk_sum, dv_sum = refs
+    tokens = grads_ref.shape[2]
+    for k in range(len(outs)):
+        grad_rows[k * tokens : (k + 1) * tokens, :] = grads_ref[ids_ref[4 + k], 0]
+    kt_ref[...] = (key_ref[0].astype(F32) * scale).T.astype(BF)
+    queries, grads = query_ref[0], grad_rows[...]
+    product = grads.astype(F32).T * ot_ref[0]
     for item in range(items):
         span = slice(item * HDIM, (item + 1) * HDIM)
-        mask = item_mask(block, LANES, item)
-        grad = jnp.where(mask, grad_block, BF(0))
+        mask = item_mask(queries.shape[0], LANES, item)
+        grad = jnp.where(mask, grads, BF(0))
         query = jnp.where(mask, queries, BF(0))
         delta = jnp.sum(product[span, :], axis=0, keepdims=True)
         weights = pt_ref[0, item]
-        back = (weights.astype(F32) * (nt(value_rows[...], grad) - delta)).astype(BF)
-        dv_sum[...] += nn(weights, grad)
-        dk_sum[...] += nn(back, query)
+        back = (weights.astype(F32) * (nt(value_ref[0], grad) - delta)).astype(BF)
+        d_value, d_key = nn(weights, grad), nn(back, query)
+        if item == 0:
+            dv_sum[...] = d_value
+            dk_sum[...] = d_key
+        else:
+            dv_sum[...] += d_value
+            dk_sum[...] += d_key
         dqt_ref[span, :] = nn(kt_ref[span, :], back)
     d_query = dqt_ref[...].T.astype(BF)
-    per = block // tokens
-    for j in range(len(outs) // per):
-
-        @pl.when(step == j)
-        def _():
-            for k in range(per):
-                outs[j * per + k][0, 0] = d_query[k * tokens : (k + 1) * tokens]
-
-    @pl.when(step == pl.num_programs(1) - 1)
-    def _():
-        for k in range(2 * len(outs)):
-            span = slice(k * tokens, (k + 1) * tokens)
-            for c, total in ((0, dk_sum), (1, dv_sum)):
-                if k < len(outs):
-                    outs[k][0, 1 + c] = total[span, :].astype(BF)
-                else:
-                    cross_ref[k - len(outs), 0, c] = total[span, :].astype(BF)
-
-
-def pair_attend_back(ids, own, other, d, ot, pt, items, scale, after):
-    _, _, tokens, lanes = own[0].shape
-    count = len(own)
+    for k in range(2 * len(outs)):
+        span = slice(k * tokens, (k + 1) * tokens)
+        if k < len(outs):
+            outs[k][0, 0] = d_query[span]
+        for c, total in ((0, dk_sum), (1, dv_sum)):
+            if k < len(outs):
+                outs[k][0, 1 + c] = total[span, :].astype(BF)
+            else:
+                cross_ref[k - len(outs), 0, c] = total[span, :].astype(BF)
+
+
+def pair_attend_back(ids, kept, d, items, scale, after):
+    count, _, tokens, lanes = d.shape
     rows, keys = count * tokens, 2 * count * tokens
-    block = rows // 2
-    head = pl.BlockSpec((1, 3, tokens, lanes), lambda h, j: (h, 0, 0, 0))
+    wide = lambda *dims: pl.BlockSpec((1, *dims), lambda h: (h, *[0] * len(dims)))
     *outs, cross, token = call(
         functools.partial(pair_attend_back_kernel, items, scale),
         "attend_back",
         [*[shape((2, 3, tokens, lanes))] * count, shape((count, 2, 2, tokens, lanes))],
-        ids, *own, *other, d, ot, pt,
+        ids, *kept, d,
         after=after,
-        grid=(2, 2),
+        grid=(2,),
         in_specs=[
             pl.BlockSpec(memory_space=pltpu.SMEM),
-            *[head] * (2 * count),
-            pl.BlockSpec((count, 1, tokens, lanes), lambda h, j: (0, h, 0, 0)),
-            pl.BlockSpec((1, lanes, block), lambda h, j: (h, 0, j)),
-            pl.BlockSpec((1, items, keys, block), lambda h, j: (h, 0, 0, j)),
+            wide(rows, lanes),
+            wide(keys, lanes),
+            wide(keys, lanes),
+            wide(lanes, rows),
+            wide(items, keys, rows),
+            pl.BlockSpec((count, 1, tokens, lanes), lambda h: (0, h, 0, 0)),
         ],
         out_specs=[
-            *[head] * count,
-            pl.BlockSpec((count, 1, 2, tokens, lanes), lambda h, j: (0, h, 0, 0, 0)),
+            *[wide(3, tokens, lanes)] * count,
+            pl.BlockSpec((count, 1, 2, tokens, lanes), lambda h: (0, h, 0, 0, 0)),
         ],
         scratch=[
-            pltpu.VMEM((rows, lanes), BF),
-            pltpu.VMEM((keys, lanes), BF),
-            pltpu.VMEM((keys, lanes), BF),
             pltpu.VMEM((lanes, keys), BF),
             pltpu.VMEM((rows, lanes), BF),
-            pltpu.VMEM((lanes, block), F32),
+            pltpu.VMEM((lanes, rows), F32),
             pltpu.VMEM((keys, lanes), F32),
             pltpu.VMEM((keys, lanes), F32),
         ],
+        limit=32,
         flops=32 * rows * keys * lanes,
     )
     return outs, cross, token
@@ -638,42 +612,85 @@
     branch_ref[...] = nn(mixed_ref[...], wo_ref[...]).astype(BF)
 
 
-def forward_kernel(ids_ref, zero_ref, own_ref, got_ref, gains_ref, wu_ref, dact_ref,
-                   one_ref, copy_ref, norm_ref, pre_ref, act_ref, other_ref, *rest):
-    turned, (normed_ref, total_ref, hold) = rest[:-3], rest[-3:]
-    step = pl.program_id(0)
-
-    @pl.when(step == 0)
-    def _():
-        hidden = zero_ref[...] + (own_ref[...].astype(F32) + got_ref[...].astype(F32))
-        one_ref[...] = hidden
-        copy_ref[...] = hidden
-        unit, _ = norm_parts(hidden)
-        normed = unit * gains_ref[1:2, :]
-        normed_ref[...] = normed.astype(BF)
-        emit_turned(normed, ids_ref, turned, hold)
-        total_ref[...] = jnp.zeros_like(total_ref)
-
-    pre = nn(normed_ref[...], wu_ref[...])
-    chance = 0.5 * (1.0 + lax.erf(pre * (1.0 / math.sqrt(2.0))))
-    slope = chance + pre * jnp.exp(-0.5 * pre * pre) * (1.0 / math.sqrt(2.0 * math.pi))
-    activated = (pre * chance).astype(BF)
-    act_ref[0] = activated
-    block = activated.shape[1]
-    per_half = other_ref.shape[1] // block
-
-    @pl.when(step // per_half == 1 - ids_ref[0])
-    def _():
-        at = pl.multiple_of(step % per_half * block, LANES)
-        other_ref[:, pl.ds(at, block)] = activated
-
-    d_pre = (dact_ref[...] * slope).astype(BF)
-    pre_ref[...] = d_pre
-    total_ref[...] += nt(d_pre, wu_ref[...])
-
-    @pl.when(step == pl.num_programs(0) - 1)
-    def _():
-        norm_ref[...] = total_ref[...].astype(BF)
+def forward_kernel(sources, ids_ref, *refs):
+    if sources:
+        own, got, refs = refs[:sources], refs[sources : 2 * sources], refs[2 * sources :]
+        wo_ref, wo_got_ref, zero_ref, gains_ref, wu_ref, dact_ref, norm_ref, mixed_out, *refs = refs
+        *refs, wo_buf, mixed, wo_sems = refs
+        me = ids_ref[9]
+        wo_loads = [
+            pltpu.make_async_copy(wo_ref, wo_buf.at[me], wo_sems.at[0]),
+            pltpu.make_async_copy(wo_got_ref, wo_buf.at[1 - me], wo_sems.at[1]),
+        ]
+        for copy in wo_loads:
+            copy.start()
+    else:
+        own_ref, got_ref, zero_ref, gains_ref, wu_ref, dact_ref, norm_ref, *refs = refs
+    one_out, pre_out, act_out, other_out, *rest = refs
+    count = (len(rest) - 11) // 2
+    turned_out, turned = rest[:count], rest[count : 2 * count]
+    zero_buf, one_ref, weights, grads, pre_ref, act_ref, normed_ref, hold, into, out_of, zero_sem = rest[2 * count :]
+    zero_load = pltpu.make_async_copy(zero_ref, zero_buf, zero_sem)
+    zero_load.start()
+    chunks, _, block = grads.shape
+    per_half = chunks // 2
+    loads, stores = [], []
+    for c in range(chunks):
+        span = slice(c * block, (c + 1) * block)
+        loads.append(
+            (
+                pltpu.make_async_copy(wu_ref.at[:, span], weights.at[c], into.at[2 * c]),
+                pltpu.make_async_copy(dact_ref.at[:, span], grads.at[c], into.at[2 * c + 1]),
+            )
+        )
+
+    def store(source, target):
+        stores.append(pltpu.make_async_copy(source, target, out_of.at[len(stores)]))
+        stores[-1].start()
+
+    if sources:
+        unpack(ids_ref, own, None, mixed.at[me], 0)
+        unpack(ids_ref, got, None, mixed.at[1 - me], 0)
+        mixed_out[...] = mixed[me]
+        for copy in wo_loads:
+            copy.wait()
+    zero_load.wait()
+    for pair in loads:
+        for copy in pair:
+            copy.start()
+    if sources:
+        branch = nn(mixed[0], wo_buf[0]) + nn(mixed[1], wo_buf[1])
+    else:
+        branch = own_ref[...].astype(F32) + got_ref[...].astype(F32)
+    hidden = zero_buf[...] + branch
+    one_ref[...] = hidden
+    store(one_ref, one_out)
+    unit, _ = norm_parts(hidden)
+    normed = unit * gains_ref[1:2, :]
+    normed_ref[...] = normed.astype(BF)
+    emit_turned(normed, ids_ref, turned, hold)
+    for source, target in zip(turned, turned_out):
+        store(source, target)
+    total = None
+    for c in range(chunks):
+        span = slice(c * block, (c + 1) * block)
+        half, place = c // per_half, slice(c % per_half * block, (c % per_half + 1) * block)
+        for copy in loads[c]:
+            copy.wait()
+        pre = nn(normed_ref[...], weights[c])
+        chance = 0.5 * (1.0 + lax.erf(pre * (1.0 / math.sqrt(2.0))))
+        slope = chance + pre * jnp.exp(-0.5 * pre * pre) * (1.0 / math.sqrt(2.0 * math.pi))
+        act_ref[half, :, place] = (pre * chance).astype(BF)
+        store(act_ref.at[half, :, place], act_out.at[half, :, place])
+        d_pre = (grads[c].astype(F32) * slope).astype(BF)
+        pre_ref[:, span] = d_pre
+        store(pre_ref.at[:, span], pre_out.at[:, span])
+        part = nt(d_pre, weights[c])
+        total = part if total is None else total + part
+    store(act_ref.at[1 - ids_ref[0]], other_out)
+    norm_ref[...] = total.astype(BF)
+    for copy in stores:
+        copy.wait()
 
 
 def second_kernel(ids_ref, one_ref, two_ref, own_ref, got_ref, gains_ref, wo_ref, d_ref, gain_ref, *rest):
@@ -902,29 +919,29 @@
             out[k, :, start:] = total
 
 
-def merge_q_kernel(ids_ref, keep_a, got_a, keep_b, got_b, oh_keep, oh_got, send, left, pair_ref, *rest):
-    *embeds, hold, hold_e = rest
-    width = embeds[0].shape[1]
+def merge_q_kernel(ids_ref, keep_a, got_a, keep_b, got_b, oh_keep, oh_got,
+                   send, left, pair_ref, embed_near, embed_both, hold, hold_e):
+    width = embed_near.shape[1]
     half = pair_ref.shape[2] // 2
     first = keep_a.shape[2]
     columns = keep_b.shape[2] - half - 2 * width
+    total = hold.shape[2]
     hold[:, :, 0:first] = plus(keep_a, got_a)
     hold[:, :, first : first + columns] = plus(keep_b.at[:, :, 0:columns], got_b.at[:, :, 0:columns])
     hold[:, :, first + columns :] = plus(oh_keep, oh_got)
+    for k in range(4):
+        span = slice(columns + k % 2 * width, columns + (k % 2 + 1) * width)
+        hold_e[k] = plus(keep_b.at[k // 2, :, span], got_b.at[k // 2, :, span])
     far, near = ids_ref[3], ids_ref[2]
-    send[...] = hold[1 - far]
-    left[...] = hold[far]
+    for out, at in ((send, 1 - far), (left, far)):
+        out[:, 0:total] = hold[at]
+        out[:, total:] = hold_e[2 * at + near]
+    embed_near[...] = hold_e[2 * far + 1 - near]
+    embed_both[...] = hold_e[2 * (1 - far) + 1 - near]
     for k in range(2):
         span = slice(k * half, (k + 1) * half)
         pair_ref[0, :, span] = keep_b[k, :, columns + 2 * width :]
         pair_ref[1, :, span] = got_b[k, :, columns + 2 * width :]
-    for k in range(4):
-        span = slice(columns + k % 2 * width, columns + (k % 2 + 1) * width)
-        hold_e[k] = plus(keep_b.at[k // 2, :, span], got_b.at[k // 2, :, span])
-    for out, at in zip(
-        embeds, (2 * far + near, 2 * far + 1 - near, 2 * (1 - far) + near, 2 * (1 - far) + 1 - near)
-    ):
-        out[...] = hold_e[at]
 
 
 def expand(ids_ref, rows_ref, pair_own, pair_got, out_ref, block):
@@ -960,10 +977,9 @@
     outs[1][...] = pos_ref[...].astype(F32) + pos_got_ref[...].astype(F32)
 
 
-def end_kernel(count, *refs):
-    parts, refs = refs[:count], refs[count:]
-    if len(refs) > 2:
-        (keep_ref, got_ref), refs = refs[:2], refs[2:]
+def end_kernel(*refs):
+    if len(refs) > 3:
+        (near_ref, both_ref, keep_ref, got_ref), refs = refs[:4], refs[4:]
         out_ref, head_ref, grad_ref = refs[2:]
         both = keep_ref[...].astype(F32) + got_ref[...].astype(F32)
         width = grad_ref.shape[2]
@@ -971,10 +987,10 @@
             grad_ref[c] = both[:, c * width : (c + 1) * width]
         out_ref[...] = both[:, 3 * width : 4 * width]
         head_ref[...] = both[:, 4 * width : 4 * width + head_ref.shape[1]]
-    parts = [parts[0].at[k] for k in range(parts[0].shape[0])] if count == 1 else parts
-    total = parts[0][...].astype(F32)
-    for part in parts[1:]:
-        total = total + part[...].astype(F32)
+        embed = both[:, both.shape[1] - near_ref.shape[1] :]
+        total = embed + near_ref[...].astype(F32) + both_ref[...].astype(F32)
+    else:
+        total, refs = jnp.sum(refs[0][...].astype(F32), axis=0), refs[1:]
     features = refs[0].shape[1]
     refs[0][...] = total[:, 0:features]
     refs[1][...] = total[:, LANES:].T[features - LANES : features - LANES + 2, :]
@@ -1013,7 +1029,7 @@
     across = [[i + group * g for g in range(far)] for i in range(group)]
     assert items * HDIM == LANES and item_tokens == LANES and height == LANES and columns == 4
     lon_at, dp_at = lax.axis_index("lon"), lax.axis_index("dp")
-    ids = [lon_at % 2, dp_at, lon_at // 2 % 2, lon_at // 4 % 2, *[lon_at // 2 ^ k for k in range(4)], dp_at * lon + lon_at]
+    ids = [lon_at % 2, dp_at, lon_at // 2 % 2, lon_at // 4 % 2, *[lon_at // 2 ^ k for k in range(4)], dp_at * lon + lon_at, lax.axis_index("mp")]
     ids = jnp.stack(ids).astype(jnp.int32)
     paired = dp == 2 and lon == 8
     parts, rows = width // (2 * (width // everyone)), width // everyone
@@ -1082,12 +1098,22 @@
         if far > 1:
             kv = lax.all_gather(sent, "lon", axis=0, tiled=True, axis_index_groups=across)
 
+    if paired:
+        wo_got, normed_got = swap(w_out, "mp", 1), swap(normed_one[1], "lon", 1)
+        other = [swap(x, "lon", 1) for x in own]
+    if paired:
+        attended, kept, token = pair_attend(own, other, items, scale, [token, normed_got, wo_got])
+        attended = along(attended)
+    else:
+        attended, attended_t, weights_t, token = attend(sent, kv, items, scale, [token])
+        attended = [lax.all_to_all(attended, "lon", 0, 0, **alone)]
+    anywhere = pl.BlockSpec(memory_space=pl.ANY)
     d_two, d_act, ct_turned, *mine, token = call(
         cotangent_kernel,
         "cotangent",
         [
             shape((tokens, width), F32),
-            shape((tokens, hidden_units), F32),
+            shape((tokens, hidden_units)),
             shape((features, tokens)),
             *[shape((rows, features))] * paired,
         ],
@@ -1099,71 +1125,73 @@
 
     if paired:
         ct_got = swap(ct_turned, "lon", 1)
-        own[0] = pin(own[0], [token])
-        other = [swap(x, "lon", 1) for x in own]
+        attended[0] = pin(attended[0], [token])
+        attended += [swap(x, "mp", 1) for x in attended]
     if paired:
-        attended, attended_t, weights_t, token = pair_attend(own, other, items, scale, [token])
-        attended = along(attended)
+        branches = [attended[0], *[Warm(x) for x in attended[1:]], w_out, Warm(wo_got)]
     else:
-        attended, attended_t, weights_t, token = attend(sent, kv, items, scale, [token])
-        attended = [lax.all_to_all(attended, "lon", 0, 0, **alone)]
-    mixed, branch, token = call(
-        project_kernel,
-        "project",
-        [shape((tokens, local_width)), warm((tokens, width))],
-        ids, attended[0], *[Warm(x) for x in attended[1:]], Warm(w_out),
-        after=[token],
-        flops=2 * tokens * width * local_width,
-    )
-    branch_got = swap(branch, "mp", 1)
+        mixed, branch, token = call(
+            project_kernel,
+            "project",
+            [shape((tokens, local_width)), warm((tokens, width))],
+            ids, *attended, w_out,
+            after=[token],
+            flops=2 * tokens * width * local_width,
+        )
+        branches = [Warm(branch), Warm(swap(branch, "mp", 1))]
     block = min(512, hidden_units // 2)
-    per_half = hidden_units // 2 // block
-    column = lambda j: (0, j)
-    whole = lambda j: (0, 0)
-    full = pl.BlockSpec((tokens, width), whole)
-    turned_specs = (
-        [pl.BlockSpec((parts, rows, tokens), lambda j: (0, 0, 0))] * 2
-        if paired
-        else [pl.BlockSpec((width, tokens), whole)]
-    )
+    chunks = hidden_units // block
     out = call(
-        forward_kernel,
+        functools.partial(forward_kernel, count if paired else 0),
         "forward",
         [
-            warm((tokens, width), F32),
+            warm((tokens, width)),
+            *[shape((tokens, local_width))] * paired,
             shape((tokens, width), F32),
-            warm((tokens, width)),
             shape((tokens, hidden_units)),
             shape((2, tokens, hidden_units // 2)),
             shape((tokens, hidden_units // 2)),
             *turned_shape,
         ],
-        ids, Warm(hidden_zero), Warm(branch), Warm(branch_got), gains, Warm(w_up), Warm(d_act),
+        ids, *branches, hidden_zero, gains, w_up, d_act,
         after=[token],
-        grid=(hidden_units // block,),
         in_specs=[
-            pl.BlockSpec(memory_space=pltpu.SMEM),
-            full,
-            full,
-            full,
-            pl.BlockSpec(gains.shape, whole),
-            pl.BlockSpec((width, block), column),
-            pl.BlockSpec((tokens, block), column),
-        ],
-        out_specs=[
-            full,
-            full,
-            full,
-            pl.BlockSpec((tokens, block), column),
-            pl.BlockSpec((1, tokens, block), lambda j: (j // per_half, 0, j % per_half)),
-            pl.BlockSpec((tokens, hidden_units // 2), whole),
-            *turned_specs,
-        ],
-        scratch=[pltpu.VMEM((tokens, width), BF), pltpu.VMEM((tokens, width), F32), turned_hold],
+            smem,
+            *([*[vmem] * (len(branches) - 2), anywhere, anywhere] if paired else [vmem] * 2),
+            anywhere,
+            vmem,
+            anywhere,
+            anywhere,
+        ],
+        out_specs=[*[vmem] * (1 + paired), *[anywhere] * (4 + len(turned_shape))],
+        scratch=[
+            *[pltpu.VMEM(x.shape, BF) for x in turned_shape],
+            pltpu.VMEM((tokens, width), F32),
+            pltpu.VMEM((tokens, width), F32),
+            pltpu.VMEM((chunks, width, block), BF),
+            pltpu.VMEM((chunks, tokens, block), BF),
+            pltpu.VMEM((tokens, hidden_units), BF),
+            pltpu.VMEM((2, tokens, hidden_units // 2), BF),
+            pltpu.VMEM((tokens, width), BF),
+            turned_hold,
+            pltpu.SemaphoreType.DMA((2 * chunks,)),
+            pltpu.SemaphoreType.DMA((2 + len(turned_shape) + 2 * chunks,)),
+            pltpu.SemaphoreType.DMA,
+            *[
+                pltpu.VMEM((2, *w_out.shape), BF),
+                pltpu.VMEM((2, tokens, local_width), BF),
+                pltpu.SemaphoreType.DMA((2,)),
+            ] * paired,
+        ],
+        limit=32,
         flops=4 * tokens * width * hidden_units,
     )
-    hidden_one, hidden_copy, d_norm, d_pre, activated, act_send = out[:6]
-    normed_two, token = out[6:-1], out[-1]
+    d_norm, *out, token = out
+    if paired:
+        mixed, out = out[0], out[1:]
+        mixed_got = swap(mixed, "lon", 1)
+    hidden_one, d_pre, activated, act_send = out[:4]
+    normed_two = out[4:]
     d_norm_got = swap(d_norm, "mp", 1)
     half = hidden_units // 2
     if paired:
@@ -1212,6 +1240,8 @@
     d_one, gain_two, d_mixed = out[0], out[1], out[2:3]
     d_one_turned, token = out[3:-1], out[-1]
     if paired:
+        d_one_got = swap(d_one_turned[1], "lon", 1)
+    if paired:
         chips = [[2 * k + c for k in range(lon // 2)] for c in range(2)]
         d_heads = lax.all_to_all(
             d_mixed[0].reshape(lon // 2, 2, item_tokens, LANES), "lon", 0, 0, axis_index_groups=chips
@@ -1237,9 +1267,7 @@
         got_a, got_b = swap(send_a, "lon", 2), swap(send_b, "dp", 1)
 
     if paired:
-        back, cross, token = pair_attend_back(
-            ids, own, other, d_heads, attended_t, weights_t, items, scale, [token]
-        )
+        back, cross, token = pair_attend_back(ids, kept, d_heads, items, scale, [token])
         *back, token = call(
             combine_kernel,
             "combine",
@@ -1261,7 +1289,7 @@
         head_kernel,
         "head",
         [shape((items, features, item_tokens), F32), *turned_shape],
-        ids, hidden_copy, forward, Warm(forward_got), wh_turned,
+        ids, hidden_one, forward, Warm(forward_got), wh_turned,
         after=[token],
         scratch=[turned_hold],
         flops=2 * tokens * width * features,
@@ -1295,7 +1323,7 @@
             grads_q_kernel,
             "grads_q",
             [first, first, second, second],
-            ids, normed_one[0], Warm(swap(normed_one[1], "lon", 1)), d_qkv, Warm(swap(d_qkv, "lon", 1)),
+            ids, normed_one[0], Warm(normed_got), d_qkv, Warm(swap(d_qkv, "lon", 1)),
             after=[token],
             scratch=[pltpu.VMEM((parts, rows, 3 * local_width), BF)],
             flops=6 * tokens * width * local_width,
@@ -1304,7 +1332,7 @@
             grads_oh_kernel,
             "grads_oh",
             [shape((parts // 2, rows, wide))] * 2,
-            ids, d_one_turned[0], Warm(swap(d_one_turned[1], "lon", 1)), mixed, Warm(swap(mixed, "lon", 1)),
+            ids, d_one_turned[0], Warm(d_one_got), mixed, Warm(mixed_got),
             hidden_turned[0], Warm(swap(hidden_turned[1], "lon", 1)), ct_turned, Warm(ct_got),
             after=[token],
             scratch=[pltpu.VMEM((parts, rows, wide), BF)],
@@ -1355,29 +1383,32 @@
             ],
         )
         got_a, got_b, oh_got = swap(send_a, "lon", 2), swap(send_b, "dp", 1), swap(oh_send, "lon", 2)
-        d_edge, pos_send = pin([d_edge, pos_send], [token])
-        east, pos_got = from_behind(d_edge, "lon", -1), swap(pos_send, "dp", 1)
-        final, block = shape((rows, 3 * local_width + wide)), shape((rows, embed_width))
-        send, keep, pair, *embed, token = call(
+        east = from_behind(pin(d_edge, [token]), "lon", -1)
+        total = 3 * local_width + wide
+        final, block = shape((rows, total + embed_width)), shape((rows, embed_width))
+        send, keep, pair, embed_near, embed_both, token = call(
             merge_q_kernel,
             "merge_q",
-            [final, final, shape((2, rows, 4 * inner_columns)), *[block] * 4],
+            [final, final, shape((2, rows, 4 * inner_columns)), block, block],
             ids, keep_a, Warm(got_a), keep_b, Warm(got_b), oh_keep, Warm(oh_got),
-            after=[token, east, pos_got],
-            scratch=[pltpu.VMEM((2, *final.shape), BF), pltpu.VMEM((4, *block.shape), BF)],
+            after=[token, east],
+            scratch=[pltpu.VMEM((2, rows, total), BF), pltpu.VMEM((4, *block.shape), BF)],
         )
-        embed = [embed[0], *[Warm(swap(e, "lon", 2 * (k + 1))) for k, e in enumerate(embed[1:])]]
+        pos_got = swap(pin(pos_send, [token]), "dp", 1)
         more = [up_keep, Warm(up_got), mine[0], pair, Warm(swap(pair, "lon", 1))]
         more_outs = [shape((rows, hidden_units), F32)] * 2
         more_scratch = [pltpu.VMEM((features, hidden_units // 4), BF)]
-        rest = [keep, Warm(swap(send, "lon", 4))]
+        rest = [
+            Warm(swap(embed_near, "lon", 2)), Warm(swap(embed_both, "lon", 6)),
+            keep, Warm(swap(send, "lon", 4)),
+        ]
         rest_outs = [
             shape((rows, local_width), F32),
             shape((rows, features), F32),
             shape((3, rows, local_width), F32),
         ]
     else:
-        embed = [lax.all_to_all(embed[0].reshape(everyone, rows, 2 * LANES), ("dp", "lon"), 0, 0)]
+        rest = [lax.all_to_all(embed[0].reshape(everyone, rows, 2 * LANES), ("dp", "lon"), 0, 0)]
     *closed, token = call(
         functools.partial(close_kernel, columns),
         "close",
@@ -1387,10 +1418,10 @@
         scratch=more_scratch,
     )
     *ended, token = call(
-        functools.partial(end_kernel, len(embed)),
+        end_kernel,
         "end",
         [shape((rows, features), F32), shape((2, rows), F32), *rest_outs],
-        *embed, *rest,
+        *rest,
         after=[token],
     )
     if paired:

time: 234 us -> 221 us (0.944)
  Pallas kernels: 87.5 us -> 82.4 us
  waiting for transfers between devices: 80 us -> 76.1 us
  local copies, waits for them, and re-layouts: 8.33 us -> 5.21 us
    ppermute x45 -> x48, waiting for transfers between devices: 67.7 us -> 62.2 us  [swap(): return lax.ppermute(block, axis, route)]
    pallas_call x22 -> x21, Pallas kernels: 87.5 us -> 82.4 us  [call(): pl.pallas_call(with_token, grid=grid, out_shape=[*[o.value if isinstance(...]
    unnamed x52 -> x34, local copies, waits for them, and re-layouts: 8.24 us -> 5.13 us
    ppermute x45 -> x48, starting transfers between devices: 42.2 us -> 45.1 us  [swap(): return lax.ppermute(block, axis, route)]
    ppermute x2, waiting for transfers between devices: 9.33 us -> 12.1 us  [from_behind(): return lax.ppermute(block, axis, route)]
  transfers between devices with their start and end apart: 49 -> 52, of which waited for: 24 -> 26; matrix products, arithmetic and copies ran while one was open for 0% -> 0% of each run, Pallas kernels for 20% -> 24%
where the time goes in v2:
time: 221 us; the launch traced here: 220 us
  Pallas kernels  82.4 us (37%)
  waiting for transfers between devices  76.1 us (34%)
  starting transfers between devices  55.1 us (25%)
  local copies, waits for them, and re-layouts  5.21 us (2%)
    pallas_call x21, Pallas kernels, call(): pl.pallas_call(with_token, grid=grid, out_shape=[*[o.value if isinstance(...  82.4 us
    ppermute x48, waiting for transfers between devices, swap(): return lax.ppermute(block, axis, route)  62.2 us
    ppermute x48, starting transfers between devices, swap(): return lax.ppermute(block, axis, route)  45.1 us
    ppermute x2, waiting for transfers between devices, from_behind(): return lax.ppermute(block, axis, route)  12.1 us
    all_to_all x1, starting transfers between devices, local(): moments = lax.all_to_all(moments, ('dp', 'lon'), 0, 0)  5.92 us
    unnamed x34, local copies, waits for them, and re-layouts  5.13 us
  transfers between devices with their start and end apart: 52, of which 26 were waited for; matrix products, arithmetic and copies ran while one was open for 0% of the time, Pallas kernels for 24%

profile of v2, /device:TPU:0, one launch (start us, length us, event | category | flops | bytes accessed | tf_op | source)
XLA Modules:
  0.0 219.7 jit_solution(13092216399805286977)
XLA Ops:
  0.6 3.0 %collective-permute-start.9 = (bf16[512,1024]{1,0:T(8,128)(2,1)}, bf16[512,1024]{1,0:T(8,128)(2,1)S(1)}, u32[]{:S(2)}, u32[]{:S(2)}) collective-permute-start(bf16[512,1024]{1,0:T(8,128)(2,1)} %refs_6_.1), channel_id=1, source_target_pairs={{0,1},{1,0},{2,3},{3,2},{4,5},{5,4},{6,7},{7,6},{8,9},{9,8},{10,11... | collective-permute-start | bytes 3145736 | tf_op jit(solution)/shard_map/ppermute | solution.py:23
  4.3 2.4 %moments.1 = (f32[2,192,128]{2,1,0:T(8,128)S(1)}, bf16[2,48,128]{2,1,0:T(8,128)(2,1)S(1)}, f32[16,8,128]{2,1,0:T(8,128)}, f32[8,128]{1,0:T(8,128)}) custom-call(s32[2]{0:T(128)S(1)} %copy-done.12, f32[12,192,128]{2,1,0:T(8,128)} %bitcast.31), custom_call_target="tpu_custom_call" | custom-call | bytes 1466376 | tf_op jit(solution)/shard_map/moments/pallas_call | solution.py:138
  6.7 5.9 %all-to-all-start = ((f32[16,8,128]{2,1,0:T(8,128)}), f32[16,8,128]{2,1,0:T(8,128)S(1)}, u32[]{:S(2)}, u32[]{:S(2)}) async-start(f32[16,8,128]{2,1,0:T(8,128)} %get-tuple-element.133), calls=%async_computation | async-start | bytes 131072 | tf_op jit(solution)/shard_map/all_to_all | solution.py:1060
  13.1 5.5 %collective-permute-done.refs_6_ = bf16[2,48,128]{2,1,0:T(8,128)(2,1)S(1)} collective-permute-done((bf16[2,48,128]{2,1,0:T(8,128)(2,1)S(1)}, bf16[2,48,128]{2,1,0:T(8,128)(2,1)S(1)}, u32[]{:S(2)}, u32[]{:S(2)}) %collective-permute-start) | collective-permute-done | bytes 24608 | tf_op jit(solution)/shard_map/ppermute | solution.py:29
  19.8 5.7 %start.1 = (f32[1,48]{1,0:T(1,128)}, f32[1,48]{1,0:T(1,128)}, f32[1,48]{1,0:T(1,128)}, f32[256,1024]{1,0:T(8,128)}, bf16[192,256]{1,0:T(8,128)(2,1)}, /*index=5*...) custom-call(s32[10]{0:T(128)S(1)} %stack.43.refs_0_, ...), custom_call_target="tpu_custom_call" | custom-call | flops 905969664 | bytes 6554792 | tf_op jit(solution)/shard_map/start/pallas_call | solution.py:138
  26.5 3.4 %collective-permute-start.3 = (bf16[2,3,128,128]{3,2,1,0:T(8,128)(2,1)}, bf16[2,3,128,128]{3,2,1,0:T(8,128)(2,1)S(1)}, u32[]{:S(2)}, u32[]{:S(2)}) collective-permute-start(bf16[2,3,128,128]{3,2,1,0:T(8,128)(2,1)} %get-tuple-element.139), channel_id=1, source_target_pairs={{0,12},{2,14},{4,8},{6,10},{8,4},{10,6},{12,0},{14,2},{1,13},{3,15... | collective-permute-start | bytes 589832 | tf_op jit(solution)/shard_map/ppermute | solution.py:23
  29.9 5.2 %collective-permute-done.1.refs_1_ = bf16[2,3,128,128]{3,2,1,0:T(8,128)(2,1)S(1)} collective-permute-done((bf16[2,3,128,128]{3,2,1,0:T(8,128)(2,1)}, bf16[2,3,128,128]{3,2,1,0:T(8,128)(2,1)S(1)}, u32[]{:S(2)}, u32[]{:S(2)}) %collective-permute-start.1) | collective-permute-done | bytes 196640 | tf_op jit(solution)/shard_map/ppermute | solution.py:23
  35.2 7.8 %collective-permute-done.2.refs_2_ = bf16[2,3,128,128]{3,2,1,0:T(8,128)(2,1)S(1)} collective-permute-done((bf16[2,3,128,128]{3,2,1,0:T(8,128)(2,1)}, bf16[2,3,128,128]{3,2,1,0:T(8,128)(2,1)S(1)}, u32[]{:S(2)}, u32[]{:S(2)}) %collective-permute-start.2) | collective-permute-done | bytes 196640 | tf_op jit(solution)/shard_map/ppermute | solution.py:23
  46.0 7.1 %attend.1 = (bf16[2,128,128]{2,1,0:T(8,128)(2,1)}, bf16[2,128,128]{2,1,0:T(8,128)(2,1)}, bf16[2,128,128]{2,1,0:T(8,128)(2,1)}, bf16[2,128,128]{2,1,0:T(8,128)(2,...) custom-call(bf16[2,3,128,128]{3,2,1,0:T(8,128)(2,1)} %get-tuple-elem, ...), custom_call_target="tpu_custom_call" | custom-call | flops 1073741824 | bytes 7864320 | tf_op jit(solution)/shard_map/attend/pallas_call | solution.py:138
  53.2 3.4 %collective-permute-start.10 = (bf16[2,128,128]{2,1,0:T(8,128)(2,1)}, bf16[2,128,128]{2,1,0:T(8,128)(2,1)S(1)}, u32[]{:S(2)}, u32[]{:S(2)}) collective-permute-start(bf16[2,128,128]{2,1,0:T(8,128)(2,1)} %get-tuple-element.145), channel_id=1, source_target_pairs={{0,4},{2,6},{4,0},{6,2},{8,12},{10,14},{12,8},{14,10},{1,5},{3,7},... | collective-permute-start | bytes 196616 | tf_op jit(solution)/shard_map/ppermute | solution.py:23
  56.7 2.3 %collective-permute-start.12 = (bf16[2,128,128]{2,1,0:T(8,128)(2,1)}, bf16[2,128,128]{2,1,0:T(8,128)(2,1)S(1)}, u32[]{:S(2)}, u32[]{:S(2)}) collective-permute-start(bf16[2,128,128]{2,1,0:T(8,128)(2,1)} %get-tuple-element.147), channel_id=1, source_target_pairs={{0,12},{2,14},{4,8},{6,10},{8,4},{10,6},{12,0},{14,2},{1,13},{3,15... | collective-permute-start | bytes 196616 | tf_op jit(solution)/shard_map/ppermute | solution.py:23
  59.0 4.9 %cotangent.1 = (f32[256,1024]{1,0:T(8,128)}, bf16[256,2048]{1,0:T(8,128)(2,1)}, bf16[192,256]{1,0:T(8,128)(2,1)}, bf16[64,192]{1,0:T(8,128)(2,1)}, f32[8,128]{1,0:T(8,128)}) custom-call(s32[10]{0:T(128)S(1)} %stack.43.refs_0_, f32[2,192,128]{2,1,0:T(8,128)} %bitcast.33, bf16[192,1024]{1,0:T(8,128)(2,1)} %bitcast.29, bf16[2048,1024]{1,0:T(8,128)(2,1)} %refs_1_.1, ...), custom_call_target="tpu_custom_call" | custom-call | flops 1174405120 | bytes 7004200 | tf_op jit(solution)/shard_map/cotangent/pallas_call | solution.py:138
  64.5 1.5 collective-permute-start.14
  66.5 1.5 collective-permute-start.16
  72.0 8.9 %forward.1 = (bf16[256,1024]{1,0:T(8,128)(2,1)S(1)}, bf16[256,512]{1,0:T(8,128)(2,1)}, f32[256,1024]{1,0:T(8,128)}, bf16[256,2048]{1,0:T(8,128)(2,1)}, bf16[2,25...) custom-call(s32[10]{0:T(128)S(1)} %stack.43.refs_0_, ...), custom_call_target="tpu_custom_call" | custom-call | flops 2147483648 | bytes 13901864 | tf_op jit(solution)/shard_map/forward/pallas_call | solution.py:138
  82.6 1.7 collective-permute-done.19.refs_6_.refs_8_
  85.2 4.7 %grads_ff.1 = (bf16[4,64,1280]{2,1,0:T(8,128)(2,1)}, bf16[4,64,1280]{2,1,0:T(8,128)(2,1)}, bf16[4,64,1152]{2,1,0:T(8,128)(2,1)}, bf16[4,64,1152]{2,1,0:T(8,128)(2,1)}, f32[8,128]{1,0:T(8,128)}) custom-call(s32[10]{0:T(128)S(1)} %stack.43.refs_0_, bf16[8,64,256]{2,1,0:T(8,128)(2,1)} %get-tuple-element.152.refs_1_, ...), custom_call_target="tpu_custom_call" | custom-call | flops 1275068416 | bytes 6881320 | tf_op jit(solution)/shard_map/grads_ff/pallas_call | solution.py:138
  91.4 4.6 %down.1 = (bf16[256,1024]{1,0:T(8,128)(2,1)}, f32[8,128]{1,0:T(8,128)}) custom-call(bf16[2,256,1024]{2,1,0:T(8,128)(2,1)} %get-tuple-element.151.refs_7_.refs_0_, bf16[2048,1024]{1,0:T(8,128)(2,1)} %refs_1_.1, f32[8,128]{1,0:T(8,128)} %get-tuple-element.158.refs_2_), custom_call_target="tpu_custom_call" | custom-call | flops 1073741824 | bytes 5767168 | tf_op jit(solution)/shard_map/down/pallas_call | solution.py:138
  96.0 3.0 %second.1 = (f32[256,1024]{1,0:T(8,128)}, f32[1,1024]{1,0:T(1,128)}, bf16[8,128,128]{2,1,0:T(8,128)(2,1)}, bf16[8,64,256]{2,1,0:T(8,128)(2,1)}, bf16[8,64,256]{2,1,0:T(8,128)(2,1)}, /*index=5*/f32[8,128]{1,0:T(8,128)}) custom-call(s32[10]{0:T(128)S(1)} %stack.43.refs_0_, f32[256,1024]{1,0:T(8,128)S(1)} %copy-done.2, f32[256,1024]{1,0:T(8,128)S(1)} %copy-done.8, ...), custom_call_target="tpu_custom_call" | custom-call | flops 268435456 | bytes 6041640 | tf_op jit(solution)/shard_map/second/pallas_call | solution.py:138
  99.0 3.6 %all-to-all-start.1 = ((bf16[4,2,128,128]{3,2,1,0:T(8,128)(2,1)}), bf16[4,2,128,128]{3,2,1,0:T(8,128)(2,1)S(1)}, u32[]{:S(2)}, u32[]{:S(2)}) async-start(bf16[4,2,128,128]{3,2,1,0:T(8,128)(2,1)} %bitcast.32), calls=%async_computation.1 | async-start | bytes 524288 | tf_op jit(solution)/shard_map/all_to_all | solution.py:1246
  103.5 4.4 %collective-permute-done.24.refs_4_ = bf16[4,64,1152]{2,1,0:T(8,128)(2,1)S(1)} collective-permute-done((bf16[4,64,1152]{2,1,0:T(8,128)(2,1)}, bf16[4,64,1152]{2,1,0:T(8,128)(2,1)S(1)}, u32[]{:S(2)}, u32[]{:S(2)}) %collective-permute-start.24) | collective-permute-done | bytes 589856 | tf_op jit(solution)/shard_map/ppermute | solution.py:23
  107.9 2.6 %fold_ff.1 = (bf16[2,64,1664]{2,1,0:T(8,128)(2,1)}, bf16[2,64,1664]{2,1,0:T(8,128)(2,1)}, bf16[2,64,1152]{2,1,0:T(8,128)(2,1)}, bf16[2,64,1152]{2,1,0:T(8,128)(2,1)}, f32[8,128]{1,0:T(8,128)}) custom-call(s32[10]{0:T(128)S(1)} %stack.43.refs_0_, bf16[4,64,1280]{2,1,0:T(8,128)(2,1)} %get-tuple-element.169.refs_1_, ...), custom_call_target="tpu_custom_call" | custom-call | bytes 3932200 | tf_op jit(solution)/shard_map/fold_ff/pallas_call | solution.py:138
  113.5 7.3 %attend_back.1 = (bf16[2,3,128,128]{3,2,1,0:T(8,128)(2,1)}, bf16[2,3,128,128]{3,2,1,0:T(8,128)(2,1)}, bf16[2,3,128,128]{3,2,1,0:T(8,128)(2,1)}, bf16[2,3,128,128...) custom-call(s32[10]{0:T(128)S(1)} %stack.43.refs_0_, ...), custom_call_target="tpu_custom_call" | custom-call | flops 2147483648 | bytes 7602216 | tf_op jit(solution)/shard_map/attend_back/pallas_call | solution.py:138
  120.8 1.5 collective-permute-done.25.refs_1_.refs_2_
  122.3 2.1 collective-permute-done.27.refs_4_
  124.4 2.2 combine.1
  128.2 2.8 %collective-permute-start.30 = (bf16[2,3,128,128]{3,2,1,0:T(8,128)(2,1)}, bf16[2,3,128,128]{3,2,1,0:T(8,128)(2,1)S(1)}, u32[]{:S(2)}, u32[]{:S(2)}) collective-permute-start(bf16[2,3,128,128]{3,2,1,0:T(8,128)(2,1)} %get-tuple-element.194), channel_id=1, source_target_pairs={{0,12},{2,14},{4,8},{6,10},{8,4},{10,6},{12,0},{14,2},{1,13},{3,15... | collective-permute-start | bytes 589832 | tf_op jit(solution)/shard_map/ppermute | solution.py:23
  130.9 2.8 %head.1 = (f32[2,192,128]{2,1,0:T(8,128)}, bf16[8,64,256]{2,1,0:T(8,128)(2,1)}, bf16[8,64,256]{2,1,0:T(8,128)(2,1)}, f32[8,128]{1,0:T(8,128)}) custom-call(s32[10]{0:T(128)S(1)} %stack.43.refs_0_, f32[256,1024]{1,0:T(8,128)} %get-tuple-element.150.refs_1_, bf16[256,1024]{1,0:T(8,128)(2,1)} %get-tuple-element.159.refs_2_, ...), custom_call_target="tpu_custom_call" | custom-call | flops 100663296 | bytes 3211304 | tf_op jit(solution)/shard_map/head/pallas_call | solution.py:138
  134.7 2.5 %merge_ff.1 = (bf16[64,3584]{1,0:T(8,128)(2,1)}, bf16[64,3584]{1,0:T(8,128)(2,1)}, f32[8,128]{1,0:T(8,128)}) custom-call(s32[10]{0:T(128)S(1)} %stack.43.refs_0_, bf16[2,64,1664]{2,1,0:T(8,128)(2,1)} %get-tuple-element.195.refs_1_, bf16[2,64,1664]{2,1,0:T(8,128)(2,1)} %collective-permute-done.25.refs_1_.refs_2_, ...), custom_call_target="tpu_custom_call" | custom-call | bytes 2359336 | tf_op jit(solution)/shard_map/merge_ff/pallas_call | solution.py:138
  137.2 7.8 %collective-permute-done.29.refs_3_ = bf16[2,3,128,128]{3,2,1,0:T(8,128)(2,1)S(1)} collective-permute-done((bf16[2,3,128,128]{3,2,1,0:T(8,128)(2,1)}, bf16[2,3,128,128]{3,2,1,0:T(8,128)(2,1)S(1)}, u32[]{:S(2)}, u32[]{:S(2)}) %collective-permute-start.29) | collective-permute-done | bytes 196640 | tf_op jit(solution)/shard_map/ppermute | solution.py:23
  145.0 3.1 %third.1 = (bf16[256,1536]{1,0:T(8,128)(2,1)}, bf16[256,1024]{1,0:T(8,128)(2,1)}, f32[8,128]{1,0:T(8,128)}) custom-call(s32[10]{0:T(128)S(1)} %stack.43.refs_0_, bf16[2,3,128,128]{3,2,1,0:T(8,128)(2,1)} %get-tuple-element.191.refs_1_, bf16[2,3,128,128]{3,2,1,0:T(8,128)(2,1)S(1)} %collective-permute-done.28.refs_2_, ...), custom_call_target="tpu_custom_call" | custom-call | flops 805306368 | bytes 5242920 | tf_op jit(solution)/shard_map/third/pallas_call | solution.py:138
  150.7 3.6 %collective-permute-start.38 = (bf16[64,3584]{1,0:T(8,128)(2,1)}, bf16[64,3584]{1,0:T(8,128)(2,1)S(1)}, u32[]{:S(2)}, u32[]{:S(2)}) collective-permute-start(bf16[64,3584]{1,0:T(8,128)(2,1)} %get-tuple-element.221), channel_id=1, source_target_pairs={{0,8},{2,10},{4,12},{6,14},{8,0},{10,2},{12,4},{14,6},{1,9},{3,11}... | collective-permute-start | bytes 1376264 | tf_op jit(solution)/shard_map/ppermute | solution.py:23
  155.2 3.6 %grads_q.1 = (bf16[4,64,896]{2,1,0:T(8,128)(2,1)}, bf16[4,64,896]{2,1,0:T(8,128)(2,1)}, bf16[4,64,640]{2,1,0:T(8,128)(2,1)}, bf16[4,64,640]{2,1,0:T(8,128)(2,1)}, f32[8,128]{1,0:T(8,128)}) custom-call(s32[10]{0:T(128)S(1)} %stack.43.refs_0_, bf16[8,64,256]{2,1,0:T(8,128)(2,1)} %get-tuple-element.210.refs_1_, bf16[8,64,256]{2,1,0:T(8,128)(2,1)S(1)} %copy-done.14, ...), custom_call_target="tpu_custom_call" | custom-call | flops 805306368 | bytes 3670056 | tf_op jit(solution)/shard_map/grads_q/pallas_call | solution.py:138
  160.2 2.7 %grads_oh.1 = (bf16[4,64,768]{2,1,0:T(8,128)(2,1)}, bf16[4,64,768]{2,1,0:T(8,128)(2,1)}, f32[8,128]{1,0:T(8,128)}) custom-call(s32[10]{0:T(128)S(1)} %stack.43.refs_0_, bf16[8,64,256]{2,1,0:T(8,128)(2,1)} %get-tuple-element.202.refs_1_, bf16[8,64,256]{2,1,0:T(8,128)(2,1)} %collective-permute-done.32.refs_2_, bf16[256,512]{1,0:T(8,128)(2,1)} %get-tuple-element.204.refs_3_, ...), custom_call_target="tpu_custom_call" | custom-call | flops 402653184 | bytes 2555944 | tf_op jit(solution)/shard_map/grads_oh/pallas_call | solution.py:138
  163.8 4.1 %last.1 = (bf16[128,512]{1,0:T(8,128)(2,1)}, bf16[128,512]{1,0:T(8,128)(2,1)}, f32[2,192,128]{2,1,0:T(8,128)}, bf16[2,48,128]{2,1,0:T(8,128)(2,1)}, bf16[8,64,25...) custom-call(s32[10]{0:T(128)S(1)} %stack.43.refs_0_, f32[256,1024]{1,0:T(8,128)S(1)} %copy-done.3, ...), custom_call_target="tpu_custom_call" | custom-call | flops 201326592 | bytes 4657192 | tf_op jit(solution)/shard_map/last/pallas_call | solution.py:138
  167.8 7.4 %collective-permute-done.38.refs_6_ = bf16[64,3584]{1,0:T(8,128)(2,1)S(1)} collective-permute-done((bf16[64,3584]{1,0:T(8,128)(2,1)}, bf16[64,3584]{1,0:T(8,128)(2,1)S(1)}, u32[]{:S(2)}, u32[]{:S(2)}) %collective-permute-start.38) | collective-permute-done | bytes 458784 | tf_op jit(solution)/shard_map/ppermute | solution.py:23
  175.3 5.0 %collective-permute-done.37.refs_4_ = bf16[4,64,640]{2,1,0:T(8,128)(2,1)S(1)} collective-permute-done((bf16[4,64,640]{2,1,0:T(8,128)(2,1)}, bf16[4,64,640]{2,1,0:T(8,128)(2,1)S(1)}, u32[]{:S(2)}, u32[]{:S(2)}) %collective-permute-start.37) | collective-permute-done | bytes 327712 | tf_op jit(solution)/shard_map/ppermute | solution.py:23
  180.3 3.1 %fold_q.1 = (bf16[2,64,896]{2,1,0:T(8,128)(2,1)}, bf16[2,64,896]{2,1,0:T(8,128)(2,1)}, bf16[2,64,1920]{2,1,0:T(8,128)(2,1)}, bf16[2,64,1920]{2,1,0:T(8,128)(2,1)...) custom-call(s32[10]{0:T(128)S(1)} %stack.43.refs_0_, ...), custom_call_target="tpu_custom_call" | custom-call | bytes 5636136 | tf_op jit(solution)/shard_map/fold_q/pallas_call | solution.py:138
  183.5 1.8 collective-permute-start.43
  185.2 2.0 collective-permute-start.44
  187.3 6.5 %collective-permute-done.41.refs_8_.refs_2_ = bf16[2,48,128]{2,1,0:T(8,128)(2,1)S(1)} collective-permute-done((bf16[2,48,128]{2,1,0:T(8,128)(2,1)}, bf16[2,48,128]{2,1,0:T(8,128)(2,1)S(1)}, u32[]{:S(2)}, u32[]{:S(2)}) %collective-permute-start.41) | collective-permute-done | bytes 24608 | tf_op jit(solution)/shard_map/ppermute | solution.py:29
  193.8 1.9 collective-permute-done.44.refs_6_
  195.8 2.5 %merge_q.1 = (bf16[64,2560]{1,0:T(8,128)(2,1)}, bf16[64,2560]{1,0:T(8,128)(2,1)}, bf16[2,64,1536]{2,1,0:T(8,128)(2,1)}, bf16[64,256]{1,0:T(8,128)(2,1)}, bf16[64,256]{1,0:T(8,128)(2,1)}, /*index=5*/f32[8,128]{1,0:T(8,128)}) custom-call(s32[10]{0:T(128)S(1)} %stack.43.refs_0_, bf16[2,64,896]{2,1,0:T(8,128)(2,1)} %get-tuple-element.230.refs_1_, ...), custom_call_target="tpu_custom_call" | custom-call | bytes 2949160 | tf_op jit(solution)/shard_map/merge_q/pallas_call | solution.py:138
  204.4 1.6 collective-permute-done.45.refs_4_
  206.8 2.8 %close.1 = (f32[2,192,128]{2,1,0:T(8,128)}, f32[128,512]{1,0:T(8,128)}, f32[64,2048]{1,0:T(8,128)}, f32[64,2048]{1,0:T(8,128)}, f32[8,128]{1,0:T(8,128)}) custom-call(s32[10]{0:T(128)S(1)} %stack.43.refs_0_, f32[2,192,128]{2,1,0:T(8,128)} %get-tuple-element.214.refs_1_, bf16[2,48,128]{2,1,0:T(8,128)(2,1)S(1)} %copy-done.11, ...), custom_call_target="tpu_custom_call" | custom-call | bytes 3719208 | tf_op jit(solution)/shard_map/close/pallas_call | solution.py:138
  209.5 2.5 %collective-permute-done.48.refs_1_ = bf16[64,256]{1,0:T(8,128)(2,1)S(1)} collective-permute-done((bf16[64,256]{1,0:T(8,128)(2,1)}, bf16[64,256]{1,0:T(8,128)(2,1)S(1)}, u32[]{:S(2)}, u32[]{:S(2)}) %collective-permute-start.48) | collective-permute-done | bytes 32800 | tf_op jit(solution)/shard_map/ppermute | solution.py:23
  212.0 5.8 %collective-permute-done.49.refs_3_ = bf16[64,2560]{1,0:T(8,128)(2,1)S(1)} collective-permute-done((bf16[64,2560]{1,0:T(8,128)(2,1)}, bf16[64,2560]{1,0:T(8,128)(2,1)S(1)}, u32[]{:S(2)}, u32[]{:S(2)}) %collective-permute-start.49) | collective-permute-done | bytes 327712 | tf_op jit(solution)/shard_map/ppermute | solution.py:23
  217.8 1.9 end.1
  (118 shorter events, 34.6 us)
Async XLA Ops:
  0.6 44.3 %collective-permute-start.9 = (bf16[512,1024]{1,0:T(8,128)(2,1)}, bf16[512,1024]{1,0:T(8,128)(2,1)S(1)}, u32[]{:S(2)}, u32[]{:S(2)}) collective-permute-start(bf16[512,1024]{1,0:T(8,128)(2,1)} %refs_6_.1), channel_id=1, source_target_pairs={{0,1},{1,0},{2,3},{3,2},{4,5},{5,4},{6,7},{7,6},{8,9},{9,8},{10,11... | collective-permute-start | bytes 3145736 | tf_op jit(solution)/shard_map/ppermute | solution.py:23
  6.7 13.1 %all-to-all-start = ((f32[16,8,128]{2,1,0:T(8,128)}), f32[16,8,128]{2,1,0:T(8,128)S(1)}, u32[]{:S(2)}, u32[]{:S(2)}) async-start(f32[16,8,128]{2,1,0:T(8,128)} %get-tuple-element.133), calls=%async_computation | async-start | bytes 131072 | tf_op jit(solution)/shard_map/all_to_all | solution.py:1060
  12.6 6.0 %collective-permute-start = (bf16[2,48,128]{2,1,0:T(8,128)(2,1)S(1)}, bf16[2,48,128]{2,1,0:T(8,128)(2,1)S(1)}, u32[]{:S(2)}, u32[]{:S(2)}) collective-permute-start(bf16[2,48,128]{2,1,0:T(8,128)(2,1)S(1)} %get-tuple-element.135), channel_id=1, source_target_pairs={{14,0},{0,2},{2,4},{4,6},{6,8},{8,10},{10,12},{12,14},{15,1},{1,3}... | collective-permute-start | bytes 73736 | tf_op jit(solution)/shard_map/ppermute | solution.py:29
  25.5 9.7 %collective-permute-start.1 = (bf16[2,3,128,128]{3,2,1,0:T(8,128)(2,1)}, bf16[2,3,128,128]{3,2,1,0:T(8,128)(2,1)S(1)}, u32[]{:S(2)}, u32[]{:S(2)}) collective-permute-start(bf16[2,3,128,128]{3,2,1,0:T(8,128)(2,1)} %get-tuple-element.137), channel_id=1, source_target_pairs={{0,4},{2,6},{4,0},{6,2},{8,12},{10,14},{12,8},{14,10},{1,5},{3,7},... | collective-permute-start | bytes 589832 | tf_op jit(solution)/shard_map/ppermute | solution.py:23
  25.6 17.4 %collective-permute-start.2 = (bf16[2,3,128,128]{3,2,1,0:T(8,128)(2,1)}, bf16[2,3,128,128]{3,2,1,0:T(8,128)(2,1)S(1)}, u32[]{:S(2)}, u32[]{:S(2)}) collective-permute-start(bf16[2,3,128,128]{3,2,1,0:T(8,128)(2,1)} %get-tuple-element.138), channel_id=1, source_target_pairs={{0,8},{2,10},{4,12},{6,14},{8,0},{10,2},{12,4},{14,6},{1,9},{3,11}... | collective-permute-start | bytes 589832 | tf_op jit(solution)/shard_map/ppermute | solution.py:23
  26.5 16.5 %collective-permute-start.3 = (bf16[2,3,128,128]{3,2,1,0:T(8,128)(2,1)}, bf16[2,3,128,128]{3,2,1,0:T(8,128)(2,1)S(1)}, u32[]{:S(2)}, u32[]{:S(2)}) collective-permute-start(bf16[2,3,128,128]{3,2,1,0:T(8,128)(2,1)} %get-tuple-element.139), channel_id=1, source_target_pairs={{0,12},{2,14},{4,8},{6,10},{8,4},{10,6},{12,0},{14,2},{1,13},{3,15... | collective-permute-start | bytes 589832 | tf_op jit(solution)/shard_map/ppermute | solution.py:23
  29.9 13.5 %collective-permute-start.4 = (bf16[2,3,128,128]{3,2,1,0:T(8,128)(2,1)}, bf16[2,3,128,128]{3,2,1,0:T(8,128)(2,1)S(1)}, u32[]{:S(2)}, u32[]{:S(2)}) collective-permute-start(bf16[2,3,128,128]{3,2,1,0:T(8,128)(2,1)} %get-tuple-element.136.refs_0_), channel_id=1, source_target_pairs={{0,2},{2,0},{4,6},{6,4},{8,10},{10,8},{12,14},{14,12},{1,3},{3,1},... | collective-permute-start | bytes 589832 | tf_op jit(solution)/shard_map/ppermute | solution.py:23
  35.2 8.4 %collective-permute-start.8 = (bf16[8,64,256]{2,1,0:T(8,128)(2,1)}, bf16[8,64,256]{2,1,0:T(8,128)(2,1)S(1)}, u32[]{:S(2)}, u32[]{:S(2)}) collective-permute-start(bf16[8,64,256]{2,1,0:T(8,128)(2,1)} %get-tuple-element.141), channel_id=1, source_target_pairs={{0,2},{2,0},{4,6},{6,4},{8,10},{10,8},{12,14},{14,12},{1,3},{3,1},... | collective-permute-start | bytes 786440 | tf_op jit(solution)/shard_map/ppermute | solution.py:23
  53.2 11.3 %collective-permute-start.10 = (bf16[2,128,128]{2,1,0:T(8,128)(2,1)}, bf16[2,128,128]{2,1,0:T(8,128)(2,1)S(1)}, u32[]{:S(2)}, u32[]{:S(2)}) collective-permute-start(bf16[2,128,128]{2,1,0:T(8,128)(2,1)} %get-tuple-element.145), channel_id=1, source_target_pairs={{0,4},{2,6},{4,0},{6,2},{8,12},{10,14},{12,8},{14,10},{1,5},{3,7},... | collective-permute-start | bytes 196616 | tf_op jit(solution)/shard_map/ppermute | solution.py:23
  56.6 9.4 %collective-permute-start.11 = (bf16[2,128,128]{2,1,0:T(8,128)(2,1)}, bf16[2,128,128]{2,1,0:T(8,128)(2,1)S(1)}, u32[]{:S(2)}, u32[]{:S(2)}) collective-permute-start(bf16[2,128,128]{2,1,0:T(8,128)(2,1)} %get-tuple-element.146), channel_id=1, source_target_pairs={{0,8},{2,10},{4,12},{6,14},{8,0},{10,2},{12,4},{14,6},{1,9},{3,11}... | collective-permute-start | bytes 196616 | tf_op jit(solution)/shard_map/ppermute | solution.py:23
  56.7 9.8 %collective-permute-start.12 = (bf16[2,128,128]{2,1,0:T(8,128)(2,1)}, bf16[2,128,128]{2,1,0:T(8,128)(2,1)S(1)}, u32[]{:S(2)}, u32[]{:S(2)}) collective-permute-start(bf16[2,128,128]{2,1,0:T(8,128)(2,1)} %get-tuple-element.147), channel_id=1, source_target_pairs={{0,12},{2,14},{4,8},{6,10},{8,4},{10,6},{12,0},{14,2},{1,13},{3,15... | collective-permute-start | bytes 196616 | tf_op jit(solution)/shard_map/ppermute | solution.py:23
  63.9 5.2 %collective-permute-start.13 = (bf16[2,128,128]{2,1,0:T(8,128)(2,1)}, bf16[2,128,128]{2,1,0:T(8,128)(2,1)S(1)}, u32[]{:S(2)}, u32[]{:S(2)}) collective-permute-start(bf16[2,128,128]{2,1,0:T(8,128)(2,1)} %pin.6.refs_1_), channel_id=1, source_target_pairs={{0,1},{1,0},{2,3},{3,2},{4,5},{5,4},{6,7},{7,6},{8,9},{9,8},{10,11... | collective-permute-start | bytes 196616 | tf_op jit(solution)/shard_map/ppermute | solution.py:23
  64.5 6.1 %collective-permute-start.14 = (bf16[2,128,128]{2,1,0:T(8,128)(2,1)S(1)}, bf16[2,128,128]{2,1,0:T(8,128)(2,1)S(1)}, u32[]{:S(2)}, u32[]{:S(2)}) collective-permute-start(bf16[2,128,128]{2,1,0:T(8,128)(2,1)S(1)} %collective-permute-done.10.refs_2_), channel_id=1, source_target_pairs={{0,1},{1,0},{2,3},{3,2},{4,5},{5,4},{6,7},{7,6},{8,9},{9,8},{10,11... | collective-permute-start | bytes 196616 | tf_op jit(solution)/shard_map/ppermute | solution.py:23
  66.0 5.4 %collective-permute-start.15 = (bf16[2,128,128]{2,1,0:T(8,128)(2,1)S(1)}, bf16[2,128,128]{2,1,0:T(8,128)(2,1)S(1)}, u32[]{:S(2)}, u32[]{:S(2)}) collective-permute-start(bf16[2,128,128]{2,1,0:T(8,128)(2,1)S(1)} %collective-permute-done.11.refs_3_), channel_id=1, source_target_pairs={{0,1},{1,0},{2,3},{3,2},{4,5},{5,4},{6,7},{7,6},{8,9},{9,8},{10,11... | collective-permute-start | bytes 196616 | tf_op jit(solution)/shard_map/ppermute | solution.py:23
  66.5 5.5 %collective-permute-start.16 = (bf16[2,128,128]{2,1,0:T(8,128)(2,1)S(1)}, bf16[2,128,128]{2,1,0:T(8,128)(2,1)S(1)}, u32[]{:S(2)}, u32[]{:S(2)}) collective-permute-start(bf16[2,128,128]{2,1,0:T(8,128)(2,1)S(1)} %collective-permute-done.12.refs_4_), channel_id=1, source_target_pairs={{0,1},{1,0},{2,3},{3,2},{4,5},{5,4},{6,7},{7,6},{8,9},{9,8},{10,11... | collective-permute-start | bytes 196616 | tf_op jit(solution)/shard_map/ppermute | solution.py:23
  80.9 4.2 %collective-permute-start.18 = (bf16[256,2048]{1,0:T(8,128)(2,1)}, bf16[256,2048]{1,0:T(8,128)(2,1)S(1)}, u32[]{:S(2)}, u32[]{:S(2)}) collective-permute-start(bf16[256,2048]{1,0:T(8,128)(2,1)} %get-tuple-element.154.refs_3_), channel_id=1, source_target_pairs={{0,2},{2,0},{4,6},{6,4},{8,10},{10,8},{12,14},{14,12},{1,3},{3,1},... | collective-permute-start | bytes 3145736 | tf_op jit(solution)/shard_map/ppermute | solution.py:23
  81.0 4.1 %collective-permute-start.20 = (bf16[256,1024]{1,0:T(8,128)(2,1)}, bf16[256,1024]{1,0:T(8,128)(2,1)S(1)}, u32[]{:S(2)}, u32[]{:S(2)}) collective-permute-start(bf16[256,1024]{1,0:T(8,128)(2,1)} %get-tuple-element.156), channel_id=1, source_target_pairs={{0,2},{2,0},{4,6},{6,4},{8,10},{10,8},{12,14},{14,12},{1,3},{3,1},... | collective-permute-start | bytes 1572872 | tf_op jit(solution)/shard_map/ppermute | solution.py:23
  81.5 3.6 %collective-permute-start.17 = (bf16[8,64,256]{2,1,0:T(8,128)(2,1)}, bf16[8,64,256]{2,1,0:T(8,128)(2,1)S(1)}, u32[]{:S(2)}, u32[]{:S(2)}) collective-permute-start(bf16[8,64,256]{2,1,0:T(8,128)(2,1)} %get-tuple-element.153), channel_id=1, source_target_pairs={{0,2},{2,0},{4,6},{6,4},{8,10},{10,8},{12,14},{14,12},{1,3},{3,1},... | collective-permute-start | bytes 786440 | tf_op jit(solution)/shard_map/ppermute | solution.py:23
  81.6 14.4 %collective-permute-start.22 = (bf16[256,1024]{1,0:T(8,128)(2,1)S(1)}, bf16[256,1024]{1,0:T(8,128)(2,1)S(1)}, u32[]{:S(2)}, u32[]{:S(2)}) collective-permute-start(bf16[256,1024]{1,0:T(8,128)(2,1)S(1)} %get-tuple-element.166.refs_3_), channel_id=1, source_target_pairs={{0,1},{1,0},{2,3},{3,2},{4,5},{5,4},{6,7},{7,6},{8,9},{9,8},{10,11... | collective-permute-start | bytes 1572872 | tf_op jit(solution)/shard_map/ppermute | solution.py:23
  89.9 18.0 %collective-permute-start.23 = (bf16[4,64,1280]{2,1,0:T(8,128)(2,1)}, bf16[4,64,1280]{2,1,0:T(8,128)(2,1)S(1)}, u32[]{:S(2)}, u32[]{:S(2)}) collective-permute-start(bf16[4,64,1280]{2,1,0:T(8,128)(2,1)} %get-tuple-element.170), channel_id=1, source_target_pairs={{0,16},{16,0},{1,17},{17,1},{2,18},{18,2},{3,19},{19,3},{4,20},{20... | collective-permute-start | bytes 1966088 | tf_op jit(solution)/shard_map/ppermute | solution.py:23
  90.6 17.3 %collective-permute-start.24 = (bf16[4,64,1152]{2,1,0:T(8,128)(2,1)}, bf16[4,64,1152]{2,1,0:T(8,128)(2,1)S(1)}, u32[]{:S(2)}, u32[]{:S(2)}) collective-permute-start(bf16[4,64,1152]{2,1,0:T(8,128)(2,1)} %get-tuple-element.172), channel_id=1, source_target_pairs={{0,4},{2,6},{4,0},{6,2},{8,12},{10,14},{12,8},{14,10},{1,5},{3,7},... | collective-permute-start | bytes 1769480 | tf_op jit(solution)/shard_map/ppermute | solution.py:23
  99.0 12.3 %all-to-all-start.1 = ((bf16[4,2,128,128]{3,2,1,0:T(8,128)(2,1)}), bf16[4,2,128,128]{3,2,1,0:T(8,128)(2,1)S(1)}, u32[]{:S(2)}, u32[]{:S(2)}) async-start(bf16[4,2,128,128]{3,2,1,0:T(8,128)(2,1)} %bitcast.32), calls=%async_computation.1 | async-start | bytes 524288 | tf_op jit(solution)/shard_map/all_to_all | solution.py:1246
  102.6 18.1 %collective-permute-start.21 = (bf16[256,1024]{1,0:T(8,128)(2,1)}, bf16[256,1024]{1,0:T(8,128)(2,1)}, u32[]{:S(2)}, u32[]{:S(2)}) collective-permute-start(bf16[256,1024]{1,0:T(8,128)(2,1)} %get-tuple-element.159.refs_2_), channel_id=1, source_target_pairs={{0,1},{1,0},{2,3},{3,2},{4,5},{5,4},{6,7},{7,6},{8,9},{9,8},{10,11... | collective-permute-start | bytes 1572872 | tf_op jit(solution)/shard_map/ppermute | solution.py:23
  112.0 10.2 %collective-permute-start.25 = (bf16[2,64,1664]{2,1,0:T(8,128)(2,1)}, bf16[2,64,1664]{2,1,0:T(8,128)(2,1)}, u32[]{:S(2)}, u32[]{:S(2)}) collective-permute-start(bf16[2,64,1664]{2,1,0:T(8,128)(2,1)} %get-tuple-element.182), channel_id=1, source_target_pairs={{0,4},{2,6},{4,0},{6,2},{8,12},{10,14},{12,8},{14,10},{1,5},{3,7},... | collective-permute-start | bytes 1277960 | tf_op jit(solution)/shard_map/ppermute | solution.py:23
  112.2 8.6 %collective-permute-start.26 = (bf16[2,64,1152]{2,1,0:T(8,128)(2,1)}, bf16[2,64,1152]{2,1,0:T(8,128)(2,1)S(1)}, u32[]{:S(2)}, u32[]{:S(2)}) collective-permute-start(bf16[2,64,1152]{2,1,0:T(8,128)(2,1)} %get-tuple-element.183), channel_id=1, source_target_pairs={{0,16},{16,0},{1,17},{17,1},{2,18},{18,2},{3,19},{19,3},{4,20},{20... | collective-permute-start | bytes 884744 | tf_op jit(solution)/shard_map/ppermute | solution.py:23
  122.3 2.1 collective-permute-start.27
  126.6 10.6 %collective-permute-start.28 = (bf16[2,3,128,128]{3,2,1,0:T(8,128)(2,1)}, bf16[2,3,128,128]{3,2,1,0:T(8,128)(2,1)S(1)}, u32[]{:S(2)}, u32[]{:S(2)}) collective-permute-start(bf16[2,3,128,128]{3,2,1,0:T(8,128)(2,1)} %get-tuple-element.192), channel_id=1, source_target_pairs={{0,4},{2,6},{4,0},{6,2},{8,12},{10,14},{12,8},{14,10},{1,5},{3,7},... | collective-permute-start | bytes 589832 | tf_op jit(solution)/shard_map/ppermute | solution.py:23
  127.6 17.3 %collective-permute-start.29 = (bf16[2,3,128,128]{3,2,1,0:T(8,128)(2,1)}, bf16[2,3,128,128]{3,2,1,0:T(8,128)(2,1)S(1)}, u32[]{:S(2)}, u32[]{:S(2)}) collective-permute-start(bf16[2,3,128,128]{3,2,1,0:T(8,128)(2,1)} %get-tuple-element.193), channel_id=1, source_target_pairs={{0,8},{2,10},{4,12},{6,14},{8,0},{10,2},{12,4},{14,6},{1,9},{3,11}... | collective-permute-start | bytes 589832 | tf_op jit(solution)/shard_map/ppermute | solution.py:23
  128.2 16.8 %collective-permute-start.30 = (bf16[2,3,128,128]{3,2,1,0:T(8,128)(2,1)}, bf16[2,3,128,128]{3,2,1,0:T(8,128)(2,1)S(1)}, u32[]{:S(2)}, u32[]{:S(2)}) collective-permute-start(bf16[2,3,128,128]{3,2,1,0:T(8,128)(2,1)} %get-tuple-element.194), channel_id=1, source_target_pairs={{0,12},{2,14},{4,8},{6,10},{8,4},{10,6},{12,0},{14,2},{1,13},{3,15... | collective-permute-start | bytes 589832 | tf_op jit(solution)/shard_map/ppermute | solution.py:23
  148.1 2.6 %collective-permute-start.35 = (bf16[256,1536]{1,0:T(8,128)(2,1)}, bf16[256,1536]{1,0:T(8,128)(2,1)}, u32[]{:S(2)}, u32[]{:S(2)}) collective-permute-start(bf16[256,1536]{1,0:T(8,128)(2,1)} %get-tuple-element.211.refs_3_), channel_id=1, source_target_pairs={{0,2},{2,0},{4,6},{6,4},{8,10},{10,8},{12,14},{14,12},{1,3},{3,1},... | collective-permute-start | bytes 2359304 | tf_op jit(solution)/shard_map/ppermute | solution.py:23
  148.1 15.7 %collective-permute-start.31 = (bf16[256,1024]{1,0:T(8,128)(2,1)}, bf16[256,1024]{1,0:T(8,128)(2,1)S(1)}, u32[]{:S(2)}, u32[]{:S(2)}) collective-permute-start(bf16[256,1024]{1,0:T(8,128)(2,1)} %get-tuple-element.199.refs_3_), channel_id=1, source_target_pairs={{0,1},{1,0},{2,3},{3,2},{4,5},{5,4},{6,7},{7,6},{8,9},{9,8},{10,11... | collective-permute-start | bytes 1572872 | tf_op jit(solution)/shard_map/ppermute | solution.py:23
  149.0 9.9 %collective-permute-start.33 = (bf16[256,512]{1,0:T(8,128)(2,1)}, bf16[256,512]{1,0:T(8,128)(2,1)S(1)}, u32[]{:S(2)}, u32[]{:S(2)}) collective-permute-start(bf16[256,512]{1,0:T(8,128)(2,1)} %get-tuple-element.204.refs_3_), channel_id=1, source_target_pairs={{0,2},{2,0},{4,6},{6,4},{8,10},{10,8},{12,14},{14,12},{1,3},{3,1},... | collective-permute-start | bytes 786440 | tf_op jit(solution)/shard_map/ppermute | solution.py:23
  149.1 11.0 %collective-permute-start.32 = (bf16[8,64,256]{2,1,0:T(8,128)(2,1)}, bf16[8,64,256]{2,1,0:T(8,128)(2,1)}, u32[]{:S(2)}, u32[]{:S(2)}) collective-permute-start(bf16[8,64,256]{2,1,0:T(8,128)(2,1)} %get-tuple-element.203), channel_id=1, source_target_pairs={{0,2},{2,0},{4,6},{6,4},{8,10},{10,8},{12,14},{14,12},{1,3},{3,1},... | collective-permute-start | bytes 786440 | tf_op jit(solution)/shard_map/ppermute | solution.py:23
  149.5 10.7 %collective-permute-start.34 = (bf16[8,64,256]{2,1,0:T(8,128)(2,1)}, bf16[8,64,256]{2,1,0:T(8,128)(2,1)S(1)}, u32[]{:S(2)}, u32[]{:S(2)}) collective-permute-start(bf16[8,64,256]{2,1,0:T(8,128)(2,1)} %get-tuple-element.209), channel_id=1, source_target_pairs={{0,2},{2,0},{4,6},{6,4},{8,10},{10,8},{12,14},{14,12},{1,3},{3,1},... | collective-permute-start | bytes 786440 | tf_op jit(solution)/shard_map/ppermute | solution.py:23
  150.7 24.6 %collective-permute-start.38 = (bf16[64,3584]{1,0:T(8,128)(2,1)}, bf16[64,3584]{1,0:T(8,128)(2,1)S(1)}, u32[]{:S(2)}, u32[]{:S(2)}) collective-permute-start(bf16[64,3584]{1,0:T(8,128)(2,1)} %get-tuple-element.221), channel_id=1, source_target_pairs={{0,8},{2,10},{4,12},{6,14},{8,0},{10,2},{12,4},{14,6},{1,9},{3,11}... | collective-permute-start | bytes 1376264 | tf_op jit(solution)/shard_map/ppermute | solution.py:23
  158.9 21.4 %collective-permute-start.36 = (bf16[4,64,896]{2,1,0:T(8,128)(2,1)}, bf16[4,64,896]{2,1,0:T(8,128)(2,1)S(1)}, u32[]{:S(2)}, u32[]{:S(2)}) collective-permute-start(bf16[4,64,896]{2,1,0:T(8,128)(2,1)} %get-tuple-element.217), channel_id=1, source_target_pairs={{0,16},{16,0},{1,17},{17,1},{2,18},{18,2},{3,19},{19,3},{4,20},{20... | collective-permute-start | bytes 1376264 | tf_op jit(solution)/shard_map/ppermute | solution.py:23
  162.9 17.4 %collective-permute-start.39 = (bf16[4,64,768]{2,1,0:T(8,128)(2,1)}, bf16[4,64,768]{2,1,0:T(8,128)(2,1)S(1)}, u32[]{:S(2)}, u32[]{:S(2)}) collective-permute-start(bf16[4,64,768]{2,1,0:T(8,128)(2,1)} %get-tuple-element.223), channel_id=1, source_target_pairs={{0,16},{16,0},{1,17},{17,1},{2,18},{18,2},{3,19},{19,3},{4,20},{20... | collective-permute-start | bytes 1179656 | tf_op jit(solution)/shard_map/ppermute | solution.py:23
  163.6 16.7 %collective-permute-start.37 = (bf16[4,64,640]{2,1,0:T(8,128)(2,1)}, bf16[4,64,640]{2,1,0:T(8,128)(2,1)S(1)}, u32[]{:S(2)}, u32[]{:S(2)}) collective-permute-start(bf16[4,64,640]{2,1,0:T(8,128)(2,1)} %get-tuple-element.219), channel_id=1, source_target_pairs={{0,4},{2,6},{4,0},{6,2},{8,12},{10,14},{12,8},{14,10},{1,5},{3,7},... | collective-permute-start | bytes 983048 | tf_op jit(solution)/shard_map/ppermute | solution.py:23
  167.8 7.5 %collective-permute-start.40 = (bf16[8,64,256]{2,1,0:T(8,128)(2,1)}, bf16[8,64,256]{2,1,0:T(8,128)(2,1)S(1)}, u32[]{:S(2)}, u32[]{:S(2)}) collective-permute-start(bf16[8,64,256]{2,1,0:T(8,128)(2,1)} %get-tuple-element.225), channel_id=1, source_target_pairs={{0,2},{2,0},{4,6},{6,4},{8,10},{10,8},{12,14},{14,12},{1,3},{3,1},... | collective-permute-start | bytes 786440 | tf_op jit(solution)/shard_map/ppermute | solution.py:23
  183.5 12.3 %collective-permute-start.43 = (bf16[2,64,1920]{2,1,0:T(8,128)(2,1)}, bf16[2,64,1920]{2,1,0:T(8,128)(2,1)S(1)}, u32[]{:S(2)}, u32[]{:S(2)}) collective-permute-start(bf16[2,64,1920]{2,1,0:T(8,128)(2,1)} %get-tuple-element.233), channel_id=1, source_target_pairs={{0,16},{16,0},{1,17},{17,1},{2,18},{18,2},{3,19},{19,3},{4,20},{20... | collective-permute-start | bytes 1474568 | tf_op jit(solution)/shard_map/ppermute | solution.py:23
  185.2 10.6 %collective-permute-start.42 = (bf16[2,64,896]{2,1,0:T(8,128)(2,1)}, bf16[2,64,896]{2,1,0:T(8,128)(2,1)S(1)}, u32[]{:S(2)}, u32[]{:S(2)}) collective-permute-start(bf16[2,64,896]{2,1,0:T(8,128)(2,1)} %get-tuple-element.231), channel_id=1, source_target_pairs={{0,4},{2,6},{4,0},{6,2},{8,12},{10,14},{12,8},{14,10},{1,5},{3,7},... | collective-permute-start | bytes 688136 | tf_op jit(solution)/shard_map/ppermute | solution.py:23
  185.2 10.5 %collective-permute-start.44 = (bf16[2,64,768]{2,1,0:T(8,128)(2,1)}, bf16[2,64,768]{2,1,0:T(8,128)(2,1)S(1)}, u32[]{:S(2)}, u32[]{:S(2)}) collective-permute-start(bf16[2,64,768]{2,1,0:T(8,128)(2,1)} %get-tuple-element.235), channel_id=1, source_target_pairs={{0,4},{2,6},{4,0},{6,2},{8,12},{10,14},{12,8},{14,10},{1,5},{3,7},... | collective-permute-start | bytes 589832 | tf_op jit(solution)/shard_map/ppermute | solution.py:23
  187.3 6.6 %collective-permute-start.41 = (bf16[2,48,128]{2,1,0:T(8,128)(2,1)}, bf16[2,48,128]{2,1,0:T(8,128)(2,1)S(1)}, u32[]{:S(2)}, u32[]{:S(2)}) collective-permute-start(bf16[2,48,128]{2,1,0:T(8,128)(2,1)} %pin.10), channel_id=1, source_target_pairs={{2,0},{4,2},{6,4},{8,6},{10,8},{12,10},{14,12},{0,14},{3,1},{5,3},... | collective-permute-start | bytes 73736 | tf_op jit(solution)/shard_map/ppermute | solution.py:29
  198.3 7.8 %collective-permute-start.46 = (bf16[2,64,1536]{2,1,0:T(8,128)(2,1)}, bf16[2,64,1536]{2,1,0:T(8,128)(2,1)S(1)}, u32[]{:S(2)}, u32[]{:S(2)}) collective-permute-start(bf16[2,64,1536]{2,1,0:T(8,128)(2,1)} %get-tuple-element.238.refs_8_), channel_id=1, source_target_pairs={{0,2},{2,0},{4,6},{6,4},{8,10},{10,8},{12,14},{14,12},{1,3},{3,1},... | collective-permute-start | bytes 1179656 | tf_op jit(solution)/shard_map/ppermute | solution.py:23
  199.0 18.9 %collective-permute-start.49 = (bf16[64,2560]{1,0:T(8,128)(2,1)}, bf16[64,2560]{1,0:T(8,128)(2,1)S(1)}, u32[]{:S(2)}, u32[]{:S(2)}) collective-permute-start(bf16[64,2560]{1,0:T(8,128)(2,1)} %get-tuple-element.243), channel_id=1, source_target_pairs={{0,8},{2,10},{4,12},{6,14},{8,0},{10,2},{12,4},{14,6},{1,9},{3,11}... | collective-permute-start | bytes 983048 | tf_op jit(solution)/shard_map/ppermute | solution.py:23
  200.5 5.6 %collective-permute-start.45 = (bf16[128,512]{1,0:T(8,128)(2,1)}, bf16[128,512]{1,0:T(8,128)(2,1)S(1)}, u32[]{:S(2)}, u32[]{:S(2)}) collective-permute-start(bf16[128,512]{1,0:T(8,128)(2,1)} %pin.11), channel_id=1, source_target_pairs={{0,16},{16,0},{1,17},{17,1},{2,18},{18,2},{3,19},{19,3},{4,20},{20... | collective-permute-start | bytes 393224 | tf_op jit(solution)/shard_map/ppermute | solution.py:23
  201.9 7.7 %collective-permute-start.47 = (bf16[64,256]{1,0:T(8,128)(2,1)}, bf16[64,256]{1,0:T(8,128)(2,1)S(1)}, u32[]{:S(2)}, u32[]{:S(2)}) collective-permute-start(bf16[64,256]{1,0:T(8,128)(2,1)} %get-tuple-element.240), channel_id=1, source_target_pairs={{0,4},{2,6},{4,0},{6,2},{8,12},{10,14},{12,8},{14,10},{1,5},{3,7},... | collective-permute-start | bytes 98312 | tf_op jit(solution)/shard_map/ppermute | solution.py:23
  203.2 8.8 %collective-permute-start.48 = (bf16[64,256]{1,0:T(8,128)(2,1)}, bf16[64,256]{1,0:T(8,128)(2,1)S(1)}, u32[]{:S(2)}, u32[]{:S(2)}) collective-permute-start(bf16[64,256]{1,0:T(8,128)(2,1)} %get-tuple-element.241), channel_id=1, source_target_pairs={{0,12},{2,14},{4,8},{6,10},{8,4},{10,6},{12,0},{14,2},{1,13},{3,15... | collective-permute-start | bytes 98312 | tf_op jit(solution)/shard_map/ppermute | solution.py:23
  (21 other events, 133.9 us)

commit v3 on v2

--- a/solution.py
+++ b/solution.py
@@ -627,11 +627,9 @@
     else:
         own_ref, got_ref, zero_ref, gains_ref, wu_ref, dact_ref, norm_ref, *refs = refs
     one_out, pre_out, act_out, other_out, *rest = refs
-    count = (len(rest) - 11) // 2
+    count = (len(rest) - 9) // 2
     turned_out, turned = rest[:count], rest[count : 2 * count]
-    zero_buf, one_ref, weights, grads, pre_ref, act_ref, normed_ref, hold, into, out_of, zero_sem = rest[2 * count :]
-    zero_load = pltpu.make_async_copy(zero_ref, zero_buf, zero_sem)
-    zero_load.start()
+    one_ref, weights, grads, pre_ref, act_ref, normed_ref, hold, into, out_of = rest[2 * count :]
     chunks, _, block = grads.shape
     per_half = chunks // 2
     loads, stores = [], []
@@ -643,6 +641,8 @@
                 pltpu.make_async_copy(dact_ref.at[:, span], grads.at[c], into.at[2 * c + 1]),
             )
         )
+        for copy in loads[-1]:
+            copy.start()
 
     def store(source, target):
         stores.append(pltpu.make_async_copy(source, target, out_of.at[len(stores)]))
@@ -654,15 +654,10 @@
         mixed_out[...] = mixed[me]
         for copy in wo_loads:
             copy.wait()
-    zero_load.wait()
-    for pair in loads:
-        for copy in pair:
-            copy.start()
-    if sources:
         branch = nn(mixed[0], wo_buf[0]) + nn(mixed[1], wo_buf[1])
     else:
         branch = own_ref[...].astype(F32) + got_ref[...].astype(F32)
-    hidden = zero_buf[...] + branch
+    hidden = zero_ref[...] + branch
     one_ref[...] = hidden
     store(one_ref, one_out)
     unit, _ = norm_parts(hidden)
@@ -903,7 +898,9 @@
     columns = hold_b.shape[2]
     split_dp(ids_ref, hold_b, send_b, left_b, columns)
     hold_o[...] = plus(oh_keep, oh_got)
-    split_near(ids_ref, hold_o, send_o, left_o, hold_o.shape[2])
+    for out, at in ((send_o, 1 - ids_ref[3]), (left_o, ids_ref[3])):
+        for k in range(2):
+            out[k] = hold_o[2 * at + k]
     hold_e[...] = plus(embed_own, embed_got)
     width = hold_e.shape[2]
     for out, at in ((send_b, 1 - ids_ref[1]), (left_b, ids_ref[1])):
@@ -920,15 +917,15 @@
 
 
 def merge_q_kernel(ids_ref, keep_a, got_a, keep_b, got_b, oh_keep, oh_got,
-                   send, left, pair_ref, embed_near, embed_both, hold, hold_e):
-    width = embed_near.shape[1]
+                   send, left, pair_ref, near_ref, embed_both, oh_left, hold, hold_e, hold_o):
+    width = embed_both.shape[1]
     half = pair_ref.shape[2] // 2
     first = keep_a.shape[2]
     columns = keep_b.shape[2] - half - 2 * width
     total = hold.shape[2]
     hold[:, :, 0:first] = plus(keep_a, got_a)
-    hold[:, :, first : first + columns] = plus(keep_b.at[:, :, 0:columns], got_b.at[:, :, 0:columns])
-    hold[:, :, first + columns :] = plus(oh_keep, oh_got)
+    hold[:, :, first:] = plus(keep_b.at[:, :, 0:columns], got_b.at[:, :, 0:columns])
+    hold_o[...] = plus(oh_keep, oh_got)
     for k in range(4):
         span = slice(columns + k % 2 * width, columns + (k % 2 + 1) * width)
         hold_e[k] = plus(keep_b.at[k // 2, :, span], got_b.at[k // 2, :, span])
@@ -936,7 +933,9 @@
     for out, at in ((send, 1 - far), (left, far)):
         out[:, 0:total] = hold[at]
         out[:, total:] = hold_e[2 * at + near]
-    embed_near[...] = hold_e[2 * far + 1 - near]
+    near_ref[:, 0:width] = hold_e[2 * far + 1 - near]
+    near_ref[:, width:] = hold_o[1 - near]
+    oh_left[...] = hold_o[near]
     embed_both[...] = hold_e[2 * (1 - far) + 1 - near]
     for k in range(2):
         span = slice(k * half, (k + 1) * half)
@@ -979,16 +978,17 @@
 
 def end_kernel(*refs):
     if len(refs) > 3:
-        (near_ref, both_ref, keep_ref, got_ref), refs = refs[:4], refs[4:]
+        (near_ref, both_ref, oh_ref, keep_ref, got_ref), refs = refs[:5], refs[5:]
         out_ref, head_ref, grad_ref = refs[2:]
+        embed_width = both_ref.shape[1]
         both = keep_ref[...].astype(F32) + got_ref[...].astype(F32)
         width = grad_ref.shape[2]
         for c in range(3):
             grad_ref[c] = both[:, c * width : (c + 1) * width]
-        out_ref[...] = both[:, 3 * width : 4 * width]
-        head_ref[...] = both[:, 4 * width : 4 * width + head_ref.shape[1]]
-        embed = both[:, both.shape[1] - near_ref.shape[1] :]
-        total = embed + near_ref[...].astype(F32) + both_ref[...].astype(F32)
+        total = both[:, 3 * width :] + near_ref[:, 0:embed_width].astype(F32) + both_ref[...].astype(F32)
+        both = oh_ref[...].astype(F32) + near_ref[:, embed_width:].astype(F32)
+        out_ref[...] = both[:, 0:width]
+        head_ref[...] = both[:, width : width + head_ref.shape[1]]
     else:
         total, refs = jnp.sum(refs[0][...].astype(F32), axis=0), refs[1:]
     features = refs[0].shape[1]
@@ -1153,12 +1153,12 @@
             shape((tokens, hidden_units // 2)),
             *turned_shape,
         ],
-        ids, *branches, hidden_zero, gains, w_up, d_act,
+        ids, *branches, Warm(hidden_zero), gains, w_up, d_act,
         after=[token],
         in_specs=[
             smem,
             *([*[vmem] * (len(branches) - 2), anywhere, anywhere] if paired else [vmem] * 2),
-            anywhere,
+            vmem,
             vmem,
             anywhere,
             anywhere,
@@ -1166,7 +1166,6 @@
         out_specs=[*[vmem] * (1 + paired), *[anywhere] * (4 + len(turned_shape))],
         scratch=[
             *[pltpu.VMEM(x.shape, BF) for x in turned_shape],
-            pltpu.VMEM((tokens, width), F32),
             pltpu.VMEM((tokens, width), F32),
             pltpu.VMEM((chunks, width, block), BF),
             pltpu.VMEM((chunks, tokens, block), BF),
@@ -1176,7 +1175,6 @@
             turned_hold,
             pltpu.SemaphoreType.DMA((2 * chunks,)),
             pltpu.SemaphoreType.DMA((2 + len(turned_shape) + 2 * chunks,)),
-            pltpu.SemaphoreType.DMA,
             *[
                 pltpu.VMEM((2, *w_out.shape), BF),
                 pltpu.VMEM((2, tokens, local_width), BF),
@@ -1219,7 +1217,7 @@
         "down",
         [shape((tokens, width))],
         activated, w_down,
-        after=[token],
+        after=[token, *([mixed_got] if paired else [])],
         flops=2 * tokens * width * hidden_units,
     )
 
@@ -1300,7 +1298,7 @@
             merge_ff_kernel,
             "merge_ff",
             [shape((rows, hidden_units + 4 * inner_columns))] * 2,
-            ids, keep_a, Warm(got_a), keep_b, Warm(got_b),
+            ids, keep_a, Warm(got_a), keep_b, got_b,
             after=[token],
             scratch=[pltpu.VMEM((2, rows, hidden_units), BF)],
         )
@@ -1323,7 +1321,7 @@
             grads_q_kernel,
             "grads_q",
             [first, first, second, second],
-            ids, normed_one[0], Warm(normed_got), d_qkv, Warm(swap(d_qkv, "lon", 1)),
+            ids, normed_one[0], normed_got, d_qkv, Warm(swap(d_qkv, "lon", 1)),
             after=[token],
             scratch=[pltpu.VMEM((parts, rows, 3 * local_width), BF)],
             flops=6 * tokens * width * local_width,
@@ -1382,24 +1380,34 @@
                 pltpu.VMEM(embed[0].shape, BF),
             ],
         )
-        got_a, got_b, oh_got = swap(send_a, "lon", 2), swap(send_b, "dp", 1), swap(oh_send, "lon", 2)
+        got_a, got_b, oh_got = swap(send_a, "lon", 2), swap(send_b, "dp", 1), swap(oh_send, "lon", 4)
         east = from_behind(pin(d_edge, [token]), "lon", -1)
-        total = 3 * local_width + wide
-        final, block = shape((rows, total + embed_width)), shape((rows, embed_width))
-        send, keep, pair, embed_near, embed_both, token = call(
+        final, block = shape((rows, 3 * local_width + embed_width)), shape((rows, embed_width))
+        send, keep, pair, near_send, embed_both, oh_keep, token = call(
             merge_q_kernel,
             "merge_q",
-            [final, final, shape((2, rows, 4 * inner_columns)), block, block],
+            [
+                final,
+                final,
+                shape((2, rows, 4 * inner_columns)),
+                shape((rows, embed_width + wide)),
+                block,
+                shape((rows, wide)),
+            ],
             ids, keep_a, Warm(got_a), keep_b, Warm(got_b), oh_keep, Warm(oh_got),
             after=[token, east],
-            scratch=[pltpu.VMEM((2, rows, total), BF), pltpu.VMEM((4, *block.shape), BF)],
+            scratch=[
+                pltpu.VMEM((2, rows, 3 * local_width), BF),
+                pltpu.VMEM((4, *block.shape), BF),
+                pltpu.VMEM((2, rows, wide), BF),
+            ],
         )
         pos_got = swap(pin(pos_send, [token]), "dp", 1)
         more = [up_keep, Warm(up_got), mine[0], pair, Warm(swap(pair, "lon", 1))]
         more_outs = [shape((rows, hidden_units), F32)] * 2
         more_scratch = [pltpu.VMEM((features, hidden_units // 4), BF)]
         rest = [
-            Warm(swap(embed_near, "lon", 2)), Warm(swap(embed_both, "lon", 6)),
+            Warm(swap(near_send, "lon", 2)), Warm(swap(embed_both, "lon", 6)), oh_keep,
             keep, Warm(swap(send, "lon", 4)),
         ]
         rest_outs = [
@@ -1413,7 +1421,7 @@
         functools.partial(close_kernel, columns),
         "close",
         [shape(d_fields.shape, F32), shape(pos.shape, F32), *more_outs],
-        ids, d_fields, Warm(east), pos, Warm(pos_got), *more,
+        ids, d_fields, east, pos, Warm(pos_got), *more,
         after=[token],
         scratch=more_scratch,
     )

time: 221 us -> 215 us (0.973)
  waiting for transfers between devices: 76.1 us -> 72.5 us
    ppermute x48, waiting for transfers between devices: 62.2 us -> 56.7 us  [swap(): return lax.ppermute(block, axis, route)]
    unnamed x34 -> x32, local copies, waits for them, and re-layouts: 5.13 us -> 3.19 us
  transfers between devices with their start and end apart: 52 -> 52, of which waited for: 26 -> 27; matrix products, arithmetic and copies ran while one was open for 0% -> 0% of each run, Pallas kernels for 24% -> 25%
where the time goes in v3:
time: 215 us; the launch traced here: 214 us
  Pallas kernels  82.3 us (38%)
  waiting for transfers between devices  72.5 us (34%)
  starting transfers between devices  55.4 us (26%)
  local copies, waits for them, and re-layouts  3.27 us (2%)
    pallas_call x21, Pallas kernels, call(): pl.pallas_call(with_token, grid=grid, out_shape=[*[o.value if isinstance(...  82.3 us
    ppermute x48, waiting for transfers between devices, swap(): return lax.ppermute(block, axis, route)  56.7 us
    ppermute x48, starting transfers between devices, swap(): return lax.ppermute(block, axis, route)  45.1 us
    ppermute x2, waiting for transfers between devices, from_behind(): return lax.ppermute(block, axis, route)  12.1 us
    all_to_all x1, starting transfers between devices, local(): moments = lax.all_to_all(moments, ('dp', 'lon'), 0, 0)  5.92 us
  transfers between devices with their start and end apart: 52, of which 27 were waited for; matrix products, arithmetic and copies ran while one was open for 0% of the time, Pallas kernels for 25%

profile of v3, /device:TPU:0, one launch (start us, length us, event | category | flops | bytes accessed | tf_op | source)
XLA Modules:
  0.0 214.2 jit_solution(5117813692824736438)
XLA Ops:
  0.6 3.0 %collective-permute-start.9 = (bf16[512,1024]{1,0:T(8,128)(2,1)}, bf16[512,1024]{1,0:T(8,128)(2,1)S(1)}, u32[]{:S(2)}, u32[]{:S(2)}) collective-permute-start(bf16[512,1024]{1,0:T(8,128)(2,1)} %refs_6_.1), channel_id=1, source_target_pairs={{0,1},{1,0},{2,3},{3,2},{4,5},{5,4},{6,7},{7,6},{8,9},{9,8},{10,11... | collective-permute-start | bytes 3145736 | tf_op jit(solution)/shard_map/ppermute | solution.py:23
  4.3 2.4 %moments.1 = (f32[2,192,128]{2,1,0:T(8,128)S(1)}, bf16[2,48,128]{2,1,0:T(8,128)(2,1)S(1)}, f32[16,8,128]{2,1,0:T(8,128)}, f32[8,128]{1,0:T(8,128)}) custom-call(s32[2]{0:T(128)S(1)} %copy-done.11, f32[12,192,128]{2,1,0:T(8,128)} %bitcast.31), custom_call_target="tpu_custom_call" | custom-call | bytes 1466376 | tf_op jit(solution)/shard_map/moments/pallas_call | solution.py:138
  6.7 5.9 %all-to-all-start = ((f32[16,8,128]{2,1,0:T(8,128)}), f32[16,8,128]{2,1,0:T(8,128)S(1)}, u32[]{:S(2)}, u32[]{:S(2)}) async-start(f32[16,8,128]{2,1,0:T(8,128)} %get-tuple-element.134), calls=%async_computation | async-start | bytes 131072 | tf_op jit(solution)/shard_map/all_to_all | solution.py:1060
  13.1 5.5 %collective-permute-done.refs_6_ = bf16[2,48,128]{2,1,0:T(8,128)(2,1)S(1)} collective-permute-done((bf16[2,48,128]{2,1,0:T(8,128)(2,1)S(1)}, bf16[2,48,128]{2,1,0:T(8,128)(2,1)S(1)}, u32[]{:S(2)}, u32[]{:S(2)}) %collective-permute-start) | collective-permute-done | bytes 24608 | tf_op jit(solution)/shard_map/ppermute | solution.py:29
  19.8 5.7 %start.1 = (f32[1,48]{1,0:T(1,128)}, f32[1,48]{1,0:T(1,128)}, f32[1,48]{1,0:T(1,128)}, f32[256,1024]{1,0:T(8,128)}, bf16[192,256]{1,0:T(8,128)(2,1)}, /*index=5*...) custom-call(s32[10]{0:T(128)S(1)} %stack.43.refs_0_, ...), custom_call_target="tpu_custom_call" | custom-call | flops 905969664 | bytes 6554792 | tf_op jit(solution)/shard_map/start/pallas_call | solution.py:138
  26.5 3.4 %collective-permute-start.3 = (bf16[2,3,128,128]{3,2,1,0:T(8,128)(2,1)}, bf16[2,3,128,128]{3,2,1,0:T(8,128)(2,1)S(1)}, u32[]{:S(2)}, u32[]{:S(2)}) collective-permute-start(bf16[2,3,128,128]{3,2,1,0:T(8,128)(2,1)} %get-tuple-element.140), channel_id=1, source_target_pairs={{0,12},{2,14},{4,8},{6,10},{8,4},{10,6},{12,0},{14,2},{1,13},{3,15... | collective-permute-start | bytes 589832 | tf_op jit(solution)/shard_map/ppermute | solution.py:23
  29.9 5.2 %collective-permute-done.1.refs_1_ = bf16[2,3,128,128]{3,2,1,0:T(8,128)(2,1)S(1)} collective-permute-done((bf16[2,3,128,128]{3,2,1,0:T(8,128)(2,1)}, bf16[2,3,128,128]{3,2,1,0:T(8,128)(2,1)S(1)}, u32[]{:S(2)}, u32[]{:S(2)}) %collective-permute-start.1) | collective-permute-done | bytes 196640 | tf_op jit(solution)/shard_map/ppermute | solution.py:23
  35.2 7.8 %collective-permute-done.2.refs_2_ = bf16[2,3,128,128]{3,2,1,0:T(8,128)(2,1)S(1)} collective-permute-done((bf16[2,3,128,128]{3,2,1,0:T(8,128)(2,1)}, bf16[2,3,128,128]{3,2,1,0:T(8,128)(2,1)S(1)}, u32[]{:S(2)}, u32[]{:S(2)}) %collective-permute-start.2) | collective-permute-done | bytes 196640 | tf_op jit(solution)/shard_map/ppermute | solution.py:23
  46.0 7.4 %attend.1 = (bf16[2,128,128]{2,1,0:T(8,128)(2,1)}, bf16[2,128,128]{2,1,0:T(8,128)(2,1)}, bf16[2,128,128]{2,1,0:T(8,128)(2,1)}, bf16[2,128,128]{2,1,0:T(8,128)(2,...) custom-call(bf16[2,3,128,128]{3,2,1,0:T(8,128)(2,1)} %get-tuple-elem, ...), custom_call_target="tpu_custom_call" | custom-call | flops 1073741824 | bytes 7864320 | tf_op jit(solution)/shard_map/attend/pallas_call | solution.py:138
  53.4 3.4 %collective-permute-start.10 = (bf16[2,128,128]{2,1,0:T(8,128)(2,1)}, bf16[2,128,128]{2,1,0:T(8,128)(2,1)S(1)}, u32[]{:S(2)}, u32[]{:S(2)}) collective-permute-start(bf16[2,128,128]{2,1,0:T(8,128)(2,1)} %get-tuple-element.146), channel_id=1, source_target_pairs={{0,4},{2,6},{4,0},{6,2},{8,12},{10,14},{12,8},{14,10},{1,5},{3,7},... | collective-permute-start | bytes 196616 | tf_op jit(solution)/shard_map/ppermute | solution.py:23
  57.0 2.3 %collective-permute-start.12 = (bf16[2,128,128]{2,1,0:T(8,128)(2,1)}, bf16[2,128,128]{2,1,0:T(8,128)(2,1)S(1)}, u32[]{:S(2)}, u32[]{:S(2)}) collective-permute-start(bf16[2,128,128]{2,1,0:T(8,128)(2,1)} %get-tuple-element.148), channel_id=1, source_target_pairs={{0,12},{2,14},{4,8},{6,10},{8,4},{10,6},{12,0},{14,2},{1,13},{3,15... | collective-permute-start | bytes 196616 | tf_op jit(solution)/shard_map/ppermute | solution.py:23
  59.3 4.9 %cotangent.1 = (f32[256,1024]{1,0:T(8,128)}, bf16[256,2048]{1,0:T(8,128)(2,1)}, bf16[192,256]{1,0:T(8,128)(2,1)}, bf16[64,192]{1,0:T(8,128)(2,1)}, f32[8,128]{1,0:T(8,128)}) custom-call(s32[10]{0:T(128)S(1)} %stack.43.refs_0_, f32[2,192,128]{2,1,0:T(8,128)} %bitcast.33, bf16[192,1024]{1,0:T(8,128)(2,1)} %bitcast.29, bf16[2048,1024]{1,0:T(8,128)(2,1)} %refs_1_.1, ...), custom_call_target="tpu_custom_call" | custom-call | flops 1174405120 | bytes 7004200 | tf_op jit(solution)/shard_map/cotangent/pallas_call | solution.py:138
  64.7 1.5 collective-permute-start.14
  66.8 1.5 collective-permute-start.16
  72.3 8.4 %forward.1 = (bf16[256,1024]{1,0:T(8,128)(2,1)S(1)}, bf16[256,512]{1,0:T(8,128)(2,1)}, f32[256,1024]{1,0:T(8,128)}, bf16[256,2048]{1,0:T(8,128)(2,1)}, bf16[2,25...) custom-call(s32[10]{0:T(128)S(1)} %stack.43.refs_0_, ...), custom_call_target="tpu_custom_call" | custom-call | flops 2147483648 | bytes 13901864 | tf_op jit(solution)/shard_map/forward/pallas_call | solution.py:138
  82.4 1.7 collective-permute-done.19.refs_6_.refs_8_
  85.0 4.7 %grads_ff.1 = (bf16[4,64,1280]{2,1,0:T(8,128)(2,1)}, bf16[4,64,1280]{2,1,0:T(8,128)(2,1)}, bf16[4,64,1152]{2,1,0:T(8,128)(2,1)}, bf16[4,64,1152]{2,1,0:T(8,128)(2,1)}, f32[8,128]{1,0:T(8,128)}) custom-call(s32[10]{0:T(128)S(1)} %stack.43.refs_0_, bf16[8,64,256]{2,1,0:T(8,128)(2,1)} %get-tuple-element.153.refs_1_, ...), custom_call_target="tpu_custom_call" | custom-call | flops 1275068416 | bytes 6881320 | tf_op jit(solution)/shard_map/grads_ff/pallas_call | solution.py:138
  92.0 4.6 %down.1 = (bf16[256,1024]{1,0:T(8,128)(2,1)}, f32[8,128]{1,0:T(8,128)}) custom-call(bf16[2,256,1024]{2,1,0:T(8,128)(2,1)} %get-tuple-element.152.refs_7_.refs_0_, bf16[2048,1024]{1,0:T(8,128)(2,1)} %refs_1_.1, f32[8,128]{1,0:T(8,128)} %get-tuple-element.159.refs_2_, bf16[256,512]{1,0:T(8,128)(2,1)} %copy-done.8), custom_call_target="tpu_custom_call" | custom-call | flops 1073741824 | bytes 5767168 | tf_op jit(solution)/shard_map/down/pallas_call | solution.py:138
  96.6 3.0 %second.1 = (f32[256,1024]{1,0:T(8,128)}, f32[1,1024]{1,0:T(1,128)}, bf16[8,128,128]{2,1,0:T(8,128)(2,1)}, bf16[8,64,256]{2,1,0:T(8,128)(2,1)}, bf16[8,64,256]{2,1,0:T(8,128)(2,1)}, /*index=5*/f32[8,128]{1,0:T(8,128)}) custom-call(s32[10]{0:T(128)S(1)} %stack.43.refs_0_, f32[256,1024]{1,0:T(8,128)S(1)} %copy-done.2, f32[256,1024]{1,0:T(8,128)S(1)} %copy-done.7, ...), custom_call_target="tpu_custom_call" | custom-call | flops 268435456 | bytes 6041640 | tf_op jit(solution)/shard_map/second/pallas_call | solution.py:138
  99.6 3.6 %all-to-all-start.1 = ((bf16[4,2,128,128]{3,2,1,0:T(8,128)(2,1)}), bf16[4,2,128,128]{3,2,1,0:T(8,128)(2,1)S(1)}, u32[]{:S(2)}, u32[]{:S(2)}) async-start(bf16[4,2,128,128]{3,2,1,0:T(8,128)(2,1)} %bitcast.32), calls=%async_computation.1 | async-start | bytes 524288 | tf_op jit(solution)/shard_map/all_to_all | solution.py:1244
  104.1 2.0 collective-permute-done.25.refs_4_
  106.7 2.6 %fold_ff.1 = (bf16[2,64,1664]{2,1,0:T(8,128)(2,1)}, bf16[2,64,1664]{2,1,0:T(8,128)(2,1)}, bf16[2,64,1152]{2,1,0:T(8,128)(2,1)}, bf16[2,64,1152]{2,1,0:T(8,128)(2,1)}, f32[8,128]{1,0:T(8,128)}) custom-call(s32[10]{0:T(128)S(1)} %stack.43.refs_0_, bf16[4,64,1280]{2,1,0:T(8,128)(2,1)} %get-tuple-element.171.refs_1_, ...), custom_call_target="tpu_custom_call" | custom-call | bytes 3932200 | tf_op jit(solution)/shard_map/fold_ff/pallas_call | solution.py:138
  109.3 2.6 %all-to-all-done.1.refs_6_.refs_2_ = bf16[4,2,128,128]{3,2,1,0:T(8,128)(2,1)S(1)} async-done(((bf16[4,2,128,128]{3,2,1,0:T(8,128)(2,1)}), bf16[4,2,128,128]{3,2,1,0:T(8,128)(2,1)S(1)}, u32[]{:S(2)}, u32[]{:S(2)}) %all-to-all-start.1) | async-done | bytes 262176 | tf_op jit(solution)/shard_map/all_to_all | solution.py:1244
  114.0 7.3 %attend_back.1 = (bf16[2,3,128,128]{3,2,1,0:T(8,128)(2,1)}, bf16[2,3,128,128]{3,2,1,0:T(8,128)(2,1)}, bf16[2,3,128,128]{3,2,1,0:T(8,128)(2,1)}, bf16[2,3,128,128...) custom-call(s32[10]{0:T(128)S(1)} %stack.43.refs_0_, ...), custom_call_target="tpu_custom_call" | custom-call | flops 2147483648 | bytes 7602216 | tf_op jit(solution)/shard_map/attend_back/pallas_call | solution.py:138
  122.8 2.1 collective-permute-done.28.refs_4_
  124.9 2.1 combine.1
  128.4 3.0 %collective-permute-start.31 = (bf16[2,3,128,128]{3,2,1,0:T(8,128)(2,1)}, bf16[2,3,128,128]{3,2,1,0:T(8,128)(2,1)S(1)}, u32[]{:S(2)}, u32[]{:S(2)}) collective-permute-start(bf16[2,3,128,128]{3,2,1,0:T(8,128)(2,1)} %get-tuple-element.196), channel_id=1, source_target_pairs={{0,12},{2,14},{4,8},{6,10},{8,4},{10,6},{12,0},{14,2},{1,13},{3,15... | collective-permute-start | bytes 589832 | tf_op jit(solution)/shard_map/ppermute | solution.py:23
  131.5 2.8 %head.1 = (f32[2,192,128]{2,1,0:T(8,128)}, bf16[8,64,256]{2,1,0:T(8,128)(2,1)}, bf16[8,64,256]{2,1,0:T(8,128)(2,1)}, f32[8,128]{1,0:T(8,128)}) custom-call(s32[10]{0:T(128)S(1)} %stack.43.refs_0_, f32[256,1024]{1,0:T(8,128)} %get-tuple-element.151.refs_1_, bf16[256,1024]{1,0:T(8,128)(2,1)} %get-tuple-element.161.refs_2_, ...), custom_call_target="tpu_custom_call" | custom-call | flops 100663296 | bytes 3211304 | tf_op jit(solution)/shard_map/head/pallas_call | solution.py:138
  134.3 2.5 %merge_ff.1 = (bf16[64,3584]{1,0:T(8,128)(2,1)}, bf16[64,3584]{1,0:T(8,128)(2,1)}, f32[8,128]{1,0:T(8,128)}) custom-call(s32[10]{0:T(128)S(1)} %stack.43.refs_0_, bf16[2,64,1664]{2,1,0:T(8,128)(2,1)} %get-tuple-element.197.refs_1_, bf16[2,64,1664]{2,1,0:T(8,128)(2,1)} %collective-permute-done.26.refs_1_.refs_2_, ...), custom_call_target="tpu_custom_call" | custom-call | bytes 2359336 | tf_op jit(solution)/shard_map/merge_ff/pallas_call | solution.py:138
  137.6 7.3 %collective-permute-done.30.refs_3_ = bf16[2,3,128,128]{3,2,1,0:T(8,128)(2,1)S(1)} collective-permute-done((bf16[2,3,128,128]{3,2,1,0:T(8,128)(2,1)}, bf16[2,3,128,128]{3,2,1,0:T(8,128)(2,1)S(1)}, u32[]{:S(2)}, u32[]{:S(2)}) %collective-permute-start.30) | collective-permute-done | bytes 196640 | tf_op jit(solution)/shard_map/ppermute | solution.py:23
  144.9 3.1 %third.1 = (bf16[256,1536]{1,0:T(8,128)(2,1)}, bf16[256,1024]{1,0:T(8,128)(2,1)}, f32[8,128]{1,0:T(8,128)}) custom-call(s32[10]{0:T(128)S(1)} %stack.43.refs_0_, bf16[2,3,128,128]{3,2,1,0:T(8,128)(2,1)} %get-tuple-element.193.refs_1_, bf16[2,3,128,128]{3,2,1,0:T(8,128)(2,1)S(1)} %collective-permute-done.29.refs_2_, ...), custom_call_target="tpu_custom_call" | custom-call | flops 805306368 | bytes 5242920 | tf_op jit(solution)/shard_map/third/pallas_call | solution.py:138
  149.4 4.3 %collective-permute-start.38 = (bf16[64,3584]{1,0:T(8,128)(2,1)}, bf16[64,3584]{1,0:T(8,128)(2,1)S(1)}, u32[]{:S(2)}, u32[]{:S(2)}) collective-permute-start(bf16[64,3584]{1,0:T(8,128)(2,1)} %get-tuple-element.222), channel_id=1, source_target_pairs={{0,8},{2,10},{4,12},{6,14},{8,0},{10,2},{12,4},{14,6},{1,9},{3,11}... | collective-permute-start | bytes 1376264 | tf_op jit(solution)/shard_map/ppermute | solution.py:23
  153.7 3.7 %grads_q.1 = (bf16[4,64,896]{2,1,0:T(8,128)(2,1)}, bf16[4,64,896]{2,1,0:T(8,128)(2,1)}, bf16[4,64,640]{2,1,0:T(8,128)(2,1)}, bf16[4,64,640]{2,1,0:T(8,128)(2,1)}, f32[8,128]{1,0:T(8,128)}) custom-call(s32[10]{0:T(128)S(1)} %stack.43.refs_0_, bf16[8,64,256]{2,1,0:T(8,128)(2,1)} %get-tuple-element.211.refs_1_, bf16[8,64,256]{2,1,0:T(8,128)(2,1)} %copy-done.15, ...), custom_call_target="tpu_custom_call" | custom-call | flops 805306368 | bytes 3670056 | tf_op jit(solution)/shard_map/grads_q/pallas_call | solution.py:138
  158.7 2.7 %grads_oh.1 = (bf16[4,64,768]{2,1,0:T(8,128)(2,1)}, bf16[4,64,768]{2,1,0:T(8,128)(2,1)}, f32[8,128]{1,0:T(8,128)}) custom-call(s32[10]{0:T(128)S(1)} %stack.43.refs_0_, bf16[8,64,256]{2,1,0:T(8,128)(2,1)} %get-tuple-element.204.refs_1_, bf16[8,64,256]{2,1,0:T(8,128)(2,1)} %collective-permute-done.33.refs_2_, bf16[256,512]{1,0:T(8,128)(2,1)} %get-tuple-element.160.refs_3_, ...), custom_call_target="tpu_custom_call" | custom-call | flops 402653184 | bytes 2555944 | tf_op jit(solution)/shard_map/grads_oh/pallas_call | solution.py:138
  162.8 4.0 %last.1 = (bf16[128,512]{1,0:T(8,128)(2,1)}, bf16[128,512]{1,0:T(8,128)(2,1)}, f32[2,192,128]{2,1,0:T(8,128)}, bf16[2,48,128]{2,1,0:T(8,128)(2,1)}, bf16[8,64,25...) custom-call(s32[10]{0:T(128)S(1)} %stack.43.refs_0_, f32[256,1024]{1,0:T(8,128)S(1)} %copy-done.4, ...), custom_call_target="tpu_custom_call" | custom-call | flops 201326592 | bytes 4657192 | tf_op jit(solution)/shard_map/last/pallas_call | solution.py:138
  166.9 7.8 %collective-permute-done.38.refs_6_ = bf16[64,3584]{1,0:T(8,128)(2,1)S(1)} collective-permute-done((bf16[64,3584]{1,0:T(8,128)(2,1)}, bf16[64,3584]{1,0:T(8,128)(2,1)S(1)}, u32[]{:S(2)}, u32[]{:S(2)}) %collective-permute-start.38) | collective-permute-done | bytes 458784 | tf_op jit(solution)/shard_map/ppermute | solution.py:23
  174.7 4.9 %collective-permute-done.37.refs_4_ = bf16[4,64,640]{2,1,0:T(8,128)(2,1)S(1)} collective-permute-done((bf16[4,64,640]{2,1,0:T(8,128)(2,1)}, bf16[4,64,640]{2,1,0:T(8,128)(2,1)S(1)}, u32[]{:S(2)}, u32[]{:S(2)}) %collective-permute-start.37) | collective-permute-done | bytes 327712 | tf_op jit(solution)/shard_map/ppermute | solution.py:23
  179.6 3.1 %fold_q.1 = (bf16[2,64,896]{2,1,0:T(8,128)(2,1)}, bf16[2,64,896]{2,1,0:T(8,128)(2,1)}, bf16[2,64,1920]{2,1,0:T(8,128)(2,1)}, bf16[2,64,1920]{2,1,0:T(8,128)(2,1)...) custom-call(s32[10]{0:T(128)S(1)} %stack.43.refs_0_, ...), custom_call_target="tpu_custom_call" | custom-call | bytes 5636136 | tf_op jit(solution)/shard_map/fold_q/pallas_call | solution.py:138
  184.1 1.5 collective-permute-start.44
  185.9 6.6 %collective-permute-done.41.refs_8_.refs_2_ = bf16[2,48,128]{2,1,0:T(8,128)(2,1)S(1)} collective-permute-done((bf16[2,48,128]{2,1,0:T(8,128)(2,1)}, bf16[2,48,128]{2,1,0:T(8,128)(2,1)S(1)}, u32[]{:S(2)}, u32[]{:S(2)}) %collective-permute-start.41) | collective-permute-done | bytes 24608 | tf_op jit(solution)/shard_map/ppermute | solution.py:29
  192.6 2.4 %collective-permute-done.44.refs_6_ = bf16[2,64,768]{2,1,0:T(8,128)(2,1)S(1)} collective-permute-done((bf16[2,64,768]{2,1,0:T(8,128)(2,1)}, bf16[2,64,768]{2,1,0:T(8,128)(2,1)S(1)}, u32[]{:S(2)}, u32[]{:S(2)}) %collective-permute-start.44) | collective-permute-done | bytes 196640 | tf_op jit(solution)/shard_map/ppermute | solution.py:23
  195.0 2.4 %merge_q.1 = (bf16[64,1792]{1,0:T(8,128)(2,1)}, bf16[64,1792]{1,0:T(8,128)(2,1)}, bf16[2,64,1536]{2,1,0:T(8,128)(2,1)}, bf16[64,1024]{1,0:T(8,128)(2,1)}, bf16[6...) custom-call(s32[10]{0:T(128)S(1)} %stack.43.refs_0_, ...), custom_call_target="tpu_custom_call" | custom-call | bytes 2949160 | tf_op jit(solution)/shard_map/merge_q/pallas_call | solution.py:138
  199.4 1.5 collective-permute-start.47
  200.9 2.0 collective-permute-start.48
  204.0 2.8 %close.1 = (f32[2,192,128]{2,1,0:T(8,128)}, f32[128,512]{1,0:T(8,128)}, f32[64,2048]{1,0:T(8,128)}, f32[64,2048]{1,0:T(8,128)}, f32[8,128]{1,0:T(8,128)}) custom-call(s32[10]{0:T(128)S(1)} %stack.43.refs_0_, f32[2,192,128]{2,1,0:T(8,128)} %get-tuple-element.215.refs_1_, bf16[2,48,128]{2,1,0:T(8,128)(2,1)} %copy-done.13, ...), custom_call_target="tpu_custom_call" | custom-call | bytes 3719208 | tf_op jit(solution)/shard_map/close/pallas_call | solution.py:138
  206.7 3.6 %collective-permute-done.48.refs_1_ = bf16[64,256]{1,0:T(8,128)(2,1)S(1)} collective-permute-done((bf16[64,256]{1,0:T(8,128)(2,1)}, bf16[64,256]{1,0:T(8,128)(2,1)S(1)}, u32[]{:S(2)}, u32[]{:S(2)}) %collective-permute-start.48) | collective-permute-done | bytes 32800 | tf_op jit(solution)/shard_map/ppermute | solution.py:23
  210.3 2.1 collective-permute-done.49.refs_4_
  212.4 1.9 end.1
  (116 shorter events, 32.4 us)
Async XLA Ops:
  0.6 44.3 %collective-permute-start.9 = (bf16[512,1024]{1,0:T(8,128)(2,1)}, bf16[512,1024]{1,0:T(8,128)(2,1)S(1)}, u32[]{:S(2)}, u32[]{:S(2)}) collective-permute-start(bf16[512,1024]{1,0:T(8,128)(2,1)} %refs_6_.1), channel_id=1, source_target_pairs={{0,1},{1,0},{2,3},{3,2},{4,5},{5,4},{6,7},{7,6},{8,9},{9,8},{10,11... | collective-permute-start | bytes 3145736 | tf_op jit(solution)/shard_map/ppermute | solution.py:23
  6.7 13.1 %all-to-all-start = ((f32[16,8,128]{2,1,0:T(8,128)}), f32[16,8,128]{2,1,0:T(8,128)S(1)}, u32[]{:S(2)}, u32[]{:S(2)}) async-start(f32[16,8,128]{2,1,0:T(8,128)} %get-tuple-element.134), calls=%async_computation | async-start | bytes 131072 | tf_op jit(solution)/shard_map/all_to_all | solution.py:1060
  12.6 6.0 %collective-permute-start = (bf16[2,48,128]{2,1,0:T(8,128)(2,1)S(1)}, bf16[2,48,128]{2,1,0:T(8,128)(2,1)S(1)}, u32[]{:S(2)}, u32[]{:S(2)}) collective-permute-start(bf16[2,48,128]{2,1,0:T(8,128)(2,1)S(1)} %get-tuple-element.136), channel_id=1, source_target_pairs={{14,0},{0,2},{2,4},{4,6},{6,8},{8,10},{10,12},{12,14},{15,1},{1,3}... | collective-permute-start | bytes 73736 | tf_op jit(solution)/shard_map/ppermute | solution.py:29
  25.5 9.7 %collective-permute-start.1 = (bf16[2,3,128,128]{3,2,1,0:T(8,128)(2,1)}, bf16[2,3,128,128]{3,2,1,0:T(8,128)(2,1)S(1)}, u32[]{:S(2)}, u32[]{:S(2)}) collective-permute-start(bf16[2,3,128,128]{3,2,1,0:T(8,128)(2,1)} %get-tuple-element.138), channel_id=1, source_target_pairs={{0,4},{2,6},{4,0},{6,2},{8,12},{10,14},{12,8},{14,10},{1,5},{3,7},... | collective-permute-start | bytes 589832 | tf_op jit(solution)/shard_map/ppermute | solution.py:23
  25.6 17.4 %collective-permute-start.2 = (bf16[2,3,128,128]{3,2,1,0:T(8,128)(2,1)}, bf16[2,3,128,128]{3,2,1,0:T(8,128)(2,1)S(1)}, u32[]{:S(2)}, u32[]{:S(2)}) collective-permute-start(bf16[2,3,128,128]{3,2,1,0:T(8,128)(2,1)} %get-tuple-element.139), channel_id=1, source_target_pairs={{0,8},{2,10},{4,12},{6,14},{8,0},{10,2},{12,4},{14,6},{1,9},{3,11}... | collective-permute-start | bytes 589832 | tf_op jit(solution)/shard_map/ppermute | solution.py:23
  26.5 16.5 %collective-permute-start.3 = (bf16[2,3,128,128]{3,2,1,0:T(8,128)(2,1)}, bf16[2,3,128,128]{3,2,1,0:T(8,128)(2,1)S(1)}, u32[]{:S(2)}, u32[]{:S(2)}) collective-permute-start(bf16[2,3,128,128]{3,2,1,0:T(8,128)(2,1)} %get-tuple-element.140), channel_id=1, source_target_pairs={{0,12},{2,14},{4,8},{6,10},{8,4},{10,6},{12,0},{14,2},{1,13},{3,15... | collective-permute-start | bytes 589832 | tf_op jit(solution)/shard_map/ppermute | solution.py:23
  29.9 13.5 %collective-permute-start.4 = (bf16[2,3,128,128]{3,2,1,0:T(8,128)(2,1)}, bf16[2,3,128,128]{3,2,1,0:T(8,128)(2,1)S(1)}, u32[]{:S(2)}, u32[]{:S(2)}) collective-permute-start(bf16[2,3,128,128]{3,2,1,0:T(8,128)(2,1)} %get-tuple-element.137.refs_0_), channel_id=1, source_target_pairs={{0,2},{2,0},{4,6},{6,4},{8,10},{10,8},{12,14},{14,12},{1,3},{3,1},... | collective-permute-start | bytes 589832 | tf_op jit(solution)/shard_map/ppermute | solution.py:23
  35.2 8.4 %collective-permute-start.8 = (bf16[8,64,256]{2,1,0:T(8,128)(2,1)}, bf16[8,64,256]{2,1,0:T(8,128)(2,1)S(1)}, u32[]{:S(2)}, u32[]{:S(2)}) collective-permute-start(bf16[8,64,256]{2,1,0:T(8,128)(2,1)} %get-tuple-element.142), channel_id=1, source_target_pairs={{0,2},{2,0},{4,6},{6,4},{8,10},{10,8},{12,14},{14,12},{1,3},{3,1},... | collective-permute-start | bytes 786440 | tf_op jit(solution)/shard_map/ppermute | solution.py:23
  53.4 11.3 %collective-permute-start.10 = (bf16[2,128,128]{2,1,0:T(8,128)(2,1)}, bf16[2,128,128]{2,1,0:T(8,128)(2,1)S(1)}, u32[]{:S(2)}, u32[]{:S(2)}) collective-permute-start(bf16[2,128,128]{2,1,0:T(8,128)(2,1)} %get-tuple-element.146), channel_id=1, source_target_pairs={{0,4},{2,6},{4,0},{6,2},{8,12},{10,14},{12,8},{14,10},{1,5},{3,7},... | collective-permute-start | bytes 196616 | tf_op jit(solution)/shard_map/ppermute | solution.py:23
  56.9 9.4 %collective-permute-start.11 = (bf16[2,128,128]{2,1,0:T(8,128)(2,1)}, bf16[2,128,128]{2,1,0:T(8,128)(2,1)S(1)}, u32[]{:S(2)}, u32[]{:S(2)}) collective-permute-start(bf16[2,128,128]{2,1,0:T(8,128)(2,1)} %get-tuple-element.147), channel_id=1, source_target_pairs={{0,8},{2,10},{4,12},{6,14},{8,0},{10,2},{12,4},{14,6},{1,9},{3,11}... | collective-permute-start | bytes 196616 | tf_op jit(solution)/shard_map/ppermute | solution.py:23
  57.0 9.8 %collective-permute-start.12 = (bf16[2,128,128]{2,1,0:T(8,128)(2,1)}, bf16[2,128,128]{2,1,0:T(8,128)(2,1)S(1)}, u32[]{:S(2)}, u32[]{:S(2)}) collective-permute-start(bf16[2,128,128]{2,1,0:T(8,128)(2,1)} %get-tuple-element.148), channel_id=1, source_target_pairs={{0,12},{2,14},{4,8},{6,10},{8,4},{10,6},{12,0},{14,2},{1,13},{3,15... | collective-permute-start | bytes 196616 | tf_op jit(solution)/shard_map/ppermute | solution.py:23
  64.2 5.2 %collective-permute-start.13 = (bf16[2,128,128]{2,1,0:T(8,128)(2,1)}, bf16[2,128,128]{2,1,0:T(8,128)(2,1)S(1)}, u32[]{:S(2)}, u32[]{:S(2)}) collective-permute-start(bf16[2,128,128]{2,1,0:T(8,128)(2,1)} %pin.6.refs_1_), channel_id=1, source_target_pairs={{0,1},{1,0},{2,3},{3,2},{4,5},{5,4},{6,7},{7,6},{8,9},{9,8},{10,11... | collective-permute-start | bytes 196616 | tf_op jit(solution)/shard_map/ppermute | solution.py:23
  64.7 6.1 %collective-permute-start.14 = (bf16[2,128,128]{2,1,0:T(8,128)(2,1)S(1)}, bf16[2,128,128]{2,1,0:T(8,128)(2,1)S(1)}, u32[]{:S(2)}, u32[]{:S(2)}) collective-permute-start(bf16[2,128,128]{2,1,0:T(8,128)(2,1)S(1)} %collective-permute-done.10.refs_2_), channel_id=1, source_target_pairs={{0,1},{1,0},{2,3},{3,2},{4,5},{5,4},{6,7},{7,6},{8,9},{9,8},{10,11... | collective-permute-start | bytes 196616 | tf_op jit(solution)/shard_map/ppermute | solution.py:23
  66.3 5.4 %collective-permute-start.15 = (bf16[2,128,128]{2,1,0:T(8,128)(2,1)S(1)}, bf16[2,128,128]{2,1,0:T(8,128)(2,1)S(1)}, u32[]{:S(2)}, u32[]{:S(2)}) collective-permute-start(bf16[2,128,128]{2,1,0:T(8,128)(2,1)S(1)} %collective-permute-done.11.refs_3_), channel_id=1, source_target_pairs={{0,1},{1,0},{2,3},{3,2},{4,5},{5,4},{6,7},{7,6},{8,9},{9,8},{10,11... | collective-permute-start | bytes 196616 | tf_op jit(solution)/shard_map/ppermute | solution.py:23
  66.8 5.5 %collective-permute-start.16 = (bf16[2,128,128]{2,1,0:T(8,128)(2,1)S(1)}, bf16[2,128,128]{2,1,0:T(8,128)(2,1)S(1)}, u32[]{:S(2)}, u32[]{:S(2)}) collective-permute-start(bf16[2,128,128]{2,1,0:T(8,128)(2,1)S(1)} %collective-permute-done.12.refs_4_), channel_id=1, source_target_pairs={{0,1},{1,0},{2,3},{3,2},{4,5},{5,4},{6,7},{7,6},{8,9},{9,8},{10,11... | collective-permute-start | bytes 196616 | tf_op jit(solution)/shard_map/ppermute | solution.py:23
  80.8 4.2 %collective-permute-start.18 = (bf16[256,2048]{1,0:T(8,128)(2,1)}, bf16[256,2048]{1,0:T(8,128)(2,1)S(1)}, u32[]{:S(2)}, u32[]{:S(2)}) collective-permute-start(bf16[256,2048]{1,0:T(8,128)(2,1)} %get-tuple-element.155.refs_3_), channel_id=1, source_target_pairs={{0,2},{2,0},{4,6},{6,4},{8,10},{10,8},{12,14},{14,12},{1,3},{3,1},... | collective-permute-start | bytes 3145736 | tf_op jit(solution)/shard_map/ppermute | solution.py:23
  80.8 4.1 %collective-permute-start.20 = (bf16[256,1024]{1,0:T(8,128)(2,1)}, bf16[256,1024]{1,0:T(8,128)(2,1)S(1)}, u32[]{:S(2)}, u32[]{:S(2)}) collective-permute-start(bf16[256,1024]{1,0:T(8,128)(2,1)} %get-tuple-element.157), channel_id=1, source_target_pairs={{0,2},{2,0},{4,6},{6,4},{8,10},{10,8},{12,14},{14,12},{1,3},{3,1},... | collective-permute-start | bytes 1572872 | tf_op jit(solution)/shard_map/ppermute | solution.py:23
  81.3 3.6 %collective-permute-start.17 = (bf16[8,64,256]{2,1,0:T(8,128)(2,1)}, bf16[8,64,256]{2,1,0:T(8,128)(2,1)S(1)}, u32[]{:S(2)}, u32[]{:S(2)}) collective-permute-start(bf16[8,64,256]{2,1,0:T(8,128)(2,1)} %get-tuple-element.154), channel_id=1, source_target_pairs={{0,2},{2,0},{4,6},{6,4},{8,10},{10,8},{12,14},{14,12},{1,3},{3,1},... | collective-permute-start | bytes 786440 | tf_op jit(solution)/shard_map/ppermute | solution.py:23
  81.4 15.1 %collective-permute-start.23 = (bf16[256,1024]{1,0:T(8,128)(2,1)S(1)}, bf16[256,1024]{1,0:T(8,128)(2,1)S(1)}, u32[]{:S(2)}, u32[]{:S(2)}) collective-permute-start(bf16[256,1024]{1,0:T(8,128)(2,1)S(1)} %get-tuple-element.168.refs_3_), channel_id=1, source_target_pairs={{0,1},{1,0},{2,3},{3,2},{4,5},{5,4},{6,7},{7,6},{8,9},{9,8},{10,11... | collective-permute-start | bytes 1572872 | tf_op jit(solution)/shard_map/ppermute | solution.py:23
  84.2 7.1 %collective-permute-start.21 = (bf16[256,512]{1,0:T(8,128)(2,1)}, bf16[256,512]{1,0:T(8,128)(2,1)S(1)}, u32[]{:S(2)}, u32[]{:S(2)}) collective-permute-start(bf16[256,512]{1,0:T(8,128)(2,1)} %get-tuple-element.160.refs_3_), channel_id=1, source_target_pairs={{0,2},{2,0},{4,6},{6,4},{8,10},{10,8},{12,14},{14,12},{1,3},{3,1},... | collective-permute-start | bytes 786440 | tf_op jit(solution)/shard_map/ppermute | solution.py:23
  89.7 17.0 %collective-permute-start.24 = (bf16[4,64,1280]{2,1,0:T(8,128)(2,1)}, bf16[4,64,1280]{2,1,0:T(8,128)(2,1)S(1)}, u32[]{:S(2)}, u32[]{:S(2)}) collective-permute-start(bf16[4,64,1280]{2,1,0:T(8,128)(2,1)} %get-tuple-element.172), channel_id=1, source_target_pairs={{0,16},{16,0},{1,17},{17,1},{2,18},{18,2},{3,19},{19,3},{4,20},{20... | collective-permute-start | bytes 1966088 | tf_op jit(solution)/shard_map/ppermute | solution.py:23
  90.5 15.7 %collective-permute-start.25 = (bf16[4,64,1152]{2,1,0:T(8,128)(2,1)}, bf16[4,64,1152]{2,1,0:T(8,128)(2,1)S(1)}, u32[]{:S(2)}, u32[]{:S(2)}) collective-permute-start(bf16[4,64,1152]{2,1,0:T(8,128)(2,1)} %get-tuple-element.174), channel_id=1, source_target_pairs={{0,4},{2,6},{4,0},{6,2},{8,12},{10,14},{12,8},{14,10},{1,5},{3,7},... | collective-permute-start | bytes 1769480 | tf_op jit(solution)/shard_map/ppermute | solution.py:23
  99.6 12.3 %all-to-all-start.1 = ((bf16[4,2,128,128]{3,2,1,0:T(8,128)(2,1)}), bf16[4,2,128,128]{3,2,1,0:T(8,128)(2,1)S(1)}, u32[]{:S(2)}, u32[]{:S(2)}) async-start(bf16[4,2,128,128]{3,2,1,0:T(8,128)(2,1)} %bitcast.32), calls=%async_computation.1 | async-start | bytes 524288 | tf_op jit(solution)/shard_map/all_to_all | solution.py:1244
  103.2 18.2 %collective-permute-start.22 = (bf16[256,1024]{1,0:T(8,128)(2,1)}, bf16[256,1024]{1,0:T(8,128)(2,1)}, u32[]{:S(2)}, u32[]{:S(2)}) collective-permute-start(bf16[256,1024]{1,0:T(8,128)(2,1)} %get-tuple-element.161.refs_2_), channel_id=1, source_target_pairs={{0,1},{1,0},{2,3},{3,2},{4,5},{5,4},{6,7},{7,6},{8,9},{9,8},{10,11... | collective-permute-start | bytes 1572872 | tf_op jit(solution)/shard_map/ppermute | solution.py:23
  112.6 10.2 %collective-permute-start.26 = (bf16[2,64,1664]{2,1,0:T(8,128)(2,1)}, bf16[2,64,1664]{2,1,0:T(8,128)(2,1)}, u32[]{:S(2)}, u32[]{:S(2)}) collective-permute-start(bf16[2,64,1664]{2,1,0:T(8,128)(2,1)} %get-tuple-element.184), channel_id=1, source_target_pairs={{0,4},{2,6},{4,0},{6,2},{8,12},{10,14},{12,8},{14,10},{1,5},{3,7},... | collective-permute-start | bytes 1277960 | tf_op jit(solution)/shard_map/ppermute | solution.py:23
  112.7 8.6 %collective-permute-start.27 = (bf16[2,64,1152]{2,1,0:T(8,128)(2,1)}, bf16[2,64,1152]{2,1,0:T(8,128)(2,1)}, u32[]{:S(2)}, u32[]{:S(2)}) collective-permute-start(bf16[2,64,1152]{2,1,0:T(8,128)(2,1)} %get-tuple-element.185), channel_id=1, source_target_pairs={{0,16},{16,0},{1,17},{17,1},{2,18},{18,2},{3,19},{19,3},{4,20},{20... | collective-permute-start | bytes 884744 | tf_op jit(solution)/shard_map/ppermute | solution.py:23
  122.8 2.1 collective-permute-start.28
  127.1 10.6 %collective-permute-start.29 = (bf16[2,3,128,128]{3,2,1,0:T(8,128)(2,1)}, bf16[2,3,128,128]{3,2,1,0:T(8,128)(2,1)S(1)}, u32[]{:S(2)}, u32[]{:S(2)}) collective-permute-start(bf16[2,3,128,128]{3,2,1,0:T(8,128)(2,1)} %get-tuple-element.194), channel_id=1, source_target_pairs={{0,4},{2,6},{4,0},{6,2},{8,12},{10,14},{12,8},{14,10},{1,5},{3,7},... | collective-permute-start | bytes 589832 | tf_op jit(solution)/shard_map/ppermute | solution.py:23
  127.6 17.3 %collective-permute-start.30 = (bf16[2,3,128,128]{3,2,1,0:T(8,128)(2,1)}, bf16[2,3,128,128]{3,2,1,0:T(8,128)(2,1)S(1)}, u32[]{:S(2)}, u32[]{:S(2)}) collective-permute-start(bf16[2,3,128,128]{3,2,1,0:T(8,128)(2,1)} %get-tuple-element.195), channel_id=1, source_target_pairs={{0,8},{2,10},{4,12},{6,14},{8,0},{10,2},{12,4},{14,6},{1,9},{3,11}... | collective-permute-start | bytes 589832 | tf_op jit(solution)/shard_map/ppermute | solution.py:23
  128.4 16.5 %collective-permute-start.31 = (bf16[2,3,128,128]{3,2,1,0:T(8,128)(2,1)}, bf16[2,3,128,128]{3,2,1,0:T(8,128)(2,1)S(1)}, u32[]{:S(2)}, u32[]{:S(2)}) collective-permute-start(bf16[2,3,128,128]{3,2,1,0:T(8,128)(2,1)} %get-tuple-element.196), channel_id=1, source_target_pairs={{0,12},{2,14},{4,8},{6,10},{8,4},{10,6},{12,0},{14,2},{1,13},{3,15... | collective-permute-start | bytes 589832 | tf_op jit(solution)/shard_map/ppermute | solution.py:23
  148.0 5.7 %collective-permute-start.35 = (bf16[256,1536]{1,0:T(8,128)(2,1)}, bf16[256,1536]{1,0:T(8,128)(2,1)}, u32[]{:S(2)}, u32[]{:S(2)}) collective-permute-start(bf16[256,1536]{1,0:T(8,128)(2,1)} %get-tuple-element.212.refs_3_), channel_id=1, source_target_pairs={{0,2},{2,0},{4,6},{6,4},{8,10},{10,8},{12,14},{14,12},{1,3},{3,1},... | collective-permute-start | bytes 2359304 | tf_op jit(solution)/shard_map/ppermute | solution.py:23
  148.0 14.8 %collective-permute-start.32 = (bf16[256,1024]{1,0:T(8,128)(2,1)}, bf16[256,1024]{1,0:T(8,128)(2,1)S(1)}, u32[]{:S(2)}, u32[]{:S(2)}) collective-permute-start(bf16[256,1024]{1,0:T(8,128)(2,1)} %get-tuple-element.201.refs_3_), channel_id=1, source_target_pairs={{0,1},{1,0},{2,3},{3,2},{4,5},{5,4},{6,7},{7,6},{8,9},{9,8},{10,11... | collective-permute-start | bytes 1572872 | tf_op jit(solution)/shard_map/ppermute | solution.py:23
  148.9 9.8 %collective-permute-start.33 = (bf16[8,64,256]{2,1,0:T(8,128)(2,1)}, bf16[8,64,256]{2,1,0:T(8,128)(2,1)}, u32[]{:S(2)}, u32[]{:S(2)}) collective-permute-start(bf16[8,64,256]{2,1,0:T(8,128)(2,1)} %get-tuple-element.205), channel_id=1, source_target_pairs={{0,2},{2,0},{4,6},{6,4},{8,10},{10,8},{12,14},{14,12},{1,3},{3,1},... | collective-permute-start | bytes 786440 | tf_op jit(solution)/shard_map/ppermute | solution.py:23
  149.1 9.6 %collective-permute-start.34 = (bf16[8,64,256]{2,1,0:T(8,128)(2,1)}, bf16[8,64,256]{2,1,0:T(8,128)(2,1)S(1)}, u32[]{:S(2)}, u32[]{:S(2)}) collective-permute-start(bf16[8,64,256]{2,1,0:T(8,128)(2,1)} %get-tuple-element.210), channel_id=1, source_target_pairs={{0,2},{2,0},{4,6},{6,4},{8,10},{10,8},{12,14},{14,12},{1,3},{3,1},... | collective-permute-start | bytes 786440 | tf_op jit(solution)/shard_map/ppermute | solution.py:23
  149.4 25.3 %collective-permute-start.38 = (bf16[64,3584]{1,0:T(8,128)(2,1)}, bf16[64,3584]{1,0:T(8,128)(2,1)S(1)}, u32[]{:S(2)}, u32[]{:S(2)}) collective-permute-start(bf16[64,3584]{1,0:T(8,128)(2,1)} %get-tuple-element.222), channel_id=1, source_target_pairs={{0,8},{2,10},{4,12},{6,14},{8,0},{10,2},{12,4},{14,6},{1,9},{3,11}... | collective-permute-start | bytes 1376264 | tf_op jit(solution)/shard_map/ppermute | solution.py:23
  157.4 22.2 %collective-permute-start.36 = (bf16[4,64,896]{2,1,0:T(8,128)(2,1)}, bf16[4,64,896]{2,1,0:T(8,128)(2,1)S(1)}, u32[]{:S(2)}, u32[]{:S(2)}) collective-permute-start(bf16[4,64,896]{2,1,0:T(8,128)(2,1)} %get-tuple-element.218), channel_id=1, source_target_pairs={{0,16},{16,0},{1,17},{17,1},{2,18},{18,2},{3,19},{19,3},{4,20},{20... | collective-permute-start | bytes 1376264 | tf_op jit(solution)/shard_map/ppermute | solution.py:23
  161.4 18.2 %collective-permute-start.39 = (bf16[4,64,768]{2,1,0:T(8,128)(2,1)}, bf16[4,64,768]{2,1,0:T(8,128)(2,1)S(1)}, u32[]{:S(2)}, u32[]{:S(2)}) collective-permute-start(bf16[4,64,768]{2,1,0:T(8,128)(2,1)} %get-tuple-element.224), channel_id=1, source_target_pairs={{0,16},{16,0},{1,17},{17,1},{2,18},{18,2},{3,19},{19,3},{4,20},{20... | collective-permute-start | bytes 1179656 | tf_op jit(solution)/shard_map/ppermute | solution.py:23
  162.2 17.4 %collective-permute-start.37 = (bf16[4,64,640]{2,1,0:T(8,128)(2,1)}, bf16[4,64,640]{2,1,0:T(8,128)(2,1)S(1)}, u32[]{:S(2)}, u32[]{:S(2)}) collective-permute-start(bf16[4,64,640]{2,1,0:T(8,128)(2,1)} %get-tuple-element.220), channel_id=1, source_target_pairs={{0,4},{2,6},{4,0},{6,2},{8,12},{10,14},{12,8},{14,10},{1,5},{3,7},... | collective-permute-start | bytes 983048 | tf_op jit(solution)/shard_map/ppermute | solution.py:23
  166.9 7.8 %collective-permute-start.40 = (bf16[8,64,256]{2,1,0:T(8,128)(2,1)}, bf16[8,64,256]{2,1,0:T(8,128)(2,1)S(1)}, u32[]{:S(2)}, u32[]{:S(2)}) collective-permute-start(bf16[8,64,256]{2,1,0:T(8,128)(2,1)} %get-tuple-element.226), channel_id=1, source_target_pairs={{0,2},{2,0},{4,6},{6,4},{8,10},{10,8},{12,14},{14,12},{1,3},{3,1},... | collective-permute-start | bytes 786440 | tf_op jit(solution)/shard_map/ppermute | solution.py:23
  182.7 12.2 %collective-permute-start.43 = (bf16[2,64,1920]{2,1,0:T(8,128)(2,1)}, bf16[2,64,1920]{2,1,0:T(8,128)(2,1)S(1)}, u32[]{:S(2)}, u32[]{:S(2)}) collective-permute-start(bf16[2,64,1920]{2,1,0:T(8,128)(2,1)} %get-tuple-element.234), channel_id=1, source_target_pairs={{0,16},{16,0},{1,17},{17,1},{2,18},{18,2},{3,19},{19,3},{4,20},{20... | collective-permute-start | bytes 1474568 | tf_op jit(solution)/shard_map/ppermute | solution.py:23
  184.1 10.8 %collective-permute-start.42 = (bf16[2,64,896]{2,1,0:T(8,128)(2,1)}, bf16[2,64,896]{2,1,0:T(8,128)(2,1)S(1)}, u32[]{:S(2)}, u32[]{:S(2)}) collective-permute-start(bf16[2,64,896]{2,1,0:T(8,128)(2,1)} %get-tuple-element.232), channel_id=1, source_target_pairs={{0,4},{2,6},{4,0},{6,2},{8,12},{10,14},{12,8},{14,10},{1,5},{3,7},... | collective-permute-start | bytes 688136 | tf_op jit(solution)/shard_map/ppermute | solution.py:23
  184.1 10.8 %collective-permute-start.44 = (bf16[2,64,768]{2,1,0:T(8,128)(2,1)}, bf16[2,64,768]{2,1,0:T(8,128)(2,1)S(1)}, u32[]{:S(2)}, u32[]{:S(2)}) collective-permute-start(bf16[2,64,768]{2,1,0:T(8,128)(2,1)} %get-tuple-element.236), channel_id=1, source_target_pairs={{0,8},{2,10},{4,12},{6,14},{8,0},{10,2},{12,4},{14,6},{1,9},{3,11}... | collective-permute-start | bytes 589832 | tf_op jit(solution)/shard_map/ppermute | solution.py:23
  185.7 6.9 %collective-permute-start.41 = (bf16[2,48,128]{2,1,0:T(8,128)(2,1)}, bf16[2,48,128]{2,1,0:T(8,128)(2,1)S(1)}, u32[]{:S(2)}, u32[]{:S(2)}) collective-permute-start(bf16[2,48,128]{2,1,0:T(8,128)(2,1)} %pin.10), channel_id=1, source_target_pairs={{2,0},{4,2},{6,4},{8,6},{10,8},{12,10},{14,12},{0,14},{3,1},{5,3},... | collective-permute-start | bytes 73736 | tf_op jit(solution)/shard_map/ppermute | solution.py:29
  197.3 6.7 %collective-permute-start.46 = (bf16[2,64,1536]{2,1,0:T(8,128)(2,1)}, bf16[2,64,1536]{2,1,0:T(8,128)(2,1)S(1)}, u32[]{:S(2)}, u32[]{:S(2)}) collective-permute-start(bf16[2,64,1536]{2,1,0:T(8,128)(2,1)} %get-tuple-element.239.refs_8_), channel_id=1, source_target_pairs={{0,2},{2,0},{4,6},{6,4},{8,10},{10,8},{12,14},{14,12},{1,3},{3,1},... | collective-permute-start | bytes 1179656 | tf_op jit(solution)/shard_map/ppermute | solution.py:23
  197.6 14.8 %collective-permute-start.49 = (bf16[64,1792]{1,0:T(8,128)(2,1)}, bf16[64,1792]{1,0:T(8,128)(2,1)S(1)}, u32[]{:S(2)}, u32[]{:S(2)}) collective-permute-start(bf16[64,1792]{1,0:T(8,128)(2,1)} %get-tuple-element.245), channel_id=1, source_target_pairs={{0,8},{2,10},{4,12},{6,14},{8,0},{10,2},{12,4},{14,6},{1,9},{3,11}... | collective-permute-start | bytes 688136 | tf_op jit(solution)/shard_map/ppermute | solution.py:23
  198.6 5.4 %collective-permute-start.45 = (bf16[128,512]{1,0:T(8,128)(2,1)}, bf16[128,512]{1,0:T(8,128)(2,1)S(1)}, u32[]{:S(2)}, u32[]{:S(2)}) collective-permute-start(bf16[128,512]{1,0:T(8,128)(2,1)} %pin.11), channel_id=1, source_target_pairs={{0,16},{16,0},{1,17},{17,1},{2,18},{18,2},{3,19},{19,3},{4,20},{20... | collective-permute-start | bytes 393224 | tf_op jit(solution)/shard_map/ppermute | solution.py:23
  199.4 11.0 %collective-permute-start.47 = (bf16[64,1024]{1,0:T(8,128)(2,1)}, bf16[64,1024]{1,0:T(8,128)(2,1)S(1)}, u32[]{:S(2)}, u32[]{:S(2)}) collective-permute-start(bf16[64,1024]{1,0:T(8,128)(2,1)} %get-tuple-element.241), channel_id=1, source_target_pairs={{0,4},{2,6},{4,0},{6,2},{8,12},{10,14},{12,8},{14,10},{1,5},{3,7},... | collective-permute-start | bytes 393224 | tf_op jit(solution)/shard_map/ppermute | solution.py:23
  200.9 9.4 %collective-permute-start.48 = (bf16[64,256]{1,0:T(8,128)(2,1)}, bf16[64,256]{1,0:T(8,128)(2,1)S(1)}, u32[]{:S(2)}, u32[]{:S(2)}) collective-permute-start(bf16[64,256]{1,0:T(8,128)(2,1)} %get-tuple-element.242), channel_id=1, source_target_pairs={{0,12},{2,14},{4,8},{6,10},{8,4},{10,6},{12,0},{14,2},{1,13},{3,15... | collective-permute-start | bytes 98312 | tf_op jit(solution)/shard_map/ppermute | solution.py:23
  (20 other events, 178.3 us)

commit v4 on v3

--- a/solution.py
+++ b/solution.py
@@ -197,11 +197,15 @@
     spread = jnp.sum(sum(jnp.square(b - mean) for b in blocks), axis=1, keepdims=True)
     turn_ref[0:variables, 0:1] = mean
     turn_ref[HDIM : HDIM + variables, 0:1] = spread
+    turn_ref[0:variables, 1:2] = spread
     turned = turn_ref[...].T
-    moments_ref[...] = jnp.broadcast_to(turned[0:1, :][None], moments_ref.shape)
-
-
-def start_kernel(local_count, ids_ref, mom_ref, count_ref, mean_ref, var_ref, fields_ref, edge_ref, we_ref,
+    if len(moments_ref.shape) == 2:
+        moments_ref[...] = turned[0 : moments_ref.shape[0], :]
+    else:
+        moments_ref[...] = jnp.broadcast_to(turned[0:1, :][None], moments_ref.shape)
+
+
+def start_kernel(local_count, members, ids_ref, mom_ref, count_ref, mean_ref, var_ref, fields_ref, edge_ref, we_ref,
                  pos_ref, gains_ref, wq_ref, new_count_ref, new_mean_ref, new_var_ref, hidden_ref, patches_ref,
                  *rest):
     (*outs, column_ref, run_ref, hold, weights, sem, qkv_ref) = rest
@@ -211,19 +215,21 @@
         messages, turned = outs[:1], outs[1:]
     copy = pltpu.make_async_copy(wq_ref, weights, sem)
     copy.start()
-    members = mom_ref.shape[0]
     items, rows, height = fields_ref.shape
     variables = edge_ref.shape[1]
     cols = rows // variables
     half = height // PATCH
-    moments = mom_ref[:, 0, :]
     run_ref[...] = jnp.zeros_like(run_ref)
     for k, ref in enumerate((count_ref, mean_ref, var_ref)):
         run_ref[k : k + 1, 0:variables] = ref[...]
     batch_count = local_count * members
-    batch_mean = jnp.sum(moments, axis=0, keepdims=True) * (1.0 / members)
-    off = moments - batch_mean
-    spread = jnp.sum(pltpu.roll(moments, HDIM, 1) + local_count * off * off, axis=0, keepdims=True)
+    if len(mom_ref.shape) == 2:
+        batch_mean, spread = mom_ref[0:1, :], mom_ref[1:2, :]
+    else:
+        moments = mom_ref[:, 0, :]
+        batch_mean = jnp.sum(moments, axis=0, keepdims=True) * (1.0 / members)
+        off = moments - batch_mean
+        spread = jnp.sum(pltpu.roll(moments, HDIM, 1) + local_count * off * off, axis=0, keepdims=True)
     run_count, run_mean, run_var = (run_ref[k : k + 1, :] for k in range(3))
     new_count = run_count + batch_count
     shift = batch_mean - run_mean
@@ -1050,18 +1056,27 @@
         [
             warm((items, variables * columns, height), F32),
             warm((items, variables, height)),
-            warm((everyone, 8, LANES), F32),
+            warm((8, LANES) if paired else (everyone, 8, LANES), F32),
         ],
         indices, data,
         in_specs=[pl.BlockSpec(memory_space=pltpu.SMEM), pl.BlockSpec(memory_space=pl.ANY)],
         scratch=[pltpu.VMEM((LANES, LANES), F32), pltpu.SemaphoreType.DMA((items,))],
     )
     edge = from_behind(edge, "lon", 1)
-    moments = lax.all_to_all(moments, ("dp", "lon"), 0, 0)
+    if paired:
+        row = lax.broadcasted_iota(jnp.int32, moments.shape, 0)
+        held = float(items * height * columns)
+        for axis, distance in (("lon", 1), ("lon", 2), ("lon", 4), ("dp", 1)):
+            got = swap(moments, axis, distance)
+            apart = jnp.square(moments[0:1] - got[0:1]) * (0.5 * held)
+            moments = jnp.where(row == 0, 0.5 * (moments + got), moments + got + apart)
+            held = 2.0 * held
+    else:
+        moments = lax.all_to_all(moments, ("dp", "lon"), 0, 0)
     wh_turned = w_head.T
 
     out = call(
-        functools.partial(start_kernel, float(items * height * columns)),
+        functools.partial(start_kernel, float(items * height * columns), everyone),
         "start",
         [
             *[shape((1, variables), F32)] * 3,
@@ -1102,7 +1117,7 @@
         wo_got, normed_got = swap(w_out, "mp", 1), swap(normed_one[1], "lon", 1)
         other = [swap(x, "lon", 1) for x in own]
     if paired:
-        attended, kept, token = pair_attend(own, other, items, scale, [token, normed_got, wo_got])
+        attended, kept, token = pair_attend(own, other, items, scale, [token, normed_got])
         attended = along(attended)
     else:
         attended, attended_t, weights_t, token = attend(sent, kv, items, scale, [token])

time: 215 us -> 212 us (0.986)
  waiting for transfers between devices: 72.5 us -> 70.2 us
    ppermute x48 -> x52, starting transfers between devices: 45.1 us -> 52.5 us  [swap(): return lax.ppermute(block, axis, route)]
    ppermute x2, waiting for transfers between devices: 12.1 us -> 6.2 us  [from_behind(): return lax.ppermute(block, axis, route)]
    all_to_all x1 -> x0, starting transfers between devices: 5.92 us -> none  [local(): moments = lax.all_to_all(moments, ('dp', 'lon'), 0, 0)]
    ppermute x48 -> x52, waiting for transfers between devices: 56.7 us -> 60.9 us  [swap(): return lax.ppermute(block, axis, route)]
  transfers between devices with their start and end apart: 52 -> 55, of which waited for: 27 -> 28; matrix products, arithmetic and copies ran while one was open for 0% -> 0% of each run, Pallas kernels for 25% -> 28%
where the time goes in v4:
time: 212 us
  Pallas kernels  81.9 us (39%)
  waiting for transfers between devices  70.2 us (33%)
  starting transfers between devices  56.1 us (26%)
  local copies, waits for them, and re-layouts  2.17 us (1%)
    pallas_call x21, Pallas kernels, call(): pl.pallas_call(with_token, grid=grid, out_shape=[*[o.value if isinstance(...  81.9 us
    ppermute x52, waiting for transfers between devices, swap(): return lax.ppermute(block, axis, route)  60.9 us
    ppermute x52, starting transfers between devices, swap(): return lax.ppermute(block, axis, route)  52.5 us
    ppermute x2, waiting for transfers between devices, from_behind(): return lax.ppermute(block, axis, route)  6.2 us
  transfers between devices with their start and end apart: 55, of which 28 were waited for; matrix products, arithmetic and copies ran while one was open for 0% of the time, Pallas kernels for 28%

profile of v4, /device:TPU:0, one launch (start us, length us, event | category | flops | bytes accessed | tf_op | source)
XLA Modules:
  0.0 211.6 jit_solution(9406654239721987483)
XLA Ops:
  1.3 2.1 moments.1
  4.8 2.9 %collective-permute-start.1 = (f32[8,128]{1,0:T(8,128)S(1)}, f32[8,128]{1,0:T(8,128)S(1)}, u32[]{:S(2)}, u32[]{:S(2)}) collective-permute-start(f32[8,128]{1,0:T(8,128)S(1)} %add_select_fusion.3), channel_id=1, source_target_pairs={{0,4},{2,6},{4,0},{6,2},{8,12},{10,14},{12,8},{14,10},{1,5},{3,7},... | collective-permute-start | bytes 12296 | tf_op jit(solution)/shard_map/ppermute | solution.py:23
  7.7 1.6 collective-permute-done.1
  9.4 3.0 %collective-permute-start.2 = (f32[8,128]{1,0:T(8,128)S(1)}, f32[8,128]{1,0:T(8,128)S(1)}, u32[]{:S(2)}, u32[]{:S(2)}) collective-permute-start(f32[8,128]{1,0:T(8,128)S(1)} %add_select_fusion.2), channel_id=1, source_target_pairs={{0,8},{2,10},{4,12},{6,14},{8,0},{10,2},{12,4},{14,6},{1,9},{3,11}... | collective-permute-start | bytes 12296 | tf_op jit(solution)/shard_map/ppermute | solution.py:23
  14.1 1.8 collective-permute-start.3
  16.0 1.7 collective-permute-done.3
  17.8 5.6 %start.1 = (f32[1,48]{1,0:T(1,128)}, f32[1,48]{1,0:T(1,128)}, f32[1,48]{1,0:T(1,128)}, f32[256,1024]{1,0:T(8,128)}, bf16[192,256]{1,0:T(8,128)(2,1)}, /*index=5*...) custom-call(s32[10]{0:T(128)S(1)} %stack.43.refs_0_, ...), custom_call_target="tpu_custom_call" | custom-call | flops 905969664 | bytes 6493352 | tf_op jit(solution)/shard_map/start/pallas_call | solution.py:138
  23.4 3.0 %collective-permute-start.6 = (bf16[2,3,128,128]{3,2,1,0:T(8,128)(2,1)}, bf16[2,3,128,128]{3,2,1,0:T(8,128)(2,1)S(1)}, u32[]{:S(2)}, u32[]{:S(2)}) collective-permute-start(bf16[2,3,128,128]{3,2,1,0:T(8,128)(2,1)} %get-tuple-element.139), channel_id=1, source_target_pairs={{0,8},{2,10},{4,12},{6,14},{8,0},{10,2},{12,4},{14,6},{1,9},{3,11}... | collective-permute-start | bytes 589832 | tf_op jit(solution)/shard_map/ppermute | solution.py:23
  28.0 12.0 %collective-permute-done.6.refs_2_ = bf16[2,3,128,128]{3,2,1,0:T(8,128)(2,1)S(1)} collective-permute-done((bf16[2,3,128,128]{3,2,1,0:T(8,128)(2,1)}, bf16[2,3,128,128]{3,2,1,0:T(8,128)(2,1)S(1)}, u32[]{:S(2)}, u32[]{:S(2)}) %collective-permute-start.6) | collective-permute-done | bytes 196640 | tf_op jit(solution)/shard_map/ppermute | solution.py:23
  43.1 7.4 %attend.1 = (bf16[2,128,128]{2,1,0:T(8,128)(2,1)}, bf16[2,128,128]{2,1,0:T(8,128)(2,1)}, bf16[2,128,128]{2,1,0:T(8,128)(2,1)}, bf16[2,128,128]{2,1,0:T(8,128)(2,...) custom-call(bf16[2,3,128,128]{3,2,1,0:T(8,128)(2,1)} %get-tuple-elem, ...), custom_call_target="tpu_custom_call" | custom-call | flops 1073741824 | bytes 7864320 | tf_op jit(solution)/shard_map/attend/pallas_call | solution.py:138
  50.5 3.7 %collective-permute-start.13 = (bf16[2,128,128]{2,1,0:T(8,128)(2,1)}, bf16[2,128,128]{2,1,0:T(8,128)(2,1)S(1)}, u32[]{:S(2)}, u32[]{:S(2)}) collective-permute-start(bf16[2,128,128]{2,1,0:T(8,128)(2,1)} %get-tuple-element.146), channel_id=1, source_target_pairs={{0,4},{2,6},{4,0},{6,2},{8,12},{10,14},{12,8},{14,10},{1,5},{3,7},... | collective-permute-start | bytes 196616 | tf_op jit(solution)/shard_map/ppermute | solution.py:23
  54.5 2.2 %collective-permute-start.15 = (bf16[2,128,128]{2,1,0:T(8,128)(2,1)}, bf16[2,128,128]{2,1,0:T(8,128)(2,1)S(1)}, u32[]{:S(2)}, u32[]{:S(2)}) collective-permute-start(bf16[2,128,128]{2,1,0:T(8,128)(2,1)} %get-tuple-element.148), channel_id=1, source_target_pairs={{0,12},{2,14},{4,8},{6,10},{8,4},{10,6},{12,0},{14,2},{1,13},{3,15... | collective-permute-start | bytes 196616 | tf_op jit(solution)/shard_map/ppermute | solution.py:23
  56.6 4.9 %cotangent.1 = (f32[256,1024]{1,0:T(8,128)}, bf16[256,2048]{1,0:T(8,128)(2,1)}, bf16[192,256]{1,0:T(8,128)(2,1)}, bf16[64,192]{1,0:T(8,128)(2,1)}, f32[8,128]{1,0:T(8,128)}) custom-call(s32[10]{0:T(128)S(1)} %stack.43.refs_0_, f32[2,192,128]{2,1,0:T(8,128)} %bitcast.41, bf16[192,1024]{1,0:T(8,128)(2,1)} %bitcast.37, bf16[2048,1024]{1,0:T(8,128)(2,1)} %refs_1_.1, ...), custom_call_target="tpu_custom_call" | custom-call | flops 1174405120 | bytes 7004200 | tf_op jit(solution)/shard_map/cotangent/pallas_call | solution.py:138
  69.6 8.4 %forward.1 = (bf16[256,1024]{1,0:T(8,128)(2,1)S(1)}, bf16[256,512]{1,0:T(8,128)(2,1)}, f32[256,1024]{1,0:T(8,128)}, bf16[256,2048]{1,0:T(8,128)(2,1)}, bf16[2,25...) custom-call(s32[10]{0:T(128)S(1)} %stack.43.refs_0_, ...), custom_call_target="tpu_custom_call" | custom-call | flops 2147483648 | bytes 13901864 | tf_op jit(solution)/shard_map/forward/pallas_call | solution.py:138
  79.7 1.7 collective-permute-done.23.refs_6_.refs_8_
  82.3 4.7 %grads_ff.1 = (bf16[4,64,1280]{2,1,0:T(8,128)(2,1)}, bf16[4,64,1280]{2,1,0:T(8,128)(2,1)}, bf16[4,64,1152]{2,1,0:T(8,128)(2,1)}, bf16[4,64,1152]{2,1,0:T(8,128)(2,1)}, f32[8,128]{1,0:T(8,128)}) custom-call(s32[10]{0:T(128)S(1)} %stack.43.refs_0_, bf16[8,64,256]{2,1,0:T(8,128)(2,1)} %get-tuple-element.153.refs_1_, ...), custom_call_target="tpu_custom_call" | custom-call | flops 1275068416 | bytes 6881320 | tf_op jit(solution)/shard_map/grads_ff/pallas_call | solution.py:138
  90.0 4.6 %down.1 = (bf16[256,1024]{1,0:T(8,128)(2,1)}, f32[8,128]{1,0:T(8,128)}) custom-call(bf16[2,256,1024]{2,1,0:T(8,128)(2,1)} %get-tuple-element.152.refs_7_.refs_0_, bf16[2048,1024]{1,0:T(8,128)(2,1)} %refs_1_.1, f32[8,128]{1,0:T(8,128)} %get-tuple-element.159.refs_2_, bf16[256,512]{1,0:T(8,128)(2,1)} %copy-done.6), custom_call_target="tpu_custom_call" | custom-call | flops 1073741824 | bytes 5767168 | tf_op jit(solution)/shard_map/down/pallas_call | solution.py:138
  94.6 3.0 %second.1 = (f32[256,1024]{1,0:T(8,128)}, f32[1,1024]{1,0:T(1,128)}, bf16[8,128,128]{2,1,0:T(8,128)(2,1)}, bf16[8,64,256]{2,1,0:T(8,128)(2,1)}, bf16[8,64,256]{2,1,0:T(8,128)(2,1)}, /*index=5*/f32[8,128]{1,0:T(8,128)}) custom-call(s32[10]{0:T(128)S(1)} %stack.43.refs_0_, f32[256,1024]{1,0:T(8,128)S(1)} %copy-done.2, f32[256,1024]{1,0:T(8,128)S(1)} %copy-done.5, ...), custom_call_target="tpu_custom_call" | custom-call | flops 268435456 | bytes 6041640 | tf_op jit(solution)/shard_map/second/pallas_call | solution.py:138
  97.5 3.6 %all-to-all-start = ((bf16[4,2,128,128]{3,2,1,0:T(8,128)(2,1)}), bf16[4,2,128,128]{3,2,1,0:T(8,128)(2,1)S(1)}, u32[]{:S(2)}, u32[]{:S(2)}) async-start(bf16[4,2,128,128]{3,2,1,0:T(8,128)(2,1)} %bitcast.40), calls=%async_computation | async-start | bytes 524288 | tf_op jit(solution)/shard_map/all_to_all | solution.py:1259
  102.1 2.1 collective-permute-done.29.refs_4_
  104.2 2.6 %fold_ff.1 = (bf16[2,64,1664]{2,1,0:T(8,128)(2,1)}, bf16[2,64,1664]{2,1,0:T(8,128)(2,1)}, bf16[2,64,1152]{2,1,0:T(8,128)(2,1)}, bf16[2,64,1152]{2,1,0:T(8,128)(2,1)}, f32[8,128]{1,0:T(8,128)}) custom-call(s32[10]{0:T(128)S(1)} %stack.43.refs_0_, bf16[4,64,1280]{2,1,0:T(8,128)(2,1)} %get-tuple-element.171.refs_1_, ...), custom_call_target="tpu_custom_call" | custom-call | bytes 3932200 | tf_op jit(solution)/shard_map/fold_ff/pallas_call | solution.py:138
  106.8 3.1 %all-to-all-done.refs_6_.refs_2_ = bf16[4,2,128,128]{3,2,1,0:T(8,128)(2,1)S(1)} async-done(((bf16[4,2,128,128]{3,2,1,0:T(8,128)(2,1)}), bf16[4,2,128,128]{3,2,1,0:T(8,128)(2,1)S(1)}, u32[]{:S(2)}, u32[]{:S(2)}) %all-to-all-start) | async-done | bytes 262176 | tf_op jit(solution)/shard_map/all_to_all | solution.py:1259
  111.3 7.3 %attend_back.1 = (bf16[2,3,128,128]{3,2,1,0:T(8,128)(2,1)}, bf16[2,3,128,128]{3,2,1,0:T(8,128)(2,1)}, bf16[2,3,128,128]{3,2,1,0:T(8,128)(2,1)}, bf16[2,3,128,128...) custom-call(s32[10]{0:T(128)S(1)} %stack.43.refs_0_, ...), custom_call_target="tpu_custom_call" | custom-call | flops 2147483648 | bytes 7602216 | tf_op jit(solution)/shard_map/attend_back/pallas_call | solution.py:138
  118.6 2.2 %collective-permute-done.30.refs_1_.refs_2_ = bf16[2,64,1664]{2,1,0:T(8,128)(2,1)} collective-permute-done((bf16[2,64,1664]{2,1,0:T(8,128)(2,1)}, bf16[2,64,1664]{2,1,0:T(8,128)(2,1)}, u32[]{:S(2)}, u32[]{:S(2)}) %collective-permute-start.30) | collective-permute-done | bytes 426016 | tf_op jit(solution)/shard_map/ppermute | solution.py:23
  120.8 2.1 %collective-permute-done.32.refs_4_ = bf16[4,2,2,128,128]{4,3,2,1,0:T(8,128)(2,1)S(1)} collective-permute-done((bf16[4,2,2,128,128]{4,3,2,1,0:T(8,128)(2,1)}, bf16[4,2,2,128,128]{4,3,2,1,0:T(8,128)(2,1)S(1)}, u32[]{:S(2)}, u32[]{:S(2)}) %collective-permute-start.32) | collective-permute-done | bytes 524320 | tf_op jit(solution)/shard_map/ppermute | solution.py:23
  123.0 2.2 %combine.1 = (bf16[2,3,128,128]{3,2,1,0:T(8,128)(2,1)}, bf16[2,3,128,128]{3,2,1,0:T(8,128)(2,1)}, bf16[2,3,128,128]{3,2,1,0:T(8,128)(2,1)}, bf16[2,3,128,128]{3,2,1,0:T(8,128)(2,1)}, f32[8,128]{1,0:T(8,128)}) custom-call(bf16[2,3,128,128]{3,2,1,0:T(8,128)(2,1)} %get-tuple-element.177.refs_0_, bf16[2,3,128,128]{3,2,1,0:T(8,128)(2,1)} %get-tuple-element.178.refs_1_, ...), custom_call_target="tpu_custom_call" | custom-call | bytes 2097152 | tf_op jit(solution)/shard_map/combine/pallas_call | solution.py:138
  126.5 3.0 %collective-permute-start.35 = (bf16[2,3,128,128]{3,2,1,0:T(8,128)(2,1)}, bf16[2,3,128,128]{3,2,1,0:T(8,128)(2,1)S(1)}, u32[]{:S(2)}, u32[]{:S(2)}) collective-permute-start(bf16[2,3,128,128]{3,2,1,0:T(8,128)(2,1)} %get-tuple-element.196), channel_id=1, source_target_pairs={{0,12},{2,14},{4,8},{6,10},{8,4},{10,6},{12,0},{14,2},{1,13},{3,15... | collective-permute-start | bytes 589832 | tf_op jit(solution)/shard_map/ppermute | solution.py:23
  129.5 2.8 %head.1 = (f32[2,192,128]{2,1,0:T(8,128)}, bf16[8,64,256]{2,1,0:T(8,128)(2,1)}, bf16[8,64,256]{2,1,0:T(8,128)(2,1)}, f32[8,128]{1,0:T(8,128)}) custom-call(s32[10]{0:T(128)S(1)} %stack.43.refs_0_, f32[256,1024]{1,0:T(8,128)} %get-tuple-element.151.refs_1_, bf16[256,1024]{1,0:T(8,128)(2,1)} %get-tuple-element.161.refs_2_, ...), custom_call_target="tpu_custom_call" | custom-call | flops 100663296 | bytes 3211304 | tf_op jit(solution)/shard_map/head/pallas_call | solution.py:138
  132.3 2.5 %merge_ff.1 = (bf16[64,3584]{1,0:T(8,128)(2,1)}, bf16[64,3584]{1,0:T(8,128)(2,1)}, f32[8,128]{1,0:T(8,128)}) custom-call(s32[10]{0:T(128)S(1)} %stack.43.refs_0_, bf16[2,64,1664]{2,1,0:T(8,128)(2,1)} %get-tuple-element.197.refs_1_, bf16[2,64,1664]{2,1,0:T(8,128)(2,1)} %collective-permute-done.30.refs_1_.refs_2_, ...), custom_call_target="tpu_custom_call" | custom-call | bytes 2359336 | tf_op jit(solution)/shard_map/merge_ff/pallas_call | solution.py:138
  135.8 7.0 %collective-permute-done.34.refs_3_ = bf16[2,3,128,128]{3,2,1,0:T(8,128)(2,1)S(1)} collective-permute-done((bf16[2,3,128,128]{3,2,1,0:T(8,128)(2,1)}, bf16[2,3,128,128]{3,2,1,0:T(8,128)(2,1)S(1)}, u32[]{:S(2)}, u32[]{:S(2)}) %collective-permute-start.34) | collective-permute-done | bytes 196640 | tf_op jit(solution)/shard_map/ppermute | solution.py:23
  142.8 3.1 %third.1 = (bf16[256,1536]{1,0:T(8,128)(2,1)}, bf16[256,1024]{1,0:T(8,128)(2,1)}, f32[8,128]{1,0:T(8,128)}) custom-call(s32[10]{0:T(128)S(1)} %stack.43.refs_0_, bf16[2,3,128,128]{3,2,1,0:T(8,128)(2,1)} %get-tuple-element.193.refs_1_, bf16[2,3,128,128]{3,2,1,0:T(8,128)(2,1)S(1)} %collective-permute-done.33.refs_2_, ...), custom_call_target="tpu_custom_call" | custom-call | flops 805306368 | bytes 5242920 | tf_op jit(solution)/shard_map/third/pallas_call | solution.py:138
  147.2 4.5 %collective-permute-start.42 = (bf16[64,3584]{1,0:T(8,128)(2,1)}, bf16[64,3584]{1,0:T(8,128)(2,1)S(1)}, u32[]{:S(2)}, u32[]{:S(2)}) collective-permute-start(bf16[64,3584]{1,0:T(8,128)(2,1)} %get-tuple-element.222), channel_id=1, source_target_pairs={{0,8},{2,10},{4,12},{6,14},{8,0},{10,2},{12,4},{14,6},{1,9},{3,11}... | collective-permute-start | bytes 1376264 | tf_op jit(solution)/shard_map/ppermute | solution.py:23
  151.7 3.7 %grads_q.1 = (bf16[4,64,896]{2,1,0:T(8,128)(2,1)}, bf16[4,64,896]{2,1,0:T(8,128)(2,1)}, bf16[4,64,640]{2,1,0:T(8,128)(2,1)}, bf16[4,64,640]{2,1,0:T(8,128)(2,1)}, f32[8,128]{1,0:T(8,128)}) custom-call(s32[10]{0:T(128)S(1)} %stack.43.refs_0_, bf16[8,64,256]{2,1,0:T(8,128)(2,1)} %get-tuple-element.211.refs_1_, bf16[8,64,256]{2,1,0:T(8,128)(2,1)} %copy-done.13, ...), custom_call_target="tpu_custom_call" | custom-call | flops 805306368 | bytes 3670056 | tf_op jit(solution)/shard_map/grads_q/pallas_call | solution.py:138
  156.0 2.7 %grads_oh.1 = (bf16[4,64,768]{2,1,0:T(8,128)(2,1)}, bf16[4,64,768]{2,1,0:T(8,128)(2,1)}, f32[8,128]{1,0:T(8,128)}) custom-call(s32[10]{0:T(128)S(1)} %stack.43.refs_0_, bf16[8,64,256]{2,1,0:T(8,128)(2,1)} %get-tuple-element.204.refs_1_, bf16[8,64,256]{2,1,0:T(8,128)(2,1)} %collective-permute-done.37.refs_2_, bf16[256,512]{1,0:T(8,128)(2,1)} %get-tuple-element.160.refs_3_, ...), custom_call_target="tpu_custom_call" | custom-call | flops 402653184 | bytes 2555944 | tf_op jit(solution)/shard_map/grads_oh/pallas_call | solution.py:138
  160.7 4.0 %last.1 = (bf16[128,512]{1,0:T(8,128)(2,1)}, bf16[128,512]{1,0:T(8,128)(2,1)}, f32[2,192,128]{2,1,0:T(8,128)}, bf16[2,48,128]{2,1,0:T(8,128)(2,1)}, bf16[8,64,25...) custom-call(s32[10]{0:T(128)S(1)} %stack.43.refs_0_, f32[256,1024]{1,0:T(8,128)S(1)} %copy-done.4, ...), custom_call_target="tpu_custom_call" | custom-call | flops 201326592 | bytes 4657192 | tf_op jit(solution)/shard_map/last/pallas_call | solution.py:138
  164.7 8.0 %collective-permute-done.42.refs_6_ = bf16[64,3584]{1,0:T(8,128)(2,1)S(1)} collective-permute-done((bf16[64,3584]{1,0:T(8,128)(2,1)}, bf16[64,3584]{1,0:T(8,128)(2,1)S(1)}, u32[]{:S(2)}, u32[]{:S(2)}) %collective-permute-start.42) | collective-permute-done | bytes 458784 | tf_op jit(solution)/shard_map/ppermute | solution.py:23
  172.7 5.1 %collective-permute-done.41.refs_4_ = bf16[4,64,640]{2,1,0:T(8,128)(2,1)S(1)} collective-permute-done((bf16[4,64,640]{2,1,0:T(8,128)(2,1)}, bf16[4,64,640]{2,1,0:T(8,128)(2,1)S(1)}, u32[]{:S(2)}, u32[]{:S(2)}) %collective-permute-start.41) | collective-permute-done | bytes 327712 | tf_op jit(solution)/shard_map/ppermute | solution.py:23
  177.8 3.1 %fold_q.1 = (bf16[2,64,896]{2,1,0:T(8,128)(2,1)}, bf16[2,64,896]{2,1,0:T(8,128)(2,1)}, bf16[2,64,1920]{2,1,0:T(8,128)(2,1)}, bf16[2,64,1920]{2,1,0:T(8,128)(2,1)...) custom-call(s32[10]{0:T(128)S(1)} %stack.43.refs_0_, ...), custom_call_target="tpu_custom_call" | custom-call | bytes 5636136 | tf_op jit(solution)/shard_map/fold_q/pallas_call | solution.py:138
  181.2 2.6 %collective-permute-start.48 = (bf16[2,64,768]{2,1,0:T(8,128)(2,1)}, bf16[2,64,768]{2,1,0:T(8,128)(2,1)S(1)}, u32[]{:S(2)}, u32[]{:S(2)}) collective-permute-start(bf16[2,64,768]{2,1,0:T(8,128)(2,1)} %get-tuple-element.236), channel_id=1, source_target_pairs={{0,8},{2,10},{4,12},{6,14},{8,0},{10,2},{12,4},{14,6},{1,9},{3,11}... | collective-permute-start | bytes 589832 | tf_op jit(solution)/shard_map/ppermute | solution.py:23
  183.8 6.2 %collective-permute-done.45.refs_8_.refs_2_ = bf16[2,48,128]{2,1,0:T(8,128)(2,1)S(1)} collective-permute-done((bf16[2,48,128]{2,1,0:T(8,128)(2,1)}, bf16[2,48,128]{2,1,0:T(8,128)(2,1)S(1)}, u32[]{:S(2)}, u32[]{:S(2)}) %collective-permute-start.45) | collective-permute-done | bytes 24608 | tf_op jit(solution)/shard_map/ppermute | solution.py:29
  190.0 2.1 %collective-permute-done.48.refs_6_ = bf16[2,64,768]{2,1,0:T(8,128)(2,1)S(1)} collective-permute-done((bf16[2,64,768]{2,1,0:T(8,128)(2,1)}, bf16[2,64,768]{2,1,0:T(8,128)(2,1)S(1)}, u32[]{:S(2)}, u32[]{:S(2)}) %collective-permute-start.48) | collective-permute-done | bytes 196640 | tf_op jit(solution)/shard_map/ppermute | solution.py:23
  192.9 2.4 %merge_q.1 = (bf16[64,1792]{1,0:T(8,128)(2,1)}, bf16[64,1792]{1,0:T(8,128)(2,1)}, bf16[2,64,1536]{2,1,0:T(8,128)(2,1)}, bf16[64,1024]{1,0:T(8,128)(2,1)}, bf16[6...) custom-call(s32[10]{0:T(128)S(1)} %stack.43.refs_0_, ...), custom_call_target="tpu_custom_call" | custom-call | bytes 2949160 | tf_op jit(solution)/shard_map/merge_q/pallas_call | solution.py:138
  197.4 1.6 collective-permute-start.51
  199.0 1.8 collective-permute-start.52
  201.9 2.8 %close.1 = (f32[2,192,128]{2,1,0:T(8,128)}, f32[128,512]{1,0:T(8,128)}, f32[64,2048]{1,0:T(8,128)}, f32[64,2048]{1,0:T(8,128)}, f32[8,128]{1,0:T(8,128)}) custom-call(s32[10]{0:T(128)S(1)} %stack.43.refs_0_, f32[2,192,128]{2,1,0:T(8,128)} %get-tuple-element.215.refs_1_, bf16[2,48,128]{2,1,0:T(8,128)(2,1)} %copy-done.11, ...), custom_call_target="tpu_custom_call" | custom-call | bytes 3719208 | tf_op jit(solution)/shard_map/close/pallas_call | solution.py:138
  204.6 3.1 %collective-permute-done.52.refs_1_ = bf16[64,256]{1,0:T(8,128)(2,1)S(1)} collective-permute-done((bf16[64,256]{1,0:T(8,128)(2,1)}, bf16[64,256]{1,0:T(8,128)(2,1)S(1)}, u32[]{:S(2)}, u32[]{:S(2)}) %collective-permute-start.52) | collective-permute-done | bytes 32800 | tf_op jit(solution)/shard_map/ppermute | solution.py:23
  207.7 2.0 collective-permute-done.53.refs_4_
  209.7 1.9 end.1
  (127 shorter events, 35.1 us)
Async XLA Ops:
  4.8 4.5 %collective-permute-start.1 = (f32[8,128]{1,0:T(8,128)S(1)}, f32[8,128]{1,0:T(8,128)S(1)}, u32[]{:S(2)}, u32[]{:S(2)}) collective-permute-start(f32[8,128]{1,0:T(8,128)S(1)} %add_select_fusion.3), channel_id=1, source_target_pairs={{0,4},{2,6},{4,0},{6,2},{8,12},{10,14},{12,8},{14,10},{1,5},{3,7},... | collective-permute-start | bytes 12296 | tf_op jit(solution)/shard_map/ppermute | solution.py:23
  9.4 4.6 %collective-permute-start.2 = (f32[8,128]{1,0:T(8,128)S(1)}, f32[8,128]{1,0:T(8,128)S(1)}, u32[]{:S(2)}, u32[]{:S(2)}) collective-permute-start(f32[8,128]{1,0:T(8,128)S(1)} %add_select_fusion.2), channel_id=1, source_target_pairs={{0,8},{2,10},{4,12},{6,14},{8,0},{10,2},{12,4},{14,6},{1,9},{3,11}... | collective-permute-start | bytes 12296 | tf_op jit(solution)/shard_map/ppermute | solution.py:23
  12.4 5.4 %collective-permute-start.4 = (bf16[2,48,128]{2,1,0:T(8,128)(2,1)S(1)}, bf16[2,48,128]{2,1,0:T(8,128)(2,1)S(1)}, u32[]{:S(2)}, u32[]{:S(2)}) collective-permute-start(bf16[2,48,128]{2,1,0:T(8,128)(2,1)S(1)} %get-tuple-element.136), channel_id=1, source_target_pairs={{14,0},{0,2},{2,4},{4,6},{6,8},{8,10},{10,12},{12,14},{15,1},{1,3}... | collective-permute-start | bytes 73736 | tf_op jit(solution)/shard_map/ppermute | solution.py:29
  12.4 57.2 %collective-permute-start.20 = (bf16[512,1024]{1,0:T(8,128)(2,1)}, bf16[512,1024]{1,0:T(8,128)(2,1)S(1)}, u32[]{:S(2)}, u32[]{:S(2)}) collective-permute-start(bf16[512,1024]{1,0:T(8,128)(2,1)} %refs_6_.1), channel_id=1, source_target_pairs={{0,1},{1,0},{2,3},{3,2},{4,5},{5,4},{6,7},{7,6},{8,9},{9,8},{10,11... | collective-permute-start | bytes 3145736 | tf_op jit(solution)/shard_map/ppermute | solution.py:23
  14.1 3.6 %collective-permute-start.3 = (f32[8,128]{1,0:T(8,128)S(1)}, f32[8,128]{1,0:T(8,128)S(1)}, u32[]{:S(2)}, u32[]{:S(2)}) collective-permute-start(f32[8,128]{1,0:T(8,128)S(1)} %add_select_fusion.1), channel_id=1, source_target_pairs={{0,16},{16,0},{1,17},{17,1},{2,18},{18,2},{3,19},{19,3},{4,20},{20... | collective-permute-start | bytes 12296 | tf_op jit(solution)/shard_map/ppermute | solution.py:23
  23.4 16.6 %collective-permute-start.6 = (bf16[2,3,128,128]{3,2,1,0:T(8,128)(2,1)}, bf16[2,3,128,128]{3,2,1,0:T(8,128)(2,1)S(1)}, u32[]{:S(2)}, u32[]{:S(2)}) collective-permute-start(bf16[2,3,128,128]{3,2,1,0:T(8,128)(2,1)} %get-tuple-element.139), channel_id=1, source_target_pairs={{0,8},{2,10},{4,12},{6,14},{8,0},{10,2},{12,4},{14,6},{1,9},{3,11}... | collective-permute-start | bytes 589832 | tf_op jit(solution)/shard_map/ppermute | solution.py:23
  26.4 13.6 %collective-permute-start.7 = (bf16[2,3,128,128]{3,2,1,0:T(8,128)(2,1)}, bf16[2,3,128,128]{3,2,1,0:T(8,128)(2,1)S(1)}, u32[]{:S(2)}, u32[]{:S(2)}) collective-permute-start(bf16[2,3,128,128]{3,2,1,0:T(8,128)(2,1)} %get-tuple-element.140), channel_id=1, source_target_pairs={{0,12},{2,14},{4,8},{6,10},{8,4},{10,6},{12,0},{14,2},{1,13},{3,15... | collective-permute-start | bytes 589832 | tf_op jit(solution)/shard_map/ppermute | solution.py:23
  27.8 13.6 %collective-permute-start.5 = (bf16[2,3,128,128]{3,2,1,0:T(8,128)(2,1)}, bf16[2,3,128,128]{3,2,1,0:T(8,128)(2,1)S(1)}, u32[]{:S(2)}, u32[]{:S(2)}) collective-permute-start(bf16[2,3,128,128]{3,2,1,0:T(8,128)(2,1)} %get-tuple-element.138), channel_id=1, source_target_pairs={{0,4},{2,6},{4,0},{6,2},{8,12},{10,14},{12,8},{14,10},{1,5},{3,7},... | collective-permute-start | bytes 589832 | tf_op jit(solution)/shard_map/ppermute | solution.py:23
  28.0 13.4 %collective-permute-start.8 = (bf16[2,3,128,128]{3,2,1,0:T(8,128)(2,1)}, bf16[2,3,128,128]{3,2,1,0:T(8,128)(2,1)S(1)}, u32[]{:S(2)}, u32[]{:S(2)}) collective-permute-start(bf16[2,3,128,128]{3,2,1,0:T(8,128)(2,1)} %get-tuple-element.137.refs_0_), channel_id=1, source_target_pairs={{0,2},{2,0},{4,6},{6,4},{8,10},{10,8},{12,14},{14,12},{1,3},{3,1},... | collective-permute-start | bytes 589832 | tf_op jit(solution)/shard_map/ppermute | solution.py:23
  50.5 11.6 %collective-permute-start.13 = (bf16[2,128,128]{2,1,0:T(8,128)(2,1)}, bf16[2,128,128]{2,1,0:T(8,128)(2,1)S(1)}, u32[]{:S(2)}, u32[]{:S(2)}) collective-permute-start(bf16[2,128,128]{2,1,0:T(8,128)(2,1)} %get-tuple-element.146), channel_id=1, source_target_pairs={{0,4},{2,6},{4,0},{6,2},{8,12},{10,14},{12,8},{14,10},{1,5},{3,7},... | collective-permute-start | bytes 196616 | tf_op jit(solution)/shard_map/ppermute | solution.py:23
  54.2 9.4 %collective-permute-start.14 = (bf16[2,128,128]{2,1,0:T(8,128)(2,1)}, bf16[2,128,128]{2,1,0:T(8,128)(2,1)S(1)}, u32[]{:S(2)}, u32[]{:S(2)}) collective-permute-start(bf16[2,128,128]{2,1,0:T(8,128)(2,1)} %get-tuple-element.147), channel_id=1, source_target_pairs={{0,8},{2,10},{4,12},{6,14},{8,0},{10,2},{12,4},{14,6},{1,9},{3,11}... | collective-permute-start | bytes 196616 | tf_op jit(solution)/shard_map/ppermute | solution.py:23
  54.5 9.7 %collective-permute-start.15 = (bf16[2,128,128]{2,1,0:T(8,128)(2,1)}, bf16[2,128,128]{2,1,0:T(8,128)(2,1)S(1)}, u32[]{:S(2)}, u32[]{:S(2)}) collective-permute-start(bf16[2,128,128]{2,1,0:T(8,128)(2,1)} %get-tuple-element.148), channel_id=1, source_target_pairs={{0,12},{2,14},{4,8},{6,10},{8,4},{10,6},{12,0},{14,2},{1,13},{3,15... | collective-permute-start | bytes 196616 | tf_op jit(solution)/shard_map/ppermute | solution.py:23
  61.5 5.2 %collective-permute-start.16 = (bf16[2,128,128]{2,1,0:T(8,128)(2,1)}, bf16[2,128,128]{2,1,0:T(8,128)(2,1)S(1)}, u32[]{:S(2)}, u32[]{:S(2)}) collective-permute-start(bf16[2,128,128]{2,1,0:T(8,128)(2,1)} %pin.6.refs_1_), channel_id=1, source_target_pairs={{0,1},{1,0},{2,3},{3,2},{4,5},{5,4},{6,7},{7,6},{8,9},{9,8},{10,11... | collective-permute-start | bytes 196616 | tf_op jit(solution)/shard_map/ppermute | solution.py:23
  62.1 6.1 %collective-permute-start.17 = (bf16[2,128,128]{2,1,0:T(8,128)(2,1)S(1)}, bf16[2,128,128]{2,1,0:T(8,128)(2,1)S(1)}, u32[]{:S(2)}, u32[]{:S(2)}) collective-permute-start(bf16[2,128,128]{2,1,0:T(8,128)(2,1)S(1)} %collective-permute-done.13.refs_2_), channel_id=1, source_target_pairs={{0,1},{1,0},{2,3},{3,2},{4,5},{5,4},{6,7},{7,6},{8,9},{9,8},{10,11... | collective-permute-start | bytes 196616 | tf_op jit(solution)/shard_map/ppermute | solution.py:23
  63.6 5.4 %collective-permute-start.18 = (bf16[2,128,128]{2,1,0:T(8,128)(2,1)S(1)}, bf16[2,128,128]{2,1,0:T(8,128)(2,1)S(1)}, u32[]{:S(2)}, u32[]{:S(2)}) collective-permute-start(bf16[2,128,128]{2,1,0:T(8,128)(2,1)S(1)} %collective-permute-done.14.refs_3_), channel_id=1, source_target_pairs={{0,1},{1,0},{2,3},{3,2},{4,5},{5,4},{6,7},{7,6},{8,9},{9,8},{10,11... | collective-permute-start | bytes 196616 | tf_op jit(solution)/shard_map/ppermute | solution.py:23
  64.1 5.5 %collective-permute-start.19 = (bf16[2,128,128]{2,1,0:T(8,128)(2,1)S(1)}, bf16[2,128,128]{2,1,0:T(8,128)(2,1)S(1)}, u32[]{:S(2)}, u32[]{:S(2)}) collective-permute-start(bf16[2,128,128]{2,1,0:T(8,128)(2,1)S(1)} %collective-permute-done.15.refs_4_), channel_id=1, source_target_pairs={{0,1},{1,0},{2,3},{3,2},{4,5},{5,4},{6,7},{7,6},{8,9},{9,8},{10,11... | collective-permute-start | bytes 196616 | tf_op jit(solution)/shard_map/ppermute | solution.py:23
  78.1 4.2 %collective-permute-start.22 = (bf16[256,2048]{1,0:T(8,128)(2,1)}, bf16[256,2048]{1,0:T(8,128)(2,1)S(1)}, u32[]{:S(2)}, u32[]{:S(2)}) collective-permute-start(bf16[256,2048]{1,0:T(8,128)(2,1)} %get-tuple-element.155.refs_3_), channel_id=1, source_target_pairs={{0,2},{2,0},{4,6},{6,4},{8,10},{10,8},{12,14},{14,12},{1,3},{3,1},... | collective-permute-start | bytes 3145736 | tf_op jit(solution)/shard_map/ppermute | solution.py:23
  78.2 4.1 %collective-permute-start.24 = (bf16[256,1024]{1,0:T(8,128)(2,1)}, bf16[256,1024]{1,0:T(8,128)(2,1)S(1)}, u32[]{:S(2)}, u32[]{:S(2)}) collective-permute-start(bf16[256,1024]{1,0:T(8,128)(2,1)} %get-tuple-element.157), channel_id=1, source_target_pairs={{0,2},{2,0},{4,6},{6,4},{8,10},{10,8},{12,14},{14,12},{1,3},{3,1},... | collective-permute-start | bytes 1572872 | tf_op jit(solution)/shard_map/ppermute | solution.py:23
  78.7 3.6 %collective-permute-start.21 = (bf16[8,64,256]{2,1,0:T(8,128)(2,1)}, bf16[8,64,256]{2,1,0:T(8,128)(2,1)S(1)}, u32[]{:S(2)}, u32[]{:S(2)}) collective-permute-start(bf16[8,64,256]{2,1,0:T(8,128)(2,1)} %get-tuple-element.154), channel_id=1, source_target_pairs={{0,2},{2,0},{4,6},{6,4},{8,10},{10,8},{12,14},{14,12},{1,3},{3,1},... | collective-permute-start | bytes 786440 | tf_op jit(solution)/shard_map/ppermute | solution.py:23
  78.7 15.8 %collective-permute-start.27 = (bf16[256,1024]{1,0:T(8,128)(2,1)S(1)}, bf16[256,1024]{1,0:T(8,128)(2,1)S(1)}, u32[]{:S(2)}, u32[]{:S(2)}) collective-permute-start(bf16[256,1024]{1,0:T(8,128)(2,1)S(1)} %get-tuple-element.168.refs_3_), channel_id=1, source_target_pairs={{0,1},{1,0},{2,3},{3,2},{4,5},{5,4},{6,7},{7,6},{8,9},{9,8},{10,11... | collective-permute-start | bytes 1572872 | tf_op jit(solution)/shard_map/ppermute | solution.py:23
  81.5 7.8 %collective-permute-start.25 = (bf16[256,512]{1,0:T(8,128)(2,1)}, bf16[256,512]{1,0:T(8,128)(2,1)S(1)}, u32[]{:S(2)}, u32[]{:S(2)}) collective-permute-start(bf16[256,512]{1,0:T(8,128)(2,1)} %get-tuple-element.160.refs_3_), channel_id=1, source_target_pairs={{0,2},{2,0},{4,6},{6,4},{8,10},{10,8},{12,14},{14,12},{1,3},{3,1},... | collective-permute-start | bytes 786440 | tf_op jit(solution)/shard_map/ppermute | solution.py:23
  87.0 17.2 %collective-permute-start.28 = (bf16[4,64,1280]{2,1,0:T(8,128)(2,1)}, bf16[4,64,1280]{2,1,0:T(8,128)(2,1)S(1)}, u32[]{:S(2)}, u32[]{:S(2)}) collective-permute-start(bf16[4,64,1280]{2,1,0:T(8,128)(2,1)} %get-tuple-element.172), channel_id=1, source_target_pairs={{0,16},{16,0},{1,17},{17,1},{2,18},{18,2},{3,19},{19,3},{4,20},{20... | collective-permute-start | bytes 1966088 | tf_op jit(solution)/shard_map/ppermute | solution.py:23
  88.5 15.7 %collective-permute-start.29 = (bf16[4,64,1152]{2,1,0:T(8,128)(2,1)}, bf16[4,64,1152]{2,1,0:T(8,128)(2,1)S(1)}, u32[]{:S(2)}, u32[]{:S(2)}) collective-permute-start(bf16[4,64,1152]{2,1,0:T(8,128)(2,1)} %get-tuple-element.174), channel_id=1, source_target_pairs={{0,4},{2,6},{4,0},{6,2},{8,12},{10,14},{12,8},{14,10},{1,5},{3,7},... | collective-permute-start | bytes 1769480 | tf_op jit(solution)/shard_map/ppermute | solution.py:23
  97.5 12.3 %all-to-all-start = ((bf16[4,2,128,128]{3,2,1,0:T(8,128)(2,1)}), bf16[4,2,128,128]{3,2,1,0:T(8,128)(2,1)S(1)}, u32[]{:S(2)}, u32[]{:S(2)}) async-start(bf16[4,2,128,128]{3,2,1,0:T(8,128)(2,1)} %bitcast.40), calls=%async_computation | async-start | bytes 524288 | tf_op jit(solution)/shard_map/all_to_all | solution.py:1259
  101.2 17.4 %collective-permute-start.26 = (bf16[256,1024]{1,0:T(8,128)(2,1)}, bf16[256,1024]{1,0:T(8,128)(2,1)}, u32[]{:S(2)}, u32[]{:S(2)}) collective-permute-start(bf16[256,1024]{1,0:T(8,128)(2,1)} %get-tuple-element.161.refs_2_), channel_id=1, source_target_pairs={{0,1},{1,0},{2,3},{3,2},{4,5},{5,4},{6,7},{7,6},{8,9},{9,8},{10,11... | collective-permute-start | bytes 1572872 | tf_op jit(solution)/shard_map/ppermute | solution.py:23
  110.6 10.2 %collective-permute-start.30 = (bf16[2,64,1664]{2,1,0:T(8,128)(2,1)}, bf16[2,64,1664]{2,1,0:T(8,128)(2,1)}, u32[]{:S(2)}, u32[]{:S(2)}) collective-permute-start(bf16[2,64,1664]{2,1,0:T(8,128)(2,1)} %get-tuple-element.184), channel_id=1, source_target_pairs={{0,4},{2,6},{4,0},{6,2},{8,12},{10,14},{12,8},{14,10},{1,5},{3,7},... | collective-permute-start | bytes 1277960 | tf_op jit(solution)/shard_map/ppermute | solution.py:23
  110.7 7.9 %collective-permute-start.31 = (bf16[2,64,1152]{2,1,0:T(8,128)(2,1)}, bf16[2,64,1152]{2,1,0:T(8,128)(2,1)}, u32[]{:S(2)}, u32[]{:S(2)}) collective-permute-start(bf16[2,64,1152]{2,1,0:T(8,128)(2,1)} %get-tuple-element.185), channel_id=1, source_target_pairs={{0,16},{16,0},{1,17},{17,1},{2,18},{18,2},{3,19},{19,3},{4,20},{20... | collective-permute-start | bytes 884744 | tf_op jit(solution)/shard_map/ppermute | solution.py:23
  125.1 10.6 %collective-permute-start.33 = (bf16[2,3,128,128]{3,2,1,0:T(8,128)(2,1)}, bf16[2,3,128,128]{3,2,1,0:T(8,128)(2,1)S(1)}, u32[]{:S(2)}, u32[]{:S(2)}) collective-permute-start(bf16[2,3,128,128]{3,2,1,0:T(8,128)(2,1)} %get-tuple-element.194), channel_id=1, source_target_pairs={{0,4},{2,6},{4,0},{6,2},{8,12},{10,14},{12,8},{14,10},{1,5},{3,7},... | collective-permute-start | bytes 589832 | tf_op jit(solution)/shard_map/ppermute | solution.py:23
  125.4 17.3 %collective-permute-start.34 = (bf16[2,3,128,128]{3,2,1,0:T(8,128)(2,1)}, bf16[2,3,128,128]{3,2,1,0:T(8,128)(2,1)S(1)}, u32[]{:S(2)}, u32[]{:S(2)}) collective-permute-start(bf16[2,3,128,128]{3,2,1,0:T(8,128)(2,1)} %get-tuple-element.195), channel_id=1, source_target_pairs={{0,8},{2,10},{4,12},{6,14},{8,0},{10,2},{12,4},{14,6},{1,9},{3,11}... | collective-permute-start | bytes 589832 | tf_op jit(solution)/shard_map/ppermute | solution.py:23
  126.5 16.3 %collective-permute-start.35 = (bf16[2,3,128,128]{3,2,1,0:T(8,128)(2,1)}, bf16[2,3,128,128]{3,2,1,0:T(8,128)(2,1)S(1)}, u32[]{:S(2)}, u32[]{:S(2)}) collective-permute-start(bf16[2,3,128,128]{3,2,1,0:T(8,128)(2,1)} %get-tuple-element.196), channel_id=1, source_target_pairs={{0,12},{2,14},{4,8},{6,10},{8,4},{10,6},{12,0},{14,2},{1,13},{3,15... | collective-permute-start | bytes 589832 | tf_op jit(solution)/shard_map/ppermute | solution.py:23
  145.9 5.9 %collective-permute-start.39 = (bf16[256,1536]{1,0:T(8,128)(2,1)}, bf16[256,1536]{1,0:T(8,128)(2,1)}, u32[]{:S(2)}, u32[]{:S(2)}) collective-permute-start(bf16[256,1536]{1,0:T(8,128)(2,1)} %get-tuple-element.212.refs_3_), channel_id=1, source_target_pairs={{0,2},{2,0},{4,6},{6,4},{8,10},{10,8},{12,14},{14,12},{1,3},{3,1},... | collective-permute-start | bytes 2359304 | tf_op jit(solution)/shard_map/ppermute | solution.py:23
  145.9 14.8 %collective-permute-start.36 = (bf16[256,1024]{1,0:T(8,128)(2,1)}, bf16[256,1024]{1,0:T(8,128)(2,1)S(1)}, u32[]{:S(2)}, u32[]{:S(2)}) collective-permute-start(bf16[256,1024]{1,0:T(8,128)(2,1)} %get-tuple-element.201.refs_3_), channel_id=1, source_target_pairs={{0,1},{1,0},{2,3},{3,2},{4,5},{5,4},{6,7},{7,6},{8,9},{9,8},{10,11... | collective-permute-start | bytes 1572872 | tf_op jit(solution)/shard_map/ppermute | solution.py:23
  146.7 9.3 %collective-permute-start.37 = (bf16[8,64,256]{2,1,0:T(8,128)(2,1)}, bf16[8,64,256]{2,1,0:T(8,128)(2,1)}, u32[]{:S(2)}, u32[]{:S(2)}) collective-permute-start(bf16[8,64,256]{2,1,0:T(8,128)(2,1)} %get-tuple-element.205), channel_id=1, source_target_pairs={{0,2},{2,0},{4,6},{6,4},{8,10},{10,8},{12,14},{14,12},{1,3},{3,1},... | collective-permute-start | bytes 786440 | tf_op jit(solution)/shard_map/ppermute | solution.py:23
  146.9 9.1 %collective-permute-start.38 = (bf16[8,64,256]{2,1,0:T(8,128)(2,1)}, bf16[8,64,256]{2,1,0:T(8,128)(2,1)S(1)}, u32[]{:S(2)}, u32[]{:S(2)}) collective-permute-start(bf16[8,64,256]{2,1,0:T(8,128)(2,1)} %get-tuple-element.210), channel_id=1, source_target_pairs={{0,2},{2,0},{4,6},{6,4},{8,10},{10,8},{12,14},{14,12},{1,3},{3,1},... | collective-permute-start | bytes 786440 | tf_op jit(solution)/shard_map/ppermute | solution.py:23
  147.2 25.5 %collective-permute-start.42 = (bf16[64,3584]{1,0:T(8,128)(2,1)}, bf16[64,3584]{1,0:T(8,128)(2,1)S(1)}, u32[]{:S(2)}, u32[]{:S(2)}) collective-permute-start(bf16[64,3584]{1,0:T(8,128)(2,1)} %get-tuple-element.222), channel_id=1, source_target_pairs={{0,8},{2,10},{4,12},{6,14},{8,0},{10,2},{12,4},{14,6},{1,9},{3,11}... | collective-permute-start | bytes 1376264 | tf_op jit(solution)/shard_map/ppermute | solution.py:23
  155.4 22.3 %collective-permute-start.40 = (bf16[4,64,896]{2,1,0:T(8,128)(2,1)}, bf16[4,64,896]{2,1,0:T(8,128)(2,1)S(1)}, u32[]{:S(2)}, u32[]{:S(2)}) collective-permute-start(bf16[4,64,896]{2,1,0:T(8,128)(2,1)} %get-tuple-element.218), channel_id=1, source_target_pairs={{0,16},{16,0},{1,17},{17,1},{2,18},{18,2},{3,19},{19,3},{4,20},{20... | collective-permute-start | bytes 1376264 | tf_op jit(solution)/shard_map/ppermute | solution.py:23
  158.7 19.1 %collective-permute-start.43 = (bf16[4,64,768]{2,1,0:T(8,128)(2,1)}, bf16[4,64,768]{2,1,0:T(8,128)(2,1)S(1)}, u32[]{:S(2)}, u32[]{:S(2)}) collective-permute-start(bf16[4,64,768]{2,1,0:T(8,128)(2,1)} %get-tuple-element.224), channel_id=1, source_target_pairs={{0,16},{16,0},{1,17},{17,1},{2,18},{18,2},{3,19},{19,3},{4,20},{20... | collective-permute-start | bytes 1179656 | tf_op jit(solution)/shard_map/ppermute | solution.py:23
  160.2 17.6 %collective-permute-start.41 = (bf16[4,64,640]{2,1,0:T(8,128)(2,1)}, bf16[4,64,640]{2,1,0:T(8,128)(2,1)S(1)}, u32[]{:S(2)}, u32[]{:S(2)}) collective-permute-start(bf16[4,64,640]{2,1,0:T(8,128)(2,1)} %get-tuple-element.220), channel_id=1, source_target_pairs={{0,4},{2,6},{4,0},{6,2},{8,12},{10,14},{12,8},{14,10},{1,5},{3,7},... | collective-permute-start | bytes 983048 | tf_op jit(solution)/shard_map/ppermute | solution.py:23
  164.7 8.0 %collective-permute-start.44 = (bf16[8,64,256]{2,1,0:T(8,128)(2,1)}, bf16[8,64,256]{2,1,0:T(8,128)(2,1)S(1)}, u32[]{:S(2)}, u32[]{:S(2)}) collective-permute-start(bf16[8,64,256]{2,1,0:T(8,128)(2,1)} %get-tuple-element.226), channel_id=1, source_target_pairs={{0,2},{2,0},{4,6},{6,4},{8,10},{10,8},{12,14},{14,12},{1,3},{3,1},... | collective-permute-start | bytes 786440 | tf_op jit(solution)/shard_map/ppermute | solution.py:23
  180.9 12.0 %collective-permute-start.47 = (bf16[2,64,1920]{2,1,0:T(8,128)(2,1)}, bf16[2,64,1920]{2,1,0:T(8,128)(2,1)S(1)}, u32[]{:S(2)}, u32[]{:S(2)}) collective-permute-start(bf16[2,64,1920]{2,1,0:T(8,128)(2,1)} %get-tuple-element.234), channel_id=1, source_target_pairs={{0,16},{16,0},{1,17},{17,1},{2,18},{18,2},{3,19},{19,3},{4,20},{20... | collective-permute-start | bytes 1474568 | tf_op jit(solution)/shard_map/ppermute | solution.py:23
  181.0 11.1 %collective-permute-start.46 = (bf16[2,64,896]{2,1,0:T(8,128)(2,1)}, bf16[2,64,896]{2,1,0:T(8,128)(2,1)S(1)}, u32[]{:S(2)}, u32[]{:S(2)}) collective-permute-start(bf16[2,64,896]{2,1,0:T(8,128)(2,1)} %get-tuple-element.232), channel_id=1, source_target_pairs={{0,4},{2,6},{4,0},{6,2},{8,12},{10,14},{12,8},{14,10},{1,5},{3,7},... | collective-permute-start | bytes 688136 | tf_op jit(solution)/shard_map/ppermute | solution.py:23
  181.2 10.9 %collective-permute-start.48 = (bf16[2,64,768]{2,1,0:T(8,128)(2,1)}, bf16[2,64,768]{2,1,0:T(8,128)(2,1)S(1)}, u32[]{:S(2)}, u32[]{:S(2)}) collective-permute-start(bf16[2,64,768]{2,1,0:T(8,128)(2,1)} %get-tuple-element.236), channel_id=1, source_target_pairs={{0,8},{2,10},{4,12},{6,14},{8,0},{10,2},{12,4},{14,6},{1,9},{3,11}... | collective-permute-start | bytes 589832 | tf_op jit(solution)/shard_map/ppermute | solution.py:23
  183.8 6.2 %collective-permute-start.45 = (bf16[2,48,128]{2,1,0:T(8,128)(2,1)}, bf16[2,48,128]{2,1,0:T(8,128)(2,1)S(1)}, u32[]{:S(2)}, u32[]{:S(2)}) collective-permute-start(bf16[2,48,128]{2,1,0:T(8,128)(2,1)} %pin.10), channel_id=1, source_target_pairs={{2,0},{4,2},{6,4},{8,6},{10,8},{12,10},{14,12},{0,14},{3,1},{5,3},... | collective-permute-start | bytes 73736 | tf_op jit(solution)/shard_map/ppermute | solution.py:29
  195.3 6.6 %collective-permute-start.50 = (bf16[2,64,1536]{2,1,0:T(8,128)(2,1)}, bf16[2,64,1536]{2,1,0:T(8,128)(2,1)S(1)}, u32[]{:S(2)}, u32[]{:S(2)}) collective-permute-start(bf16[2,64,1536]{2,1,0:T(8,128)(2,1)} %get-tuple-element.239.refs_8_), channel_id=1, source_target_pairs={{0,2},{2,0},{4,6},{6,4},{8,10},{10,8},{12,14},{14,12},{1,3},{3,1},... | collective-permute-start | bytes 1179656 | tf_op jit(solution)/shard_map/ppermute | solution.py:23
  195.3 14.4 %collective-permute-start.53 = (bf16[64,1792]{1,0:T(8,128)(2,1)}, bf16[64,1792]{1,0:T(8,128)(2,1)S(1)}, u32[]{:S(2)}, u32[]{:S(2)}) collective-permute-start(bf16[64,1792]{1,0:T(8,128)(2,1)} %get-tuple-element.245), channel_id=1, source_target_pairs={{0,8},{2,10},{4,12},{6,14},{8,0},{10,2},{12,4},{14,6},{1,9},{3,11}... | collective-permute-start | bytes 688136 | tf_op jit(solution)/shard_map/ppermute | solution.py:23
  196.1 5.8 %collective-permute-start.49 = (bf16[128,512]{1,0:T(8,128)(2,1)}, bf16[128,512]{1,0:T(8,128)(2,1)S(1)}, u32[]{:S(2)}, u32[]{:S(2)}) collective-permute-start(bf16[128,512]{1,0:T(8,128)(2,1)} %pin.11), channel_id=1, source_target_pairs={{0,16},{16,0},{1,17},{17,1},{2,18},{18,2},{3,19},{19,3},{4,20},{20... | collective-permute-start | bytes 393224 | tf_op jit(solution)/shard_map/ppermute | solution.py:23
  197.4 10.3 %collective-permute-start.51 = (bf16[64,1024]{1,0:T(8,128)(2,1)}, bf16[64,1024]{1,0:T(8,128)(2,1)S(1)}, u32[]{:S(2)}, u32[]{:S(2)}) collective-permute-start(bf16[64,1024]{1,0:T(8,128)(2,1)} %get-tuple-element.241), channel_id=1, source_target_pairs={{0,4},{2,6},{4,0},{6,2},{8,12},{10,14},{12,8},{14,10},{1,5},{3,7},... | collective-permute-start | bytes 393224 | tf_op jit(solution)/shard_map/ppermute | solution.py:23
  199.0 8.7 %collective-permute-start.52 = (bf16[64,256]{1,0:T(8,128)(2,1)}, bf16[64,256]{1,0:T(8,128)(2,1)S(1)}, u32[]{:S(2)}, u32[]{:S(2)}) collective-permute-start(bf16[64,256]{1,0:T(8,128)(2,1)} %get-tuple-element.242), channel_id=1, source_target_pairs={{0,12},{2,14},{4,8},{6,10},{8,4},{10,6},{12,0},{14,2},{1,13},{3,15... | collective-permute-start | bytes 98312 | tf_op jit(solution)/shard_map/ppermute | solution.py:23
  (21 other events, 166.7 us)

commit v5 on v4

--- a/solution.py
+++ b/solution.py
@@ -394,15 +394,15 @@
         functools.partial(pair_attend_kernel, items, scale),
         "attend",
         [
-            *[shape((2, tokens, lanes))] * len(own),
+            shape((2, tokens, lanes)),
+            *[warm((2, tokens, lanes))] * (len(own) - 1),
             shape((2, lanes, rows), F32),
             shape((2, items, keys, rows)),
             shape((2, rows, lanes)),
             shape((2, keys, lanes)),
             shape((2, keys, lanes)),
         ],
-        own[0],
-        *[Warm(x) for x in [*own[1:], *other]],
+        *[Warm(x) for x in [*own, *other]],
         after=after,
         grid=(2,),
         in_specs=[wide(3, tokens, lanes)] * (2 * len(own)),
@@ -1082,7 +1082,7 @@
             *[shape((1, variables), F32)] * 3,
             shape((tokens, width), F32),
             shape((features, tokens)),
-            *([shape((2, 3, item_tokens, LANES))] * 4 if paired else [shape((heads, 3, item_tokens, LANES))]),
+            *([warm((2, 3, item_tokens, LANES))] * 4 if paired else [shape((heads, 3, item_tokens, LANES))]),
             *turned_shape,
         ],
         ids, Warm(moments), *[r.reshape(1, variables) for r in (run_count, run_mean, run_var)],
@@ -1231,7 +1231,7 @@
         down_kernel,
         "down",
         [shape((tokens, width))],
-        activated, w_down,
+        activated, Warm(w_down),
         after=[token, *([mixed_got] if paired else [])],
         flops=2 * tokens * width * hidden_units,
     )
@@ -1242,7 +1242,7 @@
         [
             shape((tokens, width), F32),
             shape((1, width), F32),
-            shape((heads, item_tokens, LANES)),
+            warm((heads, item_tokens, LANES)),
             *turned_shape,
         ],
         ids, Warm(hidden_one), Warm(d_two), Warm(d_norm), Warm(d_norm_got), gains, Warm(w_out),
@@ -1284,7 +1284,7 @@
         *back, token = call(
             combine_kernel,
             "combine",
-            [shape(x.shape) for x in back],
+            [warm(x.shape) for x in back],
             *back, Warm(swap(pin(cross, [got_a, got_b, forward_got]), "lon", 1)),
             after=[token],
         )
@@ -1321,7 +1321,7 @@
         functools.partial(third_kernel, count),
         "third",
         [shape((tokens, 3 * local_width)), warm((tokens, width))],
-        ids, back[0], *[Warm(x) for x in back[1:]], Warm(w_qkv),
+        ids, *[Warm(x) for x in back], Warm(w_qkv),
         after=[token],
         flops=6 * tokens * width * local_width,
     )

time: 212 us -> 209 us (0.986)
  Pallas kernels: 81.9 us -> 78.1 us
    pallas_call x21, Pallas kernels: 81.9 us -> 78.1 us  [call(): pl.pallas_call(with_token, grid=grid, out_shape=[*[o.value if isinstance(...]
    all_to_all x1, waiting for transfers between devices: 3.06 us -> 0.01 us  [local(): lax.all_to_all(d_mixed[0].reshape(lon // 2, 2, item_tokens, LANES), 'lon'...]
    ppermute x52, waiting for transfers between devices: 60.9 us -> 63.7 us  [swap(): return lax.ppermute(block, axis, route)]
  transfers between devices with their start and end apart: 55 -> 55, of which waited for: 28 -> 27; matrix products, arithmetic and copies ran while one was open for 0% -> 0% of each run, Pallas kernels for 28% -> 27%
where the time goes in v5:
time: 209 us; the launch traced here: 208 us
  Pallas kernels  78.1 us (37%)
  waiting for transfers between devices  70 us (33%)
  starting transfers between devices  56.5 us (27%)
  local copies, waits for them, and re-layouts  2.15 us (1%)
    pallas_call x21, Pallas kernels, call(): pl.pallas_call(with_token, grid=grid, out_shape=[*[o.value if isinstance(...  78.1 us
    ppermute x52, waiting for transfers between devices, swap(): return lax.ppermute(block, axis, route)  63.7 us
    ppermute x52, starting transfers between devices, swap(): return lax.ppermute(block, axis, route)  52.9 us
    ppermute x2, waiting for transfers between devices, from_behind(): return lax.ppermute(block, axis, route)  6.29 us
  transfers between devices with their start and end apart: 55, of which 27 were waited for; matrix products, arithmetic and copies ran while one was open for 0% of the time, Pallas kernels for 27%

profile of v5, /device:TPU:0, one launch (start us, length us, event | category | flops | bytes accessed | tf_op | source)
XLA Modules:
  0.0 208.0 jit_solution(12264550854559234594)
XLA Ops:
  1.3 2.1 %moments.1 = (f32[2,192,128]{2,1,0:T(8,128)S(1)}, bf16[2,48,128]{2,1,0:T(8,128)(2,1)S(1)}, f32[8,128]{1,0:T(8,128)S(1)}, f32[8,128]{1,0:T(8,128)}) custom-call(s32[2]{0:T(128)S(1)} %copy-done.10, f32[12,192,128]{2,1,0:T(8,128)} %bitcast.39), custom_call_target="tpu_custom_call" | custom-call | bytes 1404936 | tf_op jit(solution)/shard_map/moments/pallas_call | solution.py:138
  4.8 2.9 %collective-permute-start.1 = (f32[8,128]{1,0:T(8,128)S(1)}, f32[8,128]{1,0:T(8,128)S(1)}, u32[]{:S(2)}, u32[]{:S(2)}) collective-permute-start(f32[8,128]{1,0:T(8,128)S(1)} %add_select_fusion.3), channel_id=1, source_target_pairs={{0,4},{2,6},{4,0},{6,2},{8,12},{10,14},{12,8},{14,10},{1,5},{3,7},... | collective-permute-start | bytes 12296 | tf_op jit(solution)/shard_map/ppermute | solution.py:23
  7.7 1.6 collective-permute-done.1
  9.4 3.0 %collective-permute-start.2 = (f32[8,128]{1,0:T(8,128)S(1)}, f32[8,128]{1,0:T(8,128)S(1)}, u32[]{:S(2)}, u32[]{:S(2)}) collective-permute-start(f32[8,128]{1,0:T(8,128)S(1)} %add_select_fusion.2), channel_id=1, source_target_pairs={{0,8},{2,10},{4,12},{6,14},{8,0},{10,2},{12,4},{14,6},{1,9},{3,11}... | collective-permute-start | bytes 12296 | tf_op jit(solution)/shard_map/ppermute | solution.py:23
  12.4 1.5 collective-permute-start.20
  14.1 1.8 collective-permute-start.3
  16.0 1.7 collective-permute-done.3
  17.8 4.8 %start.1 = (f32[1,48]{1,0:T(1,128)}, f32[1,48]{1,0:T(1,128)}, f32[1,48]{1,0:T(1,128)}, f32[256,1024]{1,0:T(8,128)}, bf16[192,256]{1,0:T(8,128)(2,1)}, /*index=5*...) custom-call(s32[10]{0:T(128)S(1)} %stack.43.refs_0_, ...), custom_call_target="tpu_custom_call" | custom-call | flops 905969664 | bytes 6493352 | tf_op jit(solution)/shard_map/start/pallas_call | solution.py:138
  22.7 3.0 %collective-permute-start.6 = (bf16[2,3,128,128]{3,2,1,0:T(8,128)(2,1)S(1)}, bf16[2,3,128,128]{3,2,1,0:T(8,128)(2,1)S(1)}, u32[]{:S(2)}, u32[]{:S(2)}) collective-permute-start(bf16[2,3,128,128]{3,2,1,0:T(8,128)(2,1)S(1)} %get-tuple-element.139), channel_id=1, source_target_pairs={{0,8},{2,10},{4,12},{6,14},{8,0},{10,2},{12,4},{14,6},{1,9},{3,11}... | collective-permute-start | bytes 589832 | tf_op jit(solution)/shard_map/ppermute | solution.py:23
  27.2 11.8 %collective-permute-done.6.refs_2_ = bf16[2,3,128,128]{3,2,1,0:T(8,128)(2,1)S(1)} collective-permute-done((bf16[2,3,128,128]{3,2,1,0:T(8,128)(2,1)S(1)}, bf16[2,3,128,128]{3,2,1,0:T(8,128)(2,1)S(1)}, u32[]{:S(2)}, u32[]{:S(2)}) %collective-permute-start.6) | collective-permute-done | bytes 196640 | tf_op jit(solution)/shard_map/ppermute | solution.py:23
  42.1 6.4 %attend.1 = (bf16[2,128,128]{2,1,0:T(8,128)(2,1)}, bf16[2,128,128]{2,1,0:T(8,128)(2,1)S(1)}, bf16[2,128,128]{2,1,0:T(8,128)(2,1)S(1)}, bf16[2,128,128]{2,1,0:T(8...) custom-call(bf16[2,3,128,128]{3,2,1,0:T(8,128)(2,1)S(1)} %get-tuple-, ...), custom_call_target="tpu_custom_call" | custom-call | flops 1073741824 | bytes 7864320 | tf_op jit(solution)/shard_map/attend/pallas_call | solution.py:138
  48.5 3.7 %collective-permute-start.13 = (bf16[2,128,128]{2,1,0:T(8,128)(2,1)S(1)}, bf16[2,128,128]{2,1,0:T(8,128)(2,1)S(1)}, u32[]{:S(2)}, u32[]{:S(2)}) collective-permute-start(bf16[2,128,128]{2,1,0:T(8,128)(2,1)S(1)} %get-tuple-element.146), channel_id=1, source_target_pairs={{0,4},{2,6},{4,0},{6,2},{8,12},{10,14},{12,8},{14,10},{1,5},{3,7},... | collective-permute-start | bytes 196616 | tf_op jit(solution)/shard_map/ppermute | solution.py:23
  52.5 2.1 %collective-permute-start.15 = (bf16[2,128,128]{2,1,0:T(8,128)(2,1)S(1)}, bf16[2,128,128]{2,1,0:T(8,128)(2,1)S(1)}, u32[]{:S(2)}, u32[]{:S(2)}) collective-permute-start(bf16[2,128,128]{2,1,0:T(8,128)(2,1)S(1)} %get-tuple-element.148), channel_id=1, source_target_pairs={{0,12},{2,14},{4,8},{6,10},{8,4},{10,6},{12,0},{14,2},{1,13},{3,15... | collective-permute-start | bytes 196616 | tf_op jit(solution)/shard_map/ppermute | solution.py:23
  54.6 4.9 %cotangent.1 = (f32[256,1024]{1,0:T(8,128)}, bf16[256,2048]{1,0:T(8,128)(2,1)}, bf16[192,256]{1,0:T(8,128)(2,1)}, bf16[64,192]{1,0:T(8,128)(2,1)}, f32[8,128]{1,0:T(8,128)}) custom-call(s32[10]{0:T(128)S(1)} %stack.43.refs_0_, f32[2,192,128]{2,1,0:T(8,128)} %bitcast.40, bf16[192,1024]{1,0:T(8,128)(2,1)} %bitcast.37, bf16[2048,1024]{1,0:T(8,128)(2,1)} %refs_1_.1, ...), custom_call_target="tpu_custom_call" | custom-call | flops 1174405120 | bytes 7004200 | tf_op jit(solution)/shard_map/cotangent/pallas_call | solution.py:138
  67.6 8.5 %forward.1 = (bf16[256,1024]{1,0:T(8,128)(2,1)S(1)}, bf16[256,512]{1,0:T(8,128)(2,1)}, f32[256,1024]{1,0:T(8,128)}, bf16[256,2048]{1,0:T(8,128)(2,1)}, bf16[2,25...) custom-call(s32[10]{0:T(128)S(1)} %stack.43.refs_0_, ...), custom_call_target="tpu_custom_call" | custom-call | flops 2147483648 | bytes 13901864 | tf_op jit(solution)/shard_map/forward/pallas_call | solution.py:138
  77.8 1.7 collective-permute-done.23.refs_6_.refs_8_
  80.3 4.7 %grads_ff.1 = (bf16[4,64,1280]{2,1,0:T(8,128)(2,1)}, bf16[4,64,1280]{2,1,0:T(8,128)(2,1)}, bf16[4,64,1152]{2,1,0:T(8,128)(2,1)}, bf16[4,64,1152]{2,1,0:T(8,128)(2,1)}, f32[8,128]{1,0:T(8,128)}) custom-call(s32[10]{0:T(128)S(1)} %stack.43.refs_0_, bf16[8,64,256]{2,1,0:T(8,128)(2,1)} %get-tuple-element.153.refs_1_, ...), custom_call_target="tpu_custom_call" | custom-call | flops 1275068416 | bytes 6881320 | tf_op jit(solution)/shard_map/grads_ff/pallas_call | solution.py:138
  88.0 3.3 %down.1 = (bf16[256,1024]{1,0:T(8,128)(2,1)}, f32[8,128]{1,0:T(8,128)}) custom-call(bf16[2,256,1024]{2,1,0:T(8,128)(2,1)} %get-tuple-element.152.refs_7_.refs_0_, bf16[2048,1024]{1,0:T(8,128)(2,1)S(1)} %copy-done, f32[8,128]{1,0:T(8,128)} %get-tuple-element.159.refs_2_, bf16[256,512]{1,0:T(8,128)(2,1)} %copy-done.7), custom_call_target="tpu_custom_call" | custom-call | flops 1073741824 | bytes 5767168 | tf_op jit(solution)/shard_map/down/pallas_call | solution.py:138
  91.3 3.0 %second.1 = (f32[256,1024]{1,0:T(8,128)}, f32[1,1024]{1,0:T(1,128)}, bf16[8,128,128]{2,1,0:T(8,128)(2,1)}, bf16[8,64,256]{2,1,0:T(8,128)(2,1)}, bf16[8,64,256]{2,1,0:T(8,128)(2,1)}, /*index=5*/f32[8,128]{1,0:T(8,128)}) custom-call(s32[10]{0:T(128)S(1)} %stack.43.refs_0_, f32[256,1024]{1,0:T(8,128)S(1)} %copy-done.3, f32[256,1024]{1,0:T(8,128)S(1)} %copy-done.6, ...), custom_call_target="tpu_custom_call" | custom-call | flops 268435456 | bytes 6041640 | tf_op jit(solution)/shard_map/second/pallas_call | solution.py:138
  94.3 3.6 %all-to-all-start = ((bf16[4,2,128,128]{3,2,1,0:T(8,128)(2,1)}), bf16[4,2,128,128]{3,2,1,0:T(8,128)(2,1)S(1)}, u32[]{:S(2)}, u32[]{:S(2)}) async-start(bf16[4,2,128,128]{3,2,1,0:T(8,128)(2,1)} %bitcast.21), calls=%async_computation | async-start | bytes 524288 | tf_op jit(solution)/shard_map/all_to_all | solution.py:1259
  98.9 5.7 %collective-permute-done.29.refs_4_ = bf16[4,64,1152]{2,1,0:T(8,128)(2,1)S(1)} collective-permute-done((bf16[4,64,1152]{2,1,0:T(8,128)(2,1)}, bf16[4,64,1152]{2,1,0:T(8,128)(2,1)S(1)}, u32[]{:S(2)}, u32[]{:S(2)}) %collective-permute-start.29) | collective-permute-done | bytes 589856 | tf_op jit(solution)/shard_map/ppermute | solution.py:23
  104.5 2.6 %fold_ff.1 = (bf16[2,64,1664]{2,1,0:T(8,128)(2,1)}, bf16[2,64,1664]{2,1,0:T(8,128)(2,1)}, bf16[2,64,1152]{2,1,0:T(8,128)(2,1)}, bf16[2,64,1152]{2,1,0:T(8,128)(2,1)}, f32[8,128]{1,0:T(8,128)}) custom-call(s32[10]{0:T(128)S(1)} %stack.43.refs_0_, bf16[4,64,1280]{2,1,0:T(8,128)(2,1)} %get-tuple-element.171.refs_1_, ...), custom_call_target="tpu_custom_call" | custom-call | bytes 3932200 | tf_op jit(solution)/shard_map/fold_ff/pallas_call | solution.py:138
  108.8 7.3 %attend_back.1 = (bf16[2,3,128,128]{3,2,1,0:T(8,128)(2,1)}, bf16[2,3,128,128]{3,2,1,0:T(8,128)(2,1)}, bf16[2,3,128,128]{3,2,1,0:T(8,128)(2,1)}, bf16[2,3,128,128...) custom-call(s32[10]{0:T(128)S(1)} %stack.43.refs_0_, ...), custom_call_target="tpu_custom_call" | custom-call | flops 2147483648 | bytes 7602216 | tf_op jit(solution)/shard_map/attend_back/pallas_call | solution.py:138
  116.8 2.1 %collective-permute-done.32.refs_4_ = bf16[4,2,2,128,128]{4,3,2,1,0:T(8,128)(2,1)S(1)} collective-permute-done((bf16[4,2,2,128,128]{4,3,2,1,0:T(8,128)(2,1)}, bf16[4,2,2,128,128]{4,3,2,1,0:T(8,128)(2,1)S(1)}, u32[]{:S(2)}, u32[]{:S(2)}) %collective-permute-start.32) | collective-permute-done | bytes 524320 | tf_op jit(solution)/shard_map/ppermute | solution.py:23
  118.9 1.8 combine.1
  120.7 1.7 collective-permute-start.33
  123.3 1.7 collective-permute-start.35
  125.1 2.8 %head.1 = (f32[2,192,128]{2,1,0:T(8,128)}, bf16[8,64,256]{2,1,0:T(8,128)(2,1)}, bf16[8,64,256]{2,1,0:T(8,128)(2,1)}, f32[8,128]{1,0:T(8,128)}) custom-call(s32[10]{0:T(128)S(1)} %stack.43.refs_0_, f32[256,1024]{1,0:T(8,128)} %get-tuple-element.151.refs_1_, bf16[256,1024]{1,0:T(8,128)(2,1)} %get-tuple-element.161.refs_2_, ...), custom_call_target="tpu_custom_call" | custom-call | flops 100663296 | bytes 3211304 | tf_op jit(solution)/shard_map/head/pallas_call | solution.py:138
  127.9 2.5 %merge_ff.1 = (bf16[64,3584]{1,0:T(8,128)(2,1)}, bf16[64,3584]{1,0:T(8,128)(2,1)}, f32[8,128]{1,0:T(8,128)}) custom-call(s32[10]{0:T(128)S(1)} %stack.43.refs_0_, bf16[2,64,1664]{2,1,0:T(8,128)(2,1)} %get-tuple-element.197.refs_1_, bf16[2,64,1664]{2,1,0:T(8,128)(2,1)} %collective-permute-done.30.refs_1_.refs_2_, ...), custom_call_target="tpu_custom_call" | custom-call | bytes 2359336 | tf_op jit(solution)/shard_map/merge_ff/pallas_call | solution.py:138
  131.1 8.5 %collective-permute-done.34.refs_3_ = bf16[2,3,128,128]{3,2,1,0:T(8,128)(2,1)S(1)} collective-permute-done((bf16[2,3,128,128]{3,2,1,0:T(8,128)(2,1)S(1)}, bf16[2,3,128,128]{3,2,1,0:T(8,128)(2,1)S(1)}, u32[]{:S(2)}, u32[]{:S(2)}) %collective-permute-start.34) | collective-permute-done | bytes 196640 | tf_op jit(solution)/shard_map/ppermute | solution.py:23
  139.6 2.7 %third.1 = (bf16[256,1536]{1,0:T(8,128)(2,1)}, bf16[256,1024]{1,0:T(8,128)(2,1)}, f32[8,128]{1,0:T(8,128)}) custom-call(s32[10]{0:T(128)S(1)} %stack.43.refs_0_, bf16[2,3,128,128]{3,2,1,0:T(8,128)(2,1)S(1)} %get-tuple-element.193.refs_1_, bf16[2,3,128,128]{3,2,1,0:T(8,128)(2,1)S(1)} %collective-permute-done.33.refs_2_, ...), custom_call_target="tpu_custom_call" | custom-call | flops 805306368 | bytes 5242920 | tf_op jit(solution)/shard_map/third/pallas_call | solution.py:138
  143.7 4.3 %collective-permute-start.42 = (bf16[64,3584]{1,0:T(8,128)(2,1)}, bf16[64,3584]{1,0:T(8,128)(2,1)S(1)}, u32[]{:S(2)}, u32[]{:S(2)}) collective-permute-start(bf16[64,3584]{1,0:T(8,128)(2,1)} %get-tuple-element.222), channel_id=1, source_target_pairs={{0,8},{2,10},{4,12},{6,14},{8,0},{10,2},{12,4},{14,6},{1,9},{3,11}... | collective-permute-start | bytes 1376264 | tf_op jit(solution)/shard_map/ppermute | solution.py:23
  148.0 3.7 %grads_q.1 = (bf16[4,64,896]{2,1,0:T(8,128)(2,1)}, bf16[4,64,896]{2,1,0:T(8,128)(2,1)}, bf16[4,64,640]{2,1,0:T(8,128)(2,1)}, bf16[4,64,640]{2,1,0:T(8,128)(2,1)}, f32[8,128]{1,0:T(8,128)}) custom-call(s32[10]{0:T(128)S(1)} %stack.43.refs_0_, bf16[8,64,256]{2,1,0:T(8,128)(2,1)} %get-tuple-element.211.refs_1_, bf16[8,64,256]{2,1,0:T(8,128)(2,1)} %copy-done.14, ...), custom_call_target="tpu_custom_call" | custom-call | flops 805306368 | bytes 3670056 | tf_op jit(solution)/shard_map/grads_q/pallas_call | solution.py:138
  152.4 2.7 %grads_oh.1 = (bf16[4,64,768]{2,1,0:T(8,128)(2,1)}, bf16[4,64,768]{2,1,0:T(8,128)(2,1)}, f32[8,128]{1,0:T(8,128)}) custom-call(s32[10]{0:T(128)S(1)} %stack.43.refs_0_, bf16[8,64,256]{2,1,0:T(8,128)(2,1)} %get-tuple-element.204.refs_1_, bf16[8,64,256]{2,1,0:T(8,128)(2,1)} %collective-permute-done.37.refs_2_, bf16[256,512]{1,0:T(8,128)(2,1)} %get-tuple-element.160.refs_3_, ...), custom_call_target="tpu_custom_call" | custom-call | flops 402653184 | bytes 2555944 | tf_op jit(solution)/shard_map/grads_oh/pallas_call | solution.py:138
  157.1 4.0 %last.1 = (bf16[128,512]{1,0:T(8,128)(2,1)}, bf16[128,512]{1,0:T(8,128)(2,1)}, f32[2,192,128]{2,1,0:T(8,128)}, bf16[2,48,128]{2,1,0:T(8,128)(2,1)}, bf16[8,64,25...) custom-call(s32[10]{0:T(128)S(1)} %stack.43.refs_0_, f32[256,1024]{1,0:T(8,128)S(1)} %copy-done.5, ...), custom_call_target="tpu_custom_call" | custom-call | flops 201326592 | bytes 4657192 | tf_op jit(solution)/shard_map/last/pallas_call | solution.py:138
  161.1 7.9 %collective-permute-done.42.refs_6_ = bf16[64,3584]{1,0:T(8,128)(2,1)S(1)} collective-permute-done((bf16[64,3584]{1,0:T(8,128)(2,1)}, bf16[64,3584]{1,0:T(8,128)(2,1)S(1)}, u32[]{:S(2)}, u32[]{:S(2)}) %collective-permute-start.42) | collective-permute-done | bytes 458784 | tf_op jit(solution)/shard_map/ppermute | solution.py:23
  169.0 4.9 %collective-permute-done.41.refs_4_ = bf16[4,64,640]{2,1,0:T(8,128)(2,1)S(1)} collective-permute-done((bf16[4,64,640]{2,1,0:T(8,128)(2,1)}, bf16[4,64,640]{2,1,0:T(8,128)(2,1)S(1)}, u32[]{:S(2)}, u32[]{:S(2)}) %collective-permute-start.41) | collective-permute-done | bytes 327712 | tf_op jit(solution)/shard_map/ppermute | solution.py:23
  173.9 3.1 %fold_q.1 = (bf16[2,64,896]{2,1,0:T(8,128)(2,1)}, bf16[2,64,896]{2,1,0:T(8,128)(2,1)}, bf16[2,64,1920]{2,1,0:T(8,128)(2,1)}, bf16[2,64,1920]{2,1,0:T(8,128)(2,1)...) custom-call(s32[10]{0:T(128)S(1)} %stack.43.refs_0_, ...), custom_call_target="tpu_custom_call" | custom-call | bytes 5636136 | tf_op jit(solution)/shard_map/fold_q/pallas_call | solution.py:138
  177.5 2.4 %collective-permute-start.48 = (bf16[2,64,768]{2,1,0:T(8,128)(2,1)}, bf16[2,64,768]{2,1,0:T(8,128)(2,1)S(1)}, u32[]{:S(2)}, u32[]{:S(2)}) collective-permute-start(bf16[2,64,768]{2,1,0:T(8,128)(2,1)} %get-tuple-element.236), channel_id=1, source_target_pairs={{0,8},{2,10},{4,12},{6,14},{8,0},{10,2},{12,4},{14,6},{1,9},{3,11}... | collective-permute-start | bytes 589832 | tf_op jit(solution)/shard_map/ppermute | solution.py:23
  180.0 6.3 %collective-permute-done.45.refs_8_.refs_2_ = bf16[2,48,128]{2,1,0:T(8,128)(2,1)S(1)} collective-permute-done((bf16[2,48,128]{2,1,0:T(8,128)(2,1)}, bf16[2,48,128]{2,1,0:T(8,128)(2,1)S(1)}, u32[]{:S(2)}, u32[]{:S(2)}) %collective-permute-start.45) | collective-permute-done | bytes 24608 | tf_op jit(solution)/shard_map/ppermute | solution.py:29
  186.3 2.2 %collective-permute-done.48.refs_6_ = bf16[2,64,768]{2,1,0:T(8,128)(2,1)S(1)} collective-permute-done((bf16[2,64,768]{2,1,0:T(8,128)(2,1)}, bf16[2,64,768]{2,1,0:T(8,128)(2,1)S(1)}, u32[]{:S(2)}, u32[]{:S(2)}) %collective-permute-start.48) | collective-permute-done | bytes 196640 | tf_op jit(solution)/shard_map/ppermute | solution.py:23
  189.0 2.4 %merge_q.1 = (bf16[64,1792]{1,0:T(8,128)(2,1)}, bf16[64,1792]{1,0:T(8,128)(2,1)}, bf16[2,64,1536]{2,1,0:T(8,128)(2,1)}, bf16[64,1024]{1,0:T(8,128)(2,1)}, bf16[6...) custom-call(s32[10]{0:T(128)S(1)} %stack.43.refs_0_, ...), custom_call_target="tpu_custom_call" | custom-call | bytes 2949160 | tf_op jit(solution)/shard_map/merge_q/pallas_call | solution.py:138
  193.6 1.5 collective-permute-start.51
  195.1 1.8 collective-permute-start.52
  198.1 2.8 %close.1 = (f32[2,192,128]{2,1,0:T(8,128)}, f32[128,512]{1,0:T(8,128)}, f32[64,2048]{1,0:T(8,128)}, f32[64,2048]{1,0:T(8,128)}, f32[8,128]{1,0:T(8,128)}) custom-call(s32[10]{0:T(128)S(1)} %stack.43.refs_0_, f32[2,192,128]{2,1,0:T(8,128)} %get-tuple-element.215.refs_1_, bf16[2,48,128]{2,1,0:T(8,128)(2,1)} %copy-done.12, ...), custom_call_target="tpu_custom_call" | custom-call | bytes 3719208 | tf_op jit(solution)/shard_map/close/pallas_call | solution.py:138
  200.9 3.2 %collective-permute-done.52.refs_1_ = bf16[64,256]{1,0:T(8,128)(2,1)S(1)} collective-permute-done((bf16[64,256]{1,0:T(8,128)(2,1)}, bf16[64,256]{1,0:T(8,128)(2,1)S(1)}, u32[]{:S(2)}, u32[]{:S(2)}) %collective-permute-start.52) | collective-permute-done | bytes 32800 | tf_op jit(solution)/shard_map/ppermute | solution.py:23
  204.1 2.0 collective-permute-done.53.refs_4_
  206.1 1.9 end.1
  (129 shorter events, 34.2 us)
Async XLA Ops:
  4.8 4.5 %collective-permute-start.1 = (f32[8,128]{1,0:T(8,128)S(1)}, f32[8,128]{1,0:T(8,128)S(1)}, u32[]{:S(2)}, u32[]{:S(2)}) collective-permute-start(f32[8,128]{1,0:T(8,128)S(1)} %add_select_fusion.3), channel_id=1, source_target_pairs={{0,4},{2,6},{4,0},{6,2},{8,12},{10,14},{12,8},{14,10},{1,5},{3,7},... | collective-permute-start | bytes 12296 | tf_op jit(solution)/shard_map/ppermute | solution.py:23
  9.4 4.6 %collective-permute-start.2 = (f32[8,128]{1,0:T(8,128)S(1)}, f32[8,128]{1,0:T(8,128)S(1)}, u32[]{:S(2)}, u32[]{:S(2)}) collective-permute-start(f32[8,128]{1,0:T(8,128)S(1)} %add_select_fusion.2), channel_id=1, source_target_pairs={{0,8},{2,10},{4,12},{6,14},{8,0},{10,2},{12,4},{14,6},{1,9},{3,11}... | collective-permute-start | bytes 12296 | tf_op jit(solution)/shard_map/ppermute | solution.py:23
  12.4 5.4 %collective-permute-start.4 = (bf16[2,48,128]{2,1,0:T(8,128)(2,1)S(1)}, bf16[2,48,128]{2,1,0:T(8,128)(2,1)S(1)}, u32[]{:S(2)}, u32[]{:S(2)}) collective-permute-start(bf16[2,48,128]{2,1,0:T(8,128)(2,1)S(1)} %get-tuple-element.136), channel_id=1, source_target_pairs={{14,0},{0,2},{2,4},{4,6},{6,8},{8,10},{10,12},{12,14},{15,1},{1,3}... | collective-permute-start | bytes 73736 | tf_op jit(solution)/shard_map/ppermute | solution.py:29
  12.4 55.2 %collective-permute-start.20 = (bf16[512,1024]{1,0:T(8,128)(2,1)}, bf16[512,1024]{1,0:T(8,128)(2,1)S(1)}, u32[]{:S(2)}, u32[]{:S(2)}) collective-permute-start(bf16[512,1024]{1,0:T(8,128)(2,1)} %refs_6_.1), channel_id=1, source_target_pairs={{0,1},{1,0},{2,3},{3,2},{4,5},{5,4},{6,7},{7,6},{8,9},{9,8},{10,11... | collective-permute-start | bytes 3145736 | tf_op jit(solution)/shard_map/ppermute | solution.py:23
  14.1 3.6 %collective-permute-start.3 = (f32[8,128]{1,0:T(8,128)S(1)}, f32[8,128]{1,0:T(8,128)S(1)}, u32[]{:S(2)}, u32[]{:S(2)}) collective-permute-start(f32[8,128]{1,0:T(8,128)S(1)} %add_select_fusion.1), channel_id=1, source_target_pairs={{0,16},{16,0},{1,17},{17,1},{2,18},{18,2},{3,19},{19,3},{4,20},{20... | collective-permute-start | bytes 12296 | tf_op jit(solution)/shard_map/ppermute | solution.py:23
  22.7 16.4 %collective-permute-start.6 = (bf16[2,3,128,128]{3,2,1,0:T(8,128)(2,1)S(1)}, bf16[2,3,128,128]{3,2,1,0:T(8,128)(2,1)S(1)}, u32[]{:S(2)}, u32[]{:S(2)}) collective-permute-start(bf16[2,3,128,128]{3,2,1,0:T(8,128)(2,1)S(1)} %get-tuple-element.139), channel_id=1, source_target_pairs={{0,8},{2,10},{4,12},{6,14},{8,0},{10,2},{12,4},{14,6},{1,9},{3,11}... | collective-permute-start | bytes 589832 | tf_op jit(solution)/shard_map/ppermute | solution.py:23
  25.6 13.4 %collective-permute-start.7 = (bf16[2,3,128,128]{3,2,1,0:T(8,128)(2,1)S(1)}, bf16[2,3,128,128]{3,2,1,0:T(8,128)(2,1)S(1)}, u32[]{:S(2)}, u32[]{:S(2)}) collective-permute-start(bf16[2,3,128,128]{3,2,1,0:T(8,128)(2,1)S(1)} %get-tuple-element.140), channel_id=1, source_target_pairs={{0,12},{2,14},{4,8},{6,10},{8,4},{10,6},{12,0},{14,2},{1,13},{3,15... | collective-permute-start | bytes 589832 | tf_op jit(solution)/shard_map/ppermute | solution.py:23
  27.0 13.4 %collective-permute-start.5 = (bf16[2,3,128,128]{3,2,1,0:T(8,128)(2,1)S(1)}, bf16[2,3,128,128]{3,2,1,0:T(8,128)(2,1)S(1)}, u32[]{:S(2)}, u32[]{:S(2)}) collective-permute-start(bf16[2,3,128,128]{3,2,1,0:T(8,128)(2,1)S(1)} %get-tuple-element.138), channel_id=1, source_target_pairs={{0,4},{2,6},{4,0},{6,2},{8,12},{10,14},{12,8},{14,10},{1,5},{3,7},... | collective-permute-start | bytes 589832 | tf_op jit(solution)/shard_map/ppermute | solution.py:23
  27.2 13.2 %collective-permute-start.8 = (bf16[2,3,128,128]{3,2,1,0:T(8,128)(2,1)S(1)}, bf16[2,3,128,128]{3,2,1,0:T(8,128)(2,1)S(1)}, u32[]{:S(2)}, u32[]{:S(2)}) collective-permute-start(bf16[2,3,128,128]{3,2,1,0:T(8,128)(2,1)S(1)} %get-tuple-element.137.refs_0_), channel_id=1, source_target_pairs={{0,2},{2,0},{4,6},{6,4},{8,10},{10,8},{12,14},{14,12},{1,3},{3,1},... | collective-permute-start | bytes 589832 | tf_op jit(solution)/shard_map/ppermute | solution.py:23
  48.5 11.6 %collective-permute-start.13 = (bf16[2,128,128]{2,1,0:T(8,128)(2,1)S(1)}, bf16[2,128,128]{2,1,0:T(8,128)(2,1)S(1)}, u32[]{:S(2)}, u32[]{:S(2)}) collective-permute-start(bf16[2,128,128]{2,1,0:T(8,128)(2,1)S(1)} %get-tuple-element.146), channel_id=1, source_target_pairs={{0,4},{2,6},{4,0},{6,2},{8,12},{10,14},{12,8},{14,10},{1,5},{3,7},... | collective-permute-start | bytes 196616 | tf_op jit(solution)/shard_map/ppermute | solution.py:23
  52.2 9.4 %collective-permute-start.14 = (bf16[2,128,128]{2,1,0:T(8,128)(2,1)S(1)}, bf16[2,128,128]{2,1,0:T(8,128)(2,1)S(1)}, u32[]{:S(2)}, u32[]{:S(2)}) collective-permute-start(bf16[2,128,128]{2,1,0:T(8,128)(2,1)S(1)} %get-tuple-element.147), channel_id=1, source_target_pairs={{0,8},{2,10},{4,12},{6,14},{8,0},{10,2},{12,4},{14,6},{1,9},{3,11}... | collective-permute-start | bytes 196616 | tf_op jit(solution)/shard_map/ppermute | solution.py:23
  52.5 9.7 %collective-permute-start.15 = (bf16[2,128,128]{2,1,0:T(8,128)(2,1)S(1)}, bf16[2,128,128]{2,1,0:T(8,128)(2,1)S(1)}, u32[]{:S(2)}, u32[]{:S(2)}) collective-permute-start(bf16[2,128,128]{2,1,0:T(8,128)(2,1)S(1)} %get-tuple-element.148), channel_id=1, source_target_pairs={{0,12},{2,14},{4,8},{6,10},{8,4},{10,6},{12,0},{14,2},{1,13},{3,15... | collective-permute-start | bytes 196616 | tf_op jit(solution)/shard_map/ppermute | solution.py:23
  59.5 5.2 %collective-permute-start.16 = (bf16[2,128,128]{2,1,0:T(8,128)(2,1)}, bf16[2,128,128]{2,1,0:T(8,128)(2,1)S(1)}, u32[]{:S(2)}, u32[]{:S(2)}) collective-permute-start(bf16[2,128,128]{2,1,0:T(8,128)(2,1)} %pin.6.refs_1_), channel_id=1, source_target_pairs={{0,1},{1,0},{2,3},{3,2},{4,5},{5,4},{6,7},{7,6},{8,9},{9,8},{10,11... | collective-permute-start | bytes 196616 | tf_op jit(solution)/shard_map/ppermute | solution.py:23
  60.1 6.1 %collective-permute-start.17 = (bf16[2,128,128]{2,1,0:T(8,128)(2,1)S(1)}, bf16[2,128,128]{2,1,0:T(8,128)(2,1)S(1)}, u32[]{:S(2)}, u32[]{:S(2)}) collective-permute-start(bf16[2,128,128]{2,1,0:T(8,128)(2,1)S(1)} %collective-permute-done.13.refs_2_), channel_id=1, source_target_pairs={{0,1},{1,0},{2,3},{3,2},{4,5},{5,4},{6,7},{7,6},{8,9},{9,8},{10,11... | collective-permute-start | bytes 196616 | tf_op jit(solution)/shard_map/ppermute | solution.py:23
  61.6 5.4 %collective-permute-start.18 = (bf16[2,128,128]{2,1,0:T(8,128)(2,1)S(1)}, bf16[2,128,128]{2,1,0:T(8,128)(2,1)S(1)}, u32[]{:S(2)}, u32[]{:S(2)}) collective-permute-start(bf16[2,128,128]{2,1,0:T(8,128)(2,1)S(1)} %collective-permute-done.14.refs_3_), channel_id=1, source_target_pairs={{0,1},{1,0},{2,3},{3,2},{4,5},{5,4},{6,7},{7,6},{8,9},{9,8},{10,11... | collective-permute-start | bytes 196616 | tf_op jit(solution)/shard_map/ppermute | solution.py:23
  62.1 5.5 %collective-permute-start.19 = (bf16[2,128,128]{2,1,0:T(8,128)(2,1)S(1)}, bf16[2,128,128]{2,1,0:T(8,128)(2,1)S(1)}, u32[]{:S(2)}, u32[]{:S(2)}) collective-permute-start(bf16[2,128,128]{2,1,0:T(8,128)(2,1)S(1)} %collective-permute-done.15.refs_4_), channel_id=1, source_target_pairs={{0,1},{1,0},{2,3},{3,2},{4,5},{5,4},{6,7},{7,6},{8,9},{9,8},{10,11... | collective-permute-start | bytes 196616 | tf_op jit(solution)/shard_map/ppermute | solution.py:23
  76.1 4.2 %collective-permute-start.22 = (bf16[256,2048]{1,0:T(8,128)(2,1)}, bf16[256,2048]{1,0:T(8,128)(2,1)S(1)}, u32[]{:S(2)}, u32[]{:S(2)}) collective-permute-start(bf16[256,2048]{1,0:T(8,128)(2,1)} %get-tuple-element.155.refs_3_), channel_id=1, source_target_pairs={{0,2},{2,0},{4,6},{6,4},{8,10},{10,8},{12,14},{14,12},{1,3},{3,1},... | collective-permute-start | bytes 3145736 | tf_op jit(solution)/shard_map/ppermute | solution.py:23
  76.2 4.1 %collective-permute-start.24 = (bf16[256,1024]{1,0:T(8,128)(2,1)}, bf16[256,1024]{1,0:T(8,128)(2,1)S(1)}, u32[]{:S(2)}, u32[]{:S(2)}) collective-permute-start(bf16[256,1024]{1,0:T(8,128)(2,1)} %get-tuple-element.157), channel_id=1, source_target_pairs={{0,2},{2,0},{4,6},{6,4},{8,10},{10,8},{12,14},{14,12},{1,3},{3,1},... | collective-permute-start | bytes 1572872 | tf_op jit(solution)/shard_map/ppermute | solution.py:23
  76.7 3.6 %collective-permute-start.21 = (bf16[8,64,256]{2,1,0:T(8,128)(2,1)}, bf16[8,64,256]{2,1,0:T(8,128)(2,1)S(1)}, u32[]{:S(2)}, u32[]{:S(2)}) collective-permute-start(bf16[8,64,256]{2,1,0:T(8,128)(2,1)} %get-tuple-element.154), channel_id=1, source_target_pairs={{0,2},{2,0},{4,6},{6,4},{8,10},{10,8},{12,14},{14,12},{1,3},{3,1},... | collective-permute-start | bytes 786440 | tf_op jit(solution)/shard_map/ppermute | solution.py:23
  76.8 14.5 %collective-permute-start.27 = (bf16[256,1024]{1,0:T(8,128)(2,1)S(1)}, bf16[256,1024]{1,0:T(8,128)(2,1)S(1)}, u32[]{:S(2)}, u32[]{:S(2)}) collective-permute-start(bf16[256,1024]{1,0:T(8,128)(2,1)S(1)} %get-tuple-element.168.refs_3_), channel_id=1, source_target_pairs={{0,1},{1,0},{2,3},{3,2},{4,5},{5,4},{6,7},{7,6},{8,9},{9,8},{10,11... | collective-permute-start | bytes 1572872 | tf_op jit(solution)/shard_map/ppermute | solution.py:23
  79.5 7.8 %collective-permute-start.25 = (bf16[256,512]{1,0:T(8,128)(2,1)}, bf16[256,512]{1,0:T(8,128)(2,1)S(1)}, u32[]{:S(2)}, u32[]{:S(2)}) collective-permute-start(bf16[256,512]{1,0:T(8,128)(2,1)} %get-tuple-element.160.refs_3_), channel_id=1, source_target_pairs={{0,2},{2,0},{4,6},{6,4},{8,10},{10,8},{12,14},{14,12},{1,3},{3,1},... | collective-permute-start | bytes 786440 | tf_op jit(solution)/shard_map/ppermute | solution.py:23
  85.1 19.5 %collective-permute-start.28 = (bf16[4,64,1280]{2,1,0:T(8,128)(2,1)}, bf16[4,64,1280]{2,1,0:T(8,128)(2,1)S(1)}, u32[]{:S(2)}, u32[]{:S(2)}) collective-permute-start(bf16[4,64,1280]{2,1,0:T(8,128)(2,1)} %get-tuple-element.172), channel_id=1, source_target_pairs={{0,16},{16,0},{1,17},{17,1},{2,18},{18,2},{3,19},{19,3},{4,20},{20... | collective-permute-start | bytes 1966088 | tf_op jit(solution)/shard_map/ppermute | solution.py:23
  86.6 18.0 %collective-permute-start.29 = (bf16[4,64,1152]{2,1,0:T(8,128)(2,1)}, bf16[4,64,1152]{2,1,0:T(8,128)(2,1)S(1)}, u32[]{:S(2)}, u32[]{:S(2)}) collective-permute-start(bf16[4,64,1152]{2,1,0:T(8,128)(2,1)} %get-tuple-element.174), channel_id=1, source_target_pairs={{0,4},{2,6},{4,0},{6,2},{8,12},{10,14},{12,8},{14,10},{1,5},{3,7},... | collective-permute-start | bytes 1769480 | tf_op jit(solution)/shard_map/ppermute | solution.py:23
  94.3 12.8 %all-to-all-start = ((bf16[4,2,128,128]{3,2,1,0:T(8,128)(2,1)}), bf16[4,2,128,128]{3,2,1,0:T(8,128)(2,1)S(1)}, u32[]{:S(2)}, u32[]{:S(2)}) async-start(bf16[4,2,128,128]{3,2,1,0:T(8,128)(2,1)} %bitcast.21), calls=%async_computation | async-start | bytes 524288 | tf_op jit(solution)/shard_map/all_to_all | solution.py:1259
  98.0 18.1 %collective-permute-start.26 = (bf16[256,1024]{1,0:T(8,128)(2,1)}, bf16[256,1024]{1,0:T(8,128)(2,1)}, u32[]{:S(2)}, u32[]{:S(2)}) collective-permute-start(bf16[256,1024]{1,0:T(8,128)(2,1)} %get-tuple-element.161.refs_2_), channel_id=1, source_target_pairs={{0,1},{1,0},{2,3},{3,2},{4,5},{5,4},{6,7},{7,6},{8,9},{9,8},{10,11... | collective-permute-start | bytes 1572872 | tf_op jit(solution)/shard_map/ppermute | solution.py:23
  107.9 8.9 %collective-permute-start.30 = (bf16[2,64,1664]{2,1,0:T(8,128)(2,1)}, bf16[2,64,1664]{2,1,0:T(8,128)(2,1)}, u32[]{:S(2)}, u32[]{:S(2)}) collective-permute-start(bf16[2,64,1664]{2,1,0:T(8,128)(2,1)} %get-tuple-element.184), channel_id=1, source_target_pairs={{0,4},{2,6},{4,0},{6,2},{8,12},{10,14},{12,8},{14,10},{1,5},{3,7},... | collective-permute-start | bytes 1277960 | tf_op jit(solution)/shard_map/ppermute | solution.py:23
  107.9 8.3 %collective-permute-start.31 = (bf16[2,64,1152]{2,1,0:T(8,128)(2,1)}, bf16[2,64,1152]{2,1,0:T(8,128)(2,1)}, u32[]{:S(2)}, u32[]{:S(2)}) collective-permute-start(bf16[2,64,1152]{2,1,0:T(8,128)(2,1)} %get-tuple-element.185), channel_id=1, source_target_pairs={{0,16},{16,0},{1,17},{17,1},{2,18},{18,2},{3,19},{19,3},{4,20},{20... | collective-permute-start | bytes 884744 | tf_op jit(solution)/shard_map/ppermute | solution.py:23
  120.7 10.4 %collective-permute-start.33 = (bf16[2,3,128,128]{3,2,1,0:T(8,128)(2,1)S(1)}, bf16[2,3,128,128]{3,2,1,0:T(8,128)(2,1)S(1)}, u32[]{:S(2)}, u32[]{:S(2)}) collective-permute-start(bf16[2,3,128,128]{3,2,1,0:T(8,128)(2,1)S(1)} %get-tuple-element.194), channel_id=1, source_target_pairs={{0,4},{2,6},{4,0},{6,2},{8,12},{10,14},{12,8},{14,10},{1,5},{3,7},... | collective-permute-start | bytes 589832 | tf_op jit(solution)/shard_map/ppermute | solution.py:23
  122.4 17.1 %collective-permute-start.34 = (bf16[2,3,128,128]{3,2,1,0:T(8,128)(2,1)S(1)}, bf16[2,3,128,128]{3,2,1,0:T(8,128)(2,1)S(1)}, u32[]{:S(2)}, u32[]{:S(2)}) collective-permute-start(bf16[2,3,128,128]{3,2,1,0:T(8,128)(2,1)S(1)} %get-tuple-element.195), channel_id=1, source_target_pairs={{0,8},{2,10},{4,12},{6,14},{8,0},{10,2},{12,4},{14,6},{1,9},{3,11}... | collective-permute-start | bytes 589832 | tf_op jit(solution)/shard_map/ppermute | solution.py:23
  123.3 16.2 %collective-permute-start.35 = (bf16[2,3,128,128]{3,2,1,0:T(8,128)(2,1)S(1)}, bf16[2,3,128,128]{3,2,1,0:T(8,128)(2,1)S(1)}, u32[]{:S(2)}, u32[]{:S(2)}) collective-permute-start(bf16[2,3,128,128]{3,2,1,0:T(8,128)(2,1)S(1)} %get-tuple-element.196), channel_id=1, source_target_pairs={{0,12},{2,14},{4,8},{6,10},{8,4},{10,6},{12,0},{14,2},{1,13},{3,15... | collective-permute-start | bytes 589832 | tf_op jit(solution)/shard_map/ppermute | solution.py:23
  142.3 5.7 %collective-permute-start.39 = (bf16[256,1536]{1,0:T(8,128)(2,1)}, bf16[256,1536]{1,0:T(8,128)(2,1)}, u32[]{:S(2)}, u32[]{:S(2)}) collective-permute-start(bf16[256,1536]{1,0:T(8,128)(2,1)} %get-tuple-element.212.refs_3_), channel_id=1, source_target_pairs={{0,2},{2,0},{4,6},{6,4},{8,10},{10,8},{12,14},{14,12},{1,3},{3,1},... | collective-permute-start | bytes 2359304 | tf_op jit(solution)/shard_map/ppermute | solution.py:23
  142.3 14.8 %collective-permute-start.36 = (bf16[256,1024]{1,0:T(8,128)(2,1)}, bf16[256,1024]{1,0:T(8,128)(2,1)S(1)}, u32[]{:S(2)}, u32[]{:S(2)}) collective-permute-start(bf16[256,1024]{1,0:T(8,128)(2,1)} %get-tuple-element.201.refs_3_), channel_id=1, source_target_pairs={{0,1},{1,0},{2,3},{3,2},{4,5},{5,4},{6,7},{7,6},{8,9},{9,8},{10,11... | collective-permute-start | bytes 1572872 | tf_op jit(solution)/shard_map/ppermute | solution.py:23
  143.2 9.2 %collective-permute-start.37 = (bf16[8,64,256]{2,1,0:T(8,128)(2,1)}, bf16[8,64,256]{2,1,0:T(8,128)(2,1)}, u32[]{:S(2)}, u32[]{:S(2)}) collective-permute-start(bf16[8,64,256]{2,1,0:T(8,128)(2,1)} %get-tuple-element.205), channel_id=1, source_target_pairs={{0,2},{2,0},{4,6},{6,4},{8,10},{10,8},{12,14},{14,12},{1,3},{3,1},... | collective-permute-start | bytes 786440 | tf_op jit(solution)/shard_map/ppermute | solution.py:23
  143.3 9.0 %collective-permute-start.38 = (bf16[8,64,256]{2,1,0:T(8,128)(2,1)}, bf16[8,64,256]{2,1,0:T(8,128)(2,1)S(1)}, u32[]{:S(2)}, u32[]{:S(2)}) collective-permute-start(bf16[8,64,256]{2,1,0:T(8,128)(2,1)} %get-tuple-element.210), channel_id=1, source_target_pairs={{0,2},{2,0},{4,6},{6,4},{8,10},{10,8},{12,14},{14,12},{1,3},{3,1},... | collective-permute-start | bytes 786440 | tf_op jit(solution)/shard_map/ppermute | solution.py:23
  143.7 25.3 %collective-permute-start.42 = (bf16[64,3584]{1,0:T(8,128)(2,1)}, bf16[64,3584]{1,0:T(8,128)(2,1)S(1)}, u32[]{:S(2)}, u32[]{:S(2)}) collective-permute-start(bf16[64,3584]{1,0:T(8,128)(2,1)} %get-tuple-element.222), channel_id=1, source_target_pairs={{0,8},{2,10},{4,12},{6,14},{8,0},{10,2},{12,4},{14,6},{1,9},{3,11}... | collective-permute-start | bytes 1376264 | tf_op jit(solution)/shard_map/ppermute | solution.py:23
  151.7 22.2 %collective-permute-start.40 = (bf16[4,64,896]{2,1,0:T(8,128)(2,1)}, bf16[4,64,896]{2,1,0:T(8,128)(2,1)S(1)}, u32[]{:S(2)}, u32[]{:S(2)}) collective-permute-start(bf16[4,64,896]{2,1,0:T(8,128)(2,1)} %get-tuple-element.218), channel_id=1, source_target_pairs={{0,16},{16,0},{1,17},{17,1},{2,18},{18,2},{3,19},{19,3},{4,20},{20... | collective-permute-start | bytes 1376264 | tf_op jit(solution)/shard_map/ppermute | solution.py:23
  155.1 18.8 %collective-permute-start.43 = (bf16[4,64,768]{2,1,0:T(8,128)(2,1)}, bf16[4,64,768]{2,1,0:T(8,128)(2,1)S(1)}, u32[]{:S(2)}, u32[]{:S(2)}) collective-permute-start(bf16[4,64,768]{2,1,0:T(8,128)(2,1)} %get-tuple-element.224), channel_id=1, source_target_pairs={{0,16},{16,0},{1,17},{17,1},{2,18},{18,2},{3,19},{19,3},{4,20},{20... | collective-permute-start | bytes 1179656 | tf_op jit(solution)/shard_map/ppermute | solution.py:23
  156.5 17.4 %collective-permute-start.41 = (bf16[4,64,640]{2,1,0:T(8,128)(2,1)}, bf16[4,64,640]{2,1,0:T(8,128)(2,1)S(1)}, u32[]{:S(2)}, u32[]{:S(2)}) collective-permute-start(bf16[4,64,640]{2,1,0:T(8,128)(2,1)} %get-tuple-element.220), channel_id=1, source_target_pairs={{0,4},{2,6},{4,0},{6,2},{8,12},{10,14},{12,8},{14,10},{1,5},{3,7},... | collective-permute-start | bytes 983048 | tf_op jit(solution)/shard_map/ppermute | solution.py:23
  161.1 7.9 %collective-permute-start.44 = (bf16[8,64,256]{2,1,0:T(8,128)(2,1)}, bf16[8,64,256]{2,1,0:T(8,128)(2,1)S(1)}, u32[]{:S(2)}, u32[]{:S(2)}) collective-permute-start(bf16[8,64,256]{2,1,0:T(8,128)(2,1)} %get-tuple-element.226), channel_id=1, source_target_pairs={{0,2},{2,0},{4,6},{6,4},{8,10},{10,8},{12,14},{14,12},{1,3},{3,1},... | collective-permute-start | bytes 786440 | tf_op jit(solution)/shard_map/ppermute | solution.py:23
  177.1 11.9 %collective-permute-start.47 = (bf16[2,64,1920]{2,1,0:T(8,128)(2,1)}, bf16[2,64,1920]{2,1,0:T(8,128)(2,1)S(1)}, u32[]{:S(2)}, u32[]{:S(2)}) collective-permute-start(bf16[2,64,1920]{2,1,0:T(8,128)(2,1)} %get-tuple-element.234), channel_id=1, source_target_pairs={{0,16},{16,0},{1,17},{17,1},{2,18},{18,2},{3,19},{19,3},{4,20},{20... | collective-permute-start | bytes 1474568 | tf_op jit(solution)/shard_map/ppermute | solution.py:23
  177.5 10.9 %collective-permute-start.46 = (bf16[2,64,896]{2,1,0:T(8,128)(2,1)}, bf16[2,64,896]{2,1,0:T(8,128)(2,1)S(1)}, u32[]{:S(2)}, u32[]{:S(2)}) collective-permute-start(bf16[2,64,896]{2,1,0:T(8,128)(2,1)} %get-tuple-element.232), channel_id=1, source_target_pairs={{0,4},{2,6},{4,0},{6,2},{8,12},{10,14},{12,8},{14,10},{1,5},{3,7},... | collective-permute-start | bytes 688136 | tf_op jit(solution)/shard_map/ppermute | solution.py:23
  177.5 10.9 %collective-permute-start.48 = (bf16[2,64,768]{2,1,0:T(8,128)(2,1)}, bf16[2,64,768]{2,1,0:T(8,128)(2,1)S(1)}, u32[]{:S(2)}, u32[]{:S(2)}) collective-permute-start(bf16[2,64,768]{2,1,0:T(8,128)(2,1)} %get-tuple-element.236), channel_id=1, source_target_pairs={{0,8},{2,10},{4,12},{6,14},{8,0},{10,2},{12,4},{14,6},{1,9},{3,11}... | collective-permute-start | bytes 589832 | tf_op jit(solution)/shard_map/ppermute | solution.py:23
  180.0 6.3 %collective-permute-start.45 = (bf16[2,48,128]{2,1,0:T(8,128)(2,1)}, bf16[2,48,128]{2,1,0:T(8,128)(2,1)S(1)}, u32[]{:S(2)}, u32[]{:S(2)}) collective-permute-start(bf16[2,48,128]{2,1,0:T(8,128)(2,1)} %pin.10), channel_id=1, source_target_pairs={{2,0},{4,2},{6,4},{8,6},{10,8},{12,10},{14,12},{0,14},{3,1},{5,3},... | collective-permute-start | bytes 73736 | tf_op jit(solution)/shard_map/ppermute | solution.py:29
  191.3 6.8 %collective-permute-start.50 = (bf16[2,64,1536]{2,1,0:T(8,128)(2,1)}, bf16[2,64,1536]{2,1,0:T(8,128)(2,1)S(1)}, u32[]{:S(2)}, u32[]{:S(2)}) collective-permute-start(bf16[2,64,1536]{2,1,0:T(8,128)(2,1)} %get-tuple-element.239.refs_8_), channel_id=1, source_target_pairs={{0,2},{2,0},{4,6},{6,4},{8,10},{10,8},{12,14},{14,12},{1,3},{3,1},... | collective-permute-start | bytes 1179656 | tf_op jit(solution)/shard_map/ppermute | solution.py:23
  191.3 14.8 %collective-permute-start.53 = (bf16[64,1792]{1,0:T(8,128)(2,1)}, bf16[64,1792]{1,0:T(8,128)(2,1)S(1)}, u32[]{:S(2)}, u32[]{:S(2)}) collective-permute-start(bf16[64,1792]{1,0:T(8,128)(2,1)} %get-tuple-element.245), channel_id=1, source_target_pairs={{0,8},{2,10},{4,12},{6,14},{8,0},{10,2},{12,4},{14,6},{1,9},{3,11}... | collective-permute-start | bytes 688136 | tf_op jit(solution)/shard_map/ppermute | solution.py:23
  192.3 5.8 %collective-permute-start.49 = (bf16[128,512]{1,0:T(8,128)(2,1)}, bf16[128,512]{1,0:T(8,128)(2,1)S(1)}, u32[]{:S(2)}, u32[]{:S(2)}) collective-permute-start(bf16[128,512]{1,0:T(8,128)(2,1)} %pin.11), channel_id=1, source_target_pairs={{0,16},{16,0},{1,17},{17,1},{2,18},{18,2},{3,19},{19,3},{4,20},{20... | collective-permute-start | bytes 393224 | tf_op jit(solution)/shard_map/ppermute | solution.py:23
  193.6 10.5 %collective-permute-start.51 = (bf16[64,1024]{1,0:T(8,128)(2,1)}, bf16[64,1024]{1,0:T(8,128)(2,1)S(1)}, u32[]{:S(2)}, u32[]{:S(2)}) collective-permute-start(bf16[64,1024]{1,0:T(8,128)(2,1)} %get-tuple-element.241), channel_id=1, source_target_pairs={{0,4},{2,6},{4,0},{6,2},{8,12},{10,14},{12,8},{14,10},{1,5},{3,7},... | collective-permute-start | bytes 393224 | tf_op jit(solution)/shard_map/ppermute | solution.py:23
  195.1 8.9 %collective-permute-start.52 = (bf16[64,256]{1,0:T(8,128)(2,1)}, bf16[64,256]{1,0:T(8,128)(2,1)S(1)}, u32[]{:S(2)}, u32[]{:S(2)}) collective-permute-start(bf16[64,256]{1,0:T(8,128)(2,1)} %get-tuple-element.242), channel_id=1, source_target_pairs={{0,12},{2,14},{4,8},{6,10},{8,4},{10,6},{12,0},{14,2},{1,13},{3,15... | collective-permute-start | bytes 98312 | tf_op jit(solution)/shard_map/ppermute | solution.py:23
  (22 other events, 173.7 us)

commit v6 on v5

--- a/solution.py
+++ b/solution.py
@@ -1215,7 +1215,7 @@
         send_a, keep_a, send_b, keep_b, token = call(
             grads_ff_kernel,
             "grads_ff",
-            [out_a, out_a, out_b, out_b],
+            [Warm(out_a), out_a, Warm(out_b), out_b],
             ids, normed_two[0], Warm(swap(normed_two[1], "lon", 1)), d_pre, Warm(swap(d_pre, "lon", 1)),
             ct_turned, Warm(ct_got), activated, Warm(swap(act_send, "lon", 1)),
             after=[token],
@@ -1384,7 +1384,7 @@
         send_a, keep_a, send_b, keep_b, oh_send, oh_keep, token = call(
             fold_q_kernel,
             "fold_q",
-            [step_a, step_a, step_b, step_b, side, side],
+            [Warm(step_a), step_a, Warm(step_b), step_b, Warm(side), side],
             ids, keep_a, Warm(got_a), keep_b, Warm(got_b), up_keep, Warm(up_got), oh_keep, Warm(oh_got),
             embed[0], Warm(swap(embed[1], "lon", 1)),
             after=[token],
@@ -1402,11 +1402,11 @@
             merge_q_kernel,
             "merge_q",
             [
-                final,
+                Warm(final),
                 final,
                 shape((2, rows, 4 * inner_columns)),
-                shape((rows, embed_width + wide)),
-                block,
+                warm((rows, embed_width + wide)),
+                Warm(block),
                 shape((rows, wide)),
             ],
             ids, keep_a, Warm(got_a), keep_b, Warm(got_b), oh_keep, Warm(oh_got),

time: 209 us -> 208 us (level)
  no operation moved by 1% of the time
where the time goes in v6:
time: 208 us; the launch traced here: 207 us
  Pallas kernels  77.5 us (37%)
  waiting for transfers between devices  69.4 us (33%)
  starting transfers between devices  56.8 us (27%)
  local copies, waits for them, and re-layouts  2.17 us (1%)
    pallas_call x21, Pallas kernels, call(): pl.pallas_call(with_token, grid=grid, out_shape=[*[o.value if isinstance(...  77.5 us
    ppermute x52, waiting for transfers between devices, swap(): return lax.ppermute(block, axis, route)  63.2 us
    ppermute x52, starting transfers between devices, swap(): return lax.ppermute(block, axis, route)  53.1 us
    ppermute x2, waiting for transfers between devices, from_behind(): return lax.ppermute(block, axis, route)  6.12 us
  transfers between devices with their start and end apart: 55, of which 27 were waited for; matrix products, arithmetic and copies ran while one was open for 0% of the time, Pallas kernels for 27%

profile of v6, /device:TPU:0, one launch (start us, length us, event | category | flops | bytes accessed | tf_op | source)
XLA Modules:
  0.0 207.0 jit_solution(1564189715847772372)
XLA Ops:
  1.3 2.1 %moments.1 = (f32[2,192,128]{2,1,0:T(8,128)S(1)}, bf16[2,48,128]{2,1,0:T(8,128)(2,1)S(1)}, f32[8,128]{1,0:T(8,128)S(1)}, f32[8,128]{1,0:T(8,128)}) custom-call(s32[2]{0:T(128)S(1)} %copy-done.10, f32[12,192,128]{2,1,0:T(8,128)} %bitcast.39), custom_call_target="tpu_custom_call" | custom-call | bytes 1404936 | tf_op jit(solution)/shard_map/moments/pallas_call | solution.py:138
  4.8 2.9 %collective-permute-start.1 = (f32[8,128]{1,0:T(8,128)S(1)}, f32[8,128]{1,0:T(8,128)S(1)}, u32[]{:S(2)}, u32[]{:S(2)}) collective-permute-start(f32[8,128]{1,0:T(8,128)S(1)} %add_select_fusion.3), channel_id=1, source_target_pairs={{0,4},{2,6},{4,0},{6,2},{8,12},{10,14},{12,8},{14,10},{1,5},{3,7},... | collective-permute-start | bytes 12296 | tf_op jit(solution)/shard_map/ppermute | solution.py:23
  7.7 1.6 collective-permute-done.1
  9.4 3.0 %collective-permute-start.2 = (f32[8,128]{1,0:T(8,128)S(1)}, f32[8,128]{1,0:T(8,128)S(1)}, u32[]{:S(2)}, u32[]{:S(2)}) collective-permute-start(f32[8,128]{1,0:T(8,128)S(1)} %add_select_fusion.2), channel_id=1, source_target_pairs={{0,8},{2,10},{4,12},{6,14},{8,0},{10,2},{12,4},{14,6},{1,9},{3,11}... | collective-permute-start | bytes 12296 | tf_op jit(solution)/shard_map/ppermute | solution.py:23
  12.4 1.5 collective-permute-start.20
  14.1 1.8 collective-permute-start.3
  16.0 1.7 collective-permute-done.3
  17.8 4.8 %start.1 = (f32[1,48]{1,0:T(1,128)}, f32[1,48]{1,0:T(1,128)}, f32[1,48]{1,0:T(1,128)}, f32[256,1024]{1,0:T(8,128)}, bf16[192,256]{1,0:T(8,128)(2,1)}, /*index=5*...) custom-call(s32[10]{0:T(128)S(1)} %stack.43.refs_0_, ...), custom_call_target="tpu_custom_call" | custom-call | flops 905969664 | bytes 6493352 | tf_op jit(solution)/shard_map/start/pallas_call | solution.py:138
  22.7 3.0 %collective-permute-start.6 = (bf16[2,3,128,128]{3,2,1,0:T(8,128)(2,1)S(1)}, bf16[2,3,128,128]{3,2,1,0:T(8,128)(2,1)S(1)}, u32[]{:S(2)}, u32[]{:S(2)}) collective-permute-start(bf16[2,3,128,128]{3,2,1,0:T(8,128)(2,1)S(1)} %get-tuple-element.139), channel_id=1, source_target_pairs={{0,8},{2,10},{4,12},{6,14},{8,0},{10,2},{12,4},{14,6},{1,9},{3,11}... | collective-permute-start | bytes 589832 | tf_op jit(solution)/shard_map/ppermute | solution.py:23
  27.2 11.8 %collective-permute-done.6.refs_2_ = bf16[2,3,128,128]{3,2,1,0:T(8,128)(2,1)S(1)} collective-permute-done((bf16[2,3,128,128]{3,2,1,0:T(8,128)(2,1)S(1)}, bf16[2,3,128,128]{3,2,1,0:T(8,128)(2,1)S(1)}, u32[]{:S(2)}, u32[]{:S(2)}) %collective-permute-start.6) | collective-permute-done | bytes 196640 | tf_op jit(solution)/shard_map/ppermute | solution.py:23
  42.1 6.4 %attend.1 = (bf16[2,128,128]{2,1,0:T(8,128)(2,1)}, bf16[2,128,128]{2,1,0:T(8,128)(2,1)S(1)}, bf16[2,128,128]{2,1,0:T(8,128)(2,1)S(1)}, bf16[2,128,128]{2,1,0:T(8...) custom-call(bf16[2,3,128,128]{3,2,1,0:T(8,128)(2,1)S(1)} %get-tuple-, ...), custom_call_target="tpu_custom_call" | custom-call | flops 1073741824 | bytes 7864320 | tf_op jit(solution)/shard_map/attend/pallas_call | solution.py:138
  48.5 3.7 %collective-permute-start.13 = (bf16[2,128,128]{2,1,0:T(8,128)(2,1)S(1)}, bf16[2,128,128]{2,1,0:T(8,128)(2,1)S(1)}, u32[]{:S(2)}, u32[]{:S(2)}) collective-permute-start(bf16[2,128,128]{2,1,0:T(8,128)(2,1)S(1)} %get-tuple-element.146), channel_id=1, source_target_pairs={{0,4},{2,6},{4,0},{6,2},{8,12},{10,14},{12,8},{14,10},{1,5},{3,7},... | collective-permute-start | bytes 196616 | tf_op jit(solution)/shard_map/ppermute | solution.py:23
  52.5 2.1 %collective-permute-start.15 = (bf16[2,128,128]{2,1,0:T(8,128)(2,1)S(1)}, bf16[2,128,128]{2,1,0:T(8,128)(2,1)S(1)}, u32[]{:S(2)}, u32[]{:S(2)}) collective-permute-start(bf16[2,128,128]{2,1,0:T(8,128)(2,1)S(1)} %get-tuple-element.148), channel_id=1, source_target_pairs={{0,12},{2,14},{4,8},{6,10},{8,4},{10,6},{12,0},{14,2},{1,13},{3,15... | collective-permute-start | bytes 196616 | tf_op jit(solution)/shard_map/ppermute | solution.py:23
  54.6 4.9 %cotangent.1 = (f32[256,1024]{1,0:T(8,128)}, bf16[256,2048]{1,0:T(8,128)(2,1)}, bf16[192,256]{1,0:T(8,128)(2,1)}, bf16[64,192]{1,0:T(8,128)(2,1)}, f32[8,128]{1,0:T(8,128)}) custom-call(s32[10]{0:T(128)S(1)} %stack.43.refs_0_, f32[2,192,128]{2,1,0:T(8,128)} %bitcast.40, bf16[192,1024]{1,0:T(8,128)(2,1)} %bitcast.37, bf16[2048,1024]{1,0:T(8,128)(2,1)} %refs_1_.1, ...), custom_call_target="tpu_custom_call" | custom-call | flops 1174405120 | bytes 7004200 | tf_op jit(solution)/shard_map/cotangent/pallas_call | solution.py:138
  67.6 8.5 %forward.1 = (bf16[256,1024]{1,0:T(8,128)(2,1)S(1)}, bf16[256,512]{1,0:T(8,128)(2,1)}, f32[256,1024]{1,0:T(8,128)}, bf16[256,2048]{1,0:T(8,128)(2,1)}, bf16[2,25...) custom-call(s32[10]{0:T(128)S(1)} %stack.43.refs_0_, ...), custom_call_target="tpu_custom_call" | custom-call | flops 2147483648 | bytes 13901864 | tf_op jit(solution)/shard_map/forward/pallas_call | solution.py:138
  77.8 1.7 collective-permute-done.23.refs_6_.refs_8_
  80.3 4.5 %grads_ff.1 = (bf16[4,64,1280]{2,1,0:T(8,128)(2,1)S(1)}, bf16[4,64,1280]{2,1,0:T(8,128)(2,1)}, bf16[4,64,1152]{2,1,0:T(8,128)(2,1)}, bf16[4,64,1152]{2,1,0:T(8,128)(2,1)}, f32[8,128]{1,0:T(8,128)}) custom-call(s32[10]{0:T(128)S(1)} %stack.43.refs_0_, bf16[8,64,256]{2,1,0:T(8,128)(2,1)} %get-tuple-element.153.refs_1_, ...), custom_call_target="tpu_custom_call" | custom-call | flops 1275068416 | bytes 6881320 | tf_op jit(solution)/shard_map/grads_ff/pallas_call | solution.py:138
  84.8 1.5 collective-permute-start.28
  87.8 3.3 %down.1 = (bf16[256,1024]{1,0:T(8,128)(2,1)}, f32[8,128]{1,0:T(8,128)}) custom-call(bf16[2,256,1024]{2,1,0:T(8,128)(2,1)} %get-tuple-element.152.refs_7_.refs_0_, bf16[2048,1024]{1,0:T(8,128)(2,1)S(1)} %copy-done, f32[8,128]{1,0:T(8,128)} %get-tuple-element.159.refs_2_, bf16[256,512]{1,0:T(8,128)(2,1)} %copy-done.7), custom_call_target="tpu_custom_call" | custom-call | flops 1073741824 | bytes 5767168 | tf_op jit(solution)/shard_map/down/pallas_call | solution.py:138
  91.1 3.0 %second.1 = (f32[256,1024]{1,0:T(8,128)}, f32[1,1024]{1,0:T(1,128)}, bf16[8,128,128]{2,1,0:T(8,128)(2,1)}, bf16[8,64,256]{2,1,0:T(8,128)(2,1)}, bf16[8,64,256]{2,1,0:T(8,128)(2,1)}, /*index=5*/f32[8,128]{1,0:T(8,128)}) custom-call(s32[10]{0:T(128)S(1)} %stack.43.refs_0_, f32[256,1024]{1,0:T(8,128)S(1)} %copy-done.3, f32[256,1024]{1,0:T(8,128)S(1)} %copy-done.6, ...), custom_call_target="tpu_custom_call" | custom-call | flops 268435456 | bytes 6041640 | tf_op jit(solution)/shard_map/second/pallas_call | solution.py:138
  94.1 3.6 %all-to-all-start = ((bf16[4,2,128,128]{3,2,1,0:T(8,128)(2,1)}), bf16[4,2,128,128]{3,2,1,0:T(8,128)(2,1)S(1)}, u32[]{:S(2)}, u32[]{:S(2)}) async-start(bf16[4,2,128,128]{3,2,1,0:T(8,128)(2,1)} %bitcast.21), calls=%async_computation | async-start | bytes 524288 | tf_op jit(solution)/shard_map/all_to_all | solution.py:1259
  98.6 5.6 %collective-permute-done.29.refs_4_ = bf16[4,64,1152]{2,1,0:T(8,128)(2,1)S(1)} collective-permute-done((bf16[4,64,1152]{2,1,0:T(8,128)(2,1)}, bf16[4,64,1152]{2,1,0:T(8,128)(2,1)S(1)}, u32[]{:S(2)}, u32[]{:S(2)}) %collective-permute-start.29) | collective-permute-done | bytes 589856 | tf_op jit(solution)/shard_map/ppermute | solution.py:23
  104.3 2.6 %fold_ff.1 = (bf16[2,64,1664]{2,1,0:T(8,128)(2,1)}, bf16[2,64,1664]{2,1,0:T(8,128)(2,1)}, bf16[2,64,1152]{2,1,0:T(8,128)(2,1)}, bf16[2,64,1152]{2,1,0:T(8,128)(2,1)}, f32[8,128]{1,0:T(8,128)}) custom-call(s32[10]{0:T(128)S(1)} %stack.43.refs_0_, bf16[4,64,1280]{2,1,0:T(8,128)(2,1)} %get-tuple-element.171.refs_1_, ...), custom_call_target="tpu_custom_call" | custom-call | bytes 3932200 | tf_op jit(solution)/shard_map/fold_ff/pallas_call | solution.py:138
  108.8 7.3 %attend_back.1 = (bf16[2,3,128,128]{3,2,1,0:T(8,128)(2,1)}, bf16[2,3,128,128]{3,2,1,0:T(8,128)(2,1)}, bf16[2,3,128,128]{3,2,1,0:T(8,128)(2,1)}, bf16[2,3,128,128...) custom-call(s32[10]{0:T(128)S(1)} %stack.43.refs_0_, ...), custom_call_target="tpu_custom_call" | custom-call | flops 2147483648 | bytes 7602216 | tf_op jit(solution)/shard_map/attend_back/pallas_call | solution.py:138
  116.5 2.1 %collective-permute-done.32.refs_4_ = bf16[4,2,2,128,128]{4,3,2,1,0:T(8,128)(2,1)S(1)} collective-permute-done((bf16[4,2,2,128,128]{4,3,2,1,0:T(8,128)(2,1)}, bf16[4,2,2,128,128]{4,3,2,1,0:T(8,128)(2,1)S(1)}, u32[]{:S(2)}, u32[]{:S(2)}) %collective-permute-start.32) | collective-permute-done | bytes 524320 | tf_op jit(solution)/shard_map/ppermute | solution.py:23
  118.7 1.8 combine.1
  120.5 1.7 collective-permute-start.33
  123.1 1.7 collective-permute-start.35
  124.9 2.8 %head.1 = (f32[2,192,128]{2,1,0:T(8,128)}, bf16[8,64,256]{2,1,0:T(8,128)(2,1)}, bf16[8,64,256]{2,1,0:T(8,128)(2,1)}, f32[8,128]{1,0:T(8,128)}) custom-call(s32[10]{0:T(128)S(1)} %stack.43.refs_0_, f32[256,1024]{1,0:T(8,128)} %get-tuple-element.151.refs_1_, bf16[256,1024]{1,0:T(8,128)(2,1)} %get-tuple-element.161.refs_2_, ...), custom_call_target="tpu_custom_call" | custom-call | flops 100663296 | bytes 3211304 | tf_op jit(solution)/shard_map/head/pallas_call | solution.py:138
  127.7 2.5 %merge_ff.1 = (bf16[64,3584]{1,0:T(8,128)(2,1)}, bf16[64,3584]{1,0:T(8,128)(2,1)}, f32[8,128]{1,0:T(8,128)}) custom-call(s32[10]{0:T(128)S(1)} %stack.43.refs_0_, bf16[2,64,1664]{2,1,0:T(8,128)(2,1)} %get-tuple-element.197.refs_1_, bf16[2,64,1664]{2,1,0:T(8,128)(2,1)} %collective-permute-done.30.refs_1_.refs_2_, ...), custom_call_target="tpu_custom_call" | custom-call | bytes 2359336 | tf_op jit(solution)/shard_map/merge_ff/pallas_call | solution.py:138
  130.8 8.5 %collective-permute-done.34.refs_3_ = bf16[2,3,128,128]{3,2,1,0:T(8,128)(2,1)S(1)} collective-permute-done((bf16[2,3,128,128]{3,2,1,0:T(8,128)(2,1)S(1)}, bf16[2,3,128,128]{3,2,1,0:T(8,128)(2,1)S(1)}, u32[]{:S(2)}, u32[]{:S(2)}) %collective-permute-start.34) | collective-permute-done | bytes 196640 | tf_op jit(solution)/shard_map/ppermute | solution.py:23
  139.3 2.7 %third.1 = (bf16[256,1536]{1,0:T(8,128)(2,1)}, bf16[256,1024]{1,0:T(8,128)(2,1)}, f32[8,128]{1,0:T(8,128)}) custom-call(s32[10]{0:T(128)S(1)} %stack.43.refs_0_, bf16[2,3,128,128]{3,2,1,0:T(8,128)(2,1)S(1)} %get-tuple-element.193.refs_1_, bf16[2,3,128,128]{3,2,1,0:T(8,128)(2,1)S(1)} %collective-permute-done.33.refs_2_, ...), custom_call_target="tpu_custom_call" | custom-call | flops 805306368 | bytes 5242920 | tf_op jit(solution)/shard_map/third/pallas_call | solution.py:138
  143.4 4.3 %collective-permute-start.42 = (bf16[64,3584]{1,0:T(8,128)(2,1)}, bf16[64,3584]{1,0:T(8,128)(2,1)S(1)}, u32[]{:S(2)}, u32[]{:S(2)}) collective-permute-start(bf16[64,3584]{1,0:T(8,128)(2,1)} %get-tuple-element.222), channel_id=1, source_target_pairs={{0,8},{2,10},{4,12},{6,14},{8,0},{10,2},{12,4},{14,6},{1,9},{3,11}... | collective-permute-start | bytes 1376264 | tf_op jit(solution)/shard_map/ppermute | solution.py:23
  147.8 3.7 %grads_q.1 = (bf16[4,64,896]{2,1,0:T(8,128)(2,1)}, bf16[4,64,896]{2,1,0:T(8,128)(2,1)}, bf16[4,64,640]{2,1,0:T(8,128)(2,1)}, bf16[4,64,640]{2,1,0:T(8,128)(2,1)}, f32[8,128]{1,0:T(8,128)}) custom-call(s32[10]{0:T(128)S(1)} %stack.43.refs_0_, bf16[8,64,256]{2,1,0:T(8,128)(2,1)} %get-tuple-element.211.refs_1_, bf16[8,64,256]{2,1,0:T(8,128)(2,1)} %copy-done.14, ...), custom_call_target="tpu_custom_call" | custom-call | flops 805306368 | bytes 3670056 | tf_op jit(solution)/shard_map/grads_q/pallas_call | solution.py:138
  152.3 2.7 %grads_oh.1 = (bf16[4,64,768]{2,1,0:T(8,128)(2,1)}, bf16[4,64,768]{2,1,0:T(8,128)(2,1)}, f32[8,128]{1,0:T(8,128)}) custom-call(s32[10]{0:T(128)S(1)} %stack.43.refs_0_, bf16[8,64,256]{2,1,0:T(8,128)(2,1)} %get-tuple-element.204.refs_1_, bf16[8,64,256]{2,1,0:T(8,128)(2,1)} %collective-permute-done.37.refs_2_, bf16[256,512]{1,0:T(8,128)(2,1)} %get-tuple-element.160.refs_3_, ...), custom_call_target="tpu_custom_call" | custom-call | flops 402653184 | bytes 2555944 | tf_op jit(solution)/shard_map/grads_oh/pallas_call | solution.py:138
  156.8 4.0 %last.1 = (bf16[128,512]{1,0:T(8,128)(2,1)}, bf16[128,512]{1,0:T(8,128)(2,1)}, f32[2,192,128]{2,1,0:T(8,128)}, bf16[2,48,128]{2,1,0:T(8,128)(2,1)}, bf16[8,64,25...) custom-call(s32[10]{0:T(128)S(1)} %stack.43.refs_0_, f32[256,1024]{1,0:T(8,128)S(1)} %copy-done.5, ...), custom_call_target="tpu_custom_call" | custom-call | flops 201326592 | bytes 4657192 | tf_op jit(solution)/shard_map/last/pallas_call | solution.py:138
  160.9 7.9 %collective-permute-done.42.refs_6_ = bf16[64,3584]{1,0:T(8,128)(2,1)S(1)} collective-permute-done((bf16[64,3584]{1,0:T(8,128)(2,1)}, bf16[64,3584]{1,0:T(8,128)(2,1)S(1)}, u32[]{:S(2)}, u32[]{:S(2)}) %collective-permute-start.42) | collective-permute-done | bytes 458784 | tf_op jit(solution)/shard_map/ppermute | solution.py:23
  168.8 4.9 %collective-permute-done.41.refs_4_ = bf16[4,64,640]{2,1,0:T(8,128)(2,1)S(1)} collective-permute-done((bf16[4,64,640]{2,1,0:T(8,128)(2,1)}, bf16[4,64,640]{2,1,0:T(8,128)(2,1)S(1)}, u32[]{:S(2)}, u32[]{:S(2)}) %collective-permute-start.41) | collective-permute-done | bytes 327712 | tf_op jit(solution)/shard_map/ppermute | solution.py:23
  173.7 2.9 %fold_q.1 = (bf16[2,64,896]{2,1,0:T(8,128)(2,1)S(1)}, bf16[2,64,896]{2,1,0:T(8,128)(2,1)}, bf16[2,64,1920]{2,1,0:T(8,128)(2,1)S(1)}, bf16[2,64,1920]{2,1,0:T(8,1...) custom-call(s32[10]{0:T(128)S(1)} %stack.43.refs_0_, ...), custom_call_target="tpu_custom_call" | custom-call | bytes 5636136 | tf_op jit(solution)/shard_map/fold_q/pallas_call | solution.py:138
  177.3 2.3 %collective-permute-start.48 = (bf16[2,64,768]{2,1,0:T(8,128)(2,1)S(1)}, bf16[2,64,768]{2,1,0:T(8,128)(2,1)S(1)}, u32[]{:S(2)}, u32[]{:S(2)}) collective-permute-start(bf16[2,64,768]{2,1,0:T(8,128)(2,1)S(1)} %get-tuple-element.236), channel_id=1, source_target_pairs={{0,8},{2,10},{4,12},{6,14},{8,0},{10,2},{12,4},{14,6},{1,9},{3,11}... | collective-permute-start | bytes 589832 | tf_op jit(solution)/shard_map/ppermute | solution.py:23
  179.6 6.1 %collective-permute-done.45.refs_8_.refs_2_ = bf16[2,48,128]{2,1,0:T(8,128)(2,1)S(1)} collective-permute-done((bf16[2,48,128]{2,1,0:T(8,128)(2,1)}, bf16[2,48,128]{2,1,0:T(8,128)(2,1)S(1)}, u32[]{:S(2)}, u32[]{:S(2)}) %collective-permute-start.45) | collective-permute-done | bytes 24608 | tf_op jit(solution)/shard_map/ppermute | solution.py:29
  185.7 2.3 %collective-permute-done.48.refs_6_ = bf16[2,64,768]{2,1,0:T(8,128)(2,1)S(1)} collective-permute-done((bf16[2,64,768]{2,1,0:T(8,128)(2,1)S(1)}, bf16[2,64,768]{2,1,0:T(8,128)(2,1)S(1)}, u32[]{:S(2)}, u32[]{:S(2)}) %collective-permute-start.48) | collective-permute-done | bytes 196640 | tf_op jit(solution)/shard_map/ppermute | solution.py:23
  188.3 2.2 %merge_q.1 = (bf16[64,1792]{1,0:T(8,128)(2,1)S(1)}, bf16[64,1792]{1,0:T(8,128)(2,1)}, bf16[2,64,1536]{2,1,0:T(8,128)(2,1)}, bf16[64,1024]{1,0:T(8,128)(2,1)S(1)}...) custom-call(s32[10]{0:T(128)S(1)} %stack.43.refs_0_, ...), custom_call_target="tpu_custom_call" | custom-call | bytes 2949160 | tf_op jit(solution)/shard_map/merge_q/pallas_call | solution.py:138
  194.3 1.8 collective-permute-start.52
  197.3 2.8 %close.1 = (f32[2,192,128]{2,1,0:T(8,128)}, f32[128,512]{1,0:T(8,128)}, f32[64,2048]{1,0:T(8,128)}, f32[64,2048]{1,0:T(8,128)}, f32[8,128]{1,0:T(8,128)}) custom-call(s32[10]{0:T(128)S(1)} %stack.43.refs_0_, f32[2,192,128]{2,1,0:T(8,128)} %get-tuple-element.215.refs_1_, bf16[2,48,128]{2,1,0:T(8,128)(2,1)} %copy-done.12, ...), custom_call_target="tpu_custom_call" | custom-call | bytes 3719208 | tf_op jit(solution)/shard_map/close/pallas_call | solution.py:138
  200.1 3.0 %collective-permute-done.52.refs_1_ = bf16[64,256]{1,0:T(8,128)(2,1)S(1)} collective-permute-done((bf16[64,256]{1,0:T(8,128)(2,1)S(1)}, bf16[64,256]{1,0:T(8,128)(2,1)S(1)}, u32[]{:S(2)}, u32[]{:S(2)}) %collective-permute-start.52) | collective-permute-done | bytes 32800 | tf_op jit(solution)/shard_map/ppermute | solution.py:23
  203.1 2.0 collective-permute-done.53.refs_4_
  205.1 1.9 end.1
  (129 shorter events, 34.2 us)
Async XLA Ops:
  4.8 4.5 %collective-permute-start.1 = (f32[8,128]{1,0:T(8,128)S(1)}, f32[8,128]{1,0:T(8,128)S(1)}, u32[]{:S(2)}, u32[]{:S(2)}) collective-permute-start(f32[8,128]{1,0:T(8,128)S(1)} %add_select_fusion.3), channel_id=1, source_target_pairs={{0,4},{2,6},{4,0},{6,2},{8,12},{10,14},{12,8},{14,10},{1,5},{3,7},... | collective-permute-start | bytes 12296 | tf_op jit(solution)/shard_map/ppermute | solution.py:23
  9.4 4.6 %collective-permute-start.2 = (f32[8,128]{1,0:T(8,128)S(1)}, f32[8,128]{1,0:T(8,128)S(1)}, u32[]{:S(2)}, u32[]{:S(2)}) collective-permute-start(f32[8,128]{1,0:T(8,128)S(1)} %add_select_fusion.2), channel_id=1, source_target_pairs={{0,8},{2,10},{4,12},{6,14},{8,0},{10,2},{12,4},{14,6},{1,9},{3,11}... | collective-permute-start | bytes 12296 | tf_op jit(solution)/shard_map/ppermute | solution.py:23
  12.4 5.4 %collective-permute-start.4 = (bf16[2,48,128]{2,1,0:T(8,128)(2,1)S(1)}, bf16[2,48,128]{2,1,0:T(8,128)(2,1)S(1)}, u32[]{:S(2)}, u32[]{:S(2)}) collective-permute-start(bf16[2,48,128]{2,1,0:T(8,128)(2,1)S(1)} %get-tuple-element.136), channel_id=1, source_target_pairs={{14,0},{0,2},{2,4},{4,6},{6,8},{8,10},{10,12},{12,14},{15,1},{1,3}... | collective-permute-start | bytes 73736 | tf_op jit(solution)/shard_map/ppermute | solution.py:29
  12.4 55.2 %collective-permute-start.20 = (bf16[512,1024]{1,0:T(8,128)(2,1)}, bf16[512,1024]{1,0:T(8,128)(2,1)S(1)}, u32[]{:S(2)}, u32[]{:S(2)}) collective-permute-start(bf16[512,1024]{1,0:T(8,128)(2,1)} %refs_6_.1), channel_id=1, source_target_pairs={{0,1},{1,0},{2,3},{3,2},{4,5},{5,4},{6,7},{7,6},{8,9},{9,8},{10,11... | collective-permute-start | bytes 3145736 | tf_op jit(solution)/shard_map/ppermute | solution.py:23
  14.1 3.6 %collective-permute-start.3 = (f32[8,128]{1,0:T(8,128)S(1)}, f32[8,128]{1,0:T(8,128)S(1)}, u32[]{:S(2)}, u32[]{:S(2)}) collective-permute-start(f32[8,128]{1,0:T(8,128)S(1)} %add_select_fusion.1), channel_id=1, source_target_pairs={{0,16},{16,0},{1,17},{17,1},{2,18},{18,2},{3,19},{19,3},{4,20},{20... | collective-permute-start | bytes 12296 | tf_op jit(solution)/shard_map/ppermute | solution.py:23
  22.7 16.4 %collective-permute-start.6 = (bf16[2,3,128,128]{3,2,1,0:T(8,128)(2,1)S(1)}, bf16[2,3,128,128]{3,2,1,0:T(8,128)(2,1)S(1)}, u32[]{:S(2)}, u32[]{:S(2)}) collective-permute-start(bf16[2,3,128,128]{3,2,1,0:T(8,128)(2,1)S(1)} %get-tuple-element.139), channel_id=1, source_target_pairs={{0,8},{2,10},{4,12},{6,14},{8,0},{10,2},{12,4},{14,6},{1,9},{3,11}... | collective-permute-start | bytes 589832 | tf_op jit(solution)/shard_map/ppermute | solution.py:23
  25.6 13.4 %collective-permute-start.7 = (bf16[2,3,128,128]{3,2,1,0:T(8,128)(2,1)S(1)}, bf16[2,3,128,128]{3,2,1,0:T(8,128)(2,1)S(1)}, u32[]{:S(2)}, u32[]{:S(2)}) collective-permute-start(bf16[2,3,128,128]{3,2,1,0:T(8,128)(2,1)S(1)} %get-tuple-element.140), channel_id=1, source_target_pairs={{0,12},{2,14},{4,8},{6,10},{8,4},{10,6},{12,0},{14,2},{1,13},{3,15... | collective-permute-start | bytes 589832 | tf_op jit(solution)/shard_map/ppermute | solution.py:23
  27.0 13.4 %collective-permute-start.5 = (bf16[2,3,128,128]{3,2,1,0:T(8,128)(2,1)S(1)}, bf16[2,3,128,128]{3,2,1,0:T(8,128)(2,1)S(1)}, u32[]{:S(2)}, u32[]{:S(2)}) collective-permute-start(bf16[2,3,128,128]{3,2,1,0:T(8,128)(2,1)S(1)} %get-tuple-element.138), channel_id=1, source_target_pairs={{0,4},{2,6},{4,0},{6,2},{8,12},{10,14},{12,8},{14,10},{1,5},{3,7},... | collective-permute-start | bytes 589832 | tf_op jit(solution)/shard_map/ppermute | solution.py:23
  27.2 13.2 %collective-permute-start.8 = (bf16[2,3,128,128]{3,2,1,0:T(8,128)(2,1)S(1)}, bf16[2,3,128,128]{3,2,1,0:T(8,128)(2,1)S(1)}, u32[]{:S(2)}, u32[]{:S(2)}) collective-permute-start(bf16[2,3,128,128]{3,2,1,0:T(8,128)(2,1)S(1)} %get-tuple-element.137.refs_0_), channel_id=1, source_target_pairs={{0,2},{2,0},{4,6},{6,4},{8,10},{10,8},{12,14},{14,12},{1,3},{3,1},... | collective-permute-start | bytes 589832 | tf_op jit(solution)/shard_map/ppermute | solution.py:23
  48.5 11.6 %collective-permute-start.13 = (bf16[2,128,128]{2,1,0:T(8,128)(2,1)S(1)}, bf16[2,128,128]{2,1,0:T(8,128)(2,1)S(1)}, u32[]{:S(2)}, u32[]{:S(2)}) collective-permute-start(bf16[2,128,128]{2,1,0:T(8,128)(2,1)S(1)} %get-tuple-element.146), channel_id=1, source_target_pairs={{0,4},{2,6},{4,0},{6,2},{8,12},{10,14},{12,8},{14,10},{1,5},{3,7},... | collective-permute-start | bytes 196616 | tf_op jit(solution)/shard_map/ppermute | solution.py:23
  52.2 9.4 %collective-permute-start.14 = (bf16[2,128,128]{2,1,0:T(8,128)(2,1)S(1)}, bf16[2,128,128]{2,1,0:T(8,128)(2,1)S(1)}, u32[]{:S(2)}, u32[]{:S(2)}) collective-permute-start(bf16[2,128,128]{2,1,0:T(8,128)(2,1)S(1)} %get-tuple-element.147), channel_id=1, source_target_pairs={{0,8},{2,10},{4,12},{6,14},{8,0},{10,2},{12,4},{14,6},{1,9},{3,11}... | collective-permute-start | bytes 196616 | tf_op jit(solution)/shard_map/ppermute | solution.py:23
  52.5 9.7 %collective-permute-start.15 = (bf16[2,128,128]{2,1,0:T(8,128)(2,1)S(1)}, bf16[2,128,128]{2,1,0:T(8,128)(2,1)S(1)}, u32[]{:S(2)}, u32[]{:S(2)}) collective-permute-start(bf16[2,128,128]{2,1,0:T(8,128)(2,1)S(1)} %get-tuple-element.148), channel_id=1, source_target_pairs={{0,12},{2,14},{4,8},{6,10},{8,4},{10,6},{12,0},{14,2},{1,13},{3,15... | collective-permute-start | bytes 196616 | tf_op jit(solution)/shard_map/ppermute | solution.py:23
  59.5 5.2 %collective-permute-start.16 = (bf16[2,128,128]{2,1,0:T(8,128)(2,1)}, bf16[2,128,128]{2,1,0:T(8,128)(2,1)S(1)}, u32[]{:S(2)}, u32[]{:S(2)}) collective-permute-start(bf16[2,128,128]{2,1,0:T(8,128)(2,1)} %pin.6.refs_1_), channel_id=1, source_target_pairs={{0,1},{1,0},{2,3},{3,2},{4,5},{5,4},{6,7},{7,6},{8,9},{9,8},{10,11... | collective-permute-start | bytes 196616 | tf_op jit(solution)/shard_map/ppermute | solution.py:23
  60.1 6.1 %collective-permute-start.17 = (bf16[2,128,128]{2,1,0:T(8,128)(2,1)S(1)}, bf16[2,128,128]{2,1,0:T(8,128)(2,1)S(1)}, u32[]{:S(2)}, u32[]{:S(2)}) collective-permute-start(bf16[2,128,128]{2,1,0:T(8,128)(2,1)S(1)} %collective-permute-done.13.refs_2_), channel_id=1, source_target_pairs={{0,1},{1,0},{2,3},{3,2},{4,5},{5,4},{6,7},{7,6},{8,9},{9,8},{10,11... | collective-permute-start | bytes 196616 | tf_op jit(solution)/shard_map/ppermute | solution.py:23
  61.6 5.4 %collective-permute-start.18 = (bf16[2,128,128]{2,1,0:T(8,128)(2,1)S(1)}, bf16[2,128,128]{2,1,0:T(8,128)(2,1)S(1)}, u32[]{:S(2)}, u32[]{:S(2)}) collective-permute-start(bf16[2,128,128]{2,1,0:T(8,128)(2,1)S(1)} %collective-permute-done.14.refs_3_), channel_id=1, source_target_pairs={{0,1},{1,0},{2,3},{3,2},{4,5},{5,4},{6,7},{7,6},{8,9},{9,8},{10,11... | collective-permute-start | bytes 196616 | tf_op jit(solution)/shard_map/ppermute | solution.py:23
  62.1 5.5 %collective-permute-start.19 = (bf16[2,128,128]{2,1,0:T(8,128)(2,1)S(1)}, bf16[2,128,128]{2,1,0:T(8,128)(2,1)S(1)}, u32[]{:S(2)}, u32[]{:S(2)}) collective-permute-start(bf16[2,128,128]{2,1,0:T(8,128)(2,1)S(1)} %collective-permute-done.15.refs_4_), channel_id=1, source_target_pairs={{0,1},{1,0},{2,3},{3,2},{4,5},{5,4},{6,7},{7,6},{8,9},{9,8},{10,11... | collective-permute-start | bytes 196616 | tf_op jit(solution)/shard_map/ppermute | solution.py:23
  76.1 4.2 %collective-permute-start.22 = (bf16[256,2048]{1,0:T(8,128)(2,1)}, bf16[256,2048]{1,0:T(8,128)(2,1)S(1)}, u32[]{:S(2)}, u32[]{:S(2)}) collective-permute-start(bf16[256,2048]{1,0:T(8,128)(2,1)} %get-tuple-element.155.refs_3_), channel_id=1, source_target_pairs={{0,2},{2,0},{4,6},{6,4},{8,10},{10,8},{12,14},{14,12},{1,3},{3,1},... | collective-permute-start | bytes 3145736 | tf_op jit(solution)/shard_map/ppermute | solution.py:23
  76.2 4.1 %collective-permute-start.24 = (bf16[256,1024]{1,0:T(8,128)(2,1)}, bf16[256,1024]{1,0:T(8,128)(2,1)S(1)}, u32[]{:S(2)}, u32[]{:S(2)}) collective-permute-start(bf16[256,1024]{1,0:T(8,128)(2,1)} %get-tuple-element.157), channel_id=1, source_target_pairs={{0,2},{2,0},{4,6},{6,4},{8,10},{10,8},{12,14},{14,12},{1,3},{3,1},... | collective-permute-start | bytes 1572872 | tf_op jit(solution)/shard_map/ppermute | solution.py:23
  76.7 3.6 %collective-permute-start.21 = (bf16[8,64,256]{2,1,0:T(8,128)(2,1)}, bf16[8,64,256]{2,1,0:T(8,128)(2,1)S(1)}, u32[]{:S(2)}, u32[]{:S(2)}) collective-permute-start(bf16[8,64,256]{2,1,0:T(8,128)(2,1)} %get-tuple-element.154), channel_id=1, source_target_pairs={{0,2},{2,0},{4,6},{6,4},{8,10},{10,8},{12,14},{14,12},{1,3},{3,1},... | collective-permute-start | bytes 786440 | tf_op jit(solution)/shard_map/ppermute | solution.py:23
  76.8 14.3 %collective-permute-start.27 = (bf16[256,1024]{1,0:T(8,128)(2,1)S(1)}, bf16[256,1024]{1,0:T(8,128)(2,1)S(1)}, u32[]{:S(2)}, u32[]{:S(2)}) collective-permute-start(bf16[256,1024]{1,0:T(8,128)(2,1)S(1)} %get-tuple-element.168.refs_3_), channel_id=1, source_target_pairs={{0,1},{1,0},{2,3},{3,2},{4,5},{5,4},{6,7},{7,6},{8,9},{9,8},{10,11... | collective-permute-start | bytes 1572872 | tf_op jit(solution)/shard_map/ppermute | solution.py:23
  79.5 7.6 %collective-permute-start.25 = (bf16[256,512]{1,0:T(8,128)(2,1)}, bf16[256,512]{1,0:T(8,128)(2,1)S(1)}, u32[]{:S(2)}, u32[]{:S(2)}) collective-permute-start(bf16[256,512]{1,0:T(8,128)(2,1)} %get-tuple-element.160.refs_3_), channel_id=1, source_target_pairs={{0,2},{2,0},{4,6},{6,4},{8,10},{10,8},{12,14},{14,12},{1,3},{3,1},... | collective-permute-start | bytes 786440 | tf_op jit(solution)/shard_map/ppermute | solution.py:23
  84.8 19.5 %collective-permute-start.28 = (bf16[4,64,1280]{2,1,0:T(8,128)(2,1)S(1)}, bf16[4,64,1280]{2,1,0:T(8,128)(2,1)S(1)}, u32[]{:S(2)}, u32[]{:S(2)}) collective-permute-start(bf16[4,64,1280]{2,1,0:T(8,128)(2,1)S(1)} %get-tuple-element.172), channel_id=1, source_target_pairs={{0,16},{16,0},{1,17},{17,1},{2,18},{18,2},{3,19},{19,3},{4,20},{20... | collective-permute-start | bytes 1966088 | tf_op jit(solution)/shard_map/ppermute | solution.py:23
  86.3 18.0 %collective-permute-start.29 = (bf16[4,64,1152]{2,1,0:T(8,128)(2,1)}, bf16[4,64,1152]{2,1,0:T(8,128)(2,1)S(1)}, u32[]{:S(2)}, u32[]{:S(2)}) collective-permute-start(bf16[4,64,1152]{2,1,0:T(8,128)(2,1)} %get-tuple-element.174), channel_id=1, source_target_pairs={{0,4},{2,6},{4,0},{6,2},{8,12},{10,14},{12,8},{14,10},{1,5},{3,7},... | collective-permute-start | bytes 1769480 | tf_op jit(solution)/shard_map/ppermute | solution.py:23
  94.1 12.8 %all-to-all-start = ((bf16[4,2,128,128]{3,2,1,0:T(8,128)(2,1)}), bf16[4,2,128,128]{3,2,1,0:T(8,128)(2,1)S(1)}, u32[]{:S(2)}, u32[]{:S(2)}) async-start(bf16[4,2,128,128]{3,2,1,0:T(8,128)(2,1)} %bitcast.21), calls=%async_computation | async-start | bytes 524288 | tf_op jit(solution)/shard_map/all_to_all | solution.py:1259
  97.7 18.4 %collective-permute-start.26 = (bf16[256,1024]{1,0:T(8,128)(2,1)}, bf16[256,1024]{1,0:T(8,128)(2,1)}, u32[]{:S(2)}, u32[]{:S(2)}) collective-permute-start(bf16[256,1024]{1,0:T(8,128)(2,1)} %get-tuple-element.161.refs_2_), channel_id=1, source_target_pairs={{0,1},{1,0},{2,3},{3,2},{4,5},{5,4},{6,7},{7,6},{8,9},{9,8},{10,11... | collective-permute-start | bytes 1572872 | tf_op jit(solution)/shard_map/ppermute | solution.py:23
  107.6 8.9 %collective-permute-start.30 = (bf16[2,64,1664]{2,1,0:T(8,128)(2,1)}, bf16[2,64,1664]{2,1,0:T(8,128)(2,1)}, u32[]{:S(2)}, u32[]{:S(2)}) collective-permute-start(bf16[2,64,1664]{2,1,0:T(8,128)(2,1)} %get-tuple-element.184), channel_id=1, source_target_pairs={{0,4},{2,6},{4,0},{6,2},{8,12},{10,14},{12,8},{14,10},{1,5},{3,7},... | collective-permute-start | bytes 1277960 | tf_op jit(solution)/shard_map/ppermute | solution.py:23
  107.6 8.5 %collective-permute-start.31 = (bf16[2,64,1152]{2,1,0:T(8,128)(2,1)}, bf16[2,64,1152]{2,1,0:T(8,128)(2,1)}, u32[]{:S(2)}, u32[]{:S(2)}) collective-permute-start(bf16[2,64,1152]{2,1,0:T(8,128)(2,1)} %get-tuple-element.185), channel_id=1, source_target_pairs={{0,16},{16,0},{1,17},{17,1},{2,18},{18,2},{3,19},{19,3},{4,20},{20... | collective-permute-start | bytes 884744 | tf_op jit(solution)/shard_map/ppermute | solution.py:23
  120.5 10.4 %collective-permute-start.33 = (bf16[2,3,128,128]{3,2,1,0:T(8,128)(2,1)S(1)}, bf16[2,3,128,128]{3,2,1,0:T(8,128)(2,1)S(1)}, u32[]{:S(2)}, u32[]{:S(2)}) collective-permute-start(bf16[2,3,128,128]{3,2,1,0:T(8,128)(2,1)S(1)} %get-tuple-element.194), channel_id=1, source_target_pairs={{0,4},{2,6},{4,0},{6,2},{8,12},{10,14},{12,8},{14,10},{1,5},{3,7},... | collective-permute-start | bytes 589832 | tf_op jit(solution)/shard_map/ppermute | solution.py:23
  122.2 17.1 %collective-permute-start.34 = (bf16[2,3,128,128]{3,2,1,0:T(8,128)(2,1)S(1)}, bf16[2,3,128,128]{3,2,1,0:T(8,128)(2,1)S(1)}, u32[]{:S(2)}, u32[]{:S(2)}) collective-permute-start(bf16[2,3,128,128]{3,2,1,0:T(8,128)(2,1)S(1)} %get-tuple-element.195), channel_id=1, source_target_pairs={{0,8},{2,10},{4,12},{6,14},{8,0},{10,2},{12,4},{14,6},{1,9},{3,11}... | collective-permute-start | bytes 589832 | tf_op jit(solution)/shard_map/ppermute | solution.py:23
  123.1 16.2 %collective-permute-start.35 = (bf16[2,3,128,128]{3,2,1,0:T(8,128)(2,1)S(1)}, bf16[2,3,128,128]{3,2,1,0:T(8,128)(2,1)S(1)}, u32[]{:S(2)}, u32[]{:S(2)}) collective-permute-start(bf16[2,3,128,128]{3,2,1,0:T(8,128)(2,1)S(1)} %get-tuple-element.196), channel_id=1, source_target_pairs={{0,12},{2,14},{4,8},{6,10},{8,4},{10,6},{12,0},{14,2},{1,13},{3,15... | collective-permute-start | bytes 589832 | tf_op jit(solution)/shard_map/ppermute | solution.py:23
  142.0 5.8 %collective-permute-start.39 = (bf16[256,1536]{1,0:T(8,128)(2,1)}, bf16[256,1536]{1,0:T(8,128)(2,1)}, u32[]{:S(2)}, u32[]{:S(2)}) collective-permute-start(bf16[256,1536]{1,0:T(8,128)(2,1)} %get-tuple-element.212.refs_3_), channel_id=1, source_target_pairs={{0,2},{2,0},{4,6},{6,4},{8,10},{10,8},{12,14},{14,12},{1,3},{3,1},... | collective-permute-start | bytes 2359304 | tf_op jit(solution)/shard_map/ppermute | solution.py:23
  142.0 14.8 %collective-permute-start.36 = (bf16[256,1024]{1,0:T(8,128)(2,1)}, bf16[256,1024]{1,0:T(8,128)(2,1)S(1)}, u32[]{:S(2)}, u32[]{:S(2)}) collective-permute-start(bf16[256,1024]{1,0:T(8,128)(2,1)} %get-tuple-element.201.refs_3_), channel_id=1, source_target_pairs={{0,1},{1,0},{2,3},{3,2},{4,5},{5,4},{6,7},{7,6},{8,9},{9,8},{10,11... | collective-permute-start | bytes 1572872 | tf_op jit(solution)/shard_map/ppermute | solution.py:23
  142.9 9.4 %collective-permute-start.37 = (bf16[8,64,256]{2,1,0:T(8,128)(2,1)}, bf16[8,64,256]{2,1,0:T(8,128)(2,1)}, u32[]{:S(2)}, u32[]{:S(2)}) collective-permute-start(bf16[8,64,256]{2,1,0:T(8,128)(2,1)} %get-tuple-element.205), channel_id=1, source_target_pairs={{0,2},{2,0},{4,6},{6,4},{8,10},{10,8},{12,14},{14,12},{1,3},{3,1},... | collective-permute-start | bytes 786440 | tf_op jit(solution)/shard_map/ppermute | solution.py:23
  143.1 9.2 %collective-permute-start.38 = (bf16[8,64,256]{2,1,0:T(8,128)(2,1)}, bf16[8,64,256]{2,1,0:T(8,128)(2,1)S(1)}, u32[]{:S(2)}, u32[]{:S(2)}) collective-permute-start(bf16[8,64,256]{2,1,0:T(8,128)(2,1)} %get-tuple-element.210), channel_id=1, source_target_pairs={{0,2},{2,0},{4,6},{6,4},{8,10},{10,8},{12,14},{14,12},{1,3},{3,1},... | collective-permute-start | bytes 786440 | tf_op jit(solution)/shard_map/ppermute | solution.py:23
  143.4 25.3 %collective-permute-start.42 = (bf16[64,3584]{1,0:T(8,128)(2,1)}, bf16[64,3584]{1,0:T(8,128)(2,1)S(1)}, u32[]{:S(2)}, u32[]{:S(2)}) collective-permute-start(bf16[64,3584]{1,0:T(8,128)(2,1)} %get-tuple-element.222), channel_id=1, source_target_pairs={{0,8},{2,10},{4,12},{6,14},{8,0},{10,2},{12,4},{14,6},{1,9},{3,11}... | collective-permute-start | bytes 1376264 | tf_op jit(solution)/shard_map/ppermute | solution.py:23
  151.5 22.2 %collective-permute-start.40 = (bf16[4,64,896]{2,1,0:T(8,128)(2,1)}, bf16[4,64,896]{2,1,0:T(8,128)(2,1)S(1)}, u32[]{:S(2)}, u32[]{:S(2)}) collective-permute-start(bf16[4,64,896]{2,1,0:T(8,128)(2,1)} %get-tuple-element.218), channel_id=1, source_target_pairs={{0,16},{16,0},{1,17},{17,1},{2,18},{18,2},{3,19},{19,3},{4,20},{20... | collective-permute-start | bytes 1376264 | tf_op jit(solution)/shard_map/ppermute | solution.py:23
  155.0 18.7 %collective-permute-start.43 = (bf16[4,64,768]{2,1,0:T(8,128)(2,1)}, bf16[4,64,768]{2,1,0:T(8,128)(2,1)S(1)}, u32[]{:S(2)}, u32[]{:S(2)}) collective-permute-start(bf16[4,64,768]{2,1,0:T(8,128)(2,1)} %get-tuple-element.224), channel_id=1, source_target_pairs={{0,16},{16,0},{1,17},{17,1},{2,18},{18,2},{3,19},{19,3},{4,20},{20... | collective-permute-start | bytes 1179656 | tf_op jit(solution)/shard_map/ppermute | solution.py:23
  156.3 17.4 %collective-permute-start.41 = (bf16[4,64,640]{2,1,0:T(8,128)(2,1)}, bf16[4,64,640]{2,1,0:T(8,128)(2,1)S(1)}, u32[]{:S(2)}, u32[]{:S(2)}) collective-permute-start(bf16[4,64,640]{2,1,0:T(8,128)(2,1)} %get-tuple-element.220), channel_id=1, source_target_pairs={{0,4},{2,6},{4,0},{6,2},{8,12},{10,14},{12,8},{14,10},{1,5},{3,7},... | collective-permute-start | bytes 983048 | tf_op jit(solution)/shard_map/ppermute | solution.py:23
  160.9 7.9 %collective-permute-start.44 = (bf16[8,64,256]{2,1,0:T(8,128)(2,1)}, bf16[8,64,256]{2,1,0:T(8,128)(2,1)S(1)}, u32[]{:S(2)}, u32[]{:S(2)}) collective-permute-start(bf16[8,64,256]{2,1,0:T(8,128)(2,1)} %get-tuple-element.226), channel_id=1, source_target_pairs={{0,2},{2,0},{4,6},{6,4},{8,10},{10,8},{12,14},{14,12},{1,3},{3,1},... | collective-permute-start | bytes 786440 | tf_op jit(solution)/shard_map/ppermute | solution.py:23
  176.6 11.7 %collective-permute-start.47 = (bf16[2,64,1920]{2,1,0:T(8,128)(2,1)S(1)}, bf16[2,64,1920]{2,1,0:T(8,128)(2,1)S(1)}, u32[]{:S(2)}, u32[]{:S(2)}) collective-permute-start(bf16[2,64,1920]{2,1,0:T(8,128)(2,1)S(1)} %get-tuple-element.234), channel_id=1, source_target_pairs={{0,16},{16,0},{1,17},{17,1},{2,18},{18,2},{3,19},{19,3},{4,20},{20... | collective-permute-start | bytes 1474568 | tf_op jit(solution)/shard_map/ppermute | solution.py:23
  177.3 10.7 %collective-permute-start.46 = (bf16[2,64,896]{2,1,0:T(8,128)(2,1)S(1)}, bf16[2,64,896]{2,1,0:T(8,128)(2,1)S(1)}, u32[]{:S(2)}, u32[]{:S(2)}) collective-permute-start(bf16[2,64,896]{2,1,0:T(8,128)(2,1)S(1)} %get-tuple-element.232), channel_id=1, source_target_pairs={{0,4},{2,6},{4,0},{6,2},{8,12},{10,14},{12,8},{14,10},{1,5},{3,7},... | collective-permute-start | bytes 688136 | tf_op jit(solution)/shard_map/ppermute | solution.py:23
  177.3 10.7 %collective-permute-start.48 = (bf16[2,64,768]{2,1,0:T(8,128)(2,1)S(1)}, bf16[2,64,768]{2,1,0:T(8,128)(2,1)S(1)}, u32[]{:S(2)}, u32[]{:S(2)}) collective-permute-start(bf16[2,64,768]{2,1,0:T(8,128)(2,1)S(1)} %get-tuple-element.236), channel_id=1, source_target_pairs={{0,8},{2,10},{4,12},{6,14},{8,0},{10,2},{12,4},{14,6},{1,9},{3,11}... | collective-permute-start | bytes 589832 | tf_op jit(solution)/shard_map/ppermute | solution.py:23
  179.6 6.1 %collective-permute-start.45 = (bf16[2,48,128]{2,1,0:T(8,128)(2,1)}, bf16[2,48,128]{2,1,0:T(8,128)(2,1)S(1)}, u32[]{:S(2)}, u32[]{:S(2)}) collective-permute-start(bf16[2,48,128]{2,1,0:T(8,128)(2,1)} %pin.10), channel_id=1, source_target_pairs={{2,0},{4,2},{6,4},{8,6},{10,8},{12,10},{14,12},{0,14},{3,1},{5,3},... | collective-permute-start | bytes 73736 | tf_op jit(solution)/shard_map/ppermute | solution.py:29
  190.5 6.8 %collective-permute-start.50 = (bf16[2,64,1536]{2,1,0:T(8,128)(2,1)}, bf16[2,64,1536]{2,1,0:T(8,128)(2,1)S(1)}, u32[]{:S(2)}, u32[]{:S(2)}) collective-permute-start(bf16[2,64,1536]{2,1,0:T(8,128)(2,1)} %get-tuple-element.239.refs_8_), channel_id=1, source_target_pairs={{0,2},{2,0},{4,6},{6,4},{8,10},{10,8},{12,14},{14,12},{1,3},{3,1},... | collective-permute-start | bytes 1179656 | tf_op jit(solution)/shard_map/ppermute | solution.py:23
  190.5 14.6 %collective-permute-start.53 = (bf16[64,1792]{1,0:T(8,128)(2,1)S(1)}, bf16[64,1792]{1,0:T(8,128)(2,1)S(1)}, u32[]{:S(2)}, u32[]{:S(2)}) collective-permute-start(bf16[64,1792]{1,0:T(8,128)(2,1)S(1)} %get-tuple-element.245), channel_id=1, source_target_pairs={{0,8},{2,10},{4,12},{6,14},{8,0},{10,2},{12,4},{14,6},{1,9},{3,11}... | collective-permute-start | bytes 688136 | tf_op jit(solution)/shard_map/ppermute | solution.py:23
  191.6 5.7 %collective-permute-start.49 = (bf16[128,512]{1,0:T(8,128)(2,1)}, bf16[128,512]{1,0:T(8,128)(2,1)S(1)}, u32[]{:S(2)}, u32[]{:S(2)}) collective-permute-start(bf16[128,512]{1,0:T(8,128)(2,1)} %pin.11), channel_id=1, source_target_pairs={{0,16},{16,0},{1,17},{17,1},{2,18},{18,2},{3,19},{19,3},{4,20},{20... | collective-permute-start | bytes 393224 | tf_op jit(solution)/shard_map/ppermute | solution.py:23
  192.8 10.3 %collective-permute-start.51 = (bf16[64,1024]{1,0:T(8,128)(2,1)S(1)}, bf16[64,1024]{1,0:T(8,128)(2,1)S(1)}, u32[]{:S(2)}, u32[]{:S(2)}) collective-permute-start(bf16[64,1024]{1,0:T(8,128)(2,1)S(1)} %get-tuple-element.241), channel_id=1, source_target_pairs={{0,4},{2,6},{4,0},{6,2},{8,12},{10,14},{12,8},{14,10},{1,5},{3,7},... | collective-permute-start | bytes 393224 | tf_op jit(solution)/shard_map/ppermute | solution.py:23
  194.3 8.8 %collective-permute-start.52 = (bf16[64,256]{1,0:T(8,128)(2,1)S(1)}, bf16[64,256]{1,0:T(8,128)(2,1)S(1)}, u32[]{:S(2)}, u32[]{:S(2)}) collective-permute-start(bf16[64,256]{1,0:T(8,128)(2,1)S(1)} %get-tuple-element.242), channel_id=1, source_target_pairs={{0,12},{2,14},{4,8},{6,10},{8,4},{10,6},{12,0},{14,2},{1,13},{3,15... | collective-permute-start | bytes 98312 | tf_op jit(solution)/shard_map/ppermute | solution.py:23
  (22 other events, 172.6 us)

commit v7 on v6

--- a/solution.py
+++ b/solution.py
@@ -1335,7 +1335,7 @@
         send_a, keep_a, send_b, keep_b, token = call(
             grads_q_kernel,
             "grads_q",
-            [first, first, second, second],
+            [Warm(first), first, Warm(second), second],
             ids, normed_one[0], normed_got, d_qkv, Warm(swap(d_qkv, "lon", 1)),
             after=[token],
             scratch=[pltpu.VMEM((parts, rows, 3 * local_width), BF)],
@@ -1361,7 +1361,7 @@
             *[shape((item_tokens, width // 2))] * 2,
             shape((items, variables * columns, height), F32),
             shape((items, variables, height)),
-            *([shape((parts, rows, 2 * LANES))] * 2 if paired else [shape((width, 2 * LANES))]),
+            *([shape((parts, rows, 2 * LANES)), warm((parts, rows, 2 * LANES))] if paired else [shape((width, 2 * LANES))]),
         ],
         ids, Warm(hidden_zero), Warm(d_one), Warm(d_norm), Warm(d_norm_got), gains, gain_two, patches, w_embed,
         after=[token],

time: 208 us -> 207 us (level)
  no operation moved by 1% of the time
where the time goes in v7:
time: 207 us
  Pallas kernels  77.2 us (37%)
  waiting for transfers between devices  69.2 us (33%)
  starting transfers between devices  56.8 us (27%)
  local copies, waits for them, and re-layouts  2.17 us (1%)
    pallas_call x21, Pallas kernels, call(): pl.pallas_call(with_token, grid=grid, out_shape=[*[o.value if isinstance(...  77.2 us
    ppermute x52, waiting for transfers between devices, swap(): return lax.ppermute(block, axis, route)  63.1 us
    ppermute x52, starting transfers between devices, swap(): return lax.ppermute(block, axis, route)  53.2 us
    ppermute x2, waiting for transfers between devices, from_behind(): return lax.ppermute(block, axis, route)  6.12 us
  transfers between devices with their start and end apart: 55, of which 27 were waited for; matrix products, arithmetic and copies ran while one was open for 0% of the time, Pallas kernels for 27%

profile of v7, /device:TPU:0, one launch (start us, length us, event | category | flops | bytes accessed | tf_op | source)
XLA Modules:
  0.0 206.6 jit_solution(6323942510499642676)
XLA Ops:
  1.3 2.1 %moments.1 = (f32[2,192,128]{2,1,0:T(8,128)S(1)}, bf16[2,48,128]{2,1,0:T(8,128)(2,1)S(1)}, f32[8,128]{1,0:T(8,128)S(1)}, f32[8,128]{1,0:T(8,128)}) custom-call(s32[2]{0:T(128)S(1)} %copy-done.10, f32[12,192,128]{2,1,0:T(8,128)} %bitcast.39), custom_call_target="tpu_custom_call" | custom-call | bytes 1404936 | tf_op jit(solution)/shard_map/moments/pallas_call | solution.py:138
  4.8 2.9 %collective-permute-start.1 = (f32[8,128]{1,0:T(8,128)S(1)}, f32[8,128]{1,0:T(8,128)S(1)}, u32[]{:S(2)}, u32[]{:S(2)}) collective-permute-start(f32[8,128]{1,0:T(8,128)S(1)} %add_select_fusion.3), channel_id=1, source_target_pairs={{0,4},{2,6},{4,0},{6,2},{8,12},{10,14},{12,8},{14,10},{1,5},{3,7},... | collective-permute-start | bytes 12296 | tf_op jit(solution)/shard_map/ppermute | solution.py:23
  7.7 1.6 collective-permute-done.1
  9.4 3.0 %collective-permute-start.2 = (f32[8,128]{1,0:T(8,128)S(1)}, f32[8,128]{1,0:T(8,128)S(1)}, u32[]{:S(2)}, u32[]{:S(2)}) collective-permute-start(f32[8,128]{1,0:T(8,128)S(1)} %add_select_fusion.2), channel_id=1, source_target_pairs={{0,8},{2,10},{4,12},{6,14},{8,0},{10,2},{12,4},{14,6},{1,9},{3,11}... | collective-permute-start | bytes 12296 | tf_op jit(solution)/shard_map/ppermute | solution.py:23
  12.4 1.5 collective-permute-start.20
  14.1 1.8 collective-permute-start.3
  16.0 1.7 collective-permute-done.3
  17.8 4.8 %start.1 = (f32[1,48]{1,0:T(1,128)}, f32[1,48]{1,0:T(1,128)}, f32[1,48]{1,0:T(1,128)}, f32[256,1024]{1,0:T(8,128)}, bf16[192,256]{1,0:T(8,128)(2,1)}, /*index=5*...) custom-call(s32[10]{0:T(128)S(1)} %stack.43.refs_0_, ...), custom_call_target="tpu_custom_call" | custom-call | flops 905969664 | bytes 6493352 | tf_op jit(solution)/shard_map/start/pallas_call | solution.py:138
  22.7 3.0 %collective-permute-start.6 = (bf16[2,3,128,128]{3,2,1,0:T(8,128)(2,1)S(1)}, bf16[2,3,128,128]{3,2,1,0:T(8,128)(2,1)S(1)}, u32[]{:S(2)}, u32[]{:S(2)}) collective-permute-start(bf16[2,3,128,128]{3,2,1,0:T(8,128)(2,1)S(1)} %get-tuple-element.139), channel_id=1, source_target_pairs={{0,8},{2,10},{4,12},{6,14},{8,0},{10,2},{12,4},{14,6},{1,9},{3,11}... | collective-permute-start | bytes 589832 | tf_op jit(solution)/shard_map/ppermute | solution.py:23
  27.2 11.8 %collective-permute-done.6.refs_2_ = bf16[2,3,128,128]{3,2,1,0:T(8,128)(2,1)S(1)} collective-permute-done((bf16[2,3,128,128]{3,2,1,0:T(8,128)(2,1)S(1)}, bf16[2,3,128,128]{3,2,1,0:T(8,128)(2,1)S(1)}, u32[]{:S(2)}, u32[]{:S(2)}) %collective-permute-start.6) | collective-permute-done | bytes 196640 | tf_op jit(solution)/shard_map/ppermute | solution.py:23
  42.1 6.4 %attend.1 = (bf16[2,128,128]{2,1,0:T(8,128)(2,1)}, bf16[2,128,128]{2,1,0:T(8,128)(2,1)S(1)}, bf16[2,128,128]{2,1,0:T(8,128)(2,1)S(1)}, bf16[2,128,128]{2,1,0:T(8...) custom-call(bf16[2,3,128,128]{3,2,1,0:T(8,128)(2,1)S(1)} %get-tuple-, ...), custom_call_target="tpu_custom_call" | custom-call | flops 1073741824 | bytes 7864320 | tf_op jit(solution)/shard_map/attend/pallas_call | solution.py:138
  48.5 3.7 %collective-permute-start.13 = (bf16[2,128,128]{2,1,0:T(8,128)(2,1)S(1)}, bf16[2,128,128]{2,1,0:T(8,128)(2,1)S(1)}, u32[]{:S(2)}, u32[]{:S(2)}) collective-permute-start(bf16[2,128,128]{2,1,0:T(8,128)(2,1)S(1)} %get-tuple-element.146), channel_id=1, source_target_pairs={{0,4},{2,6},{4,0},{6,2},{8,12},{10,14},{12,8},{14,10},{1,5},{3,7},... | collective-permute-start | bytes 196616 | tf_op jit(solution)/shard_map/ppermute | solution.py:23
  52.5 2.1 %collective-permute-start.15 = (bf16[2,128,128]{2,1,0:T(8,128)(2,1)S(1)}, bf16[2,128,128]{2,1,0:T(8,128)(2,1)S(1)}, u32[]{:S(2)}, u32[]{:S(2)}) collective-permute-start(bf16[2,128,128]{2,1,0:T(8,128)(2,1)S(1)} %get-tuple-element.148), channel_id=1, source_target_pairs={{0,12},{2,14},{4,8},{6,10},{8,4},{10,6},{12,0},{14,2},{1,13},{3,15... | collective-permute-start | bytes 196616 | tf_op jit(solution)/shard_map/ppermute | solution.py:23
  54.6 4.9 %cotangent.1 = (f32[256,1024]{1,0:T(8,128)}, bf16[256,2048]{1,0:T(8,128)(2,1)}, bf16[192,256]{1,0:T(8,128)(2,1)}, bf16[64,192]{1,0:T(8,128)(2,1)}, f32[8,128]{1,0:T(8,128)}) custom-call(s32[10]{0:T(128)S(1)} %stack.43.refs_0_, f32[2,192,128]{2,1,0:T(8,128)} %bitcast.40, bf16[192,1024]{1,0:T(8,128)(2,1)} %bitcast.37, bf16[2048,1024]{1,0:T(8,128)(2,1)} %refs_1_.1, ...), custom_call_target="tpu_custom_call" | custom-call | flops 1174405120 | bytes 7004200 | tf_op jit(solution)/shard_map/cotangent/pallas_call | solution.py:138
  67.6 8.5 %forward.1 = (bf16[256,1024]{1,0:T(8,128)(2,1)S(1)}, bf16[256,512]{1,0:T(8,128)(2,1)}, f32[256,1024]{1,0:T(8,128)}, bf16[256,2048]{1,0:T(8,128)(2,1)}, bf16[2,25...) custom-call(s32[10]{0:T(128)S(1)} %stack.43.refs_0_, ...), custom_call_target="tpu_custom_call" | custom-call | flops 2147483648 | bytes 13901864 | tf_op jit(solution)/shard_map/forward/pallas_call | solution.py:138
  77.8 1.7 collective-permute-done.23.refs_6_.refs_8_
  80.3 4.5 %grads_ff.1 = (bf16[4,64,1280]{2,1,0:T(8,128)(2,1)S(1)}, bf16[4,64,1280]{2,1,0:T(8,128)(2,1)}, bf16[4,64,1152]{2,1,0:T(8,128)(2,1)}, bf16[4,64,1152]{2,1,0:T(8,128)(2,1)}, f32[8,128]{1,0:T(8,128)}) custom-call(s32[10]{0:T(128)S(1)} %stack.43.refs_0_, bf16[8,64,256]{2,1,0:T(8,128)(2,1)} %get-tuple-element.153.refs_1_, ...), custom_call_target="tpu_custom_call" | custom-call | flops 1275068416 | bytes 6881320 | tf_op jit(solution)/shard_map/grads_ff/pallas_call | solution.py:138
  84.8 1.5 collective-permute-start.28
  87.8 3.3 %down.1 = (bf16[256,1024]{1,0:T(8,128)(2,1)}, f32[8,128]{1,0:T(8,128)}) custom-call(bf16[2,256,1024]{2,1,0:T(8,128)(2,1)} %get-tuple-element.152.refs_7_.refs_0_, bf16[2048,1024]{1,0:T(8,128)(2,1)S(1)} %copy-done, f32[8,128]{1,0:T(8,128)} %get-tuple-element.159.refs_2_, bf16[256,512]{1,0:T(8,128)(2,1)} %copy-done.7), custom_call_target="tpu_custom_call" | custom-call | flops 1073741824 | bytes 5767168 | tf_op jit(solution)/shard_map/down/pallas_call | solution.py:138
  91.1 3.0 %second.1 = (f32[256,1024]{1,0:T(8,128)}, f32[1,1024]{1,0:T(1,128)}, bf16[8,128,128]{2,1,0:T(8,128)(2,1)}, bf16[8,64,256]{2,1,0:T(8,128)(2,1)}, bf16[8,64,256]{2,1,0:T(8,128)(2,1)}, /*index=5*/f32[8,128]{1,0:T(8,128)}) custom-call(s32[10]{0:T(128)S(1)} %stack.43.refs_0_, f32[256,1024]{1,0:T(8,128)S(1)} %copy-done.3, f32[256,1024]{1,0:T(8,128)S(1)} %copy-done.6, ...), custom_call_target="tpu_custom_call" | custom-call | flops 268435456 | bytes 6041640 | tf_op jit(solution)/shard_map/second/pallas_call | solution.py:138
  94.1 3.6 %all-to-all-start = ((bf16[4,2,128,128]{3,2,1,0:T(8,128)(2,1)}), bf16[4,2,128,128]{3,2,1,0:T(8,128)(2,1)S(1)}, u32[]{:S(2)}, u32[]{:S(2)}) async-start(bf16[4,2,128,128]{3,2,1,0:T(8,128)(2,1)} %bitcast.21), calls=%async_computation | async-start | bytes 524288 | tf_op jit(solution)/shard_map/all_to_all | solution.py:1259
  98.6 5.6 %collective-permute-done.29.refs_4_ = bf16[4,64,1152]{2,1,0:T(8,128)(2,1)S(1)} collective-permute-done((bf16[4,64,1152]{2,1,0:T(8,128)(2,1)}, bf16[4,64,1152]{2,1,0:T(8,128)(2,1)S(1)}, u32[]{:S(2)}, u32[]{:S(2)}) %collective-permute-start.29) | collective-permute-done | bytes 589856 | tf_op jit(solution)/shard_map/ppermute | solution.py:23
  104.3 2.6 %fold_ff.1 = (bf16[2,64,1664]{2,1,0:T(8,128)(2,1)}, bf16[2,64,1664]{2,1,0:T(8,128)(2,1)}, bf16[2,64,1152]{2,1,0:T(8,128)(2,1)}, bf16[2,64,1152]{2,1,0:T(8,128)(2,1)}, f32[8,128]{1,0:T(8,128)}) custom-call(s32[10]{0:T(128)S(1)} %stack.43.refs_0_, bf16[4,64,1280]{2,1,0:T(8,128)(2,1)} %get-tuple-element.171.refs_1_, ...), custom_call_target="tpu_custom_call" | custom-call | bytes 3932200 | tf_op jit(solution)/shard_map/fold_ff/pallas_call | solution.py:138
  108.8 7.3 %attend_back.1 = (bf16[2,3,128,128]{3,2,1,0:T(8,128)(2,1)}, bf16[2,3,128,128]{3,2,1,0:T(8,128)(2,1)}, bf16[2,3,128,128]{3,2,1,0:T(8,128)(2,1)}, bf16[2,3,128,128...) custom-call(s32[10]{0:T(128)S(1)} %stack.43.refs_0_, ...), custom_call_target="tpu_custom_call" | custom-call | flops 2147483648 | bytes 7602216 | tf_op jit(solution)/shard_map/attend_back/pallas_call | solution.py:138
  116.5 2.1 %collective-permute-done.32.refs_4_ = bf16[4,2,2,128,128]{4,3,2,1,0:T(8,128)(2,1)S(1)} collective-permute-done((bf16[4,2,2,128,128]{4,3,2,1,0:T(8,128)(2,1)}, bf16[4,2,2,128,128]{4,3,2,1,0:T(8,128)(2,1)S(1)}, u32[]{:S(2)}, u32[]{:S(2)}) %collective-permute-start.32) | collective-permute-done | bytes 524320 | tf_op jit(solution)/shard_map/ppermute | solution.py:23
  118.7 1.8 combine.1
  120.5 1.7 collective-permute-start.33
  123.1 1.7 collective-permute-start.35
  124.9 2.8 %head.1 = (f32[2,192,128]{2,1,0:T(8,128)}, bf16[8,64,256]{2,1,0:T(8,128)(2,1)}, bf16[8,64,256]{2,1,0:T(8,128)(2,1)}, f32[8,128]{1,0:T(8,128)}) custom-call(s32[10]{0:T(128)S(1)} %stack.43.refs_0_, f32[256,1024]{1,0:T(8,128)} %get-tuple-element.151.refs_1_, bf16[256,1024]{1,0:T(8,128)(2,1)} %get-tuple-element.161.refs_2_, ...), custom_call_target="tpu_custom_call" | custom-call | flops 100663296 | bytes 3211304 | tf_op jit(solution)/shard_map/head/pallas_call | solution.py:138
  127.7 2.5 %merge_ff.1 = (bf16[64,3584]{1,0:T(8,128)(2,1)}, bf16[64,3584]{1,0:T(8,128)(2,1)}, f32[8,128]{1,0:T(8,128)}) custom-call(s32[10]{0:T(128)S(1)} %stack.43.refs_0_, bf16[2,64,1664]{2,1,0:T(8,128)(2,1)} %get-tuple-element.197.refs_1_, bf16[2,64,1664]{2,1,0:T(8,128)(2,1)} %collective-permute-done.30.refs_1_.refs_2_, ...), custom_call_target="tpu_custom_call" | custom-call | bytes 2359336 | tf_op jit(solution)/shard_map/merge_ff/pallas_call | solution.py:138
  130.8 8.5 %collective-permute-done.34.refs_3_ = bf16[2,3,128,128]{3,2,1,0:T(8,128)(2,1)S(1)} collective-permute-done((bf16[2,3,128,128]{3,2,1,0:T(8,128)(2,1)S(1)}, bf16[2,3,128,128]{3,2,1,0:T(8,128)(2,1)S(1)}, u32[]{:S(2)}, u32[]{:S(2)}) %collective-permute-start.34) | collective-permute-done | bytes 196640 | tf_op jit(solution)/shard_map/ppermute | solution.py:23
  139.3 2.7 %third.1 = (bf16[256,1536]{1,0:T(8,128)(2,1)}, bf16[256,1024]{1,0:T(8,128)(2,1)}, f32[8,128]{1,0:T(8,128)}) custom-call(s32[10]{0:T(128)S(1)} %stack.43.refs_0_, bf16[2,3,128,128]{3,2,1,0:T(8,128)(2,1)S(1)} %get-tuple-element.193.refs_1_, bf16[2,3,128,128]{3,2,1,0:T(8,128)(2,1)S(1)} %collective-permute-done.33.refs_2_, ...), custom_call_target="tpu_custom_call" | custom-call | flops 805306368 | bytes 5242920 | tf_op jit(solution)/shard_map/third/pallas_call | solution.py:138
  143.4 4.3 %collective-permute-start.42 = (bf16[64,3584]{1,0:T(8,128)(2,1)}, bf16[64,3584]{1,0:T(8,128)(2,1)S(1)}, u32[]{:S(2)}, u32[]{:S(2)}) collective-permute-start(bf16[64,3584]{1,0:T(8,128)(2,1)} %get-tuple-element.222), channel_id=1, source_target_pairs={{0,8},{2,10},{4,12},{6,14},{8,0},{10,2},{12,4},{14,6},{1,9},{3,11}... | collective-permute-start | bytes 1376264 | tf_op jit(solution)/shard_map/ppermute | solution.py:23
  147.8 3.4 %grads_q.1 = (bf16[4,64,896]{2,1,0:T(8,128)(2,1)S(1)}, bf16[4,64,896]{2,1,0:T(8,128)(2,1)}, bf16[4,64,640]{2,1,0:T(8,128)(2,1)S(1)}, bf16[4,64,640]{2,1,0:T(8,128)(2,1)}, f32[8,128]{1,0:T(8,128)}) custom-call(s32[10]{0:T(128)S(1)} %stack.43.refs_0_, bf16[8,64,256]{2,1,0:T(8,128)(2,1)} %get-tuple-element.211.refs_1_, bf16[8,64,256]{2,1,0:T(8,128)(2,1)} %copy-done.14, ...), custom_call_target="tpu_custom_call" | custom-call | flops 805306368 | bytes 3670056 | tf_op jit(solution)/shard_map/grads_q/pallas_call | solution.py:138
  152.0 2.7 %grads_oh.1 = (bf16[4,64,768]{2,1,0:T(8,128)(2,1)}, bf16[4,64,768]{2,1,0:T(8,128)(2,1)}, f32[8,128]{1,0:T(8,128)}) custom-call(s32[10]{0:T(128)S(1)} %stack.43.refs_0_, bf16[8,64,256]{2,1,0:T(8,128)(2,1)} %get-tuple-element.204.refs_1_, bf16[8,64,256]{2,1,0:T(8,128)(2,1)} %collective-permute-done.37.refs_2_, bf16[256,512]{1,0:T(8,128)(2,1)} %get-tuple-element.160.refs_3_, ...), custom_call_target="tpu_custom_call" | custom-call | flops 402653184 | bytes 2555944 | tf_op jit(solution)/shard_map/grads_oh/pallas_call | solution.py:138
  156.6 3.9 %last.1 = (bf16[128,512]{1,0:T(8,128)(2,1)}, bf16[128,512]{1,0:T(8,128)(2,1)}, f32[2,192,128]{2,1,0:T(8,128)}, bf16[2,48,128]{2,1,0:T(8,128)(2,1)}, bf16[8,64,25...) custom-call(s32[10]{0:T(128)S(1)} %stack.43.refs_0_, f32[256,1024]{1,0:T(8,128)S(1)} %copy-done.5, ...), custom_call_target="tpu_custom_call" | custom-call | flops 201326592 | bytes 4657192 | tf_op jit(solution)/shard_map/last/pallas_call | solution.py:138
  160.5 8.2 %collective-permute-done.42.refs_6_ = bf16[64,3584]{1,0:T(8,128)(2,1)S(1)} collective-permute-done((bf16[64,3584]{1,0:T(8,128)(2,1)}, bf16[64,3584]{1,0:T(8,128)(2,1)S(1)}, u32[]{:S(2)}, u32[]{:S(2)}) %collective-permute-start.42) | collective-permute-done | bytes 458784 | tf_op jit(solution)/shard_map/ppermute | solution.py:23
  168.8 4.4 %collective-permute-done.41.refs_4_ = bf16[4,64,640]{2,1,0:T(8,128)(2,1)S(1)} collective-permute-done((bf16[4,64,640]{2,1,0:T(8,128)(2,1)S(1)}, bf16[4,64,640]{2,1,0:T(8,128)(2,1)S(1)}, u32[]{:S(2)}, u32[]{:S(2)}) %collective-permute-start.41) | collective-permute-done | bytes 327712 | tf_op jit(solution)/shard_map/ppermute | solution.py:23
  173.2 2.9 %fold_q.1 = (bf16[2,64,896]{2,1,0:T(8,128)(2,1)S(1)}, bf16[2,64,896]{2,1,0:T(8,128)(2,1)}, bf16[2,64,1920]{2,1,0:T(8,128)(2,1)S(1)}, bf16[2,64,1920]{2,1,0:T(8,1...) custom-call(s32[10]{0:T(128)S(1)} %stack.43.refs_0_, ...), custom_call_target="tpu_custom_call" | custom-call | bytes 5636136 | tf_op jit(solution)/shard_map/fold_q/pallas_call | solution.py:138
  176.8 2.3 %collective-permute-start.48 = (bf16[2,64,768]{2,1,0:T(8,128)(2,1)S(1)}, bf16[2,64,768]{2,1,0:T(8,128)(2,1)S(1)}, u32[]{:S(2)}, u32[]{:S(2)}) collective-permute-start(bf16[2,64,768]{2,1,0:T(8,128)(2,1)S(1)} %get-tuple-element.236), channel_id=1, source_target_pairs={{0,8},{2,10},{4,12},{6,14},{8,0},{10,2},{12,4},{14,6},{1,9},{3,11}... | collective-permute-start | bytes 589832 | tf_op jit(solution)/shard_map/ppermute | solution.py:23
  179.1 6.1 %collective-permute-done.45.refs_8_.refs_2_ = bf16[2,48,128]{2,1,0:T(8,128)(2,1)S(1)} collective-permute-done((bf16[2,48,128]{2,1,0:T(8,128)(2,1)}, bf16[2,48,128]{2,1,0:T(8,128)(2,1)S(1)}, u32[]{:S(2)}, u32[]{:S(2)}) %collective-permute-start.45) | collective-permute-done | bytes 24608 | tf_op jit(solution)/shard_map/ppermute | solution.py:29
  185.2 2.3 %collective-permute-done.48.refs_6_ = bf16[2,64,768]{2,1,0:T(8,128)(2,1)S(1)} collective-permute-done((bf16[2,64,768]{2,1,0:T(8,128)(2,1)S(1)}, bf16[2,64,768]{2,1,0:T(8,128)(2,1)S(1)}, u32[]{:S(2)}, u32[]{:S(2)}) %collective-permute-start.48) | collective-permute-done | bytes 196640 | tf_op jit(solution)/shard_map/ppermute | solution.py:23
  187.7 2.2 %merge_q.1 = (bf16[64,1792]{1,0:T(8,128)(2,1)S(1)}, bf16[64,1792]{1,0:T(8,128)(2,1)}, bf16[2,64,1536]{2,1,0:T(8,128)(2,1)}, bf16[64,1024]{1,0:T(8,128)(2,1)S(1)}...) custom-call(s32[10]{0:T(128)S(1)} %stack.43.refs_0_, ...), custom_call_target="tpu_custom_call" | custom-call | bytes 2949160 | tf_op jit(solution)/shard_map/merge_q/pallas_call | solution.py:138
  193.8 1.6 collective-permute-start.52
  196.8 2.8 %close.1 = (f32[2,192,128]{2,1,0:T(8,128)}, f32[128,512]{1,0:T(8,128)}, f32[64,2048]{1,0:T(8,128)}, f32[64,2048]{1,0:T(8,128)}, f32[8,128]{1,0:T(8,128)}) custom-call(s32[10]{0:T(128)S(1)} %stack.43.refs_0_, f32[2,192,128]{2,1,0:T(8,128)} %get-tuple-element.215.refs_1_, bf16[2,48,128]{2,1,0:T(8,128)(2,1)} %copy-done.12, ...), custom_call_target="tpu_custom_call" | custom-call | bytes 3719208 | tf_op jit(solution)/shard_map/close/pallas_call | solution.py:138
  199.6 3.0 %collective-permute-done.52.refs_1_ = bf16[64,256]{1,0:T(8,128)(2,1)S(1)} collective-permute-done((bf16[64,256]{1,0:T(8,128)(2,1)S(1)}, bf16[64,256]{1,0:T(8,128)(2,1)S(1)}, u32[]{:S(2)}, u32[]{:S(2)}) %collective-permute-start.52) | collective-permute-done | bytes 32800 | tf_op jit(solution)/shard_map/ppermute | solution.py:23
  202.6 2.1 collective-permute-done.53.refs_4_
  204.7 1.9 end.1
  (129 shorter events, 34.4 us)
Async XLA Ops:
  4.8 4.5 %collective-permute-start.1 = (f32[8,128]{1,0:T(8,128)S(1)}, f32[8,128]{1,0:T(8,128)S(1)}, u32[]{:S(2)}, u32[]{:S(2)}) collective-permute-start(f32[8,128]{1,0:T(8,128)S(1)} %add_select_fusion.3), channel_id=1, source_target_pairs={{0,4},{2,6},{4,0},{6,2},{8,12},{10,14},{12,8},{14,10},{1,5},{3,7},... | collective-permute-start | bytes 12296 | tf_op jit(solution)/shard_map/ppermute | solution.py:23
  9.4 4.6 %collective-permute-start.2 = (f32[8,128]{1,0:T(8,128)S(1)}, f32[8,128]{1,0:T(8,128)S(1)}, u32[]{:S(2)}, u32[]{:S(2)}) collective-permute-start(f32[8,128]{1,0:T(8,128)S(1)} %add_select_fusion.2), channel_id=1, source_target_pairs={{0,8},{2,10},{4,12},{6,14},{8,0},{10,2},{12,4},{14,6},{1,9},{3,11}... | collective-permute-start | bytes 12296 | tf_op jit(solution)/shard_map/ppermute | solution.py:23
  12.4 5.4 %collective-permute-start.4 = (bf16[2,48,128]{2,1,0:T(8,128)(2,1)S(1)}, bf16[2,48,128]{2,1,0:T(8,128)(2,1)S(1)}, u32[]{:S(2)}, u32[]{:S(2)}) collective-permute-start(bf16[2,48,128]{2,1,0:T(8,128)(2,1)S(1)} %get-tuple-element.136), channel_id=1, source_target_pairs={{14,0},{0,2},{2,4},{4,6},{6,8},{8,10},{10,12},{12,14},{15,1},{1,3}... | collective-permute-start | bytes 73736 | tf_op jit(solution)/shard_map/ppermute | solution.py:29
  12.4 55.2 %collective-permute-start.20 = (bf16[512,1024]{1,0:T(8,128)(2,1)}, bf16[512,1024]{1,0:T(8,128)(2,1)S(1)}, u32[]{:S(2)}, u32[]{:S(2)}) collective-permute-start(bf16[512,1024]{1,0:T(8,128)(2,1)} %refs_6_.1), channel_id=1, source_target_pairs={{0,1},{1,0},{2,3},{3,2},{4,5},{5,4},{6,7},{7,6},{8,9},{9,8},{10,11... | collective-permute-start | bytes 3145736 | tf_op jit(solution)/shard_map/ppermute | solution.py:23
  14.1 3.6 %collective-permute-start.3 = (f32[8,128]{1,0:T(8,128)S(1)}, f32[8,128]{1,0:T(8,128)S(1)}, u32[]{:S(2)}, u32[]{:S(2)}) collective-permute-start(f32[8,128]{1,0:T(8,128)S(1)} %add_select_fusion.1), channel_id=1, source_target_pairs={{0,16},{16,0},{1,17},{17,1},{2,18},{18,2},{3,19},{19,3},{4,20},{20... | collective-permute-start | bytes 12296 | tf_op jit(solution)/shard_map/ppermute | solution.py:23
  22.7 16.4 %collective-permute-start.6 = (bf16[2,3,128,128]{3,2,1,0:T(8,128)(2,1)S(1)}, bf16[2,3,128,128]{3,2,1,0:T(8,128)(2,1)S(1)}, u32[]{:S(2)}, u32[]{:S(2)}) collective-permute-start(bf16[2,3,128,128]{3,2,1,0:T(8,128)(2,1)S(1)} %get-tuple-element.139), channel_id=1, source_target_pairs={{0,8},{2,10},{4,12},{6,14},{8,0},{10,2},{12,4},{14,6},{1,9},{3,11}... | collective-permute-start | bytes 589832 | tf_op jit(solution)/shard_map/ppermute | solution.py:23
  25.6 13.4 %collective-permute-start.7 = (bf16[2,3,128,128]{3,2,1,0:T(8,128)(2,1)S(1)}, bf16[2,3,128,128]{3,2,1,0:T(8,128)(2,1)S(1)}, u32[]{:S(2)}, u32[]{:S(2)}) collective-permute-start(bf16[2,3,128,128]{3,2,1,0:T(8,128)(2,1)S(1)} %get-tuple-element.140), channel_id=1, source_target_pairs={{0,12},{2,14},{4,8},{6,10},{8,4},{10,6},{12,0},{14,2},{1,13},{3,15... | collective-permute-start | bytes 589832 | tf_op jit(solution)/shard_map/ppermute | solution.py:23
  27.0 13.4 %collective-permute-start.5 = (bf16[2,3,128,128]{3,2,1,0:T(8,128)(2,1)S(1)}, bf16[2,3,128,128]{3,2,1,0:T(8,128)(2,1)S(1)}, u32[]{:S(2)}, u32[]{:S(2)}) collective-permute-start(bf16[2,3,128,128]{3,2,1,0:T(8,128)(2,1)S(1)} %get-tuple-element.138), channel_id=1, source_target_pairs={{0,4},{2,6},{4,0},{6,2},{8,12},{10,14},{12,8},{14,10},{1,5},{3,7},... | collective-permute-start | bytes 589832 | tf_op jit(solution)/shard_map/ppermute | solution.py:23
  27.2 13.2 %collective-permute-start.8 = (bf16[2,3,128,128]{3,2,1,0:T(8,128)(2,1)S(1)}, bf16[2,3,128,128]{3,2,1,0:T(8,128)(2,1)S(1)}, u32[]{:S(2)}, u32[]{:S(2)}) collective-permute-start(bf16[2,3,128,128]{3,2,1,0:T(8,128)(2,1)S(1)} %get-tuple-element.137.refs_0_), channel_id=1, source_target_pairs={{0,2},{2,0},{4,6},{6,4},{8,10},{10,8},{12,14},{14,12},{1,3},{3,1},... | collective-permute-start | bytes 589832 | tf_op jit(solution)/shard_map/ppermute | solution.py:23
  48.5 11.6 %collective-permute-start.13 = (bf16[2,128,128]{2,1,0:T(8,128)(2,1)S(1)}, bf16[2,128,128]{2,1,0:T(8,128)(2,1)S(1)}, u32[]{:S(2)}, u32[]{:S(2)}) collective-permute-start(bf16[2,128,128]{2,1,0:T(8,128)(2,1)S(1)} %get-tuple-element.146), channel_id=1, source_target_pairs={{0,4},{2,6},{4,0},{6,2},{8,12},{10,14},{12,8},{14,10},{1,5},{3,7},... | collective-permute-start | bytes 196616 | tf_op jit(solution)/shard_map/ppermute | solution.py:23
  52.2 9.4 %collective-permute-start.14 = (bf16[2,128,128]{2,1,0:T(8,128)(2,1)S(1)}, bf16[2,128,128]{2,1,0:T(8,128)(2,1)S(1)}, u32[]{:S(2)}, u32[]{:S(2)}) collective-permute-start(bf16[2,128,128]{2,1,0:T(8,128)(2,1)S(1)} %get-tuple-element.147), channel_id=1, source_target_pairs={{0,8},{2,10},{4,12},{6,14},{8,0},{10,2},{12,4},{14,6},{1,9},{3,11}... | collective-permute-start | bytes 196616 | tf_op jit(solution)/shard_map/ppermute | solution.py:23
  52.5 9.7 %collective-permute-start.15 = (bf16[2,128,128]{2,1,0:T(8,128)(2,1)S(1)}, bf16[2,128,128]{2,1,0:T(8,128)(2,1)S(1)}, u32[]{:S(2)}, u32[]{:S(2)}) collective-permute-start(bf16[2,128,128]{2,1,0:T(8,128)(2,1)S(1)} %get-tuple-element.148), channel_id=1, source_target_pairs={{0,12},{2,14},{4,8},{6,10},{8,4},{10,6},{12,0},{14,2},{1,13},{3,15... | collective-permute-start | bytes 196616 | tf_op jit(solution)/shard_map/ppermute | solution.py:23
  59.5 5.2 %collective-permute-start.16 = (bf16[2,128,128]{2,1,0:T(8,128)(2,1)}, bf16[2,128,128]{2,1,0:T(8,128)(2,1)S(1)}, u32[]{:S(2)}, u32[]{:S(2)}) collective-permute-start(bf16[2,128,128]{2,1,0:T(8,128)(2,1)} %pin.6.refs_1_), channel_id=1, source_target_pairs={{0,1},{1,0},{2,3},{3,2},{4,5},{5,4},{6,7},{7,6},{8,9},{9,8},{10,11... | collective-permute-start | bytes 196616 | tf_op jit(solution)/shard_map/ppermute | solution.py:23
  60.1 6.1 %collective-permute-start.17 = (bf16[2,128,128]{2,1,0:T(8,128)(2,1)S(1)}, bf16[2,128,128]{2,1,0:T(8,128)(2,1)S(1)}, u32[]{:S(2)}, u32[]{:S(2)}) collective-permute-start(bf16[2,128,128]{2,1,0:T(8,128)(2,1)S(1)} %collective-permute-done.13.refs_2_), channel_id=1, source_target_pairs={{0,1},{1,0},{2,3},{3,2},{4,5},{5,4},{6,7},{7,6},{8,9},{9,8},{10,11... | collective-permute-start | bytes 196616 | tf_op jit(solution)/shard_map/ppermute | solution.py:23
  61.6 5.4 %collective-permute-start.18 = (bf16[2,128,128]{2,1,0:T(8,128)(2,1)S(1)}, bf16[2,128,128]{2,1,0:T(8,128)(2,1)S(1)}, u32[]{:S(2)}, u32[]{:S(2)}) collective-permute-start(bf16[2,128,128]{2,1,0:T(8,128)(2,1)S(1)} %collective-permute-done.14.refs_3_), channel_id=1, source_target_pairs={{0,1},{1,0},{2,3},{3,2},{4,5},{5,4},{6,7},{7,6},{8,9},{9,8},{10,11... | collective-permute-start | bytes 196616 | tf_op jit(solution)/shard_map/ppermute | solution.py:23
  62.1 5.5 %collective-permute-start.19 = (bf16[2,128,128]{2,1,0:T(8,128)(2,1)S(1)}, bf16[2,128,128]{2,1,0:T(8,128)(2,1)S(1)}, u32[]{:S(2)}, u32[]{:S(2)}) collective-permute-start(bf16[2,128,128]{2,1,0:T(8,128)(2,1)S(1)} %collective-permute-done.15.refs_4_), channel_id=1, source_target_pairs={{0,1},{1,0},{2,3},{3,2},{4,5},{5,4},{6,7},{7,6},{8,9},{9,8},{10,11... | collective-permute-start | bytes 196616 | tf_op jit(solution)/shard_map/ppermute | solution.py:23
  76.1 4.2 %collective-permute-start.22 = (bf16[256,2048]{1,0:T(8,128)(2,1)}, bf16[256,2048]{1,0:T(8,128)(2,1)S(1)}, u32[]{:S(2)}, u32[]{:S(2)}) collective-permute-start(bf16[256,2048]{1,0:T(8,128)(2,1)} %get-tuple-element.155.refs_3_), channel_id=1, source_target_pairs={{0,2},{2,0},{4,6},{6,4},{8,10},{10,8},{12,14},{14,12},{1,3},{3,1},... | collective-permute-start | bytes 3145736 | tf_op jit(solution)/shard_map/ppermute | solution.py:23
  76.2 4.1 %collective-permute-start.24 = (bf16[256,1024]{1,0:T(8,128)(2,1)}, bf16[256,1024]{1,0:T(8,128)(2,1)S(1)}, u32[]{:S(2)}, u32[]{:S(2)}) collective-permute-start(bf16[256,1024]{1,0:T(8,128)(2,1)} %get-tuple-element.157), channel_id=1, source_target_pairs={{0,2},{2,0},{4,6},{6,4},{8,10},{10,8},{12,14},{14,12},{1,3},{3,1},... | collective-permute-start | bytes 1572872 | tf_op jit(solution)/shard_map/ppermute | solution.py:23
  76.7 3.6 %collective-permute-start.21 = (bf16[8,64,256]{2,1,0:T(8,128)(2,1)}, bf16[8,64,256]{2,1,0:T(8,128)(2,1)S(1)}, u32[]{:S(2)}, u32[]{:S(2)}) collective-permute-start(bf16[8,64,256]{2,1,0:T(8,128)(2,1)} %get-tuple-element.154), channel_id=1, source_target_pairs={{0,2},{2,0},{4,6},{6,4},{8,10},{10,8},{12,14},{14,12},{1,3},{3,1},... | collective-permute-start | bytes 786440 | tf_op jit(solution)/shard_map/ppermute | solution.py:23
  76.8 14.3 %collective-permute-start.27 = (bf16[256,1024]{1,0:T(8,128)(2,1)S(1)}, bf16[256,1024]{1,0:T(8,128)(2,1)S(1)}, u32[]{:S(2)}, u32[]{:S(2)}) collective-permute-start(bf16[256,1024]{1,0:T(8,128)(2,1)S(1)} %get-tuple-element.168.refs_3_), channel_id=1, source_target_pairs={{0,1},{1,0},{2,3},{3,2},{4,5},{5,4},{6,7},{7,6},{8,9},{9,8},{10,11... | collective-permute-start | bytes 1572872 | tf_op jit(solution)/shard_map/ppermute | solution.py:23
  79.5 7.6 %collective-permute-start.25 = (bf16[256,512]{1,0:T(8,128)(2,1)}, bf16[256,512]{1,0:T(8,128)(2,1)S(1)}, u32[]{:S(2)}, u32[]{:S(2)}) collective-permute-start(bf16[256,512]{1,0:T(8,128)(2,1)} %get-tuple-element.160.refs_3_), channel_id=1, source_target_pairs={{0,2},{2,0},{4,6},{6,4},{8,10},{10,8},{12,14},{14,12},{1,3},{3,1},... | collective-permute-start | bytes 786440 | tf_op jit(solution)/shard_map/ppermute | solution.py:23
  84.8 19.5 %collective-permute-start.28 = (bf16[4,64,1280]{2,1,0:T(8,128)(2,1)S(1)}, bf16[4,64,1280]{2,1,0:T(8,128)(2,1)S(1)}, u32[]{:S(2)}, u32[]{:S(2)}) collective-permute-start(bf16[4,64,1280]{2,1,0:T(8,128)(2,1)S(1)} %get-tuple-element.172), channel_id=1, source_target_pairs={{0,16},{16,0},{1,17},{17,1},{2,18},{18,2},{3,19},{19,3},{4,20},{20... | collective-permute-start | bytes 1966088 | tf_op jit(solution)/shard_map/ppermute | solution.py:23
  86.3 18.0 %collective-permute-start.29 = (bf16[4,64,1152]{2,1,0:T(8,128)(2,1)}, bf16[4,64,1152]{2,1,0:T(8,128)(2,1)S(1)}, u32[]{:S(2)}, u32[]{:S(2)}) collective-permute-start(bf16[4,64,1152]{2,1,0:T(8,128)(2,1)} %get-tuple-element.174), channel_id=1, source_target_pairs={{0,4},{2,6},{4,0},{6,2},{8,12},{10,14},{12,8},{14,10},{1,5},{3,7},... | collective-permute-start | bytes 1769480 | tf_op jit(solution)/shard_map/ppermute | solution.py:23
  94.1 12.8 %all-to-all-start = ((bf16[4,2,128,128]{3,2,1,0:T(8,128)(2,1)}), bf16[4,2,128,128]{3,2,1,0:T(8,128)(2,1)S(1)}, u32[]{:S(2)}, u32[]{:S(2)}) async-start(bf16[4,2,128,128]{3,2,1,0:T(8,128)(2,1)} %bitcast.21), calls=%async_computation | async-start | bytes 524288 | tf_op jit(solution)/shard_map/all_to_all | solution.py:1259
  97.7 18.4 %collective-permute-start.26 = (bf16[256,1024]{1,0:T(8,128)(2,1)}, bf16[256,1024]{1,0:T(8,128)(2,1)}, u32[]{:S(2)}, u32[]{:S(2)}) collective-permute-start(bf16[256,1024]{1,0:T(8,128)(2,1)} %get-tuple-element.161.refs_2_), channel_id=1, source_target_pairs={{0,1},{1,0},{2,3},{3,2},{4,5},{5,4},{6,7},{7,6},{8,9},{9,8},{10,11... | collective-permute-start | bytes 1572872 | tf_op jit(solution)/shard_map/ppermute | solution.py:23
  107.6 8.9 %collective-permute-start.30 = (bf16[2,64,1664]{2,1,0:T(8,128)(2,1)}, bf16[2,64,1664]{2,1,0:T(8,128)(2,1)}, u32[]{:S(2)}, u32[]{:S(2)}) collective-permute-start(bf16[2,64,1664]{2,1,0:T(8,128)(2,1)} %get-tuple-element.184), channel_id=1, source_target_pairs={{0,4},{2,6},{4,0},{6,2},{8,12},{10,14},{12,8},{14,10},{1,5},{3,7},... | collective-permute-start | bytes 1277960 | tf_op jit(solution)/shard_map/ppermute | solution.py:23
  107.6 8.5 %collective-permute-start.31 = (bf16[2,64,1152]{2,1,0:T(8,128)(2,1)}, bf16[2,64,1152]{2,1,0:T(8,128)(2,1)}, u32[]{:S(2)}, u32[]{:S(2)}) collective-permute-start(bf16[2,64,1152]{2,1,0:T(8,128)(2,1)} %get-tuple-element.185), channel_id=1, source_target_pairs={{0,16},{16,0},{1,17},{17,1},{2,18},{18,2},{3,19},{19,3},{4,20},{20... | collective-permute-start | bytes 884744 | tf_op jit(solution)/shard_map/ppermute | solution.py:23
  120.5 10.4 %collective-permute-start.33 = (bf16[2,3,128,128]{3,2,1,0:T(8,128)(2,1)S(1)}, bf16[2,3,128,128]{3,2,1,0:T(8,128)(2,1)S(1)}, u32[]{:S(2)}, u32[]{:S(2)}) collective-permute-start(bf16[2,3,128,128]{3,2,1,0:T(8,128)(2,1)S(1)} %get-tuple-element.194), channel_id=1, source_target_pairs={{0,4},{2,6},{4,0},{6,2},{8,12},{10,14},{12,8},{14,10},{1,5},{3,7},... | collective-permute-start | bytes 589832 | tf_op jit(solution)/shard_map/ppermute | solution.py:23
  122.2 17.1 %collective-permute-start.34 = (bf16[2,3,128,128]{3,2,1,0:T(8,128)(2,1)S(1)}, bf16[2,3,128,128]{3,2,1,0:T(8,128)(2,1)S(1)}, u32[]{:S(2)}, u32[]{:S(2)}) collective-permute-start(bf16[2,3,128,128]{3,2,1,0:T(8,128)(2,1)S(1)} %get-tuple-element.195), channel_id=1, source_target_pairs={{0,8},{2,10},{4,12},{6,14},{8,0},{10,2},{12,4},{14,6},{1,9},{3,11}... | collective-permute-start | bytes 589832 | tf_op jit(solution)/shard_map/ppermute | solution.py:23
  123.1 16.2 %collective-permute-start.35 = (bf16[2,3,128,128]{3,2,1,0:T(8,128)(2,1)S(1)}, bf16[2,3,128,128]{3,2,1,0:T(8,128)(2,1)S(1)}, u32[]{:S(2)}, u32[]{:S(2)}) collective-permute-start(bf16[2,3,128,128]{3,2,1,0:T(8,128)(2,1)S(1)} %get-tuple-element.196), channel_id=1, source_target_pairs={{0,12},{2,14},{4,8},{6,10},{8,4},{10,6},{12,0},{14,2},{1,13},{3,15... | collective-permute-start | bytes 589832 | tf_op jit(solution)/shard_map/ppermute | solution.py:23
  142.0 5.8 %collective-permute-start.39 = (bf16[256,1536]{1,0:T(8,128)(2,1)}, bf16[256,1536]{1,0:T(8,128)(2,1)}, u32[]{:S(2)}, u32[]{:S(2)}) collective-permute-start(bf16[256,1536]{1,0:T(8,128)(2,1)} %get-tuple-element.212.refs_3_), channel_id=1, source_target_pairs={{0,2},{2,0},{4,6},{6,4},{8,10},{10,8},{12,14},{14,12},{1,3},{3,1},... | collective-permute-start | bytes 2359304 | tf_op jit(solution)/shard_map/ppermute | solution.py:23
  142.0 14.5 %collective-permute-start.36 = (bf16[256,1024]{1,0:T(8,128)(2,1)}, bf16[256,1024]{1,0:T(8,128)(2,1)S(1)}, u32[]{:S(2)}, u32[]{:S(2)}) collective-permute-start(bf16[256,1024]{1,0:T(8,128)(2,1)} %get-tuple-element.201.refs_3_), channel_id=1, source_target_pairs={{0,1},{1,0},{2,3},{3,2},{4,5},{5,4},{6,7},{7,6},{8,9},{9,8},{10,11... | collective-permute-start | bytes 1572872 | tf_op jit(solution)/shard_map/ppermute | solution.py:23
  142.9 9.1 %collective-permute-start.37 = (bf16[8,64,256]{2,1,0:T(8,128)(2,1)}, bf16[8,64,256]{2,1,0:T(8,128)(2,1)}, u32[]{:S(2)}, u32[]{:S(2)}) collective-permute-start(bf16[8,64,256]{2,1,0:T(8,128)(2,1)} %get-tuple-element.205), channel_id=1, source_target_pairs={{0,2},{2,0},{4,6},{6,4},{8,10},{10,8},{12,14},{14,12},{1,3},{3,1},... | collective-permute-start | bytes 786440 | tf_op jit(solution)/shard_map/ppermute | solution.py:23
  143.1 8.9 %collective-permute-start.38 = (bf16[8,64,256]{2,1,0:T(8,128)(2,1)}, bf16[8,64,256]{2,1,0:T(8,128)(2,1)S(1)}, u32[]{:S(2)}, u32[]{:S(2)}) collective-permute-start(bf16[8,64,256]{2,1,0:T(8,128)(2,1)} %get-tuple-element.210), channel_id=1, source_target_pairs={{0,2},{2,0},{4,6},{6,4},{8,10},{10,8},{12,14},{14,12},{1,3},{3,1},... | collective-permute-start | bytes 786440 | tf_op jit(solution)/shard_map/ppermute | solution.py:23
  143.4 25.3 %collective-permute-start.42 = (bf16[64,3584]{1,0:T(8,128)(2,1)}, bf16[64,3584]{1,0:T(8,128)(2,1)S(1)}, u32[]{:S(2)}, u32[]{:S(2)}) collective-permute-start(bf16[64,3584]{1,0:T(8,128)(2,1)} %get-tuple-element.222), channel_id=1, source_target_pairs={{0,8},{2,10},{4,12},{6,14},{8,0},{10,2},{12,4},{14,6},{1,9},{3,11}... | collective-permute-start | bytes 1376264 | tf_op jit(solution)/shard_map/ppermute | solution.py:23
  151.2 22.0 %collective-permute-start.40 = (bf16[4,64,896]{2,1,0:T(8,128)(2,1)S(1)}, bf16[4,64,896]{2,1,0:T(8,128)(2,1)S(1)}, u32[]{:S(2)}, u32[]{:S(2)}) collective-permute-start(bf16[4,64,896]{2,1,0:T(8,128)(2,1)S(1)} %get-tuple-element.218), channel_id=1, source_target_pairs={{0,16},{16,0},{1,17},{17,1},{2,18},{18,2},{3,19},{19,3},{4,20},{20... | collective-permute-start | bytes 1376264 | tf_op jit(solution)/shard_map/ppermute | solution.py:23
  154.7 18.5 %collective-permute-start.43 = (bf16[4,64,768]{2,1,0:T(8,128)(2,1)}, bf16[4,64,768]{2,1,0:T(8,128)(2,1)S(1)}, u32[]{:S(2)}, u32[]{:S(2)}) collective-permute-start(bf16[4,64,768]{2,1,0:T(8,128)(2,1)} %get-tuple-element.224), channel_id=1, source_target_pairs={{0,16},{16,0},{1,17},{17,1},{2,18},{18,2},{3,19},{19,3},{4,20},{20... | collective-permute-start | bytes 1179656 | tf_op jit(solution)/shard_map/ppermute | solution.py:23
  156.0 17.2 %collective-permute-start.41 = (bf16[4,64,640]{2,1,0:T(8,128)(2,1)S(1)}, bf16[4,64,640]{2,1,0:T(8,128)(2,1)S(1)}, u32[]{:S(2)}, u32[]{:S(2)}) collective-permute-start(bf16[4,64,640]{2,1,0:T(8,128)(2,1)S(1)} %get-tuple-element.220), channel_id=1, source_target_pairs={{0,4},{2,6},{4,0},{6,2},{8,12},{10,14},{12,8},{14,10},{1,5},{3,7},... | collective-permute-start | bytes 983048 | tf_op jit(solution)/shard_map/ppermute | solution.py:23
  160.5 8.2 %collective-permute-start.44 = (bf16[8,64,256]{2,1,0:T(8,128)(2,1)S(1)}, bf16[8,64,256]{2,1,0:T(8,128)(2,1)S(1)}, u32[]{:S(2)}, u32[]{:S(2)}) collective-permute-start(bf16[8,64,256]{2,1,0:T(8,128)(2,1)S(1)} %get-tuple-element.226), channel_id=1, source_target_pairs={{0,2},{2,0},{4,6},{6,4},{8,10},{10,8},{12,14},{14,12},{1,3},{3,1},... | collective-permute-start | bytes 786440 | tf_op jit(solution)/shard_map/ppermute | solution.py:23
  176.1 11.5 %collective-permute-start.47 = (bf16[2,64,1920]{2,1,0:T(8,128)(2,1)S(1)}, bf16[2,64,1920]{2,1,0:T(8,128)(2,1)S(1)}, u32[]{:S(2)}, u32[]{:S(2)}) collective-permute-start(bf16[2,64,1920]{2,1,0:T(8,128)(2,1)S(1)} %get-tuple-element.234), channel_id=1, source_target_pairs={{0,16},{16,0},{1,17},{17,1},{2,18},{18,2},{3,19},{19,3},{4,20},{20... | collective-permute-start | bytes 1474568 | tf_op jit(solution)/shard_map/ppermute | solution.py:23
  176.8 10.7 %collective-permute-start.46 = (bf16[2,64,896]{2,1,0:T(8,128)(2,1)S(1)}, bf16[2,64,896]{2,1,0:T(8,128)(2,1)S(1)}, u32[]{:S(2)}, u32[]{:S(2)}) collective-permute-start(bf16[2,64,896]{2,1,0:T(8,128)(2,1)S(1)} %get-tuple-element.232), channel_id=1, source_target_pairs={{0,4},{2,6},{4,0},{6,2},{8,12},{10,14},{12,8},{14,10},{1,5},{3,7},... | collective-permute-start | bytes 688136 | tf_op jit(solution)/shard_map/ppermute | solution.py:23
  176.8 10.7 %collective-permute-start.48 = (bf16[2,64,768]{2,1,0:T(8,128)(2,1)S(1)}, bf16[2,64,768]{2,1,0:T(8,128)(2,1)S(1)}, u32[]{:S(2)}, u32[]{:S(2)}) collective-permute-start(bf16[2,64,768]{2,1,0:T(8,128)(2,1)S(1)} %get-tuple-element.236), channel_id=1, source_target_pairs={{0,8},{2,10},{4,12},{6,14},{8,0},{10,2},{12,4},{14,6},{1,9},{3,11}... | collective-permute-start | bytes 589832 | tf_op jit(solution)/shard_map/ppermute | solution.py:23
  179.1 6.1 %collective-permute-start.45 = (bf16[2,48,128]{2,1,0:T(8,128)(2,1)}, bf16[2,48,128]{2,1,0:T(8,128)(2,1)S(1)}, u32[]{:S(2)}, u32[]{:S(2)}) collective-permute-start(bf16[2,48,128]{2,1,0:T(8,128)(2,1)} %pin.10), channel_id=1, source_target_pairs={{2,0},{4,2},{6,4},{8,6},{10,8},{12,10},{14,12},{0,14},{3,1},{5,3},... | collective-permute-start | bytes 73736 | tf_op jit(solution)/shard_map/ppermute | solution.py:29
  189.9 7.0 %collective-permute-start.50 = (bf16[2,64,1536]{2,1,0:T(8,128)(2,1)}, bf16[2,64,1536]{2,1,0:T(8,128)(2,1)S(1)}, u32[]{:S(2)}, u32[]{:S(2)}) collective-permute-start(bf16[2,64,1536]{2,1,0:T(8,128)(2,1)} %get-tuple-element.239.refs_8_), channel_id=1, source_target_pairs={{0,2},{2,0},{4,6},{6,4},{8,10},{10,8},{12,14},{14,12},{1,3},{3,1},... | collective-permute-start | bytes 1179656 | tf_op jit(solution)/shard_map/ppermute | solution.py:23
  189.9 14.8 %collective-permute-start.53 = (bf16[64,1792]{1,0:T(8,128)(2,1)S(1)}, bf16[64,1792]{1,0:T(8,128)(2,1)S(1)}, u32[]{:S(2)}, u32[]{:S(2)}) collective-permute-start(bf16[64,1792]{1,0:T(8,128)(2,1)S(1)} %get-tuple-element.245), channel_id=1, source_target_pairs={{0,8},{2,10},{4,12},{6,14},{8,0},{10,2},{12,4},{14,6},{1,9},{3,11}... | collective-permute-start | bytes 688136 | tf_op jit(solution)/shard_map/ppermute | solution.py:23
  191.1 5.7 %collective-permute-start.49 = (bf16[128,512]{1,0:T(8,128)(2,1)}, bf16[128,512]{1,0:T(8,128)(2,1)S(1)}, u32[]{:S(2)}, u32[]{:S(2)}) collective-permute-start(bf16[128,512]{1,0:T(8,128)(2,1)} %pin.11), channel_id=1, source_target_pairs={{0,16},{16,0},{1,17},{17,1},{2,18},{18,2},{3,19},{19,3},{4,20},{20... | collective-permute-start | bytes 393224 | tf_op jit(solution)/shard_map/ppermute | solution.py:23
  192.4 10.3 %collective-permute-start.51 = (bf16[64,1024]{1,0:T(8,128)(2,1)S(1)}, bf16[64,1024]{1,0:T(8,128)(2,1)S(1)}, u32[]{:S(2)}, u32[]{:S(2)}) collective-permute-start(bf16[64,1024]{1,0:T(8,128)(2,1)S(1)} %get-tuple-element.241), channel_id=1, source_target_pairs={{0,4},{2,6},{4,0},{6,2},{8,12},{10,14},{12,8},{14,10},{1,5},{3,7},... | collective-permute-start | bytes 393224 | tf_op jit(solution)/shard_map/ppermute | solution.py:23
  193.8 8.8 %collective-permute-start.52 = (bf16[64,256]{1,0:T(8,128)(2,1)S(1)}, bf16[64,256]{1,0:T(8,128)(2,1)S(1)}, u32[]{:S(2)}, u32[]{:S(2)}) collective-permute-start(bf16[64,256]{1,0:T(8,128)(2,1)S(1)} %get-tuple-element.242), channel_id=1, source_target_pairs={{0,12},{2,14},{4,8},{6,10},{8,4},{10,6},{12,0},{14,2},{1,13},{3,15... | collective-permute-start | bytes 98312 | tf_op jit(solution)/shard_map/ppermute | solution.py:23
  (22 other events, 171.7 us)
